TPU v7x, 512 devices: a whole 4x8x8 slice. The times are simulated.
512 devices in a mesh: dp: 32 (over x, z_lo, core), fsdp: 16 (over z_hi, y).
Axes of the slice: x: 4, y: 8, z: 8 (z_hi: 2, z_lo: 4; z = z_hi * 4 + z_lo), core: 2. Of those that a mesh axis runs over, the one named last changes fastest.
Arguments:
- hidden: bfloat16 [4096, 1536], P('dp', 'fsdp'), may hold values from -0.5 to 0.5
- teacher: bfloat16 [4096, 4096], P('dp', 'fsdp'), may hold values from -40 to 40
- projector: bfloat16 [1536, 1536], P('fsdp'), may hold values from -0.15625 to 0.15625
Outputs:
- grad_hidden: float32 [4096, 1536], P('dp', 'fsdp')
- grad_proj: float32 [1536, 1536], P('fsdp')
- loss: float32 [], replicated
All inputs are finite; a program needn't handle non-finite values.
Results may differ from a plain program's by a relative error of at most 0.0085.
The roundings to bfloat16 on the way count: a program that leaves them out, or rounds other values in their place, can miss the bound.
Values may be sent and summed in bfloat16 or wider, within the bound.
No kernel may reach another device: no remote copies, remote signals or barrier semaphores. Data moves between devices by JAX's collectives and lax.ppermute only.
A program may use at most 64 MiB of HBM per device.

v0:
```python
import jax
import jax.numpy as jnp
from jax import lax
from jax.sharding import PartitionSpec as P

EPSILON = 1e-06
HIGHEST = lax.Precision.HIGHEST


def radial_sum(unit_f, grad_unit):
    return lax.psum(jnp.sum(unit_f * grad_unit, axis=1), "fsdp")


def body(hidden, teacher, projector):
    row_count = hidden.shape[0]
    width_local = hidden.shape[1]
    contract = (((1,), (1,)), ((), ()))
    rows_first = (((0,), (0,)), ((), ()))
    width_cross = (((0,), (1,)), ((), ()))
    embed = lax.psum_scatter(
        lax.dot_general(projector, hidden, width_cross, preferred_element_type=jnp.float32),
        "fsdp",
        scatter_dimension=0,
        tiled=True,
    ).T
    teach_f = teacher.astype(jnp.float32)
    sq_student, sq_teacher = lax.psum(
        (jnp.sum(embed * embed, axis=1), jnp.sum(teach_f * teach_f, axis=1)), "fsdp"
    )
    inv_student = lax.rsqrt(sq_student + EPSILON)[:, None]
    unit_f = embed * inv_student
    student = unit_f.astype(jnp.bfloat16)
    target = (teach_f * lax.rsqrt(sq_teacher + EPSILON)[:, None]).astype(jnp.bfloat16)
    upper = jnp.concatenate([student, target], axis=1)
    lower = jnp.concatenate([student, -target], axis=1)
    lower_all = lax.all_gather(lower, "dp", axis=0, tiled=True)
    partial_value = lax.dot_general(upper, lower_all, contract, preferred_element_type=jnp.float32)
    differ = lax.psum(partial_value, "fsdp")
    squares = jnp.sum(differ * differ)
    grad_unit = 4.0 * jnp.dot(
        differ,
        lower_all[:, :width_local].astype(jnp.float32),
        precision=HIGHEST,
        preferred_element_type=jnp.float32,
    )
    radial = radial_sum(unit_f, grad_unit)
    grad_embed = (inv_student * (grad_unit - unit_f * radial[:, None])).astype(jnp.bfloat16)
    piece = lax.all_gather(grad_embed, "fsdp", axis=1, tiled=True)
    hidden_acc = lax.dot_general(piece, projector, contract, preferred_element_type=jnp.float32)
    proj_piece = lax.dot_general(hidden, piece, rows_first, preferred_element_type=jnp.float32)
    grad_proj, squares_all = lax.psum((proj_piece, squares), "dp")
    loss = squares_all / (row_count * lax.axis_size("dp"))
    return (hidden_acc, grad_proj, loss)


def solution(mesh):
    placed = (P("dp", "fsdp"), P("dp", "fsdp"), P("fsdp", None))
    return jax.shard_map(
        body,
        mesh=mesh,
        in_specs=placed,
        out_specs=(P("dp", "fsdp"), P("fsdp", None), P()),
        check_vma=False,
    )
```

profile of v0, /device:TPU:1, one launch (start us, length us, event | category | flops | bytes accessed | tf_op | source)
XLA Modules:
  0.0 944.0 jit_solution(3194999770944170075)
XLA Ops:
  7.2 0.0 copy-start
  7.2 0.0 copy-start.3
  7.2 0.0 reduce-scatter.2.cloned.1.call-start
  7.2 0.9 copy-done
  8.1 1.9 fusion.12
  10.0 0.0 reduce-scatter.2.cloned.1.call-update
  10.1 0.0 all-gather.2.cloned.1.call-start
  10.1 0.9 fusion.1
  11.1 226.2 %reduce-scatter.2.cloned.1.call-done = f32[96,128]{1,0:T(8,128)} async-done(((f32[1536,128]{1,0:T(8,128)}), f32[96,128]{1,0:T(8,128)}) %reduce-scatter.2.cloned.1.call-update) | async-done | bytes 49168 | tf_op jit(solution)/shard_map/reduce_scatter | solution.py:20
  237.2 0.8 multiply_reduce_fusion.1
  238.0 41.6 %all-reduce = (f32[128]{0:T(128)S(1)}, f32[128]{0:T(128)S(1)}) all-reduce(f32[128]{0:T(128)S(1)} %multiply_reduce_fusion.1, f32[128]{0:T(128)S(1)} %fusion.1), channel_id=1, replica_groups=mesh['dp'=32,'fsdp'=16] {'fsdp'}, use_global_device_ids=true, to_apply=%region_2.0 | all-reduce | flops 256 | bytes 2048 | tf_op jit(solution)/shard_map/psum | solution.py:27
  279.7 0.8 bitcast_convert_fusion
  280.5 0.1 copy.6
  280.6 0.0 copy-done.3
  280.6 0.1 fusion.10
  280.7 0.7 pad_maximum_fusion
  281.4 0.0 all-gather.2.cloned.1.call-update
  281.4 0.0 all-reduce.4.cloned.1.call-start
  281.5 72.4 %all-gather.2.cloned.1.call-done = bf16[4096,352]{1,0:T(8,128)(2,1)} async-done(((bf16[128,352]{1,0:T(8,128)(2,1)}), bf16[4096,352]{1,0:T(8,128)(2,1)}) %all-gather.2.cloned.1.call-update) | async-done | bytes 2883600 | tf_op jit(solution)/shard_map/all_gather | solution.py:36
  353.9 4.4 fusion.3
  358.3 0.0 copy-start.2
  358.3 0.0 all-reduce.4.cloned.1.call-update
  358.4 0.0 copy-start.4
  358.4 0.0 all-reduce.6.cloned.1.call-start
  358.4 195.2 %all-reduce.4.cloned.1.call-done = f32[128,4096]{1,0:T(8,128)} async-done(((f32[128,4096]{1,0:T(8,128)}), f32[128,4096]{1,0:T(8,128)}) %all-reduce.4.cloned.1.call-update) | async-done | bytes 2097168 | tf_op jit(solution)/shard_map/psum | solution.py:38
  553.6 0.0 copy-done.2
  553.6 0.0 copy-start.1
  553.6 3.5 fusion.5
  557.1 45.6 %psum.45 = f32[128]{0:T(128)S(1)} all-reduce(f32[128]{0:T(128)S(1)} %get-tuple-element.7), channel_id=1, replica_groups=mesh['dp'=32,'fsdp'=16] {'fsdp'}, use_global_device_ids=true, to_apply=%region_7.0 | all-reduce | flops 128 | bytes 1024 | tf_op jit(solution)/shard_map/psum | solution.py:11
  602.7 41.7 %all_gather.7 = bf16[128,1536]{0,1:T(8,128)(2,1)S(1)} all-gather(bf16[128,96]{0,1:T(8,128)(2,1)S(1)} %fusion.8), channel_id=1, replica_groups=mesh['dp'=32,'fsdp'=16] {'fsdp'}, dimensions={1}, use_global_device_ids=true | all-gather | bytes 417792 | tf_op jit(solution)/shard_map/all_gather | solution.py:48
  644.4 0.0 copy-done.4
  644.4 1.1 convolution_bitcast_fusion
  645.5 0.0 all-reduce.6.cloned.1.call-update
  645.5 0.0 copy-done.1
  645.6 1.1 multiply_reduce_fusion
  646.7 92.7 %psum.47 = f32[]{:T(128)} all-reduce(f32[]{:T(128)} %multiply_reduce_fusion), channel_id=1, replica_groups=mesh['dp'=32,'fsdp'=16] {'dp'}, use_global_device_ids=true, to_apply=%region_10.0 | all-reduce | flops 1 | bytes 8 | tf_op jit(solution)/shard_map/psum | solution.py:51
  740.0 0.8 fusion.13
  740.9 193.5 %all-reduce.6.cloned.1.call-done = f32[96,1536]{1,0:T(8,128)} async-done(((f32[96,1536]{1,0:T(8,128)}), f32[96,1536]{1,0:T(8,128)}) %all-reduce.6.cloned.1.call-update) | async-done | bytes 589840 | tf_op jit(solution)/shard_map/psum | solution.py:51
  934.4 1.9 copy.10
  (2 shorter events, 0.0 us)
Async XLA Ops:
  7.2 1.0 copy-start
  7.2 273.4 %copy-start.3 = (bf16[128,256]{1,0:T(8,128)(2,1)S(1)}, bf16[128,256]{1,0:T(8,128)(2,1)}, u32[]{:S(2)}) copy-start(bf16[128,256]{1,0:T(8,128)(2,1)} %param.4) | copy-start | bytes 196612
  7.2 230.0 %reduce-scatter.2.cloned.1.call-start = ((), (), s32[]{:S(2)}) async-start(), calls=%async_computation.1 | async-start | bytes 835584 | tf_op jit(solution)/shard_map/reduce_scatter | solution.py:20
  10.1 343.8 %all-gather.2.cloned.1.call-start = ((), (), s32[]{:S(2)}) async-start(), calls=%async_computation.2 | async-start | bytes 3244032 | tf_op jit(solution)/shard_map/all_gather | solution.py:36
  281.4 272.2 %all-reduce.4.cloned.1.call-start = ((), (), s32[]{:S(2)}) async-start(), calls=%async_computation.3 | async-start | bytes 4194304 | tf_op jit(solution)/shard_map/psum | solution.py:38
  358.3 195.3 %copy-start.2 = (f32[96,128]{1,0:T(8,128)S(1)}, f32[96,128]{1,0:T(8,128)}, u32[]{:S(2)}) copy-start(f32[96,128]{1,0:T(8,128)} %reduce-scatter.2.cloned.1.call-done) | copy-start | bytes 147460
  358.4 286.1 %copy-start.4 = (bf16[128,96]{0,1:T(8,128)(2,1)S(1)}, bf16[128,96]{0,1:T(8,128)(2,1)}, u32[]{:S(2)}) copy-start(bf16[128,96]{0,1:T(8,128)(2,1)} %param.3) | copy-start | bytes 73732
  358.4 576.0 %all-reduce.6.cloned.1.call-start = ((), (), s32[]{:S(2)}) async-start(), calls=%async_computation.4 | async-start | bytes 1179648 | tf_op jit(solution)/shard_map/psum | solution.py:51
  553.6 91.9 %copy-start.1 = (f32[128,4096]{1,0:T(8,128)S(1)}, f32[128,4096]{1,0:T(8,128)}, u32[]{:S(2)}) copy-start(f32[128,4096]{1,0:T(8,128)} %all-reduce.4.cloned.1.call-done) | copy-start | bytes 6291460
Sparse Core Ops, SparseCore 0:
  12.5 224.6 reduce-scatter.1
  281.6 72.2 all-gather.1
  358.5 195.0 all-reduce.3
  645.7 288.6 all-reduce.5
where the time goes:
time: 945 us; the launch traced here: 944 us
  waiting for transfers between devices  687 us (73%)
  blocking collectives  222 us (23%)
  between operations  15.6 us (2%)
  matrix products  11.7 us (1%)
    reduce_scatter x1, waiting for transfers between devices, body(): lax.psum_scatter(lax.dot_general(projector, hidden, width_cross, preferre...  226 us
    psum x1, waiting for transfers between devices, body(): differ = lax.psum(partial_value, 'fsdp')  195 us
    psum x1, waiting for transfers between devices, body(): grad_proj, squares_all = lax.psum((proj_piece, squares), 'dp')  193 us
    psum x1, blocking collectives, body(): grad_proj, squares_all = lax.psum((proj_piece, squares), 'dp')  92.7 us
    all_gather x1, waiting for transfers between devices, body(): lower_all = lax.all_gather(lower, 'dp', axis=0, tiled=True)  72.4 us
    psum x1, blocking collectives, radial_sum(): return lax.psum(jnp.sum(unit_f * grad_unit, axis=1), 'fsdp')  45.6 us
    all_gather x1, blocking collectives, body(): piece = lax.all_gather(grad_embed, 'fsdp', axis=1, tiled=True)  41.7 us
    psum x1, blocking collectives, body(): lax.psum((jnp.sum(embed * embed, axis=1), jnp.sum(teach_f * teach_f, axis...  41.6 us
  transfers between devices with their start and end apart: 4, of which 4 were waited for; matrix products, arithmetic and copies ran while one was open for 0% of the time, Pallas kernels for 0%

commit v1 on v0

v1 whole, which is shorter than its diff:
```python
import jax
import jax.numpy as jnp
from jax import lax
from jax.sharding import Mesh
from jax.sharding import PartitionSpec as P

EPSILON = 1e-06
DP = ("x", "zl", "c")
FS = ("zh", "y")
XZ = ("x", "zl")
SIZES = {"x": 4, "zl": 4, "c": 2, "zh": 2, "y": 8}
SWAP = [(0, 1), (1, 0)]
ROWS_T = (((1,), (1,)), ((), ()))
COLS_T = (((0,), (0,)), ((), ()))


def dot(a, b, dims=(((1,), (0,)), ((), ()))):
    return lax.dot_general(a, b, dims, preferred_element_type=jnp.float32)


def group(axes):
    total = 1
    for axis in axes:
        total *= SIZES[axis]
    return total


def exchange(blocks, axes):
    return lax.all_to_all(blocks, axes, split_axis=0, concat_axis=0, tiled=True)


def gather(block, axes):
    copies = jnp.broadcast_to(block[None], (group(axes),) + block.shape)
    return exchange(copies, axes)


def pieces(value):
    high = lax.reduce_precision(value, 8, 7)
    rest = value - high
    middle = lax.reduce_precision(rest, 8, 7)
    low = rest - middle
    return [part.astype(jnp.bfloat16) for part in (high, middle, low)]


def body(hidden, teacher, projector):
    rows, width = hidden.shape
    full = projector.shape[1]
    group_fs, group_xz = group(FS), group(XZ)
    mine = rows // group_fs
    half = width // 2
    place = lax.axis_index(FS)
    core = lax.axis_index("c")

    teach = gather(teacher, FS).astype(jnp.float32)
    sq_teacher = jnp.sum(teach * teach, axis=(0, 2))
    target = (teach * lax.rsqrt(sq_teacher + EPSILON)[None, :, None]).astype(jnp.bfloat16)
    target = target.transpose(1, 0, 2).reshape(rows, -1)
    target_mine = lax.dynamic_slice_in_dim(target, place * mine, mine, 0)

    partial_embed = dot(hidden, projector).reshape(group_fs, mine, full)
    embed = jnp.sum(exchange(partial_embed, FS), axis=0)
    inv_student = lax.rsqrt(jnp.sum(embed * embed, axis=1, keepdims=True) + EPSILON)
    unit = embed * inv_student
    student = unit.astype(jnp.bfloat16)

    both = gather(jnp.concatenate([student, target_mine], axis=1), XZ).reshape(group_xz * mine, -1)
    s_rows, t_rows = both[:, :full], both[:, full:]
    s_here = gather(student, FS).reshape(rows, full)
    s_there = lax.ppermute(s_here, "c", SWAP)
    t_there = lax.ppermute(target, "c", SWAP)
    s_cols = jnp.concatenate([s_here, s_there], axis=0)
    t_cols = jnp.concatenate([target, t_there], axis=0)
    differ = dot(s_rows, s_cols, ROWS_T) - dot(t_rows, t_cols, ROWS_T)
    squares = jnp.sum(differ * differ)
    partial_grad = sum(dot(part, s_cols) for part in pieces(differ)[::-1])
    grad_unit = 4.0 * jnp.sum(
        exchange(partial_grad.reshape(group_xz, mine, full), XZ), axis=0
    )
    radial = jnp.sum(unit * grad_unit, axis=1, keepdims=True)
    grad_embed = (inv_student * (grad_unit - unit * radial)).astype(jnp.bfloat16)

    lane = lax.broadcasted_iota(jnp.int32, (mine, 128), 1)
    tail = jnp.zeros((mine, 128), jnp.bfloat16)
    for index, part in enumerate(pieces(squares)):
        tail = jnp.where(lane == index, part, tail)
    wide = gather(jnp.concatenate([grad_embed, tail], axis=1), FS).reshape(rows, -1)
    wide_there = lax.ppermute(wide, "c", SWAP)
    piece, piece_there = wide[:, :full], wide_there[:, :full]
    grad_hidden = dot(piece, projector, ROWS_T)

    hidden_there = lax.ppermute(hidden, "c", SWAP)
    left = lax.dynamic_slice_in_dim(hidden, core * half, half, 1)
    left_there = lax.dynamic_slice_in_dim(hidden_there, core * half, half, 1)
    proj_piece = dot(left, piece, COLS_T) + dot(left_there, piece_there, COLS_T)

    def loss_of(array):
        return jnp.sum(array.reshape(group_fs, mine, -1)[:, 0, full:].astype(jnp.float32))

    loss_part = loss_of(wide) + loss_of(wide_there)
    blocks = jnp.concatenate(
        [
            proj_piece.reshape(group_xz, half // group_xz, full),
            jnp.broadcast_to(loss_part, (group_xz, 1, full)),
        ],
        axis=1,
    )
    summed = jnp.sum(exchange(blocks, XZ), axis=0)
    loss = summed[-1, 0] / (rows * group(DP))
    grad_proj = lax.all_gather(
        gather(summed[:-1], XZ).reshape(half, full), "c", axis=0, tiled=True
    )
    return (grad_hidden, grad_proj, loss)


def solution(mesh):
    fine = Mesh(mesh.devices.reshape([SIZES[axis] for axis in DP + FS]), DP + FS)
    return jax.shard_map(
        body,
        mesh=fine,
        in_specs=(P(DP, FS), P(DP, FS), P(FS, None)),
        out_specs=(P(DP, FS), P(FS, None), P()),
        check_vma=False,
    )
```

time: 945 us -> 251 us (0.27)
  waiting for transfers between devices: 687 us -> 121 us
  blocking collectives: 222 us -> 42.5 us
  starting transfers between devices: 0.16 us -> 57.8 us
    psum x2 -> x0, waiting for transfers between devices: 389 us -> none  [the longest x1 195 us: body(): differ = lax.psum(partial_value, 'fsdp')]
    reduce_scatter x1 -> x0, waiting for transfers between devices: 226 us -> none  [body(): lax.psum_scatter(lax.dot_general(projector, hidden, width_cross, preferre...]
    psum x3 -> x0, blocking collectives: 180 us -> none  [the longest x1 92.7 us: body(): grad_proj, squares_all = lax.psum((proj_piece, squares), 'dp')]
    all_to_all x0 -> x6, waiting for transfers between devices: none -> 121 us  [exchange(): return lax.all_to_all(blocks, axes, split_axis=0, concat_axis=0, tiled=True)]
    all_gather x1 -> x0, waiting for transfers between devices: 72.4 us -> none  [body(): lower_all = lax.all_gather(lower, 'dp', axis=0, tiled=True)]
    all_to_all x0 -> x6, starting transfers between devices: none -> 44 us  [exchange(): return lax.all_to_all(blocks, axes, split_axis=0, concat_axis=0, tiled=True)]
    all_to_all x0 -> x2, blocking collectives: none -> 38.9 us  [exchange(): return lax.all_to_all(blocks, axes, split_axis=0, concat_axis=0, tiled=True)]
    all_gather x1, blocking collectives: 41.7 us -> 3.64 us  [body(): lax.all_gather(gather(summed[:-1], XZ).reshape(half, full), 'c', axis=0,...]
  transfers between devices with their start and end apart: 4 -> 10, of which waited for: 4 -> 7; matrix products, arithmetic and copies ran while one was open for 0% -> 3% of each run, Pallas kernels for 0% -> 0%
where the time goes in v1:
time: 251 us; the launch traced here: 250 us
  waiting for transfers between devices  121 us (48%)
  starting transfers between devices  57.8 us (23%)
  blocking collectives  42.5 us (17%)
  between operations  8.91 us (4%)
  matrix products  8.84 us (4%)
  local copies, waits for them, and re-layouts  7.43 us (3%)
  other arithmetic  2.74 us (1%)
    all_to_all x6, waiting for transfers between devices, exchange(): return lax.all_to_all(blocks, axes, split_axis=0, concat_axis=0, tiled=True)  121 us
    all_to_all x6, starting transfers between devices, exchange(): return lax.all_to_all(blocks, axes, split_axis=0, concat_axis=0, tiled=True)  44 us
    all_to_all x2, blocking collectives, exchange(): return lax.all_to_all(blocks, axes, split_axis=0, concat_axis=0, tiled=True)  38.9 us
    dot_general x9, matrix products, dot(): return lax.dot_general(a, b, dims, preferred_element_type=jnp.float32)  8.84 us
    ppermute x1, starting transfers between devices, body(): wide_there = lax.ppermute(wide, 'c', SWAP)  5.07 us
  transfers between devices with their start and end apart: 10, of which 7 were waited for; matrix products, arithmetic and copies ran while one was open for 3% of the time, Pallas kernels for 0%

profile of v1, /device:TPU:1, one launch (start us, length us, event | category | flops | bytes accessed | tf_op | source)
XLA Modules:
  0.0 249.8 jit_solution(17274881886913596232)
XLA Ops:
  0.6 0.0 copy-start
  0.6 1.0 copy-done
  1.6 0.0 copy-start.1
  1.6 1.9 convolution_bitcast_fusion
  3.5 16.2 %all-to-all-start = ((f32[16,8,1536]{2,1,0:T(8,128)}), f32[16,8,1536]{2,1,0:T(8,128)S(1)}, u32[]{:S(2)}, u32[]{:S(2)}) async-start(f32[16,8,1536]{2,1,0:T(8,128)} %convolution_bitcast_fusion), calls=%async_computation | async-start | bytes 1572864 | tf_op jit(solution)/shard_map/all_to_all | solution.py:29
  19.7 0.0 copy-done.1
  19.8 0.1 copy.18
  19.9 23.3 %all-to-all-done = f32[16,8,1536]{2,1,0:T(8,128)S(1)} async-done(((f32[16,8,1536]{2,1,0:T(8,128)}), f32[16,8,1536]{2,1,0:T(8,128)S(1)}, u32[]{:S(2)}, u32[]{:S(2)}) %all-to-all-start) | async-done | bytes 786464 | tf_op jit(solution)/shard_map/all_to_all | solution.py:29
  43.1 1.2 broadcast_in_dim.22
  44.3 7.2 %all-to-all-start.1 = ((bf16[16,128,256]{1,2,0:T(8,128)(2,1)}), bf16[16,128,256]{1,2,0:T(8,128)(2,1)S(1)}, u32[]{:S(2)}, u32[]{:S(2)}) async-start(bf16[16,128,256]{1,2,0:T(8,128)(2,1)} %broadcast_in_dim.22), calls=%async_computation.1 | async-start | bytes 2097152 | tf_op jit(solution)/shard_map/all_to_all | solution.py:29
  51.6 0.1 multiply_reduce_fusion.2
  51.8 0.1 multiply_convert_fusion.1
  51.8 29.1 %all-to-all-done.1 = bf16[16,128,256]{1,2,0:T(8,128)(2,1)S(1)} async-done(((bf16[16,128,256]{1,2,0:T(8,128)(2,1)}), bf16[16,128,256]{1,2,0:T(8,128)(2,1)S(1)}, u32[]{:S(2)}, u32[]{:S(2)}) %all-to-all-start.1) | async-done | bytes 1048608 | tf_op jit(solution)/shard_map/all_to_all | solution.py:29
  81.0 0.8 broadcast_in_dim.24
  81.7 8.4 %all-to-all-start.3 = ((bf16[16,8,1536]{2,1,0:T(8,128)(2,1)}), bf16[16,8,1536]{2,1,0:T(8,128)(2,1)S(1)}, u32[]{:S(2)}, u32[]{:S(2)}) async-start(bf16[16,8,1536]{2,1,0:T(8,128)(2,1)} %broadcast_in_dim.24), calls=%async_computation.3 | async-start | bytes 786432 | tf_op jit(solution)/shard_map/all_to_all | solution.py:29
  90.2 0.6 fusion.2
  90.8 0.3 fusion.3
  91.0 0.4 constant_dynamic-slice_fusion
  91.4 0.3 copy.19
  91.7 13.4 %all-to-all-done.3 = bf16[16,8,1536]{2,1,0:T(8,128)(2,1)S(1)} async-done(((bf16[16,8,1536]{2,1,0:T(8,128)(2,1)}), bf16[16,8,1536]{2,1,0:T(8,128)(2,1)S(1)}, u32[]{:S(2)}, u32[]{:S(2)}) %all-to-all-start.3) | async-done | bytes 393248 | tf_op jit(solution)/shard_map/all_to_all | solution.py:29
  105.1 1.2 broadcast_in_dim.23
  106.3 4.9 %all-to-all-start.2 = ((bf16[16,8,5632]{2,1,0:T(8,128)(2,1)}), bf16[16,8,5632]{2,1,0:T(8,128)(2,1)}, u32[]{:S(2)}, u32[]{:S(2)}) async-start(bf16[16,8,5632]{2,1,0:T(8,128)(2,1)} %broadcast_in_dim.23), calls=%async_computation.2 | async-start | bytes 2883584 | tf_op jit(solution)/shard_map/all_to_all | solution.py:29
  111.2 4.9 %collective-permute-start.1 = (bf16[128,4096]{0,1:T(8,128)(2,1)S(1)}, bf16[128,4096]{0,1:T(8,128)(2,1)}, u32[]{:S(2)}, u32[]{:S(2)}) collective-permute-start(bf16[128,4096]{0,1:T(8,128)(2,1)S(1)} %bitcast.22), channel_id=1, source_target_pairs={{0,16},{16,0},{1,17},{17,1},{2,18},{18,2},{3,19},{19,3},{4,20},{20... | collective-permute-start | bytes 3145736 | tf_op jit(solution)/shard_map/ppermute | solution.py:70
  116.1 1.9 collective-permute-start
  118.1 0.5 collective-permute-done.1
  118.5 28.1 %all-to-all-done.2 = bf16[16,8,5632]{2,1,0:T(8,128)(2,1)} async-done(((bf16[16,8,5632]{2,1,0:T(8,128)(2,1)}), bf16[16,8,5632]{2,1,0:T(8,128)(2,1)}, u32[]{:S(2)}, u32[]{:S(2)}) %all-to-all-start.2) | async-done | bytes 1441824 | tf_op jit(solution)/shard_map/all_to_all | solution.py:29
  146.6 2.0 fusion.4
  148.6 0.0 collective-permute-done
  148.6 2.0 multiply_reduce_fusion
  150.6 0.3 fusion.18
  150.9 0.3 fusion.17
  151.2 1.2 fusion.1
  152.3 3.6 %all-to-all-start.4 = ((f32[16,8,1536]{2,1,0:T(8,128)}), f32[16,8,1536]{2,1,0:T(8,128)S(1)}, u32[]{:S(2)}, u32[]{:S(2)}) async-start(f32[16,8,1536]{2,1,0:T(8,128)} %fusion.1), calls=%async_computation.4 | async-start | bytes 1572864 | tf_op jit(solution)/shard_map/all_to_all | solution.py:29
  155.9 0.0 copy-start.2
  160.9 16.3 %all-to-all-done.4 = f32[16,8,1536]{2,1,0:T(8,128)S(1)} async-done(((f32[16,8,1536]{2,1,0:T(8,128)}), f32[16,8,1536]{2,1,0:T(8,128)S(1)}, u32[]{:S(2)}, u32[]{:S(2)}) %all-to-all-start.4) | async-done | bytes 786464 | tf_op jit(solution)/shard_map/all_to_all | solution.py:29
  177.3 0.2 multiply_reduce_fusion.1
  177.5 0.1 multiply_convert_fusion
  177.6 22.0 %all_to_all.40 = bf16[16,8,1664]{2,1,0:T(8,128)(2,1)S(1)} all-to-all(bf16[16,8,1664]{2,1,0:T(8,128)(2,1)S(1)} %broadcast_in_dim.54), channel_id=1, replica_groups=mesh['x'=4,'zl'=4,'c'=2,'zh'=2,'y'=8] {'zh','y'}, dimensions={0} | all-to-all | bytes 851968 | tf_op jit(solution)/shard_map/all_to_all | solution.py:29
  199.6 5.1 %collective-permute-start.3 = (bf16[128,1664]{1,0:T(8,128)(2,1)S(1)}, bf16[128,1664]{1,0:T(8,128)(2,1)S(1)}, u32[]{:S(2)}, u32[]{:S(2)}) collective-permute-start(bf16[128,1664]{1,0:T(8,128)(2,1)S(1)} %bitcast.24), channel_id=1, source_target_pairs={{0,16},{16,0},{1,17},{17,1},{2,18},{18,2},{3,19},{19,3},{4,20},{20... | collective-permute-start | bytes 1277960 | tf_op jit(solution)/shard_map/ppermute | solution.py:87
  204.6 0.0 copy-done.2
  204.7 1.9 collective-permute-start.2
  206.6 0.6 convert_reduce_fusion.1
  207.2 0.2 fusion.11
  207.4 0.0 collective-permute-done.3
  207.4 0.6 convert_reduce_fusion
  208.0 0.0 collective-permute-done.2
  208.0 0.2 convolution_add_fusion.1
  208.2 0.1 reshape.74
  209.6 0.1 concatenate.19
  209.7 17.0 %all_to_all.41 = f32[16,4,1536]{2,1,0:T(4,128)S(1)} all-to-all(f32[16,4,1536]{2,1,0:T(4,128)S(1)} %concatenate.19), channel_id=1, replica_groups=mesh['x'=4,'zl'=4,'c'=2,'zh'=2,'y'=8] {'x','zl'}, dimensions={0} | all-to-all | bytes 786432 | tf_op jit(solution)/shard_map/all_to_all | solution.py:29
  226.7 0.1 reduce_sum.89
  226.7 0.8 broadcast_in_dim.55
  227.5 3.6 %all-to-all-start.7 = ((f32[16,3,1536]{2,1,0:T(4,128)}), f32[16,3,1536]{2,1,0:T(4,128)S(1)}, u32[]{:S(2)}, u32[]{:S(2)}) async-start(f32[16,3,1536]{2,1,0:T(4,128)} %broadcast_in_dim.55), calls=%async_computation.7 | async-start | bytes 786432 | tf_op jit(solution)/shard_map/all_to_all | solution.py:29
  231.2 0.9 fusion.13
  232.1 0.5 slice.39
  233.2 10.8 %all-to-all-done.7 = f32[16,3,1536]{2,1,0:T(4,128)S(1)} async-done(((f32[16,3,1536]{2,1,0:T(4,128)}), f32[16,3,1536]{2,1,0:T(4,128)S(1)}, u32[]{:S(2)}, u32[]{:S(2)}) %all-to-all-start.7) | async-done | bytes 294944 | tf_op jit(solution)/shard_map/all_to_all | solution.py:29
  244.0 0.1 reshape.76
  244.2 3.6 %all_gather.3 = f32[96,1536]{1,0:T(8,128)S(1)} all-gather(f32[48,1536]{1,0:T(8,128)S(1)} %reshape.76), channel_id=1, replica_groups=mesh['x'=4,'zl'=4,'c'=2,'zh'=2,'y'=8] {'c'}, dimensions={0}, use_global_device_ids=true | all-gather | bytes 884736 | tf_op jit(solution)/shard_map/all_gather | solution.py:109
  247.8 0.8 copy.26
  (12 shorter events, 0.2 us)
Async XLA Ops:
  0.6 1.0 copy-start
  1.6 18.1 %copy-start.1 = (bf16[128,256]{1,0:T(8,128)(2,1)S(1)}, bf16[128,256]{1,0:T(8,128)(2,1)}, u32[]{:S(2)}) copy-start(bf16[128,256]{1,0:T(8,128)(2,1)} %param.4) | copy-start | bytes 196612
  3.5 39.6 %all-to-all-start = ((f32[16,8,1536]{2,1,0:T(8,128)}), f32[16,8,1536]{2,1,0:T(8,128)S(1)}, u32[]{:S(2)}, u32[]{:S(2)}) async-start(f32[16,8,1536]{2,1,0:T(8,128)} %convolution_bitcast_fusion), calls=%async_computation | async-start | bytes 1572864 | tf_op jit(solution)/shard_map/all_to_all | solution.py:29
  44.3 36.6 %all-to-all-start.1 = ((bf16[16,128,256]{1,2,0:T(8,128)(2,1)}), bf16[16,128,256]{1,2,0:T(8,128)(2,1)S(1)}, u32[]{:S(2)}, u32[]{:S(2)}) async-start(bf16[16,128,256]{1,2,0:T(8,128)(2,1)} %broadcast_in_dim.22), calls=%async_computation.1 | async-start | bytes 2097152 | tf_op jit(solution)/shard_map/all_to_all | solution.py:29
  81.7 23.4 %all-to-all-start.3 = ((bf16[16,8,1536]{2,1,0:T(8,128)(2,1)}), bf16[16,8,1536]{2,1,0:T(8,128)(2,1)S(1)}, u32[]{:S(2)}, u32[]{:S(2)}) async-start(bf16[16,8,1536]{2,1,0:T(8,128)(2,1)} %broadcast_in_dim.24), calls=%async_computation.3 | async-start | bytes 786432 | tf_op jit(solution)/shard_map/all_to_all | solution.py:29
  106.3 40.3 %all-to-all-start.2 = ((bf16[16,8,5632]{2,1,0:T(8,128)(2,1)}), bf16[16,8,5632]{2,1,0:T(8,128)(2,1)}, u32[]{:S(2)}, u32[]{:S(2)}) async-start(bf16[16,8,5632]{2,1,0:T(8,128)(2,1)} %broadcast_in_dim.23), calls=%async_computation.2 | async-start | bytes 2883584 | tf_op jit(solution)/shard_map/all_to_all | solution.py:29
  111.2 7.3 %collective-permute-start.1 = (bf16[128,4096]{0,1:T(8,128)(2,1)S(1)}, bf16[128,4096]{0,1:T(8,128)(2,1)}, u32[]{:S(2)}, u32[]{:S(2)}) collective-permute-start(bf16[128,4096]{0,1:T(8,128)(2,1)S(1)} %bitcast.22), channel_id=1, source_target_pairs={{0,16},{16,0},{1,17},{17,1},{2,18},{18,2},{3,19},{19,3},{4,20},{20... | collective-permute-start | bytes 3145736 | tf_op jit(solution)/shard_map/ppermute | solution.py:70
  116.1 32.5 %collective-permute-start = (bf16[128,1536]{1,0:T(8,128)(2,1)S(1)}, bf16[128,1536]{1,0:T(8,128)(2,1)S(1)}, u32[]{:S(2)}, u32[]{:S(2)}) collective-permute-start(bf16[128,1536]{1,0:T(8,128)(2,1)S(1)} %bitcast.16), channel_id=1, source_target_pairs={{0,16},{16,0},{1,17},{17,1},{2,18},{18,2},{3,19},{19,3},{4,20},{20... | collective-permute-start | bytes 1179656 | tf_op jit(solution)/shard_map/ppermute | solution.py:69
  152.3 24.9 %all-to-all-start.4 = ((f32[16,8,1536]{2,1,0:T(8,128)}), f32[16,8,1536]{2,1,0:T(8,128)S(1)}, u32[]{:S(2)}, u32[]{:S(2)}) async-start(f32[16,8,1536]{2,1,0:T(8,128)} %fusion.1), calls=%async_computation.4 | async-start | bytes 1572864 | tf_op jit(solution)/shard_map/all_to_all | solution.py:29
  155.9 48.7 %copy-start.2 = (bf16[128,96]{0,1:T(8,128)(2,1)S(1)}, bf16[128,96]{0,1:T(8,128)(2,1)}, u32[]{:S(2)}) copy-start(bf16[128,96]{0,1:T(8,128)(2,1)} %param.3) | copy-start | bytes 73732
  199.6 7.8 %collective-permute-start.3 = (bf16[128,1664]{1,0:T(8,128)(2,1)S(1)}, bf16[128,1664]{1,0:T(8,128)(2,1)S(1)}, u32[]{:S(2)}, u32[]{:S(2)}) collective-permute-start(bf16[128,1664]{1,0:T(8,128)(2,1)S(1)} %bitcast.24), channel_id=1, source_target_pairs={{0,16},{16,0},{1,17},{17,1},{2,18},{18,2},{3,19},{19,3},{4,20},{20... | collective-permute-start | bytes 1277960 | tf_op jit(solution)/shard_map/ppermute | solution.py:87
  204.7 3.4 %collective-permute-start.2 = (bf16[128,96]{0,1:T(8,128)(2,1)S(1)}, bf16[128,96]{0,1:T(8,128)(2,1)S(1)}, u32[]{:S(2)}, u32[]{:S(2)}) collective-permute-start(bf16[128,96]{0,1:T(8,128)(2,1)S(1)} %copy-done.2), channel_id=1, source_target_pairs={{0,16},{16,0},{1,17},{17,1},{2,18},{18,2},{3,19},{19,3},{4,20},{20... | collective-permute-start | bytes 73736 | tf_op jit(solution)/shard_map/ppermute | solution.py:91
  227.5 16.5 %all-to-all-start.7 = ((f32[16,3,1536]{2,1,0:T(4,128)}), f32[16,3,1536]{2,1,0:T(4,128)S(1)}, u32[]{:S(2)}, u32[]{:S(2)}) async-start(f32[16,3,1536]{2,1,0:T(4,128)} %broadcast_in_dim.55), calls=%async_computation.7 | async-start | bytes 786432 | tf_op jit(solution)/shard_map/all_to_all | solution.py:29

commit v2 on v1

--- a/solution.py
+++ b/solution.py
@@ -51,10 +51,13 @@
     place = lax.axis_index(FS)
     core = lax.axis_index("c")
 
-    teach = gather(teacher, FS).astype(jnp.float32)
+    teach_pair = jnp.concatenate([teacher, lax.ppermute(teacher, "zh", SWAP)], axis=1)
+    teach = lax.all_gather(teach_pair, "y", axis=0).astype(jnp.float32)
     sq_teacher = jnp.sum(teach * teach, axis=(0, 2))
     target = (teach * lax.rsqrt(sq_teacher + EPSILON)[None, :, None]).astype(jnp.bfloat16)
     target = target.transpose(1, 0, 2).reshape(rows, -1)
+    hidden_there = lax.ppermute(hidden, "c", SWAP)
+    target, hidden_there = lax.optimization_barrier((target, hidden_there))
     target_mine = lax.dynamic_slice_in_dim(target, place * mine, mine, 0)
 
     partial_embed = dot(hidden, projector).reshape(group_fs, mine, full)
@@ -72,6 +75,7 @@
     t_cols = jnp.concatenate([target, t_there], axis=0)
     differ = dot(s_rows, s_cols, ROWS_T) - dot(t_rows, t_cols, ROWS_T)
     squares = jnp.sum(differ * differ)
+    squares = (squares + lax.ppermute(squares, "c", SWAP))
     partial_grad = sum(dot(part, s_cols) for part in pieces(differ)[::-1])
     grad_unit = 4.0 * jnp.sum(
         exchange(partial_grad.reshape(group_xz, mine, full), XZ), axis=0
@@ -84,19 +88,17 @@
     for index, part in enumerate(pieces(squares)):
         tail = jnp.where(lane == index, part, tail)
     wide = gather(jnp.concatenate([grad_embed, tail], axis=1), FS).reshape(rows, -1)
-    wide_there = lax.ppermute(wide, "c", SWAP)
-    piece, piece_there = wide[:, :full], wide_there[:, :full]
+    piece = wide[:, :full]
+    piece_there = lax.ppermute(piece, "c", SWAP)
     grad_hidden = dot(piece, projector, ROWS_T)
 
-    hidden_there = lax.ppermute(hidden, "c", SWAP)
     left = lax.dynamic_slice_in_dim(hidden, core * half, half, 1)
     left_there = lax.dynamic_slice_in_dim(hidden_there, core * half, half, 1)
     proj_piece = dot(left, piece, COLS_T) + dot(left_there, piece_there, COLS_T)
 
-    def loss_of(array):
-        return jnp.sum(array.reshape(group_fs, mine, -1)[:, 0, full:].astype(jnp.float32))
-
-    loss_part = loss_of(wide) + loss_of(wide_there)
+    loss_part = jnp.sum(
+        wide.reshape(group_fs, mine, -1)[:, 0, full:].astype(jnp.float32)
+    )
     blocks = jnp.concatenate(
         [
             proj_piece.reshape(group_xz, half // group_xz, full),

time: 251 us -> 248 us (0.988)
  waiting for transfers between devices: 121 us -> 95.6 us
  between operations: 8.91 us -> 21 us
  starting transfers between devices: 57.8 us -> 69.1 us
    all_to_all x6 -> x5, waiting for transfers between devices: 121 us -> 49.7 us  [exchange(): return lax.all_to_all(blocks, axes, split_axis=0, concat_axis=0, tiled=True)]
    all_gather x0 -> x1, waiting for transfers between devices: none -> 27.2 us  [body(): teach = lax.all_gather(teach_pair, 'y', axis=0).astype(jnp.float32)]
    ppermute x1 -> x3, waiting for transfers between devices: 0.01 us -> 18.2 us  [the longest x1 16.6 us: body(): lax.ppermute(teacher, 'zh', SWAP)]
    ppermute x1 -> x3, starting transfers between devices: 5.07 us -> 16 us  [the longest x1 7.18 us: body(): lax.ppermute(teacher, 'zh', SWAP)]
    all_to_all x6 -> x5, starting transfers between devices: 44 us -> 42.3 us  [exchange(): return lax.all_to_all(blocks, axes, split_axis=0, concat_axis=0, tiled=True)]
  transfers between devices with their start and end apart: 10 -> 12, of which waited for: 7 -> 8; matrix products, arithmetic and copies ran while one was open for 3% -> 4% of each run, Pallas kernels for 0% -> 0%
where the time goes in v2:
time: 248 us; the launch traced here: 247 us
  waiting for transfers between devices  95.6 us (39%)
  starting transfers between devices  69.1 us (28%)
  blocking collectives  41 us (17%)
  between operations  21 us (8%)
  matrix products  8.87 us (4%)
  local copies, waits for them, and re-layouts  7.46 us (3%)
  other arithmetic  4 us (2%)
    all_to_all x5, waiting for transfers between devices, exchange(): return lax.all_to_all(blocks, axes, split_axis=0, concat_axis=0, tiled=True)  49.7 us
    all_to_all x5, starting transfers between devices, exchange(): return lax.all_to_all(blocks, axes, split_axis=0, concat_axis=0, tiled=True)  42.3 us
    all_to_all x2, blocking collectives, exchange(): return lax.all_to_all(blocks, axes, split_axis=0, concat_axis=0, tiled=True)  37.4 us
    all_gather x1, waiting for transfers between devices, body(): teach = lax.all_gather(teach_pair, 'y', axis=0).astype(jnp.float32)  27.2 us
    ppermute x1, waiting for transfers between devices, body(): lax.ppermute(teacher, 'zh', SWAP)  16.6 us
    dot_general x9, matrix products, dot(): return lax.dot_general(a, b, dims, preferred_element_type=jnp.float32)  8.87 us
    ppermute x1, starting transfers between devices, body(): lax.ppermute(teacher, 'zh', SWAP)  7.18 us
    ppermute x1, starting transfers between devices, body(): t_there = lax.ppermute(target, 'c', SWAP)  5.74 us
  transfers between devices with their start and end apart: 12, of which 8 were waited for; matrix products, arithmetic and copies ran while one was open for 4% of the time, Pallas kernels for 0%

profile of v2, /device:TPU:1, one launch (start us, length us, event | category | flops | bytes accessed | tf_op | source)
XLA Modules:
  0.0 247.1 jit_solution(10048681377382679307)
XLA Ops:
  7.2 0.0 copy-start
  7.2 0.0 copy-start.3
  7.2 0.9 copy-done
  8.1 0.0 copy-start.2
  8.1 2.0 convolution_bitcast_fusion
  10.1 16.2 %all-to-all-start = ((f32[16,8,1536]{2,1,0:T(8,128)}), f32[16,8,1536]{2,1,0:T(8,128)S(1)}, u32[]{:S(2)}, u32[]{:S(2)}) async-start(f32[16,8,1536]{2,1,0:T(8,128)} %convolution_bitcast_fusion), calls=%async_computation | async-start | bytes 1572864 | tf_op jit(solution)/shard_map/all_to_all | solution.py:29
  26.3 0.0 all-gather.3.cloned.1.call-start
  26.4 0.0 copy-done.2
  26.4 7.2 %collective-permute-start = (bf16[128,256]{1,0:T(8,128)(2,1)S(1)}, bf16[128,256]{1,0:T(8,128)(2,1)S(1)}, u32[]{:S(2)}, u32[]{:S(2)}) collective-permute-start(bf16[128,256]{1,0:T(8,128)(2,1)S(1)} %copy-done.2), channel_id=1, source_target_pairs={{0,8},{8,0},{1,9},{9,1},{2,10},{10,2},{3,11},{11,3},{4,12},{12,4},... | collective-permute-start | bytes 196616 | tf_op jit(solution)/shard_map/ppermute | solution.py:54
  33.6 16.6 %collective-permute-done = bf16[128,256]{1,0:T(8,128)(2,1)S(1)} collective-permute-done((bf16[128,256]{1,0:T(8,128)(2,1)S(1)}, bf16[128,256]{1,0:T(8,128)(2,1)S(1)}, u32[]{:S(2)}, u32[]{:S(2)}) %collective-permute-start) | collective-permute-done | bytes 65568 | tf_op jit(solution)/shard_map/ppermute | solution.py:54
  50.1 0.7 pad_maximum_fusion.1
  50.8 0.0 all-gather.3.cloned.1.call-update
  50.8 0.0 copy-done.3
  50.8 3.0 %collective-permute-start.1 = (bf16[128,96]{0,1:T(8,128)(2,1)S(1)}, bf16[128,96]{0,1:T(8,128)(2,1)S(1)}, u32[]{:S(2)}, u32[]{:S(2)}) collective-permute-start(bf16[128,96]{0,1:T(8,128)(2,1)S(1)} %copy-done.3), channel_id=1, source_target_pairs={{0,16},{16,0},{1,17},{17,1},{2,18},{18,2},{3,19},{19,3},{4,20},{20... | collective-permute-start | bytes 73736 | tf_op jit(solution)/shard_map/ppermute | solution.py:59
  53.9 0.0 all-to-all-done
  54.0 0.1 multiply_reduce_fusion.2
  54.1 0.1 multiply_convert_fusion.1
  54.2 0.8 broadcast_in_dim.21
  54.9 10.2 %all-to-all-start.2 = ((bf16[16,8,1536]{2,1,0:T(8,128)(2,1)}), bf16[16,8,1536]{2,1,0:T(8,128)(2,1)S(1)}, u32[]{:S(2)}, u32[]{:S(2)}) async-start(bf16[16,8,1536]{2,1,0:T(8,128)(2,1)} %broadcast_in_dim.21), calls=%async_computation.2 | async-start | bytes 786432 | tf_op jit(solution)/shard_map/all_to_all | solution.py:29
  65.1 27.2 %all-gather.3.cloned.1.call-done = bf16[1024,512]{1,0:T(8,128)(2,1)} async-done(((bf16[128,512]{1,0:T(8,128)(2,1)}), bf16[1024,512]{1,0:T(8,128)(2,1)}) %all-gather.3.cloned.1.call-update) | async-done | bytes 1048592 | tf_op jit(solution)/shard_map/all_gather | solution.py:55
  92.3 1.6 fusion.2
  93.9 0.0 copy-done.1
  93.9 0.4 fusion.8
  94.4 0.7 copy.17
  95.1 0.0 collective-permute-done.1
  95.1 0.4 constant_dynamic-slice_fusion
  95.4 0.3 copy.18
  95.8 0.0 all-to-all-done.2
  95.8 1.2 broadcast_in_dim.20
  97.0 8.8 %all-to-all-start.1 = ((bf16[16,8,5632]{2,1,0:T(8,128)(2,1)}), bf16[16,8,5632]{2,1,0:T(8,128)(2,1)}, u32[]{:S(2)}, u32[]{:S(2)}) async-start(bf16[16,8,5632]{2,1,0:T(8,128)(2,1)} %broadcast_in_dim.20), calls=%async_computation.1 | async-start | bytes 2883584 | tf_op jit(solution)/shard_map/all_to_all | solution.py:29
  105.8 5.7 %collective-permute-start.3 = (bf16[128,4096]{0,1:T(8,128)(2,1)S(1)}, bf16[128,4096]{0,1:T(8,128)(2,1)}, u32[]{:S(2)}, u32[]{:S(2)}) collective-permute-start(bf16[128,4096]{0,1:T(8,128)(2,1)S(1)} %bitcast.29), channel_id=1, source_target_pairs={{0,16},{16,0},{1,17},{17,1},{2,18},{18,2},{3,19},{19,3},{4,20},{20... | collective-permute-start | bytes 3145736 | tf_op jit(solution)/shard_map/ppermute | solution.py:73
  111.5 1.9 collective-permute-start.2
  113.4 0.5 collective-permute-done.3
  113.9 27.3 %all-to-all-done.1 = bf16[16,8,5632]{2,1,0:T(8,128)(2,1)} async-done(((bf16[16,8,5632]{2,1,0:T(8,128)(2,1)}), bf16[16,8,5632]{2,1,0:T(8,128)(2,1)}, u32[]{:S(2)}, u32[]{:S(2)}) %all-to-all-start.1) | async-done | bytes 1441824 | tf_op jit(solution)/shard_map/all_to_all | solution.py:29
  141.2 2.0 fusion.4
  143.2 0.0 collective-permute-done.2
  143.2 2.0 multiply_reduce_fusion
  145.2 0.3 fusion.14
  145.5 0.3 fusion.13
  145.8 1.2 fusion.1
  146.9 3.6 %all-to-all-start.3 = ((f32[16,8,1536]{2,1,0:T(8,128)}), f32[16,8,1536]{2,1,0:T(8,128)S(1)}, u32[]{:S(2)}, u32[]{:S(2)}) async-start(f32[16,8,1536]{2,1,0:T(8,128)} %fusion.1), calls=%async_computation.3 | async-start | bytes 1572864 | tf_op jit(solution)/shard_map/all_to_all | solution.py:29
  150.6 3.7 %collective-permute-start.4 = (f32[]{:T(128)}, f32[]{:T(128)}, u32[]{:S(2)}, u32[]{:S(2)}) collective-permute-start(f32[]{:T(128)} %get-tuple-element.7), channel_id=1, source_target_pairs={{0,16},{16,0},{1,17},{17,1},{2,18},{18,2},{3,19},{19,3},{4,20},{20... | collective-permute-start | bytes 20 | tf_op jit(solution)/shard_map/ppermute | solution.py:78
  154.2 1.1 collective-permute-done.4
  160.2 11.6 %all-to-all-done.3 = f32[16,8,1536]{2,1,0:T(8,128)S(1)} async-done(((f32[16,8,1536]{2,1,0:T(8,128)}), f32[16,8,1536]{2,1,0:T(8,128)S(1)}, u32[]{:S(2)}, u32[]{:S(2)}) %all-to-all-start.3) | async-done | bytes 786464 | tf_op jit(solution)/shard_map/all_to_all | solution.py:29
  171.9 0.2 multiply_reduce_fusion.1
  172.1 0.1 multiply_convert_fusion
  172.2 21.3 %all_to_all.35 = bf16[16,8,1664]{2,1,0:T(8,128)(2,1)S(1)} all-to-all(bf16[16,8,1664]{2,1,0:T(8,128)(2,1)S(1)} %broadcast_in_dim.47), channel_id=1, replica_groups=mesh['x'=4,'zl'=4,'c'=2,'zh'=2,'y'=8] {'zh','y'}, dimensions={0} | all-to-all | bytes 851968 | tf_op jit(solution)/shard_map/all_to_all | solution.py:29
  193.6 5.2 %collective-permute-start.5 = (bf16[128,1536]{1,0:T(8,128)(2,1)S(1)}, bf16[128,1536]{1,0:T(8,128)(2,1)S(1)}, u32[]{:S(2)}, u32[]{:S(2)}) collective-permute-start(bf16[128,1536]{1,0:T(8,128)(2,1)S(1)} %slice.26), channel_id=1, source_target_pairs={{0,16},{16,0},{1,17},{17,1},{2,18},{18,2},{3,19},{19,3},{4,20},{20... | collective-permute-start | bytes 1179656 | tf_op jit(solution)/shard_map/ppermute | solution.py:92
  198.8 0.6 convert_reduce_fusion
  199.4 0.2 fusion.16
  199.6 0.5 collective-permute-done.5
  200.1 0.2 convolution_add_fusion.1
  200.3 0.1 reshape.69
  200.4 0.7 concatenate.23
  201.1 16.0 %all_to_all.36 = f32[16,4,1536]{2,1,0:T(4,128)S(1)} all-to-all(f32[16,4,1536]{2,1,0:T(4,128)S(1)} %concatenate.23), channel_id=1, replica_groups=mesh['x'=4,'zl'=4,'c'=2,'zh'=2,'y'=8] {'x','zl'}, dimensions={0} | all-to-all | bytes 786432 | tf_op jit(solution)/shard_map/all_to_all | solution.py:29
  217.2 0.1 reduce_sum.79
  217.2 0.8 broadcast_in_dim.48
  218.0 3.6 %all-to-all-start.6 = ((f32[16,3,1536]{2,1,0:T(4,128)}), f32[16,3,1536]{2,1,0:T(4,128)S(1)}, u32[]{:S(2)}, u32[]{:S(2)}) async-start(f32[16,3,1536]{2,1,0:T(4,128)} %broadcast_in_dim.48), calls=%async_computation.6 | async-start | bytes 786432 | tf_op jit(solution)/shard_map/all_to_all | solution.py:29
  221.7 0.9 fusion.22
  222.5 0.5 slice.29
  223.7 10.8 %all-to-all-done.6 = f32[16,3,1536]{2,1,0:T(4,128)S(1)} async-done(((f32[16,3,1536]{2,1,0:T(4,128)}), f32[16,3,1536]{2,1,0:T(4,128)S(1)}, u32[]{:S(2)}, u32[]{:S(2)}) %all-to-all-start.6) | async-done | bytes 294944 | tf_op jit(solution)/shard_map/all_to_all | solution.py:29
  234.5 0.1 reshape.70
  234.7 3.6 %all_gather.11 = f32[96,1536]{1,0:T(8,128)S(1)} all-gather(f32[48,1536]{1,0:T(8,128)S(1)} %reshape.70), channel_id=1, replica_groups=mesh['x'=4,'zl'=4,'c'=2,'zh'=2,'y'=8] {'c'}, dimensions={0}, use_global_device_ids=true | all-gather | bytes 884736 | tf_op jit(solution)/shard_map/all_gather | solution.py:111
  238.3 0.8 copy.22
  (13 shorter events, 0.2 us)
Async XLA Ops:
  7.2 1.0 copy-start
  7.2 43.6 %copy-start.3 = (bf16[128,96]{0,1:T(8,128)(2,1)S(1)}, bf16[128,96]{0,1:T(8,128)(2,1)}, u32[]{:S(2)}) copy-start(bf16[128,96]{0,1:T(8,128)(2,1)} %param.3) | copy-start | bytes 73732
  8.1 18.2 %copy-start.2 = (bf16[128,256]{1,0:T(8,128)(2,1)S(1)}, bf16[128,256]{1,0:T(8,128)(2,1)}, u32[]{:S(2)}) copy-start(bf16[128,256]{1,0:T(8,128)(2,1)} %param.4) | copy-start | bytes 196612
  10.1 43.8 %all-to-all-start = ((f32[16,8,1536]{2,1,0:T(8,128)}), f32[16,8,1536]{2,1,0:T(8,128)S(1)}, u32[]{:S(2)}, u32[]{:S(2)}) async-start(f32[16,8,1536]{2,1,0:T(8,128)} %convolution_bitcast_fusion), calls=%async_computation | async-start | bytes 1572864 | tf_op jit(solution)/shard_map/all_to_all | solution.py:29
  26.3 66.0 %all-gather.3.cloned.1.call-start = ((), (), s32[]{:S(2)}) async-start(), calls=%async_computation.7 | async-start | bytes 1179648 | tf_op jit(solution)/shard_map/all_gather | solution.py:55
  26.4 23.8 %collective-permute-start = (bf16[128,256]{1,0:T(8,128)(2,1)S(1)}, bf16[128,256]{1,0:T(8,128)(2,1)S(1)}, u32[]{:S(2)}, u32[]{:S(2)}) collective-permute-start(bf16[128,256]{1,0:T(8,128)(2,1)S(1)} %copy-done.2), channel_id=1, source_target_pairs={{0,8},{8,0},{1,9},{9,1},{2,10},{10,2},{3,11},{11,3},{4,12},{12,4},... | collective-permute-start | bytes 196616 | tf_op jit(solution)/shard_map/ppermute | solution.py:54
  50.8 44.2 %collective-permute-start.1 = (bf16[128,96]{0,1:T(8,128)(2,1)S(1)}, bf16[128,96]{0,1:T(8,128)(2,1)S(1)}, u32[]{:S(2)}, u32[]{:S(2)}) collective-permute-start(bf16[128,96]{0,1:T(8,128)(2,1)S(1)} %copy-done.3), channel_id=1, source_target_pairs={{0,16},{16,0},{1,17},{17,1},{2,18},{18,2},{3,19},{19,3},{4,20},{20... | collective-permute-start | bytes 73736 | tf_op jit(solution)/shard_map/ppermute | solution.py:59
  54.9 40.8 %all-to-all-start.2 = ((bf16[16,8,1536]{2,1,0:T(8,128)(2,1)}), bf16[16,8,1536]{2,1,0:T(8,128)(2,1)S(1)}, u32[]{:S(2)}, u32[]{:S(2)}) async-start(bf16[16,8,1536]{2,1,0:T(8,128)(2,1)} %broadcast_in_dim.21), calls=%async_computation.2 | async-start | bytes 786432 | tf_op jit(solution)/shard_map/all_to_all | solution.py:29
  92.3 1.6 copy-start.1
  97.0 44.3 %all-to-all-start.1 = ((bf16[16,8,5632]{2,1,0:T(8,128)(2,1)}), bf16[16,8,5632]{2,1,0:T(8,128)(2,1)}, u32[]{:S(2)}, u32[]{:S(2)}) async-start(bf16[16,8,5632]{2,1,0:T(8,128)(2,1)} %broadcast_in_dim.20), calls=%async_computation.1 | async-start | bytes 2883584 | tf_op jit(solution)/shard_map/all_to_all | solution.py:29
  105.8 8.1 %collective-permute-start.3 = (bf16[128,4096]{0,1:T(8,128)(2,1)S(1)}, bf16[128,4096]{0,1:T(8,128)(2,1)}, u32[]{:S(2)}, u32[]{:S(2)}) collective-permute-start(bf16[128,4096]{0,1:T(8,128)(2,1)S(1)} %bitcast.29), channel_id=1, source_target_pairs={{0,16},{16,0},{1,17},{17,1},{2,18},{18,2},{3,19},{19,3},{4,20},{20... | collective-permute-start | bytes 3145736 | tf_op jit(solution)/shard_map/ppermute | solution.py:73
  111.5 31.7 %collective-permute-start.2 = (bf16[128,1536]{1,0:T(8,128)(2,1)S(1)}, bf16[128,1536]{1,0:T(8,128)(2,1)S(1)}, u32[]{:S(2)}, u32[]{:S(2)}) collective-permute-start(bf16[128,1536]{1,0:T(8,128)(2,1)S(1)} %bitcast.19), channel_id=1, source_target_pairs={{0,16},{16,0},{1,17},{17,1},{2,18},{18,2},{3,19},{19,3},{4,20},{20... | collective-permute-start | bytes 1179656 | tf_op jit(solution)/shard_map/ppermute | solution.py:72
  146.9 24.9 %all-to-all-start.3 = ((f32[16,8,1536]{2,1,0:T(8,128)}), f32[16,8,1536]{2,1,0:T(8,128)S(1)}, u32[]{:S(2)}, u32[]{:S(2)}) async-start(f32[16,8,1536]{2,1,0:T(8,128)} %fusion.1), calls=%async_computation.3 | async-start | bytes 1572864 | tf_op jit(solution)/shard_map/all_to_all | solution.py:29
  150.6 4.7 %collective-permute-start.4 = (f32[]{:T(128)}, f32[]{:T(128)}, u32[]{:S(2)}, u32[]{:S(2)}) collective-permute-start(f32[]{:T(128)} %get-tuple-element.7), channel_id=1, source_target_pairs={{0,16},{16,0},{1,17},{17,1},{2,18},{18,2},{3,19},{19,3},{4,20},{20... | collective-permute-start | bytes 20 | tf_op jit(solution)/shard_map/ppermute | solution.py:78
  193.6 6.5 %collective-permute-start.5 = (bf16[128,1536]{1,0:T(8,128)(2,1)S(1)}, bf16[128,1536]{1,0:T(8,128)(2,1)S(1)}, u32[]{:S(2)}, u32[]{:S(2)}) collective-permute-start(bf16[128,1536]{1,0:T(8,128)(2,1)S(1)} %slice.26), channel_id=1, source_target_pairs={{0,16},{16,0},{1,17},{17,1},{2,18},{18,2},{3,19},{19,3},{4,20},{20... | collective-permute-start | bytes 1179656 | tf_op jit(solution)/shard_map/ppermute | solution.py:92
  218.0 16.5 %all-to-all-start.6 = ((f32[16,3,1536]{2,1,0:T(4,128)}), f32[16,3,1536]{2,1,0:T(4,128)S(1)}, u32[]{:S(2)}, u32[]{:S(2)}) async-start(f32[16,3,1536]{2,1,0:T(4,128)} %broadcast_in_dim.48), calls=%async_computation.6 | async-start | bytes 786432 | tf_op jit(solution)/shard_map/all_to_all | solution.py:29
Sparse Core Ops, SparseCore 0:
  50.9 41.3 all-gather.2

commit v3 on v2

--- a/solution.py
+++ b/solution.py
@@ -42,34 +42,55 @@
     return [part.astype(jnp.bfloat16) for part in (high, middle, low)]
 
 
+def normal(values, axes):
+    total = jnp.sum(values * values, axis=axes, keepdims=True)
+    return (values * lax.rsqrt(total + EPSILON)).astype(jnp.bfloat16)
+
+
 def body(hidden, teacher, projector):
     rows, width = hidden.shape
     full = projector.shape[1]
     group_fs, group_xz = group(FS), group(XZ)
     mine = rows // group_fs
     half = width // 2
-    place = lax.axis_index(FS)
+    width_t = teacher.shape[1]
     core = lax.axis_index("c")
 
-    teach_pair = jnp.concatenate([teacher, lax.ppermute(teacher, "zh", SWAP)], axis=1)
-    teach = lax.all_gather(teach_pair, "y", axis=0).astype(jnp.float32)
-    sq_teacher = jnp.sum(teach * teach, axis=(0, 2))
-    target = (teach * lax.rsqrt(sq_teacher + EPSILON)[None, :, None]).astype(jnp.bfloat16)
-    target = target.transpose(1, 0, 2).reshape(rows, -1)
-    hidden_there = lax.ppermute(hidden, "c", SWAP)
-    target, hidden_there = lax.optimization_barrier((target, hidden_there))
-    target_mine = lax.dynamic_slice_in_dim(target, place * mine, mine, 0)
+    over = lax.ppermute(teacher, "zh", SWAP)
+    first = lax.axis_index("zh") == 0
+    pair = jnp.concatenate(
+        [jnp.where(first, teacher, over), jnp.where(first, over, teacher)], axis=1
+    )
+    teach = lax.all_gather(pair, "y", axis=0).astype(jnp.float32)
+    target = normal(teach, (0, 2)).transpose(1, 0, 2).reshape(rows, -1)
 
-    partial_embed = dot(hidden, projector).reshape(group_fs, mine, full)
-    embed = jnp.sum(exchange(partial_embed, FS), axis=0)
+    partial_embed = dot(hidden, projector).astype(jnp.bfloat16)
+    sent = jnp.concatenate(
+        [
+            partial_embed.reshape(group_fs, mine, full),
+            teacher.reshape(group_fs, mine, width_t),
+        ],
+        axis=2,
+    )
+    got = exchange(sent, FS)
+    embed = jnp.sum(got[:, :, :full].astype(jnp.float32), axis=0)
     inv_student = lax.rsqrt(jnp.sum(embed * embed, axis=1, keepdims=True) + EPSILON)
     unit = embed * inv_student
     student = unit.astype(jnp.bfloat16)
+    target_mine = (
+        normal(got[:, :, full:].astype(jnp.float32), (0, 2))
+        .reshape(SIZES["zh"], SIZES["y"], mine, width_t)
+        .transpose(2, 1, 0, 3)
+        .reshape(mine, -1)
+    )
 
-    both = gather(jnp.concatenate([student, target_mine], axis=1), XZ).reshape(group_xz * mine, -1)
+    s_here = gather(student, FS).reshape(rows, full)
+    both = gather(jnp.concatenate([student, target_mine], axis=1), ("zl",))
+    both = gather(both.reshape(-1, both.shape[2]), ("x",)).reshape(group_xz * mine, -1)
     s_rows, t_rows = both[:, :full], both[:, full:]
-    s_here = gather(student, FS).reshape(rows, full)
     s_there = lax.ppermute(s_here, "c", SWAP)
+    hidden_there = lax.ppermute(hidden, "c", SWAP)
+    target, hidden_there = lax.optimization_barrier((target, hidden_there))
     t_there = lax.ppermute(target, "c", SWAP)
     s_cols = jnp.concatenate([s_here, s_there], axis=0)
     t_cols = jnp.concatenate([target, t_there], axis=0)
@@ -77,9 +98,8 @@
     squares = jnp.sum(differ * differ)
     squares = (squares + lax.ppermute(squares, "c", SWAP))
     partial_grad = sum(dot(part, s_cols) for part in pieces(differ)[::-1])
-    grad_unit = 4.0 * jnp.sum(
-        exchange(partial_grad.reshape(group_xz, mine, full), XZ), axis=0
-    )
+    partial_grad = partial_grad.astype(jnp.bfloat16).reshape(group_xz, mine, full)
+    grad_unit = 4.0 * jnp.sum(exchange(partial_grad, XZ).astype(jnp.float32), axis=0)
     radial = jnp.sum(unit * grad_unit, axis=1, keepdims=True)
     grad_embed = (inv_student * (grad_unit - unit * radial)).astype(jnp.bfloat16)
 

time: 248 us -> 214 us (0.86)
  waiting for transfers between devices: 95.6 us -> 41.3 us
  blocking collectives: 41 us -> 60.1 us
    all_to_all x5, waiting for transfers between devices: 49.7 us -> 16.7 us  [exchange(): return lax.all_to_all(blocks, axes, split_axis=0, concat_axis=0, tiled=True)]
    all_to_all x2 -> x3, blocking collectives: 37.4 us -> 56.5 us  [exchange(): return lax.all_to_all(blocks, axes, split_axis=0, concat_axis=0, tiled=True)]
    all_gather x1, waiting for transfers between devices: 27.2 us -> 12.8 us  [body(): teach = lax.all_gather(pair, 'y', axis=0).astype(jnp.float32)]
    all_to_all x5, starting transfers between devices: 42.3 us -> 35.5 us  [exchange(): return lax.all_to_all(blocks, axes, split_axis=0, concat_axis=0, tiled=True)]
    ppermute x1, waiting for transfers between devices: 16.6 us -> 10.3 us  [body(): over = lax.ppermute(teacher, 'zh', SWAP)]
    ppermute x1, starting transfers between devices: 3.67 us -> 7.61 us  [body(): squares = squares + lax.ppermute(squares, 'c', SWAP)]
  transfers between devices with their start and end apart: 12 -> 12, of which waited for: 8 -> 6; matrix products, arithmetic and copies ran while one was open for 4% -> 5% of each run, Pallas kernels for 0% -> 0%
where the time goes in v3:
time: 214 us; the launch traced here: 213 us
  starting transfers between devices  69.2 us (32%)
  blocking collectives  60.1 us (28%)
  waiting for transfers between devices  41.3 us (19%)
  between operations  21.1 us (10%)
  matrix products  7.82 us (4%)
  local copies, waits for them, and re-layouts  7.57 us (4%)
  other arithmetic  5.81 us (3%)
    all_to_all x3, blocking collectives, exchange(): return lax.all_to_all(blocks, axes, split_axis=0, concat_axis=0, tiled=True)  56.5 us
    all_to_all x5, starting transfers between devices, exchange(): return lax.all_to_all(blocks, axes, split_axis=0, concat_axis=0, tiled=True)  35.5 us
    all_to_all x5, waiting for transfers between devices, exchange(): return lax.all_to_all(blocks, axes, split_axis=0, concat_axis=0, tiled=True)  16.7 us
    all_gather x1, waiting for transfers between devices, body(): teach = lax.all_gather(pair, 'y', axis=0).astype(jnp.float32)  12.8 us
    ppermute x1, waiting for transfers between devices, body(): over = lax.ppermute(teacher, 'zh', SWAP)  10.3 us
    dot_general x9, matrix products, dot(): return lax.dot_general(a, b, dims, preferred_element_type=jnp.float32)  7.82 us
    ppermute x1, starting transfers between devices, body(): squares = squares + lax.ppermute(squares, 'c', SWAP)  7.61 us
    ppermute x1, starting transfers between devices, body(): over = lax.ppermute(teacher, 'zh', SWAP)  7.18 us
  transfers between devices with their start and end apart: 12, of which 6 were waited for; matrix products, arithmetic and copies ran while one was open for 5% of the time, Pallas kernels for 0%

profile of v3, /device:TPU:1, one launch (start us, length us, event | category | flops | bytes accessed | tf_op | source)
XLA Modules:
  0.0 212.9 jit_solution(3591470428692612637)
XLA Ops:
  7.2 0.0 copy-start
  7.2 1.0 copy-done
  8.1 1.0 fusion.2
  9.2 1.6 pad_maximum_fusion.1
  10.8 16.2 %all-to-all-start = ((bf16[16,8,1792]{2,1,0:T(8,128)(2,1)}), bf16[16,8,1792]{2,1,0:T(8,128)(2,1)S(1)}, u32[]{:S(2)}, u32[]{:S(2)}) async-start(bf16[16,8,1792]{2,1,0:T(8,128)(2,1)} %pad_maximum_fusion.1), calls=%async_computation | async-start | bytes 917504 | tf_op jit(solution)/shard_map/all_to_all | solution.py:29
  27.0 0.0 all-gather.3.cloned.1.call-start
  27.1 7.2 %collective-permute-start.1 = (bf16[128,256]{1,0:T(8,128)(2,1)S(1)}, bf16[128,256]{1,0:T(8,128)(2,1)S(1)}, u32[]{:S(2)}, u32[]{:S(2)}) collective-permute-start(bf16[128,256]{1,0:T(8,128)(2,1)S(1)} %copy-done.2), channel_id=1, source_target_pairs={{0,8},{8,0},{1,9},{9,1},{2,10},{10,2},{3,11},{11,3},{4,12},{12,4},... | collective-permute-start | bytes 196616 | tf_op jit(solution)/shard_map/ppermute | solution.py:59
  34.3 10.3 %collective-permute-done.1 = bf16[128,256]{1,0:T(8,128)(2,1)S(1)} collective-permute-done((bf16[128,256]{1,0:T(8,128)(2,1)S(1)}, bf16[128,256]{1,0:T(8,128)(2,1)S(1)}, u32[]{:S(2)}, u32[]{:S(2)}) %collective-permute-start.1) | collective-permute-done | bytes 65568 | tf_op jit(solution)/shard_map/ppermute | solution.py:59
  44.6 0.6 pad_maximum_fusion.2
  45.2 0.0 all-gather.3.cloned.1.call-update
  45.2 0.0 all-to-all-done
  45.3 0.1 convert_reduce_fusion.1
  45.3 0.1 multiply_reduce_fusion.2
  45.4 0.1 fusion.13
  45.6 0.1 fusion.14
  45.7 0.0 copy-start.3
  45.7 0.1 copy.10
  45.8 0.1 multiply_convert_fusion.1
  45.9 15.8 %all_to_all.40 = bf16[4,8,5632]{2,1,0:T(8,128)(2,1)S(1)} all-to-all(bf16[4,8,5632]{2,1,0:T(8,128)(2,1)S(1)} %broadcast_in_dim.24), channel_id=1, replica_groups=mesh['x'=4,'zl'=4,'c'=2,'zh'=2,'y'=8] {'zl'}, dimensions={0} | all-to-all | bytes 720896 | tf_op jit(solution)/shard_map/all_to_all | solution.py:29
  61.7 0.8 broadcast_in_dim.52
  62.5 6.2 %all-to-all-start.3 = ((bf16[16,8,1536]{2,1,0:T(8,128)(2,1)}), bf16[16,8,1536]{2,1,0:T(8,128)(2,1)S(1)}, u32[]{:S(2)}, u32[]{:S(2)}) async-start(bf16[16,8,1536]{2,1,0:T(8,128)(2,1)} %broadcast_in_dim.52), calls=%async_computation.3 | async-start | bytes 786432 | tf_op jit(solution)/shard_map/all_to_all | solution.py:29
  68.7 4.1 %collective-permute-start.2 = (bf16[128,96]{0,1:T(8,128)(2,1)S(1)}, bf16[128,96]{0,1:T(8,128)(2,1)S(1)}, u32[]{:S(2)}, u32[]{:S(2)}) collective-permute-start(bf16[128,96]{0,1:T(8,128)(2,1)S(1)} %copy-done.3), channel_id=1, source_target_pairs={{0,16},{16,0},{1,17},{17,1},{2,18},{18,2},{3,19},{19,3},{4,20},{20... | collective-permute-start | bytes 73736 | tf_op jit(solution)/shard_map/ppermute | solution.py:92
  72.8 12.8 %all-gather.3.cloned.1.call-done = bf16[1024,512]{1,0:T(8,128)(2,1)} async-done(((bf16[128,512]{1,0:T(8,128)(2,1)}), bf16[1024,512]{1,0:T(8,128)(2,1)}) %all-gather.3.cloned.1.call-update) | async-done | bytes 1048592 | tf_op jit(solution)/shard_map/all_gather | solution.py:64
  85.6 1.5 fusion.4
  87.2 0.0 all-to-all-done.3
  87.2 1.2 broadcast_in_dim.26
  88.4 4.4 %all-to-all-start.2 = ((bf16[4,32,5632]{2,1,0:T(8,128)(2,1)}), bf16[4,32,5632]{2,1,0:T(8,128)(2,1)}, u32[]{:S(2)}, u32[]{:S(2)}) async-start(bf16[4,32,5632]{2,1,0:T(8,128)(2,1)} %broadcast_in_dim.26), calls=%async_computation.2 | async-start | bytes 2883584 | tf_op jit(solution)/shard_map/all_to_all | solution.py:29
  92.8 0.4 fusion.10
  93.3 1.3 copy.11
  94.6 0.0 collective-permute-done.2
  94.6 5.7 %collective-permute-start.3 = (bf16[128,4096]{0,1:T(8,128)(2,1)}, bf16[128,4096]{0,1:T(8,128)(2,1)S(1)}, u32[]{:S(2)}, u32[]{:S(2)}) collective-permute-start(bf16[128,4096]{0,1:T(8,128)(2,1)} %bitcast.10), channel_id=1, source_target_pairs={{0,16},{16,0},{1,17},{17,1},{2,18},{18,2},{3,19},{19,3},{4,20},{20... | collective-permute-start | bytes 3145736 | tf_op jit(solution)/shard_map/ppermute | solution.py:94
  100.3 1.9 collective-permute-start
  102.3 5.9 %all-to-all-done.2 = bf16[4,32,5632]{2,1,0:T(8,128)(2,1)} async-done(((bf16[4,32,5632]{2,1,0:T(8,128)(2,1)}), bf16[4,32,5632]{2,1,0:T(8,128)(2,1)}, u32[]{:S(2)}, u32[]{:S(2)}) %all-to-all-start.2) | async-done | bytes 1441824 | tf_op jit(solution)/shard_map/all_to_all | solution.py:29
  108.1 0.0 collective-permute-done.3
  108.1 2.0 fusion.6
  110.1 0.0 collective-permute-done
  110.1 2.0 multiply_reduce_fusion
  112.1 0.3 fusion.18
  112.4 0.3 fusion.17
  112.7 1.0 fusion.3
  113.7 5.1 %all-to-all-start.4 = ((bf16[16,8,1536]{2,1,0:T(8,128)(2,1)}), bf16[16,8,1536]{2,1,0:T(8,128)(2,1)S(1)}, u32[]{:S(2)}, u32[]{:S(2)}) async-start(bf16[16,8,1536]{2,1,0:T(8,128)(2,1)} %fusion.3), calls=%async_computation.4 | async-start | bytes 786432 | tf_op jit(solution)/shard_map/all_to_all | solution.py:29
  118.8 7.6 %collective-permute-start.4 = (f32[]{:T(128)}, f32[]{:T(128)}, u32[]{:S(2)}, u32[]{:S(2)}) collective-permute-start(f32[]{:T(128)} %get-tuple-element.9), channel_id=1, source_target_pairs={{0,16},{16,0},{1,17},{17,1},{2,18},{18,2},{3,19},{19,3},{4,20},{20... | collective-permute-start | bytes 20 | tf_op jit(solution)/shard_map/ppermute | solution.py:99
  126.4 0.9 collective-permute-done.4
  132.4 0.1 convert_reduce_fusion
  132.4 0.2 multiply_reduce_fusion.1
  132.6 0.1 multiply_convert_fusion
  132.8 21.1 %all_to_all.41 = bf16[16,8,1664]{2,1,0:T(8,128)(2,1)S(1)} all-to-all(bf16[16,8,1664]{2,1,0:T(8,128)(2,1)S(1)} %broadcast_in_dim.57), channel_id=1, replica_groups=mesh['x'=4,'zl'=4,'c'=2,'zh'=2,'y'=8] {'zh','y'}, dimensions={0} | all-to-all | bytes 851968 | tf_op jit(solution)/shard_map/all_to_all | solution.py:29
  153.9 7.1 %collective-permute-start.5 = (bf16[128,1536]{1,0:T(8,128)(2,1)S(1)}, bf16[128,1536]{1,0:T(8,128)(2,1)S(1)}, u32[]{:S(2)}, u32[]{:S(2)}) collective-permute-start(bf16[128,1536]{1,0:T(8,128)(2,1)S(1)} %slice.36), channel_id=1, source_target_pairs={{0,16},{16,0},{1,17},{17,1},{2,18},{18,2},{3,19},{19,3},{4,20},{20... | collective-permute-start | bytes 1179656 | tf_op jit(solution)/shard_map/ppermute | solution.py:112
  161.0 0.6 convert_reduce_fusion.2
  161.6 0.2 fusion.20
  161.8 0.5 collective-permute-done.5
  162.3 0.2 convolution_add_fusion.1
  162.5 0.1 reshape.90
  162.6 0.7 concatenate.27
  163.3 19.6 %all_to_all.42 = f32[16,4,1536]{2,1,0:T(4,128)S(1)} all-to-all(f32[16,4,1536]{2,1,0:T(4,128)S(1)} %concatenate.27), channel_id=1, replica_groups=mesh['x'=4,'zl'=4,'c'=2,'zh'=2,'y'=8] {'x','zl'}, dimensions={0} | all-to-all | bytes 786432 | tf_op jit(solution)/shard_map/all_to_all | solution.py:29
  183.0 0.1 reduce_sum.89
  183.0 0.8 broadcast_in_dim.58
  183.8 3.6 %all-to-all-start.7 = ((f32[16,3,1536]{2,1,0:T(4,128)}), f32[16,3,1536]{2,1,0:T(4,128)S(1)}, u32[]{:S(2)}, u32[]{:S(2)}) async-start(f32[16,3,1536]{2,1,0:T(4,128)} %broadcast_in_dim.58), calls=%async_computation.7 | async-start | bytes 786432 | tf_op jit(solution)/shard_map/all_to_all | solution.py:29
  187.4 0.9 fusion.26
  188.3 0.5 slice.39
  189.5 10.8 %all-to-all-done.7 = f32[16,3,1536]{2,1,0:T(4,128)S(1)} async-done(((f32[16,3,1536]{2,1,0:T(4,128)}), f32[16,3,1536]{2,1,0:T(4,128)S(1)}, u32[]{:S(2)}, u32[]{:S(2)}) %all-to-all-start.7) | async-done | bytes 294944 | tf_op jit(solution)/shard_map/all_to_all | solution.py:29
  200.3 0.1 reshape.91
  200.5 3.6 %all_gather.11 = f32[96,1536]{1,0:T(8,128)S(1)} all-gather(f32[48,1536]{1,0:T(8,128)S(1)} %reshape.91), channel_id=1, replica_groups=mesh['x'=4,'zl'=4,'c'=2,'zh'=2,'y'=8] {'c'}, dimensions={0}, use_global_device_ids=true | all-gather | bytes 884736 | tf_op jit(solution)/shard_map/all_gather | solution.py:131
  204.1 0.8 copy.15
  (20 shorter events, 0.2 us)
Async XLA Ops:
  7.2 1.0 copy-start
  8.1 19.0 %copy-start.2 = (bf16[128,256]{1,0:T(8,128)(2,1)S(1)}, bf16[128,256]{1,0:T(8,128)(2,1)}, u32[]{:S(2)}) copy-start(bf16[128,256]{1,0:T(8,128)(2,1)} %param.4) | copy-start | bytes 196612
  10.8 34.4 %all-to-all-start = ((bf16[16,8,1792]{2,1,0:T(8,128)(2,1)}), bf16[16,8,1792]{2,1,0:T(8,128)(2,1)S(1)}, u32[]{:S(2)}, u32[]{:S(2)}) async-start(bf16[16,8,1792]{2,1,0:T(8,128)(2,1)} %pad_maximum_fusion.1), calls=%async_computation | async-start | bytes 917504 | tf_op jit(solution)/shard_map/all_to_all | solution.py:29
  27.0 58.6 %all-gather.3.cloned.1.call-start = ((), (), s32[]{:S(2)}) async-start(), calls=%async_computation.8 | async-start | bytes 1179648 | tf_op jit(solution)/shard_map/all_gather | solution.py:64
  27.1 17.5 %collective-permute-start.1 = (bf16[128,256]{1,0:T(8,128)(2,1)S(1)}, bf16[128,256]{1,0:T(8,128)(2,1)S(1)}, u32[]{:S(2)}, u32[]{:S(2)}) collective-permute-start(bf16[128,256]{1,0:T(8,128)(2,1)S(1)} %copy-done.2), channel_id=1, source_target_pairs={{0,8},{8,0},{1,9},{9,1},{2,10},{10,2},{3,11},{11,3},{4,12},{12,4},... | collective-permute-start | bytes 196616 | tf_op jit(solution)/shard_map/ppermute | solution.py:59
  45.7 23.0 %copy-start.3 = (bf16[128,96]{0,1:T(8,128)(2,1)S(1)}, bf16[128,96]{0,1:T(8,128)(2,1)}, u32[]{:S(2)}) copy-start(bf16[128,96]{0,1:T(8,128)(2,1)} %param.3) | copy-start | bytes 73732
  62.5 24.7 %all-to-all-start.3 = ((bf16[16,8,1536]{2,1,0:T(8,128)(2,1)}), bf16[16,8,1536]{2,1,0:T(8,128)(2,1)S(1)}, u32[]{:S(2)}, u32[]{:S(2)}) async-start(bf16[16,8,1536]{2,1,0:T(8,128)(2,1)} %broadcast_in_dim.52), calls=%async_computation.3 | async-start | bytes 786432 | tf_op jit(solution)/shard_map/all_to_all | solution.py:29
  68.7 25.9 %collective-permute-start.2 = (bf16[128,96]{0,1:T(8,128)(2,1)S(1)}, bf16[128,96]{0,1:T(8,128)(2,1)S(1)}, u32[]{:S(2)}, u32[]{:S(2)}) collective-permute-start(bf16[128,96]{0,1:T(8,128)(2,1)S(1)} %copy-done.3), channel_id=1, source_target_pairs={{0,16},{16,0},{1,17},{17,1},{2,18},{18,2},{3,19},{19,3},{4,20},{20... | collective-permute-start | bytes 73736 | tf_op jit(solution)/shard_map/ppermute | solution.py:92
  88.4 4.5 %copy-start.1 = (bf16[1024,512]{1,0:T(8,128)(2,1)S(1)}, bf16[1024,512]{1,0:T(8,128)(2,1)}, u32[]{:S(2)}) copy-start(bf16[1024,512]{1,0:T(8,128)(2,1)} %all-gather.3.cloned.1.call-done) | copy-start | bytes 3145732
  88.4 19.7 %all-to-all-start.2 = ((bf16[4,32,5632]{2,1,0:T(8,128)(2,1)}), bf16[4,32,5632]{2,1,0:T(8,128)(2,1)}, u32[]{:S(2)}, u32[]{:S(2)}) async-start(bf16[4,32,5632]{2,1,0:T(8,128)(2,1)} %broadcast_in_dim.26), calls=%async_computation.2 | async-start | bytes 2883584 | tf_op jit(solution)/shard_map/all_to_all | solution.py:29
  94.6 13.5 %collective-permute-start.3 = (bf16[128,4096]{0,1:T(8,128)(2,1)}, bf16[128,4096]{0,1:T(8,128)(2,1)S(1)}, u32[]{:S(2)}, u32[]{:S(2)}) collective-permute-start(bf16[128,4096]{0,1:T(8,128)(2,1)} %bitcast.10), channel_id=1, source_target_pairs={{0,16},{16,0},{1,17},{17,1},{2,18},{18,2},{3,19},{19,3},{4,20},{20... | collective-permute-start | bytes 3145736 | tf_op jit(solution)/shard_map/ppermute | solution.py:94
  100.3 9.8 %collective-permute-start = (bf16[128,1536]{1,0:T(8,128)(2,1)S(1)}, bf16[128,1536]{1,0:T(8,128)(2,1)S(1)}, u32[]{:S(2)}, u32[]{:S(2)}) collective-permute-start(bf16[128,1536]{1,0:T(8,128)(2,1)S(1)} %bitcast.24), channel_id=1, source_target_pairs={{0,16},{16,0},{1,17},{17,1},{2,18},{18,2},{3,19},{19,3},{4,20},{20... | collective-permute-start | bytes 1179656 | tf_op jit(solution)/shard_map/ppermute | solution.py:91
  113.7 18.6 %all-to-all-start.4 = ((bf16[16,8,1536]{2,1,0:T(8,128)(2,1)}), bf16[16,8,1536]{2,1,0:T(8,128)(2,1)S(1)}, u32[]{:S(2)}, u32[]{:S(2)}) async-start(bf16[16,8,1536]{2,1,0:T(8,128)(2,1)} %fusion.3), calls=%async_computation.4 | async-start | bytes 786432 | tf_op jit(solution)/shard_map/all_to_all | solution.py:29
  118.8 8.5 %collective-permute-start.4 = (f32[]{:T(128)}, f32[]{:T(128)}, u32[]{:S(2)}, u32[]{:S(2)}) collective-permute-start(f32[]{:T(128)} %get-tuple-element.9), channel_id=1, source_target_pairs={{0,16},{16,0},{1,17},{17,1},{2,18},{18,2},{3,19},{19,3},{4,20},{20... | collective-permute-start | bytes 20 | tf_op jit(solution)/shard_map/ppermute | solution.py:99
  153.9 8.4 %collective-permute-start.5 = (bf16[128,1536]{1,0:T(8,128)(2,1)S(1)}, bf16[128,1536]{1,0:T(8,128)(2,1)S(1)}, u32[]{:S(2)}, u32[]{:S(2)}) collective-permute-start(bf16[128,1536]{1,0:T(8,128)(2,1)S(1)} %slice.36), channel_id=1, source_target_pairs={{0,16},{16,0},{1,17},{17,1},{2,18},{18,2},{3,19},{19,3},{4,20},{20... | collective-permute-start | bytes 1179656 | tf_op jit(solution)/shard_map/ppermute | solution.py:112
  183.8 16.5 %all-to-all-start.7 = ((f32[16,3,1536]{2,1,0:T(4,128)}), f32[16,3,1536]{2,1,0:T(4,128)S(1)}, u32[]{:S(2)}, u32[]{:S(2)}) async-start(f32[16,3,1536]{2,1,0:T(4,128)} %broadcast_in_dim.58), calls=%async_computation.7 | async-start | bytes 786432 | tf_op jit(solution)/shard_map/all_to_all | solution.py:29
Sparse Core Ops, SparseCore 0:
  45.4 40.2 all-gather.2

commit v4 on v3

--- a/solution.py
+++ b/solution.py
@@ -47,6 +47,22 @@
     return (values * lax.rsqrt(total + EPSILON)).astype(jnp.bfloat16)
 
 
+def around(block, axis):
+    blocks = [block]
+    for step in (1, 2, 3):
+        blocks.append(lax.ppermute(block, axis, [(at, at ^ step) for at in range(4)]))
+    return jnp.concatenate(blocks, axis=0)
+
+
+def in_order(values):
+    shape = values.shape
+    values = values.reshape(2, 2, 2, 2, -1, shape[1])
+    for dim, (axis, bit) in enumerate((("x", 2), ("x", 1), ("zl", 2), ("zl", 1))):
+        swap = (lax.axis_index(axis) & bit) != 0
+        values = jnp.where(swap, jnp.flip(values, dim), values)
+    return values.reshape(shape)
+
+
 def body(hidden, teacher, projector):
     rows, width = hidden.shape
     full = projector.shape[1]
@@ -55,14 +71,6 @@
     half = width // 2
     width_t = teacher.shape[1]
     core = lax.axis_index("c")
-
-    over = lax.ppermute(teacher, "zh", SWAP)
-    first = lax.axis_index("zh") == 0
-    pair = jnp.concatenate(
-        [jnp.where(first, teacher, over), jnp.where(first, over, teacher)], axis=1
-    )
-    teach = lax.all_gather(pair, "y", axis=0).astype(jnp.float32)
-    target = normal(teach, (0, 2)).transpose(1, 0, 2).reshape(rows, -1)
 
     partial_embed = dot(hidden, projector).astype(jnp.bfloat16)
     sent = jnp.concatenate(
@@ -77,26 +85,18 @@
     inv_student = lax.rsqrt(jnp.sum(embed * embed, axis=1, keepdims=True) + EPSILON)
     unit = embed * inv_student
     student = unit.astype(jnp.bfloat16)
-    target_mine = (
-        normal(got[:, :, full:].astype(jnp.float32), (0, 2))
-        .reshape(SIZES["zh"], SIZES["y"], mine, width_t)
-        .transpose(2, 1, 0, 3)
-        .reshape(mine, -1)
-    )
+    target = normal(got[:, :, full:].astype(jnp.float32), (0, 2))
+    target = target.transpose(1, 0, 2).reshape(mine, -1)
 
-    s_here = gather(student, FS).reshape(rows, full)
-    both = gather(jnp.concatenate([student, target_mine], axis=1), ("zl",))
-    both = gather(both.reshape(-1, both.shape[2]), ("x",)).reshape(group_xz * mine, -1)
-    s_rows, t_rows = both[:, :full], both[:, full:]
-    s_there = lax.ppermute(s_here, "c", SWAP)
+    here = gather(jnp.concatenate([student, -target], axis=1), FS).reshape(rows, -1)
+    row_block = around(around(jnp.concatenate([student, target], axis=1), "zl"), "x")
     hidden_there = lax.ppermute(hidden, "c", SWAP)
-    target, hidden_there = lax.optimization_barrier((target, hidden_there))
-    t_there = lax.ppermute(target, "c", SWAP)
-    s_cols = jnp.concatenate([s_here, s_there], axis=0)
-    t_cols = jnp.concatenate([target, t_there], axis=0)
-    differ = dot(s_rows, s_cols, ROWS_T) - dot(t_rows, t_cols, ROWS_T)
+    columns = jnp.concatenate([here, lax.ppermute(here, "c", SWAP)], axis=0)
+    s_cols = columns[:, :full]
+    differ = dot(row_block, columns, ROWS_T)
+    differ = in_order(differ)
     squares = jnp.sum(differ * differ)
-    squares = (squares + lax.ppermute(squares, "c", SWAP))
+    squares = squares + lax.ppermute(squares, "c", SWAP)
     partial_grad = sum(dot(part, s_cols) for part in pieces(differ)[::-1])
     partial_grad = partial_grad.astype(jnp.bfloat16).reshape(group_xz, mine, full)
     grad_unit = 4.0 * jnp.sum(exchange(partial_grad, XZ).astype(jnp.float32), axis=0)

time: 214 us -> 198 us (0.925)
  starting transfers between devices: 69.2 us -> 50.5 us
  blocking collectives: 60.1 us -> 75.3 us
  between operations: 21.1 us -> 7.75 us
  local copies, waits for them, and re-layouts: 7.57 us -> 10.4 us
    all_to_all x5 -> x3, waiting for transfers between devices: 16.7 us -> 40.5 us  [exchange(): return lax.all_to_all(blocks, axes, split_axis=0, concat_axis=0, tiled=True)]
    all_to_all x5 -> x3, starting transfers between devices: 35.5 us -> 17.3 us  [exchange(): return lax.all_to_all(blocks, axes, split_axis=0, concat_axis=0, tiled=True)]
    all_to_all x3, blocking collectives: 56.5 us -> 71.7 us  [exchange(): return lax.all_to_all(blocks, axes, split_axis=0, concat_axis=0, tiled=True)]
    all_gather x1 -> x0, waiting for transfers between devices: 12.8 us -> none  [body(): teach = lax.all_gather(pair, 'y', axis=0).astype(jnp.float32)]
    ppermute x3 -> x7, waiting for transfers between devices: 10.3 us -> 0.55 us  [the longest x1 0.54 us: body(): columns = jnp.concatenate([here, lax.ppermute(here, 'c', SWAP)], axis=0)]
    ppermute x3 -> x7, starting transfers between devices: 14.8 us -> 23.8 us  [the longest x6 18.8 us: around(): lax.ppermute(block, axis, [(at, at ^ step) for at in range(4)])]
    ppermute x1, starting transfers between devices: 7.61 us -> 2.57 us  [body(): squares = squares + lax.ppermute(squares, 'c', SWAP)]
    unnamed x9 -> x12, local copies, waits for them, and re-layouts: 1.79 us -> 6.1 us
  transfers between devices with their start and end apart: 12 -> 13, of which waited for: 6 -> 6; matrix products, arithmetic and copies ran while one was open for 5% -> 4% of each run, Pallas kernels for 0% -> 0%
where the time goes in v4:
time: 198 us; the launch traced here: 196 us
  blocking collectives  75.3 us (38%)
  starting transfers between devices  50.5 us (26%)
  waiting for transfers between devices  42.3 us (21%)
  local copies, waits for them, and re-layouts  10.4 us (5%)
  between operations  7.75 us (4%)
  matrix products  6.22 us (3%)
  other arithmetic  3.9 us (2%)
    all_to_all x3, blocking collectives, exchange(): return lax.all_to_all(blocks, axes, split_axis=0, concat_axis=0, tiled=True)  71.7 us
    all_to_all x3, waiting for transfers between devices, exchange(): return lax.all_to_all(blocks, axes, split_axis=0, concat_axis=0, tiled=True)  40.5 us
    ppermute x6, starting transfers between devices, around(): lax.ppermute(block, axis, [(at, at ^ step) for at in range(4)])  18.8 us
    all_to_all x3, starting transfers between devices, exchange(): return lax.all_to_all(blocks, axes, split_axis=0, concat_axis=0, tiled=True)  17.3 us
    dot_general x8, matrix products, dot(): return lax.dot_general(a, b, dims, preferred_element_type=jnp.float32)  6.22 us
    unnamed x12, local copies, waits for them, and re-layouts  6.1 us
    ppermute x1, starting transfers between devices, body(): columns = jnp.concatenate([here, lax.ppermute(here, 'c', SWAP)], axis=0)  5 us
    ppermute x1, starting transfers between devices, body(): piece_there = lax.ppermute(piece, 'c', SWAP)  4.87 us
  transfers between devices with their start and end apart: 13, of which 6 were waited for; matrix products, arithmetic and copies ran while one was open for 4% of the time, Pallas kernels for 0%

profile of v4, /device:TPU:1, one launch (start us, length us, event | category | flops | bytes accessed | tf_op | source)
XLA Modules:
  0.0 196.5 jit_solution(4778475196909032422)
XLA Ops:
  0.6 0.0 copy-start
  0.6 1.0 copy-done
  1.6 1.0 fusion.6
  2.6 0.9 pad_maximum_fusion.1
  3.5 32.0 %all_to_all.30 = bf16[16,8,1792]{2,1,0:T(8,128)(2,1)S(1)} all-to-all(bf16[16,8,1792]{2,1,0:T(8,128)(2,1)S(1)} %pad_maximum_fusion.1), channel_id=1, replica_groups=mesh['x'=4,'zl'=4,'c'=2,'zh'=2,'y'=8] {'zh','y'}, dimensions={0} | all-to-all | bytes 917504 | tf_op jit(solution)/shard_map/all_to_all | solution.py:29
  35.5 0.1 convert_reduce_fusion.1
  35.5 0.1 multiply_reduce_fusion.2
  35.7 0.1 multiply_convert_fusion.1
  35.8 0.1 fusion.8
  35.9 0.1 fusion.9
  36.0 0.7 pad_maximum_fusion.4
  36.7 3.0 %collective-permute-start = (bf16[8,5632]{1,0:T(8,128)(2,1)S(1)}, bf16[8,5632]{1,0:T(8,128)(2,1)S(1)}, u32[]{:S(2)}, u32[]{:S(2)}) collective-permute-start(bf16[8,5632]{1,0:T(8,128)(2,1)S(1)} %get-tuple-element.8), channel_id=1, source_target_pairs={{0,32},{32,0},{64,96},{96,64},{1,33},{33,1},{65,97},{97,65},{2,34}... | collective-permute-start | bytes 270344 | tf_op jit(solution)/shard_map/ppermute | solution.py:53
  39.7 3.9 %collective-permute-start.1 = (bf16[8,5632]{1,0:T(8,128)(2,1)S(1)}, bf16[8,5632]{1,0:T(8,128)(2,1)S(1)}, u32[]{:S(2)}, u32[]{:S(2)}) collective-permute-start(bf16[8,5632]{1,0:T(8,128)(2,1)S(1)} %get-tuple-element.8), channel_id=1, source_target_pairs={{0,64},{32,96},{64,0},{96,32},{1,65},{33,97},{65,1},{97,33},{2,66}... | collective-permute-start | bytes 270344 | tf_op jit(solution)/shard_map/ppermute | solution.py:53
  43.6 2.4 %collective-permute-start.2 = (bf16[8,5632]{1,0:T(8,128)(2,1)S(1)}, bf16[8,5632]{1,0:T(8,128)(2,1)S(1)}, u32[]{:S(2)}, u32[]{:S(2)}) collective-permute-start(bf16[8,5632]{1,0:T(8,128)(2,1)S(1)} %get-tuple-element.8), channel_id=1, source_target_pairs={{0,96},{32,64},{64,32},{96,0},{1,97},{33,65},{65,33},{97,1},{2,98}... | collective-permute-start | bytes 270344 | tf_op jit(solution)/shard_map/ppermute | solution.py:53
  46.0 1.2 broadcast_in_dim.18
  47.2 6.7 %all-to-all-start.1 = ((bf16[16,8,5632]{2,1,0:T(8,128)(2,1)}), bf16[16,8,5632]{2,1,0:T(8,128)(2,1)S(1)}, u32[]{:S(2)}, u32[]{:S(2)}) async-start(bf16[16,8,5632]{2,1,0:T(8,128)(2,1)} %broadcast_in_dim.18), calls=%async_computation.1 | async-start | bytes 2883584 | tf_op jit(solution)/shard_map/all_to_all | solution.py:29
  53.9 0.0 collective-permute-done.2
  53.9 0.0 copy-start.1
  53.9 3.1 %collective-permute-start.3 = (bf16[32,5632]{1,0:T(8,128)(2,1)S(1)}, bf16[32,5632]{1,0:T(8,128)(2,1)S(1)}, u32[]{:S(2)}, u32[]{:S(2)}) collective-permute-start(bf16[32,5632]{1,0:T(8,128)(2,1)S(1)} %pad_maximum_fusion.2), channel_id=1, source_target_pairs={{0,128},{128,0},{256,384},{384,256},{1,129},{129,1},{257,385},{385... | collective-permute-start | bytes 1081352 | tf_op jit(solution)/shard_map/ppermute | solution.py:53
  57.1 4.4 %collective-permute-start.4 = (bf16[32,5632]{1,0:T(8,128)(2,1)S(1)}, bf16[32,5632]{1,0:T(8,128)(2,1)S(1)}, u32[]{:S(2)}, u32[]{:S(2)}) collective-permute-start(bf16[32,5632]{1,0:T(8,128)(2,1)S(1)} %pad_maximum_fusion.2), channel_id=1, source_target_pairs={{0,256},{128,384},{256,0},{384,128},{1,257},{129,385},{257,1},{385... | collective-permute-start | bytes 1081352 | tf_op jit(solution)/shard_map/ppermute | solution.py:53
  61.5 2.1 %collective-permute-start.5 = (bf16[32,5632]{1,0:T(8,128)(2,1)S(1)}, bf16[32,5632]{1,0:T(8,128)(2,1)S(1)}, u32[]{:S(2)}, u32[]{:S(2)}) collective-permute-start(bf16[32,5632]{1,0:T(8,128)(2,1)S(1)} %pad_maximum_fusion.2), channel_id=1, source_target_pairs={{0,384},{128,256},{256,128},{384,0},{1,385},{129,257},{257,129},{3... | collective-permute-start | bytes 1081352 | tf_op jit(solution)/shard_map/ppermute | solution.py:53
  63.6 0.6 constant_dynamic-update-slice_fusion.5
  64.2 0.6 constant_dynamic-update-slice_fusion.4
  64.8 1.5 constant_dynamic-update-slice_fusion.3
  66.4 25.2 %all-to-all-done.1 = bf16[16,8,5632]{2,1,0:T(8,128)(2,1)S(1)} async-done(((bf16[16,8,5632]{2,1,0:T(8,128)(2,1)}), bf16[16,8,5632]{2,1,0:T(8,128)(2,1)S(1)}, u32[]{:S(2)}, u32[]{:S(2)}) %all-to-all-start.1) | async-done | bytes 1441824 | tf_op jit(solution)/shard_map/all_to_all | solution.py:29
  91.6 5.0 %collective-permute-start.6 = (bf16[128,5632]{1,0:T(8,128)(2,1)S(1)}, bf16[128,5632]{1,0:T(8,128)(2,1)S(1)}, u32[]{:S(2)}, u32[]{:S(2)}) collective-permute-start(bf16[128,5632]{1,0:T(8,128)(2,1)S(1)} %bitcast.34), channel_id=1, source_target_pairs={{0,16},{16,0},{1,17},{17,1},{2,18},{18,2},{3,19},{19,3},{4,20},{20... | collective-permute-start | bytes 4325384 | tf_op jit(solution)/shard_map/ppermute | solution.py:94
  96.6 0.0 collective-permute-done.3
  96.6 0.8 constant_dynamic-update-slice_fusion.2
  97.4 0.8 constant_dynamic-update-slice_fusion.1
  98.1 0.8 constant_dynamic-update-slice_fusion
  98.9 0.5 collective-permute-done.6
  99.4 2.4 %fusion = f32[128,256]{1,0:T(8,128)S(1)} fusion(bf16[128,5632]{1,0:T(8,128)(2,1)} %constant_dynamic-update-slice_fusion, bf16[128,5632]{1,0:T(8,128)(2,1)S(1)} %collective-permute-done.6, bf16[128,5632]{1,0:T(8,128)(2,1)S(1)} %bitcast.35), kind=kOutput, calls=%fused_computation | convolution fusion | flops 374865920 | bytes 4456448 | tf_op jit(solution)/shard_map/dot_general | solution.py:18
  101.9 0.6 multiply_reduce_fusion
  102.6 0.1 pad_maximum_fusion
  102.6 0.3 fusion.20
  102.9 0.3 fusion.21
  103.2 1.0 fusion.7
  104.2 6.8 %all-to-all-start.2 = ((bf16[16,8,1536]{2,1,0:T(8,128)(2,1)}), bf16[16,8,1536]{2,1,0:T(8,128)(2,1)S(1)}, u32[]{:S(2)}, u32[]{:S(2)}) async-start(bf16[16,8,1536]{2,1,0:T(8,128)(2,1)} %fusion.7), calls=%async_computation.2 | async-start | bytes 786432 | tf_op jit(solution)/shard_map/all_to_all | solution.py:29
  111.0 0.0 copy-start.2
  111.0 2.6 %collective-permute-start.7 = (f32[]{:T(128)}, f32[]{:T(128)}, u32[]{:S(2)}, u32[]{:S(2)}) collective-permute-start(f32[]{:T(128)} %get-tuple-element.3), channel_id=1, source_target_pairs={{0,16},{16,0},{1,17},{17,1},{2,18},{18,2},{3,19},{19,3},{4,20},{20... | collective-permute-start | bytes 20 | tf_op jit(solution)/shard_map/ppermute | solution.py:99
  113.6 0.9 collective-permute-done.7
  119.5 4.4 %all-to-all-done.2 = bf16[16,8,1536]{2,1,0:T(8,128)(2,1)S(1)} async-done(((bf16[16,8,1536]{2,1,0:T(8,128)(2,1)}), bf16[16,8,1536]{2,1,0:T(8,128)(2,1)S(1)}, u32[]{:S(2)}, u32[]{:S(2)}) %all-to-all-start.2) | async-done | bytes 393248 | tf_op jit(solution)/shard_map/all_to_all | solution.py:29
  123.9 0.1 convert_reduce_fusion
  124.0 0.2 multiply_reduce_fusion.1
  124.2 0.1 multiply_convert_fusion
  124.3 23.2 %all_to_all.31 = bf16[16,8,1664]{2,1,0:T(8,128)(2,1)S(1)} all-to-all(bf16[16,8,1664]{2,1,0:T(8,128)(2,1)S(1)} %broadcast_in_dim.40), channel_id=1, replica_groups=mesh['x'=4,'zl'=4,'c'=2,'zh'=2,'y'=8] {'zh','y'}, dimensions={0} | all-to-all | bytes 851968 | tf_op jit(solution)/shard_map/all_to_all | solution.py:29
  147.6 4.9 %collective-permute-start.9 = (bf16[128,1536]{1,0:T(8,128)(2,1)S(1)}, bf16[128,1536]{1,0:T(8,128)(2,1)S(1)}, u32[]{:S(2)}, u32[]{:S(2)}) collective-permute-start(bf16[128,1536]{1,0:T(8,128)(2,1)S(1)} %slice.30), channel_id=1, source_target_pairs={{0,16},{16,0},{1,17},{17,1},{2,18},{18,2},{3,19},{19,3},{4,20},{20... | collective-permute-start | bytes 1179656 | tf_op jit(solution)/shard_map/ppermute | solution.py:112
  152.4 1.9 collective-permute-start.8
  154.4 0.2 fusion.12
  154.6 0.6 convert_reduce_fusion.2
  155.2 0.3 collective-permute-done.8
  155.5 0.2 convolution_add_fusion.1
  155.7 0.1 reshape.63
  155.9 0.7 concatenate.32
  156.6 16.5 %all_to_all.32 = f32[16,4,1536]{2,1,0:T(4,128)S(1)} all-to-all(f32[16,4,1536]{2,1,0:T(4,128)S(1)} %concatenate.32), channel_id=1, replica_groups=mesh['x'=4,'zl'=4,'c'=2,'zh'=2,'y'=8] {'x','zl'}, dimensions={0} | all-to-all | bytes 786432 | tf_op jit(solution)/shard_map/all_to_all | solution.py:29
  173.1 0.1 reduce_sum.79
  173.1 0.8 broadcast_in_dim.41
  173.9 3.9 %all-to-all-start.5 = ((f32[16,3,1536]{2,1,0:T(4,128)}), f32[16,3,1536]{2,1,0:T(4,128)S(1)}, u32[]{:S(2)}, u32[]{:S(2)}) async-start(f32[16,3,1536]{2,1,0:T(4,128)} %broadcast_in_dim.41), calls=%async_computation.5 | async-start | bytes 786432 | tf_op jit(solution)/shard_map/all_to_all | solution.py:29
  177.9 0.9 fusion.18
  178.7 0.5 slice.33
  179.9 10.8 %all-to-all-done.5 = f32[16,3,1536]{2,1,0:T(4,128)S(1)} async-done(((f32[16,3,1536]{2,1,0:T(4,128)}), f32[16,3,1536]{2,1,0:T(4,128)S(1)}, u32[]{:S(2)}, u32[]{:S(2)}) %all-to-all-start.5) | async-done | bytes 294944 | tf_op jit(solution)/shard_map/all_to_all | solution.py:29
  190.8 0.1 reshape.64
  190.9 3.6 %all_gather.3 = f32[96,1536]{1,0:T(8,128)S(1)} all-gather(f32[48,1536]{1,0:T(8,128)S(1)} %reshape.64), channel_id=1, replica_groups=mesh['x'=4,'zl'=4,'c'=2,'zh'=2,'y'=8] {'c'}, dimensions={0}, use_global_device_ids=true | all-gather | bytes 884736 | tf_op jit(solution)/shard_map/all_gather | solution.py:131
  194.5 0.8 copy.15
  (22 shorter events, 0.2 us)
Async XLA Ops:
  0.6 1.0 copy-start
  36.7 17.2 %collective-permute-start = (bf16[8,5632]{1,0:T(8,128)(2,1)S(1)}, bf16[8,5632]{1,0:T(8,128)(2,1)S(1)}, u32[]{:S(2)}, u32[]{:S(2)}) collective-permute-start(bf16[8,5632]{1,0:T(8,128)(2,1)S(1)} %get-tuple-element.8), channel_id=1, source_target_pairs={{0,32},{32,0},{64,96},{96,64},{1,33},{33,1},{65,97},{97,65},{2,34}... | collective-permute-start | bytes 270344 | tf_op jit(solution)/shard_map/ppermute | solution.py:53
  39.7 14.2 %collective-permute-start.1 = (bf16[8,5632]{1,0:T(8,128)(2,1)S(1)}, bf16[8,5632]{1,0:T(8,128)(2,1)S(1)}, u32[]{:S(2)}, u32[]{:S(2)}) collective-permute-start(bf16[8,5632]{1,0:T(8,128)(2,1)S(1)} %get-tuple-element.8), channel_id=1, source_target_pairs={{0,64},{32,96},{64,0},{96,32},{1,65},{33,97},{65,1},{97,33},{2,66}... | collective-permute-start | bytes 270344 | tf_op jit(solution)/shard_map/ppermute | solution.py:53
  43.6 10.3 %collective-permute-start.2 = (bf16[8,5632]{1,0:T(8,128)(2,1)S(1)}, bf16[8,5632]{1,0:T(8,128)(2,1)S(1)}, u32[]{:S(2)}, u32[]{:S(2)}) collective-permute-start(bf16[8,5632]{1,0:T(8,128)(2,1)S(1)} %get-tuple-element.8), channel_id=1, source_target_pairs={{0,96},{32,64},{64,32},{96,0},{1,97},{33,65},{65,33},{97,1},{2,98}... | collective-permute-start | bytes 270344 | tf_op jit(solution)/shard_map/ppermute | solution.py:53
  47.2 44.4 %all-to-all-start.1 = ((bf16[16,8,5632]{2,1,0:T(8,128)(2,1)}), bf16[16,8,5632]{2,1,0:T(8,128)(2,1)S(1)}, u32[]{:S(2)}, u32[]{:S(2)}) async-start(bf16[16,8,5632]{2,1,0:T(8,128)(2,1)} %broadcast_in_dim.18), calls=%async_computation.1 | async-start | bytes 2883584 | tf_op jit(solution)/shard_map/all_to_all | solution.py:29
  53.9 3.2 %copy-start.1 = (bf16[8,5632]{1,0:T(8,128)(2,1)}, bf16[8,5632]{1,0:T(8,128)(2,1)S(1)}, u32[]{:S(2)}) copy-start(bf16[8,5632]{1,0:T(8,128)(2,1)S(1)} %collective-permute-done.2) | copy-start | bytes 270340
  53.9 42.6 %collective-permute-start.3 = (bf16[32,5632]{1,0:T(8,128)(2,1)S(1)}, bf16[32,5632]{1,0:T(8,128)(2,1)S(1)}, u32[]{:S(2)}, u32[]{:S(2)}) collective-permute-start(bf16[32,5632]{1,0:T(8,128)(2,1)S(1)} %pad_maximum_fusion.2), channel_id=1, source_target_pairs={{0,128},{128,0},{256,384},{384,256},{1,129},{129,1},{257,385},{385... | collective-permute-start | bytes 1081352 | tf_op jit(solution)/shard_map/ppermute | solution.py:53
  57.1 40.3 %collective-permute-start.4 = (bf16[32,5632]{1,0:T(8,128)(2,1)S(1)}, bf16[32,5632]{1,0:T(8,128)(2,1)S(1)}, u32[]{:S(2)}, u32[]{:S(2)}) collective-permute-start(bf16[32,5632]{1,0:T(8,128)(2,1)S(1)} %pad_maximum_fusion.2), channel_id=1, source_target_pairs={{0,256},{128,384},{256,0},{384,128},{1,257},{129,385},{257,1},{385... | collective-permute-start | bytes 1081352 | tf_op jit(solution)/shard_map/ppermute | solution.py:53
  61.5 36.7 %collective-permute-start.5 = (bf16[32,5632]{1,0:T(8,128)(2,1)S(1)}, bf16[32,5632]{1,0:T(8,128)(2,1)S(1)}, u32[]{:S(2)}, u32[]{:S(2)}) collective-permute-start(bf16[32,5632]{1,0:T(8,128)(2,1)S(1)} %pad_maximum_fusion.2), channel_id=1, source_target_pairs={{0,384},{128,256},{256,128},{384,0},{1,385},{129,257},{257,129},{3... | collective-permute-start | bytes 1081352 | tf_op jit(solution)/shard_map/ppermute | solution.py:53
  91.6 7.8 %collective-permute-start.6 = (bf16[128,5632]{1,0:T(8,128)(2,1)S(1)}, bf16[128,5632]{1,0:T(8,128)(2,1)S(1)}, u32[]{:S(2)}, u32[]{:S(2)}) collective-permute-start(bf16[128,5632]{1,0:T(8,128)(2,1)S(1)} %bitcast.34), channel_id=1, source_target_pairs={{0,16},{16,0},{1,17},{17,1},{2,18},{18,2},{3,19},{19,3},{4,20},{20... | collective-permute-start | bytes 4325384 | tf_op jit(solution)/shard_map/ppermute | solution.py:94
  104.2 19.7 %all-to-all-start.2 = ((bf16[16,8,1536]{2,1,0:T(8,128)(2,1)}), bf16[16,8,1536]{2,1,0:T(8,128)(2,1)S(1)}, u32[]{:S(2)}, u32[]{:S(2)}) async-start(bf16[16,8,1536]{2,1,0:T(8,128)(2,1)} %fusion.7), calls=%async_computation.2 | async-start | bytes 786432 | tf_op jit(solution)/shard_map/all_to_all | solution.py:29
  111.0 41.5 %copy-start.2 = (bf16[128,96]{0,1:T(8,128)(2,1)S(1)}, bf16[128,96]{0,1:T(8,128)(2,1)}, u32[]{:S(2)}) copy-start(bf16[128,96]{0,1:T(8,128)(2,1)} %param.3) | copy-start | bytes 73732
  111.0 3.5 %collective-permute-start.7 = (f32[]{:T(128)}, f32[]{:T(128)}, u32[]{:S(2)}, u32[]{:S(2)}) collective-permute-start(f32[]{:T(128)} %get-tuple-element.3), channel_id=1, source_target_pairs={{0,16},{16,0},{1,17},{17,1},{2,18},{18,2},{3,19},{19,3},{4,20},{20... | collective-permute-start | bytes 20 | tf_op jit(solution)/shard_map/ppermute | solution.py:99
  147.6 8.0 %collective-permute-start.9 = (bf16[128,1536]{1,0:T(8,128)(2,1)S(1)}, bf16[128,1536]{1,0:T(8,128)(2,1)S(1)}, u32[]{:S(2)}, u32[]{:S(2)}) collective-permute-start(bf16[128,1536]{1,0:T(8,128)(2,1)S(1)} %slice.30), channel_id=1, source_target_pairs={{0,16},{16,0},{1,17},{17,1},{2,18},{18,2},{3,19},{19,3},{4,20},{20... | collective-permute-start | bytes 1179656 | tf_op jit(solution)/shard_map/ppermute | solution.py:112
  152.4 3.1 %collective-permute-start.8 = (bf16[128,96]{0,1:T(8,128)(2,1)S(1)}, bf16[128,96]{0,1:T(8,128)(2,1)S(1)}, u32[]{:S(2)}, u32[]{:S(2)}) collective-permute-start(bf16[128,96]{0,1:T(8,128)(2,1)S(1)} %copy-done.2), channel_id=1, source_target_pairs={{0,16},{16,0},{1,17},{17,1},{2,18},{18,2},{3,19},{19,3},{4,20},{20... | collective-permute-start | bytes 73736 | tf_op jit(solution)/shard_map/ppermute | solution.py:93
  173.9 16.8 %all-to-all-start.5 = ((f32[16,3,1536]{2,1,0:T(4,128)}), f32[16,3,1536]{2,1,0:T(4,128)S(1)}, u32[]{:S(2)}, u32[]{:S(2)}) async-start(f32[16,3,1536]{2,1,0:T(4,128)} %broadcast_in_dim.41), calls=%async_computation.5 | async-start | bytes 786432 | tf_op jit(solution)/shard_map/all_to_all | solution.py:29

commit v5 on v4

--- a/solution.py
+++ b/solution.py
@@ -47,6 +47,14 @@
     return (values * lax.rsqrt(total + EPSILON)).astype(jnp.bfloat16)
 
 
+def spread(value, shape):
+    lane = lax.broadcasted_iota(jnp.int32, shape, 1)
+    lanes = jnp.zeros(shape, jnp.bfloat16)
+    for index, part in enumerate(pieces(value)):
+        lanes = jnp.where(lane == index, part, lanes)
+    return lanes
+
+
 def around(block, axis):
     blocks = [block]
     for step in (1, 2, 3):
@@ -88,9 +96,13 @@
     target = normal(got[:, :, full:].astype(jnp.float32), (0, 2))
     target = target.transpose(1, 0, 2).reshape(mine, -1)
 
+    both, hidden_sent = lax.optimization_barrier(
+        (jnp.concatenate([student, target], axis=1), hidden)
+    )
     here = gather(jnp.concatenate([student, -target], axis=1), FS).reshape(rows, -1)
-    row_block = around(around(jnp.concatenate([student, target], axis=1), "zl"), "x")
-    hidden_there = lax.ppermute(hidden, "c", SWAP)
+    hidden_there = lax.ppermute(hidden_sent, "c", SWAP)
+    both, hidden_there = lax.optimization_barrier((both, hidden_there))
+    row_block = around(around(both, "zl"), "x")
     columns = jnp.concatenate([here, lax.ppermute(here, "c", SWAP)], axis=0)
     s_cols = columns[:, :full]
     differ = dot(row_block, columns, ROWS_T)
@@ -103,11 +115,9 @@
     radial = jnp.sum(unit * grad_unit, axis=1, keepdims=True)
     grad_embed = (inv_student * (grad_unit - unit * radial)).astype(jnp.bfloat16)
 
-    lane = lax.broadcasted_iota(jnp.int32, (mine, 128), 1)
-    tail = jnp.zeros((mine, 128), jnp.bfloat16)
-    for index, part in enumerate(pieces(squares)):
-        tail = jnp.where(lane == index, part, tail)
-    wide = gather(jnp.concatenate([grad_embed, tail], axis=1), FS).reshape(rows, -1)
+    wide = gather(
+        jnp.concatenate([grad_embed, spread(squares, (mine, 128))], axis=1), FS
+    ).reshape(rows, -1)
     piece = wide[:, :full]
     piece_there = lax.ppermute(piece, "c", SWAP)
     grad_hidden = dot(piece, projector, ROWS_T)
@@ -121,16 +131,17 @@
     )
     blocks = jnp.concatenate(
         [
-            proj_piece.reshape(group_xz, half // group_xz, full),
-            jnp.broadcast_to(loss_part, (group_xz, 1, full)),
+            proj_piece.astype(jnp.bfloat16).reshape(group_xz, half // group_xz, full),
+            jnp.broadcast_to(spread(loss_part, (1, full)), (group_xz, 1, full)),
         ],
         axis=1,
     )
-    summed = jnp.sum(exchange(blocks, XZ), axis=0)
-    loss = summed[-1, 0] / (rows * group(DP))
+    summed = jnp.sum(exchange(blocks, XZ).astype(jnp.float32), axis=0)
+    loss = jnp.sum(summed[-1]) / (rows * group(DP))
+    summed = summed[:-1].astype(jnp.bfloat16)
     grad_proj = lax.all_gather(
-        gather(summed[:-1], XZ).reshape(half, full), "c", axis=0, tiled=True
-    )
+        gather(summed, XZ).reshape(half, full), "c", axis=0, tiled=True
+    ).astype(jnp.float32)
     return (grad_hidden, grad_proj, loss)
 
 

time: 198 us -> 217 us (1.096)
  waiting for transfers between devices: 42.3 us -> 70 us
  blocking collectives: 75.3 us -> 48.9 us
  starting transfers between devices: 50.5 us -> 64.4 us
  between operations: 7.75 us -> 12.6 us
    ppermute x6, waiting for transfers between devices: 0.02 us -> 45.4 us  [around(): lax.ppermute(block, axis, [(at, at ^ step) for at in range(4)])]
    all_to_all x3 -> x2, blocking collectives: 71.7 us -> 44.4 us  [exchange(): return lax.all_to_all(blocks, axes, split_axis=0, concat_axis=0, tiled=True)]
    all_to_all x3 -> x4, waiting for transfers between devices: 40.5 us -> 23.6 us  [exchange(): return lax.all_to_all(blocks, axes, split_axis=0, concat_axis=0, tiled=True)]
    all_to_all x3 -> x4, starting transfers between devices: 17.3 us -> 28.6 us  [exchange(): return lax.all_to_all(blocks, axes, split_axis=0, concat_axis=0, tiled=True)]
    ppermute x1, starting transfers between devices: 1.92 us -> 4.89 us  [body(): hidden_there = lax.ppermute(hidden_sent, 'c', SWAP)]
    unnamed x12 -> x9, local copies, waits for them, and re-layouts: 6.1 us -> 4.41 us
  transfers between devices with their start and end apart: 13 -> 14, of which waited for: 6 -> 8; matrix products, arithmetic and copies ran while one was open for 4% -> 4% of each run, Pallas kernels for 0% -> 0%
where the time goes in v5:
time: 217 us; the launch traced here: 216 us
  waiting for transfers between devices  70 us (32%)
  starting transfers between devices  64.4 us (30%)
  blocking collectives  48.9 us (23%)
  between operations  12.6 us (6%)
  local copies, waits for them, and re-layouts  8.87 us (4%)
  matrix products  6.22 us (3%)
  other arithmetic  4.93 us (2%)
    ppermute x6, waiting for transfers between devices, around(): lax.ppermute(block, axis, [(at, at ^ step) for at in range(4)])  45.4 us
    all_to_all x2, blocking collectives, exchange(): return lax.all_to_all(blocks, axes, split_axis=0, concat_axis=0, tiled=True)  44.4 us
    all_to_all x4, starting transfers between devices, exchange(): return lax.all_to_all(blocks, axes, split_axis=0, concat_axis=0, tiled=True)  28.6 us
    all_to_all x4, waiting for transfers between devices, exchange(): return lax.all_to_all(blocks, axes, split_axis=0, concat_axis=0, tiled=True)  23.6 us
    ppermute x6, starting transfers between devices, around(): lax.ppermute(block, axis, [(at, at ^ step) for at in range(4)])  18.8 us
    dot_general x8, matrix products, dot(): return lax.dot_general(a, b, dims, preferred_element_type=jnp.float32)  6.22 us
    ppermute x1, starting transfers between devices, body(): piece_there = lax.ppermute(piece, 'c', SWAP)  5.22 us
    ppermute x1, starting transfers between devices, body(): hidden_there = lax.ppermute(hidden_sent, 'c', SWAP)  4.89 us
  transfers between devices with their start and end apart: 14, of which 8 were waited for; matrix products, arithmetic and copies ran while one was open for 4% of the time, Pallas kernels for 0%

profile of v5, /device:TPU:1, one launch (start us, length us, event | category | flops | bytes accessed | tf_op | source)
XLA Modules:
  0.0 216.0 jit_solution(14212683239509632742)
XLA Ops:
  0.6 0.0 copy-start
  0.6 1.0 copy-done
  1.6 1.0 fusion.6
  2.6 0.9 pad_maximum_fusion.1
  3.5 32.0 %all_to_all.30 = bf16[16,8,1792]{2,1,0:T(8,128)(2,1)S(1)} all-to-all(bf16[16,8,1792]{2,1,0:T(8,128)(2,1)S(1)} %pad_maximum_fusion.1), channel_id=1, replica_groups=mesh['x'=4,'zl'=4,'c'=2,'zh'=2,'y'=8] {'zh','y'}, dimensions={0} | all-to-all | bytes 917504 | tf_op jit(solution)/shard_map/all_to_all | solution.py:29
  35.5 0.1 convert_reduce_fusion.1
  35.6 0.1 multiply_reduce_fusion.2
  35.7 0.1 multiply_convert_fusion.1
  35.8 0.1 fusion.9
  35.9 0.1 fusion.10
  36.1 4.9 %collective-permute-start = (bf16[128,96]{0,1:T(8,128)(2,1)S(1)}, bf16[128,96]{0,1:T(8,128)(2,1)S(1)}, u32[]{:S(2)}, u32[]{:S(2)}) collective-permute-start(bf16[128,96]{0,1:T(8,128)(2,1)S(1)} %copy-done.1), channel_id=1, source_target_pairs={{0,16},{16,0},{1,17},{17,1},{2,18},{18,2},{3,19},{19,3},{4,20},{20... | collective-permute-start | bytes 73736 | tf_op jit(solution)/shard_map/ppermute | solution.py:103
  41.0 1.2 broadcast_in_dim.50
  42.2 4.7 %all-to-all-start.1 = ((bf16[16,8,5632]{2,1,0:T(8,128)(2,1)}), bf16[16,8,5632]{2,1,0:T(8,128)(2,1)S(1)}, u32[]{:S(2)}, u32[]{:S(2)}) async-start(bf16[16,8,5632]{2,1,0:T(8,128)(2,1)} %broadcast_in_dim.50), calls=%async_computation.1 | async-start | bytes 2883584 | tf_op jit(solution)/shard_map/all_to_all | solution.py:29
  46.9 2.8 %collective-permute-start.1 = (bf16[8,5632]{1,0:T(8,128)(2,1)S(1)}, bf16[8,5632]{1,0:T(8,128)(2,1)S(1)}, u32[]{:S(2)}, u32[]{:S(2)}) collective-permute-start(bf16[8,5632]{1,0:T(8,128)(2,1)S(1)} %get-tuple-element.9), channel_id=1, source_target_pairs={{0,32},{32,0},{64,96},{96,64},{1,33},{33,1},{65,97},{97,65},{2,34}... | collective-permute-start | bytes 270344 | tf_op jit(solution)/shard_map/ppermute | solution.py:61
  49.8 0.6 constant_dynamic-update-slice_fusion.3
  50.4 4.0 %collective-permute-start.2 = (bf16[8,5632]{1,0:T(8,128)(2,1)S(1)}, bf16[8,5632]{1,0:T(8,128)(2,1)S(1)}, u32[]{:S(2)}, u32[]{:S(2)}) collective-permute-start(bf16[8,5632]{1,0:T(8,128)(2,1)S(1)} %get-tuple-element.9), channel_id=1, source_target_pairs={{0,64},{32,96},{64,0},{96,32},{1,65},{33,97},{65,1},{97,33},{2,66}... | collective-permute-start | bytes 270344 | tf_op jit(solution)/shard_map/ppermute | solution.py:61
  54.4 2.4 %collective-permute-start.3 = (bf16[8,5632]{1,0:T(8,128)(2,1)S(1)}, bf16[8,5632]{1,0:T(8,128)(2,1)S(1)}, u32[]{:S(2)}, u32[]{:S(2)}) collective-permute-start(bf16[8,5632]{1,0:T(8,128)(2,1)S(1)} %get-tuple-element.9), channel_id=1, source_target_pairs={{0,96},{32,64},{64,32},{96,0},{1,97},{33,65},{65,33},{97,1},{2,98}... | collective-permute-start | bytes 270344 | tf_op jit(solution)/shard_map/ppermute | solution.py:61
  56.9 22.7 %collective-permute-done.1 = bf16[8,5632]{1,0:T(8,128)(2,1)S(1)} collective-permute-done((bf16[8,5632]{1,0:T(8,128)(2,1)S(1)}, bf16[8,5632]{1,0:T(8,128)(2,1)S(1)}, u32[]{:S(2)}, u32[]{:S(2)}) %collective-permute-start.1) | collective-permute-done | bytes 90144 | tf_op jit(solution)/shard_map/ppermute | solution.py:61
  79.6 0.6 constant_dynamic-update-slice_fusion.2
  80.3 9.3 %collective-permute-done.2 = bf16[8,5632]{1,0:T(8,128)(2,1)S(1)} collective-permute-done((bf16[8,5632]{1,0:T(8,128)(2,1)S(1)}, bf16[8,5632]{1,0:T(8,128)(2,1)S(1)}, u32[]{:S(2)}, u32[]{:S(2)}) %collective-permute-start.2) | collective-permute-done | bytes 90144 | tf_op jit(solution)/shard_map/ppermute | solution.py:61
  89.6 0.6 constant_dynamic-update-slice_fusion.1
  90.2 0.6 constant_dynamic-update-slice_fusion
  90.9 3.1 %collective-permute-start.4 = (bf16[32,5632]{1,0:T(8,128)(2,1)S(1)}, bf16[32,5632]{1,0:T(8,128)(2,1)S(1)}, u32[]{:S(2)}, u32[]{:S(2)}) collective-permute-start(bf16[32,5632]{1,0:T(8,128)(2,1)S(1)} %get-tuple-element.16), channel_id=1, source_target_pairs={{0,128},{128,0},{256,384},{384,256},{1,129},{129,1},{257,385},{385... | collective-permute-start | bytes 1081352 | tf_op jit(solution)/shard_map/ppermute | solution.py:61
  94.0 4.3 %collective-permute-start.5 = (bf16[32,5632]{1,0:T(8,128)(2,1)S(1)}, bf16[32,5632]{1,0:T(8,128)(2,1)S(1)}, u32[]{:S(2)}, u32[]{:S(2)}) collective-permute-start(bf16[32,5632]{1,0:T(8,128)(2,1)S(1)} %get-tuple-element.16), channel_id=1, source_target_pairs={{0,256},{128,384},{256,0},{384,128},{1,257},{129,385},{257,1},{385... | collective-permute-start | bytes 1081352 | tf_op jit(solution)/shard_map/ppermute | solution.py:61
  98.3 2.1 collective-permute-start.6
  100.5 3.3 %collective-permute-start.7 = (bf16[128,5632]{1,0:T(8,128)(2,1)S(1)}, bf16[128,5632]{1,0:T(8,128)(2,1)S(1)}, u32[]{:S(2)}, u32[]{:S(2)}) collective-permute-start(bf16[128,5632]{1,0:T(8,128)(2,1)S(1)} %bitcast.32), channel_id=1, source_target_pairs={{0,16},{16,0},{1,17},{17,1},{2,18},{18,2},{3,19},{19,3},{4,20},{20... | collective-permute-start | bytes 4325384 | tf_op jit(solution)/shard_map/ppermute | solution.py:106
  103.8 0.8 constant_dynamic-update-slice_fusion.6
  104.6 7.5 %collective-permute-done.5 = bf16[32,5632]{1,0:T(8,128)(2,1)S(1)} collective-permute-done((bf16[32,5632]{1,0:T(8,128)(2,1)S(1)}, bf16[32,5632]{1,0:T(8,128)(2,1)S(1)}, u32[]{:S(2)}, u32[]{:S(2)}) %collective-permute-start.5) | collective-permute-done | bytes 360480 | tf_op jit(solution)/shard_map/ppermute | solution.py:61
  112.1 0.8 constant_dynamic-update-slice_fusion.5
  112.8 5.8 %collective-permute-done.6 = bf16[32,5632]{1,0:T(8,128)(2,1)S(1)} collective-permute-done((bf16[32,5632]{1,0:T(8,128)(2,1)S(1)}, bf16[32,5632]{1,0:T(8,128)(2,1)S(1)}, u32[]{:S(2)}, u32[]{:S(2)}) %collective-permute-start.6) | collective-permute-done | bytes 360480 | tf_op jit(solution)/shard_map/ppermute | solution.py:61
  118.7 0.8 constant_dynamic-update-slice_fusion.4
  119.4 2.4 %fusion = f32[128,256]{1,0:T(8,128)S(1)} fusion(bf16[128,5632]{1,0:T(8,128)(2,1)} %constant_dynamic-update-slice_fusion.4, bf16[128,5632]{1,0:T(8,128)(2,1)S(1)} %collective-permute-done.7, bf16[128,5632]{1,0:T(8,128)(2,1)S(1)} %bitcast.33), kind=kOutput, calls=%fused_computation | convolution fusion | flops 374865920 | bytes 4456448 | tf_op jit(solution)/shard_map/dot_general | solution.py:18
  121.9 0.6 multiply_reduce_fusion
  122.6 0.1 pad_maximum_fusion
  122.6 0.3 fusion.24
  122.9 0.3 fusion.25
  123.2 1.0 fusion.7
  124.2 5.2 %all-to-all-start.2 = ((bf16[16,8,1536]{2,1,0:T(8,128)(2,1)}), bf16[16,8,1536]{2,1,0:T(8,128)(2,1)S(1)}, u32[]{:S(2)}, u32[]{:S(2)}) async-start(bf16[16,8,1536]{2,1,0:T(8,128)(2,1)} %fusion.7), calls=%async_computation.2 | async-start | bytes 786432 | tf_op jit(solution)/shard_map/all_to_all | solution.py:29
  129.5 3.5 %collective-permute-start.8 = (f32[]{:T(128)}, f32[]{:T(128)}, u32[]{:S(2)}, u32[]{:S(2)}) collective-permute-start(f32[]{:T(128)} %get-tuple-element.11), channel_id=1, source_target_pairs={{0,16},{16,0},{1,17},{17,1},{2,18},{18,2},{3,19},{19,3},{4,20},{20... | collective-permute-start | bytes 20 | tf_op jit(solution)/shard_map/ppermute | solution.py:111
  133.0 1.1 collective-permute-done.8
  139.0 3.3 %all-to-all-done.2 = bf16[16,8,1536]{2,1,0:T(8,128)(2,1)S(1)} async-done(((bf16[16,8,1536]{2,1,0:T(8,128)(2,1)}), bf16[16,8,1536]{2,1,0:T(8,128)(2,1)S(1)}, u32[]{:S(2)}, u32[]{:S(2)}) %all-to-all-start.2) | async-done | bytes 393248 | tf_op jit(solution)/shard_map/all_to_all | solution.py:29
  142.3 0.1 convert_reduce_fusion
  142.4 0.2 multiply_reduce_fusion.1
  142.6 0.1 multiply_convert_fusion
  142.7 0.8 broadcast_in_dim.55
  143.5 14.9 %all-to-all-start.3 = ((bf16[16,8,1664]{2,1,0:T(8,128)(2,1)}), bf16[16,8,1664]{2,1,0:T(8,128)(2,1)S(1)}, u32[]{:S(2)}, u32[]{:S(2)}) async-start(bf16[16,8,1664]{2,1,0:T(8,128)(2,1)} %broadcast_in_dim.55), calls=%async_computation.3 | async-start | bytes 851968 | tf_op jit(solution)/shard_map/all_to_all | solution.py:29
  158.4 14.8 %all-to-all-done.3 = bf16[16,8,1664]{2,1,0:T(8,128)(2,1)S(1)} async-done(((bf16[16,8,1664]{2,1,0:T(8,128)(2,1)}), bf16[16,8,1664]{2,1,0:T(8,128)(2,1)S(1)}, u32[]{:S(2)}, u32[]{:S(2)}) %all-to-all-start.3) | async-done | bytes 426016 | tf_op jit(solution)/shard_map/all_to_all | solution.py:29
  173.2 5.2 %collective-permute-start.9 = (bf16[128,1536]{1,0:T(8,128)(2,1)S(1)}, bf16[128,1536]{1,0:T(8,128)(2,1)S(1)}, u32[]{:S(2)}, u32[]{:S(2)}) collective-permute-start(bf16[128,1536]{1,0:T(8,128)(2,1)S(1)} %slice.31), channel_id=1, source_target_pairs={{0,16},{16,0},{1,17},{17,1},{2,18},{18,2},{3,19},{19,3},{4,20},{20... | collective-permute-start | bytes 1179656 | tf_op jit(solution)/shard_map/ppermute | solution.py:122
  178.5 0.6 convert_reduce_fusion.3
  184.0 0.2 fusion.13
  184.2 0.2 fusion.8
  184.4 0.1 reshape.72
  184.5 0.1 broadcast_in_dim.60
  184.6 0.2 pad_maximum_fusion.2
  184.8 12.4 %all_to_all.31 = bf16[16,4,1536]{2,1,0:T(4,128)(2,1)S(1)} all-to-all(bf16[16,4,1536]{2,1,0:T(4,128)(2,1)S(1)} %pad_maximum_fusion.2), channel_id=1, replica_groups=mesh['x'=4,'zl'=4,'c'=2,'zh'=2,'y'=8] {'x','zl'}, dimensions={0} | all-to-all | bytes 393216 | tf_op jit(solution)/shard_map/all_to_all | solution.py:29
  197.2 0.1 convert_reduce_fusion.2
  197.3 0.7 broadcast_in_dim.61
  198.0 3.7 %all-to-all-start.5 = ((bf16[16,3,1536]{2,1,0:T(4,128)(2,1)}), bf16[16,3,1536]{2,1,0:T(4,128)(2,1)S(1)}, u32[]{:S(2)}, u32[]{:S(2)}) async-start(bf16[16,3,1536]{2,1,0:T(4,128)(2,1)} %broadcast_in_dim.61), calls=%async_computation.5 | async-start | bytes 393216 | tf_op jit(solution)/shard_map/all_to_all | solution.py:29
  201.7 0.9 fusion.22
  202.6 0.6 slice_reduce_fusion
  203.9 5.5 %all-to-all-done.5 = bf16[16,3,1536]{2,1,0:T(4,128)(2,1)S(1)} async-done(((bf16[16,3,1536]{2,1,0:T(4,128)(2,1)}), bf16[16,3,1536]{2,1,0:T(4,128)(2,1)S(1)}, u32[]{:S(2)}, u32[]{:S(2)}) %all-to-all-start.5) | async-done | bytes 147488 | tf_op jit(solution)/shard_map/all_to_all | solution.py:29
  209.4 0.1 reshape.73
  209.5 4.5 %all_gather.3 = bf16[96,1536]{1,0:T(8,128)(2,1)S(1)} all-gather(bf16[48,1536]{1,0:T(8,128)(2,1)S(1)} %reshape.73), channel_id=1, replica_groups=mesh['x'=4,'zl'=4,'c'=2,'zh'=2,'y'=8] {'c'}, dimensions={0}, use_global_device_ids=true | all-gather | bytes 442368 | tf_op jit(solution)/shard_map/all_gather | solution.py:142
  214.0 0.9 convert_element_type.85
  (24 shorter events, 0.2 us)
Async XLA Ops:
  0.6 1.0 copy-start
  2.6 33.4 %copy-start.1 = (bf16[128,96]{0,1:T(8,128)(2,1)S(1)}, bf16[128,96]{0,1:T(8,128)(2,1)}, u32[]{:S(2)}) copy-start(bf16[128,96]{0,1:T(8,128)(2,1)} %param.3) | copy-start | bytes 73732
  36.1 10.9 %collective-permute-start = (bf16[128,96]{0,1:T(8,128)(2,1)S(1)}, bf16[128,96]{0,1:T(8,128)(2,1)S(1)}, u32[]{:S(2)}, u32[]{:S(2)}) collective-permute-start(bf16[128,96]{0,1:T(8,128)(2,1)S(1)} %copy-done.1), channel_id=1, source_target_pairs={{0,16},{16,0},{1,17},{17,1},{2,18},{18,2},{3,19},{19,3},{4,20},{20... | collective-permute-start | bytes 73736 | tf_op jit(solution)/shard_map/ppermute | solution.py:103
  42.2 58.3 %all-to-all-start.1 = ((bf16[16,8,5632]{2,1,0:T(8,128)(2,1)}), bf16[16,8,5632]{2,1,0:T(8,128)(2,1)S(1)}, u32[]{:S(2)}, u32[]{:S(2)}) async-start(bf16[16,8,5632]{2,1,0:T(8,128)(2,1)} %broadcast_in_dim.50), calls=%async_computation.1 | async-start | bytes 2883584 | tf_op jit(solution)/shard_map/all_to_all | solution.py:29
  46.9 32.7 %collective-permute-start.1 = (bf16[8,5632]{1,0:T(8,128)(2,1)S(1)}, bf16[8,5632]{1,0:T(8,128)(2,1)S(1)}, u32[]{:S(2)}, u32[]{:S(2)}) collective-permute-start(bf16[8,5632]{1,0:T(8,128)(2,1)S(1)} %get-tuple-element.9), channel_id=1, source_target_pairs={{0,32},{32,0},{64,96},{96,64},{1,33},{33,1},{65,97},{97,65},{2,34}... | collective-permute-start | bytes 270344 | tf_op jit(solution)/shard_map/ppermute | solution.py:61
  50.4 39.1 %collective-permute-start.2 = (bf16[8,5632]{1,0:T(8,128)(2,1)S(1)}, bf16[8,5632]{1,0:T(8,128)(2,1)S(1)}, u32[]{:S(2)}, u32[]{:S(2)}) collective-permute-start(bf16[8,5632]{1,0:T(8,128)(2,1)S(1)} %get-tuple-element.9), channel_id=1, source_target_pairs={{0,64},{32,96},{64,0},{96,32},{1,65},{33,97},{65,1},{97,33},{2,66}... | collective-permute-start | bytes 270344 | tf_op jit(solution)/shard_map/ppermute | solution.py:61
  54.4 35.8 %collective-permute-start.3 = (bf16[8,5632]{1,0:T(8,128)(2,1)S(1)}, bf16[8,5632]{1,0:T(8,128)(2,1)S(1)}, u32[]{:S(2)}, u32[]{:S(2)}) collective-permute-start(bf16[8,5632]{1,0:T(8,128)(2,1)S(1)} %get-tuple-element.9), channel_id=1, source_target_pairs={{0,96},{32,64},{64,32},{96,0},{1,97},{33,65},{65,33},{97,1},{2,98}... | collective-permute-start | bytes 270344 | tf_op jit(solution)/shard_map/ppermute | solution.py:61
  90.9 13.0 %collective-permute-start.4 = (bf16[32,5632]{1,0:T(8,128)(2,1)S(1)}, bf16[32,5632]{1,0:T(8,128)(2,1)S(1)}, u32[]{:S(2)}, u32[]{:S(2)}) collective-permute-start(bf16[32,5632]{1,0:T(8,128)(2,1)S(1)} %get-tuple-element.16), channel_id=1, source_target_pairs={{0,128},{128,0},{256,384},{384,256},{1,129},{129,1},{257,385},{385... | collective-permute-start | bytes 1081352 | tf_op jit(solution)/shard_map/ppermute | solution.py:61
  94.0 18.1 %collective-permute-start.5 = (bf16[32,5632]{1,0:T(8,128)(2,1)S(1)}, bf16[32,5632]{1,0:T(8,128)(2,1)S(1)}, u32[]{:S(2)}, u32[]{:S(2)}) collective-permute-start(bf16[32,5632]{1,0:T(8,128)(2,1)S(1)} %get-tuple-element.16), channel_id=1, source_target_pairs={{0,256},{128,384},{256,0},{384,128},{1,257},{129,385},{257,1},{385... | collective-permute-start | bytes 1081352 | tf_op jit(solution)/shard_map/ppermute | solution.py:61
  98.3 20.3 %collective-permute-start.6 = (bf16[32,5632]{1,0:T(8,128)(2,1)S(1)}, bf16[32,5632]{1,0:T(8,128)(2,1)S(1)}, u32[]{:S(2)}, u32[]{:S(2)}) collective-permute-start(bf16[32,5632]{1,0:T(8,128)(2,1)S(1)} %get-tuple-element.16), channel_id=1, source_target_pairs={{0,384},{128,256},{256,128},{384,0},{1,385},{129,257},{257,129},{3... | collective-permute-start | bytes 1081352 | tf_op jit(solution)/shard_map/ppermute | solution.py:61
  100.5 19.0 %collective-permute-start.7 = (bf16[128,5632]{1,0:T(8,128)(2,1)S(1)}, bf16[128,5632]{1,0:T(8,128)(2,1)S(1)}, u32[]{:S(2)}, u32[]{:S(2)}) collective-permute-start(bf16[128,5632]{1,0:T(8,128)(2,1)S(1)} %bitcast.32), channel_id=1, source_target_pairs={{0,16},{16,0},{1,17},{17,1},{2,18},{18,2},{3,19},{19,3},{4,20},{20... | collective-permute-start | bytes 4325384 | tf_op jit(solution)/shard_map/ppermute | solution.py:106
  124.2 18.1 %all-to-all-start.2 = ((bf16[16,8,1536]{2,1,0:T(8,128)(2,1)}), bf16[16,8,1536]{2,1,0:T(8,128)(2,1)S(1)}, u32[]{:S(2)}, u32[]{:S(2)}) async-start(bf16[16,8,1536]{2,1,0:T(8,128)(2,1)} %fusion.7), calls=%async_computation.2 | async-start | bytes 786432 | tf_op jit(solution)/shard_map/all_to_all | solution.py:29
  129.5 4.6 %collective-permute-start.8 = (f32[]{:T(128)}, f32[]{:T(128)}, u32[]{:S(2)}, u32[]{:S(2)}) collective-permute-start(f32[]{:T(128)} %get-tuple-element.11), channel_id=1, source_target_pairs={{0,16},{16,0},{1,17},{17,1},{2,18},{18,2},{3,19},{19,3},{4,20},{20... | collective-permute-start | bytes 20 | tf_op jit(solution)/shard_map/ppermute | solution.py:111
  143.5 29.7 %all-to-all-start.3 = ((bf16[16,8,1664]{2,1,0:T(8,128)(2,1)}), bf16[16,8,1664]{2,1,0:T(8,128)(2,1)S(1)}, u32[]{:S(2)}, u32[]{:S(2)}) async-start(bf16[16,8,1664]{2,1,0:T(8,128)(2,1)} %broadcast_in_dim.55), calls=%async_computation.3 | async-start | bytes 851968 | tf_op jit(solution)/shard_map/all_to_all | solution.py:29
  173.2 11.0 %collective-permute-start.9 = (bf16[128,1536]{1,0:T(8,128)(2,1)S(1)}, bf16[128,1536]{1,0:T(8,128)(2,1)S(1)}, u32[]{:S(2)}, u32[]{:S(2)}) collective-permute-start(bf16[128,1536]{1,0:T(8,128)(2,1)S(1)} %slice.31), channel_id=1, source_target_pairs={{0,16},{16,0},{1,17},{17,1},{2,18},{18,2},{3,19},{19,3},{4,20},{20... | collective-permute-start | bytes 1179656 | tf_op jit(solution)/shard_map/ppermute | solution.py:122
  198.0 11.3 %all-to-all-start.5 = ((bf16[16,3,1536]{2,1,0:T(4,128)(2,1)}), bf16[16,3,1536]{2,1,0:T(4,128)(2,1)S(1)}, u32[]{:S(2)}, u32[]{:S(2)}) async-start(bf16[16,3,1536]{2,1,0:T(4,128)(2,1)} %broadcast_in_dim.61), calls=%async_computation.5 | async-start | bytes 393216 | tf_op jit(solution)/shard_map/all_to_all | solution.py:29

commit v6 on v5

--- a/solution.py
+++ b/solution.py
@@ -47,6 +47,10 @@
     return (values * lax.rsqrt(total + EPSILON)).astype(jnp.bfloat16)
 
 
+def wide_rows(blocks):
+    return blocks.transpose(1, 0, 2).reshape(blocks.shape[1], -1)
+
+
 def spread(value, shape):
     lane = lax.broadcasted_iota(jnp.int32, shape, 1)
     lanes = jnp.zeros(shape, jnp.bfloat16)
@@ -80,32 +84,34 @@
     width_t = teacher.shape[1]
     core = lax.axis_index("c")
 
+    lanes = width_t
+    deep = full // lanes
     partial_embed = dot(hidden, projector).astype(jnp.bfloat16)
-    sent = jnp.concatenate(
-        [
-            partial_embed.reshape(group_fs, mine, full),
-            teacher.reshape(group_fs, mine, width_t),
-        ],
-        axis=2,
-    )
-    got = exchange(sent, FS)
-    embed = jnp.sum(got[:, :, :full].astype(jnp.float32), axis=0)
+    partial_embed = partial_embed.reshape(group_fs, mine, deep, lanes)
+    partial_embed = partial_embed.transpose(0, 2, 1, 3).reshape(group_fs, -1, lanes)
+    copies = jnp.broadcast_to(teacher[None], (group_fs,) + teacher.shape)
+    got = exchange(jnp.concatenate([partial_embed, copies], axis=1), FS)
+    cut = deep * mine
+
+    embed = jnp.sum(got[:, :cut].astype(jnp.float32), axis=0)
+    embed = embed.reshape(deep, mine, lanes).transpose(1, 0, 2).reshape(mine, full)
     inv_student = lax.rsqrt(jnp.sum(embed * embed, axis=1, keepdims=True) + EPSILON)
     unit = embed * inv_student
     student = unit.astype(jnp.bfloat16)
-    target = normal(got[:, :, full:].astype(jnp.float32), (0, 2))
-    target = target.transpose(1, 0, 2).reshape(mine, -1)
+    teach_mine = lax.dynamic_slice_in_dim(got, cut + lax.axis_index(FS) * mine, mine, 1)
+    target_mine = wide_rows(normal(teach_mine.astype(jnp.float32), (0, 2)))
 
-    both, hidden_sent = lax.optimization_barrier(
-        (jnp.concatenate([student, target], axis=1), hidden)
-    )
-    here = gather(jnp.concatenate([student, -target], axis=1), FS).reshape(rows, -1)
-    hidden_there = lax.ppermute(hidden_sent, "c", SWAP)
-    both, hidden_there = lax.optimization_barrier((both, hidden_there))
-    row_block = around(around(both, "zl"), "x")
-    columns = jnp.concatenate([here, lax.ppermute(here, "c", SWAP)], axis=0)
-    s_cols = columns[:, :full]
-    differ = dot(row_block, columns, ROWS_T)
+    near = around(jnp.concatenate([student, target_mine], axis=1), "zl")
+    near, got = lax.optimization_barrier((near, got))
+    row_block = around(near, "x")
+    s_here = gather(student, FS).reshape(rows, full)
+    target = wide_rows(normal(got[:, cut:].astype(jnp.float32), (0, 2)))
+    hidden_there = lax.ppermute(hidden, "c", SWAP)
+    target, hidden_there = lax.optimization_barrier((target, hidden_there))
+    s_cols = jnp.concatenate([s_here, lax.ppermute(s_here, "c", SWAP)], axis=0)
+    t_cols = jnp.concatenate([target, lax.ppermute(target, "c", SWAP)], axis=0)
+    s_rows, t_rows = row_block[:, :full], row_block[:, full:]
+    differ = dot(s_rows, s_cols, ROWS_T) - dot(t_rows, t_cols, ROWS_T)
     differ = in_order(differ)
     squares = jnp.sum(differ * differ)
     squares = squares + lax.ppermute(squares, "c", SWAP)

time: 217 us -> 210 us (0.968)
  blocking collectives: 48.9 us -> 16.5 us
  starting transfers between devices: 64.4 us -> 87.3 us
  waiting for transfers between devices: 70 us -> 67.5 us
  other arithmetic: 4.93 us -> 7.33 us
    ppermute x6, waiting for transfers between devices: 45.4 us -> 5.27 us  [around(): lax.ppermute(block, axis, [(at, at ^ step) for at in range(4)])]
    all_to_all x4 -> x5, waiting for transfers between devices: 23.6 us -> 61.3 us  [exchange(): return lax.all_to_all(blocks, axes, split_axis=0, concat_axis=0, tiled=True)]
    all_to_all x2 -> x1, blocking collectives: 44.4 us -> 12 us  [exchange(): return lax.all_to_all(blocks, axes, split_axis=0, concat_axis=0, tiled=True)]
    all_to_all x4 -> x5, starting transfers between devices: 28.6 us -> 47.4 us  [exchange(): return lax.all_to_all(blocks, axes, split_axis=0, concat_axis=0, tiled=True)]
    ppermute x2 -> x3, starting transfers between devices: 8.23 us -> 11 us  [the longest x1 4.93 us: body(): hidden_there = lax.ppermute(hidden, 'c', SWAP)]
    optimization_barrier x0 -> x1, local copies, waits for them, and re-layouts: none -> 2.71 us  [body(): near, got = lax.optimization_barrier((near, got))]
    dot_general x8 -> x9, matrix products: 6.22 us -> 7.64 us  [dot(): return lax.dot_general(a, b, dims, preferred_element_type=jnp.float32)]
    unnamed x9 -> x11, local copies, waits for them, and re-layouts: 4.41 us -> 3.55 us
  transfers between devices with their start and end apart: 14 -> 16, of which waited for: 8 -> 7; matrix products, arithmetic and copies ran while one was open for 4% -> 6% of each run, Pallas kernels for 0% -> 0%
where the time goes in v6:
time: 210 us; the launch traced here: 209 us
  starting transfers between devices  87.3 us (42%)
  waiting for transfers between devices  67.5 us (32%)
  blocking collectives  16.5 us (8%)
  between operations  12.8 us (6%)
  local copies, waits for them, and re-layouts  9.83 us (5%)
  matrix products  7.64 us (4%)
  other arithmetic  7.33 us (3%)
    all_to_all x5, waiting for transfers between devices, exchange(): return lax.all_to_all(blocks, axes, split_axis=0, concat_axis=0, tiled=True)  61.3 us
    all_to_all x5, starting transfers between devices, exchange(): return lax.all_to_all(blocks, axes, split_axis=0, concat_axis=0, tiled=True)  47.4 us
    ppermute x6, starting transfers between devices, around(): lax.ppermute(block, axis, [(at, at ^ step) for at in range(4)])  20.4 us
    all_to_all x1, blocking collectives, exchange(): return lax.all_to_all(blocks, axes, split_axis=0, concat_axis=0, tiled=True)  12 us
    dot_general x9, matrix products, dot(): return lax.dot_general(a, b, dims, preferred_element_type=jnp.float32)  7.64 us
    ppermute x6, waiting for transfers between devices, around(): lax.ppermute(block, axis, [(at, at ^ step) for at in range(4)])  5.27 us
    ppermute x1, starting transfers between devices, body(): piece_there = lax.ppermute(piece, 'c', SWAP)  5.19 us
    ppermute x1, starting transfers between devices, body(): hidden_there = lax.ppermute(hidden, 'c', SWAP)  4.93 us
  transfers between devices with their start and end apart: 16, of which 7 were waited for; matrix products, arithmetic and copies ran while one was open for 6% of the time, Pallas kernels for 0%

profile of v6, /device:TPU:1, one launch (start us, length us, event | category | flops | bytes accessed | tf_op | source)
XLA Modules:
  0.0 208.8 jit_solution(14671312554084799474)
XLA Ops:
  0.6 0.0 copy-start
  0.6 1.0 copy-done
  1.6 1.0 convolution_convert_fusion
  2.6 0.9 broadcast_in_dim.57
  3.6 1.2 pad_maximum_fusion
  4.8 16.2 %all-to-all-start = ((bf16[16,176,256]{2,1,0:T(8,128)(2,1)}), bf16[16,176,256]{2,1,0:T(8,128)(2,1)S(1)}, u32[]{:S(2)}, u32[]{:S(2)}) async-start(bf16[16,176,256]{2,1,0:T(8,128)(2,1)} %pad_maximum_fusion), calls=%async_computation | async-start | bytes 2883584 | tf_op jit(solution)/shard_map/all_to_all | solution.py:29
  21.0 37.3 %all-to-all-done = bf16[16,176,256]{2,1,0:T(8,128)(2,1)S(1)} async-done(((bf16[16,176,256]{2,1,0:T(8,128)(2,1)}), bf16[16,176,256]{2,1,0:T(8,128)(2,1)S(1)}, u32[]{:S(2)}, u32[]{:S(2)}) %all-to-all-start) | async-done | bytes 1441824 | tf_op jit(solution)/shard_map/all_to_all | solution.py:29
  58.3 0.1 fusion.12
  58.5 0.1 convert_reduce_fusion.1
  58.5 0.1 fusion.15
  58.7 0.5 copy-done.2
  59.2 0.1 multiply_convert_fusion.1
  59.3 0.1 fusion.13
  59.4 3.0 %collective-permute-start = (bf16[8,5632]{1,0:T(8,128)(2,1)S(1)}, bf16[8,5632]{1,0:T(8,128)(2,1)S(1)}, u32[]{:S(2)}, u32[]{:S(2)}) collective-permute-start(bf16[8,5632]{1,0:T(8,128)(2,1)S(1)} %pad_maximum_fusion.4), channel_id=1, source_target_pairs={{0,32},{32,0},{64,96},{96,64},{1,33},{33,1},{65,97},{97,65},{2,34}... | collective-permute-start | bytes 270344 | tf_op jit(solution)/shard_map/ppermute | solution.py:65
  62.4 4.7 %collective-permute-start.1 = (bf16[8,5632]{1,0:T(8,128)(2,1)S(1)}, bf16[8,5632]{1,0:T(8,128)(2,1)S(1)}, u32[]{:S(2)}, u32[]{:S(2)}) collective-permute-start(bf16[8,5632]{1,0:T(8,128)(2,1)S(1)} %pad_maximum_fusion.4), channel_id=1, source_target_pairs={{0,64},{32,96},{64,0},{96,32},{1,65},{33,97},{65,1},{97,33},{2,66}... | collective-permute-start | bytes 270344 | tf_op jit(solution)/shard_map/ppermute | solution.py:65
  67.2 3.1 %collective-permute-start.2 = (bf16[8,5632]{1,0:T(8,128)(2,1)S(1)}, bf16[8,5632]{1,0:T(8,128)(2,1)S(1)}, u32[]{:S(2)}, u32[]{:S(2)}) collective-permute-start(bf16[8,5632]{1,0:T(8,128)(2,1)S(1)} %pad_maximum_fusion.4), channel_id=1, source_target_pairs={{0,96},{32,64},{64,32},{96,0},{1,97},{33,65},{65,33},{97,1},{2,98}... | collective-permute-start | bytes 270344 | tf_op jit(solution)/shard_map/ppermute | solution.py:65
  70.2 4.9 %collective-permute-start.7 = (bf16[128,96]{0,1:T(8,128)(2,1)}, bf16[128,96]{0,1:T(8,128)(2,1)}, u32[]{:S(2)}, u32[]{:S(2)}) collective-permute-start(bf16[128,96]{0,1:T(8,128)(2,1)} %param.3), channel_id=1, source_target_pairs={{0,16},{16,0},{1,17},{17,1},{2,18},{18,2},{3,19},{19,3},{4,20},{20... | collective-permute-start | bytes 73736 | tf_op jit(solution)/shard_map/ppermute | solution.py:109
  75.2 0.8 broadcast_in_dim.58
  76.0 12.4 %all-to-all-start.1 = ((bf16[16,8,1536]{2,1,0:T(8,128)(2,1)}), bf16[16,8,1536]{2,1,0:T(8,128)(2,1)S(1)}, u32[]{:S(2)}, u32[]{:S(2)}) async-start(bf16[16,8,1536]{2,1,0:T(8,128)(2,1)} %broadcast_in_dim.58), calls=%async_computation.1 | async-start | bytes 786432 | tf_op jit(solution)/shard_map/all_to_all | solution.py:29
  88.5 3.2 %collective-permute-start.3 = (bf16[32,5632]{1,0:T(8,128)(2,1)S(1)}, bf16[32,5632]{1,0:T(8,128)(2,1)}, u32[]{:S(2)}, u32[]{:S(2)}) collective-permute-start(bf16[32,5632]{1,0:T(8,128)(2,1)S(1)} %pad_maximum_fusion.2), channel_id=1, source_target_pairs={{0,128},{128,0},{256,384},{384,256},{1,129},{129,1},{257,385},{385... | collective-permute-start | bytes 1081352 | tf_op jit(solution)/shard_map/ppermute | solution.py:65
  91.7 4.4 %collective-permute-start.4 = (bf16[32,5632]{1,0:T(8,128)(2,1)S(1)}, bf16[32,5632]{1,0:T(8,128)(2,1)}, u32[]{:S(2)}, u32[]{:S(2)}) collective-permute-start(bf16[32,5632]{1,0:T(8,128)(2,1)S(1)} %pad_maximum_fusion.2), channel_id=1, source_target_pairs={{0,256},{128,384},{256,0},{384,128},{1,257},{129,385},{257,1},{385... | collective-permute-start | bytes 1081352 | tf_op jit(solution)/shard_map/ppermute | solution.py:65
  96.1 2.0 collective-permute-start.5
  98.1 2.7 %copy.25 = bf16[16,176,256]{1,2,0:T(8,128)(2,1)S(1)} copy(bf16[16,176,256]{2,1,0:T(8,128)(2,1)} %copy-done.1) | data formatting | bytes 2883584 | tf_op jit(solution)/shard_map/optimization_barrier | solution.py:105
  100.8 0.6 fusion.4
  101.5 1.5 fusion.5
  102.9 3.0 %collective-permute-start.8 = (bf16[128,4096]{0,1:T(8,128)(2,1)}, bf16[128,4096]{0,1:T(8,128)(2,1)}, u32[]{:S(2)}, u32[]{:S(2)}) collective-permute-start(bf16[128,4096]{0,1:T(8,128)(2,1)} %bitcast.11), channel_id=1, source_target_pairs={{0,16},{16,0},{1,17},{17,1},{2,18},{18,2},{3,19},{19,3},{4,20},{20... | collective-permute-start | bytes 3145736 | tf_op jit(solution)/shard_map/ppermute | solution.py:112
  106.0 1.0 constant_dynamic-update-slice_fusion.2
  107.0 3.2 %collective-permute-done.4 = bf16[32,5632]{1,0:T(8,128)(2,1)} collective-permute-done((bf16[32,5632]{1,0:T(8,128)(2,1)S(1)}, bf16[32,5632]{1,0:T(8,128)(2,1)}, u32[]{:S(2)}, u32[]{:S(2)}) %collective-permute-start.4) | collective-permute-done | bytes 360480 | tf_op jit(solution)/shard_map/ppermute | solution.py:65
  110.3 1.0 constant_dynamic-update-slice_fusion.1
  111.3 3.1 %collective-permute-start.6 = (bf16[128,1536]{1,0:T(8,128)(2,1)S(1)}, bf16[128,1536]{1,0:T(8,128)(2,1)S(1)}, u32[]{:S(2)}, u32[]{:S(2)}) collective-permute-start(bf16[128,1536]{1,0:T(8,128)(2,1)S(1)} %bitcast.44), channel_id=1, source_target_pairs={{0,16},{16,0},{1,17},{17,1},{2,18},{18,2},{3,19},{19,3},{4,20},{20... | collective-permute-start | bytes 1179656 | tf_op jit(solution)/shard_map/ppermute | solution.py:111
  114.4 2.0 collective-permute-done.5
  116.4 2.0 fusion.6
  118.5 0.4 convolution_subtract_fusion
  118.9 0.6 multiply_reduce_fusion
  119.6 0.3 fusion.28
  119.9 0.3 fusion.27
  120.2 1.0 fusion.2
  121.2 3.6 %all-to-all-start.2 = ((bf16[16,8,1536]{2,1,0:T(8,128)(2,1)}), bf16[16,8,1536]{2,1,0:T(8,128)(2,1)S(1)}, u32[]{:S(2)}, u32[]{:S(2)}) async-start(bf16[16,8,1536]{2,1,0:T(8,128)(2,1)} %fusion.2), calls=%async_computation.2 | async-start | bytes 786432 | tf_op jit(solution)/shard_map/all_to_all | solution.py:29
  124.7 3.2 %collective-permute-start.9 = (f32[]{:T(128)}, f32[]{:T(128)}, u32[]{:S(2)}, u32[]{:S(2)}) collective-permute-start(f32[]{:T(128)} %get-tuple-element.11), channel_id=1, source_target_pairs={{0,16},{16,0},{1,17},{17,1},{2,18},{18,2},{3,19},{19,3},{4,20},{20... | collective-permute-start | bytes 20 | tf_op jit(solution)/shard_map/ppermute | solution.py:117
  128.0 0.9 collective-permute-done.9
  133.9 3.7 %all-to-all-done.2 = bf16[16,8,1536]{2,1,0:T(8,128)(2,1)S(1)} async-done(((bf16[16,8,1536]{2,1,0:T(8,128)(2,1)}), bf16[16,8,1536]{2,1,0:T(8,128)(2,1)S(1)}, u32[]{:S(2)}, u32[]{:S(2)}) %all-to-all-start.2) | async-done | bytes 393248 | tf_op jit(solution)/shard_map/all_to_all | solution.py:29
  137.6 0.1 convert_reduce_fusion
  137.7 0.2 fusion.17
  137.9 0.1 multiply_convert_fusion
  138.0 0.8 broadcast_in_dim.63
  138.8 11.5 %all-to-all-start.3 = ((bf16[16,8,1664]{2,1,0:T(8,128)(2,1)}), bf16[16,8,1664]{2,1,0:T(8,128)(2,1)S(1)}, u32[]{:S(2)}, u32[]{:S(2)}) async-start(bf16[16,8,1664]{2,1,0:T(8,128)(2,1)} %broadcast_in_dim.63), calls=%async_computation.3 | async-start | bytes 851968 | tf_op jit(solution)/shard_map/all_to_all | solution.py:29
  150.2 14.8 %all-to-all-done.3 = bf16[16,8,1664]{2,1,0:T(8,128)(2,1)S(1)} async-done(((bf16[16,8,1664]{2,1,0:T(8,128)(2,1)}), bf16[16,8,1664]{2,1,0:T(8,128)(2,1)S(1)}, u32[]{:S(2)}, u32[]{:S(2)}) %all-to-all-start.3) | async-done | bytes 426016 | tf_op jit(solution)/shard_map/all_to_all | solution.py:29
  165.1 5.2 %collective-permute-start.10 = (bf16[128,1536]{1,0:T(8,128)(2,1)S(1)}, bf16[128,1536]{1,0:T(8,128)(2,1)S(1)}, u32[]{:S(2)}, u32[]{:S(2)}) collective-permute-start(bf16[128,1536]{1,0:T(8,128)(2,1)S(1)} %slice.37), channel_id=1, source_target_pairs={{0,16},{16,0},{1,17},{17,1},{2,18},{18,2},{3,19},{19,3},{4,20},{20... | collective-permute-start | bytes 1179656 | tf_op jit(solution)/shard_map/ppermute | solution.py:128
  170.3 0.6 convert_reduce_fusion.3
  175.8 0.9 fusion.19
  176.7 0.9 fusion.3
  177.7 0.1 reshape.116
  177.8 0.1 broadcast_in_dim.68
  177.8 0.2 pad_maximum_fusion.3
  178.0 12.0 %all_to_all.30 = bf16[16,4,1536]{2,1,0:T(4,128)(2,1)S(1)} all-to-all(bf16[16,4,1536]{2,1,0:T(4,128)(2,1)S(1)} %pad_maximum_fusion.3), channel_id=1, replica_groups=mesh['x'=4,'zl'=4,'c'=2,'zh'=2,'y'=8] {'x','zl'}, dimensions={0} | all-to-all | bytes 393216 | tf_op jit(solution)/shard_map/all_to_all | solution.py:29
  190.0 0.1 convert_reduce_fusion.2
  190.1 0.7 broadcast_in_dim.69
  190.9 3.7 %all-to-all-start.5 = ((bf16[16,3,1536]{2,1,0:T(4,128)(2,1)}), bf16[16,3,1536]{2,1,0:T(4,128)(2,1)S(1)}, u32[]{:S(2)}, u32[]{:S(2)}) async-start(bf16[16,3,1536]{2,1,0:T(4,128)(2,1)} %broadcast_in_dim.69), calls=%async_computation.5 | async-start | bytes 393216 | tf_op jit(solution)/shard_map/all_to_all | solution.py:29
  194.6 0.9 fusion.30
  195.5 0.6 slice_reduce_fusion
  196.7 5.5 %all-to-all-done.5 = bf16[16,3,1536]{2,1,0:T(4,128)(2,1)S(1)} async-done(((bf16[16,3,1536]{2,1,0:T(4,128)(2,1)}), bf16[16,3,1536]{2,1,0:T(4,128)(2,1)S(1)}, u32[]{:S(2)}, u32[]{:S(2)}) %all-to-all-start.5) | async-done | bytes 147488 | tf_op jit(solution)/shard_map/all_to_all | solution.py:29
  202.2 0.1 reshape.117
  202.3 4.5 %all_gather.3 = bf16[96,1536]{1,0:T(8,128)(2,1)S(1)} all-gather(bf16[48,1536]{1,0:T(8,128)(2,1)S(1)} %reshape.117), channel_id=1, replica_groups=mesh['x'=4,'zl'=4,'c'=2,'zh'=2,'y'=8] {'c'}, dimensions={0}, use_global_device_ids=true | all-gather | bytes 442368 | tf_op jit(solution)/shard_map/all_gather | solution.py:148
  206.8 0.9 convert_element_type.97
  (34 shorter events, 0.3 us)
Async XLA Ops:
  0.6 1.0 copy-start
  4.8 53.5 %all-to-all-start = ((bf16[16,176,256]{2,1,0:T(8,128)(2,1)}), bf16[16,176,256]{2,1,0:T(8,128)(2,1)S(1)}, u32[]{:S(2)}, u32[]{:S(2)}) async-start(bf16[16,176,256]{2,1,0:T(8,128)(2,1)} %pad_maximum_fusion), calls=%async_computation | async-start | bytes 2883584 | tf_op jit(solution)/shard_map/all_to_all | solution.py:29
  58.3 37.8 %copy-start.1 = (bf16[16,176,256]{2,1,0:T(8,128)(2,1)}, bf16[16,176,256]{2,1,0:T(8,128)(2,1)S(1)}, u32[]{:S(2)}) copy-start(bf16[16,176,256]{2,1,0:T(8,128)(2,1)S(1)} %all-to-all-done) | copy-start | bytes 4325380
  58.7 0.6 copy-start.2
  59.4 29.0 %collective-permute-start = (bf16[8,5632]{1,0:T(8,128)(2,1)S(1)}, bf16[8,5632]{1,0:T(8,128)(2,1)S(1)}, u32[]{:S(2)}, u32[]{:S(2)}) collective-permute-start(bf16[8,5632]{1,0:T(8,128)(2,1)S(1)} %pad_maximum_fusion.4), channel_id=1, source_target_pairs={{0,32},{32,0},{64,96},{96,64},{1,33},{33,1},{65,97},{97,65},{2,34}... | collective-permute-start | bytes 270344 | tf_op jit(solution)/shard_map/ppermute | solution.py:65
  62.4 26.0 %collective-permute-start.1 = (bf16[8,5632]{1,0:T(8,128)(2,1)S(1)}, bf16[8,5632]{1,0:T(8,128)(2,1)S(1)}, u32[]{:S(2)}, u32[]{:S(2)}) collective-permute-start(bf16[8,5632]{1,0:T(8,128)(2,1)S(1)} %pad_maximum_fusion.4), channel_id=1, source_target_pairs={{0,64},{32,96},{64,0},{96,32},{1,65},{33,97},{65,1},{97,33},{2,66}... | collective-permute-start | bytes 270344 | tf_op jit(solution)/shard_map/ppermute | solution.py:65
  67.2 21.3 %collective-permute-start.2 = (bf16[8,5632]{1,0:T(8,128)(2,1)S(1)}, bf16[8,5632]{1,0:T(8,128)(2,1)S(1)}, u32[]{:S(2)}, u32[]{:S(2)}) collective-permute-start(bf16[8,5632]{1,0:T(8,128)(2,1)S(1)} %pad_maximum_fusion.4), channel_id=1, source_target_pairs={{0,96},{32,64},{64,32},{96,0},{1,97},{33,65},{65,33},{97,1},{2,98}... | collective-permute-start | bytes 270344 | tf_op jit(solution)/shard_map/ppermute | solution.py:65
  70.2 32.7 %collective-permute-start.7 = (bf16[128,96]{0,1:T(8,128)(2,1)}, bf16[128,96]{0,1:T(8,128)(2,1)}, u32[]{:S(2)}, u32[]{:S(2)}) collective-permute-start(bf16[128,96]{0,1:T(8,128)(2,1)} %param.3), channel_id=1, source_target_pairs={{0,16},{16,0},{1,17},{17,1},{2,18},{18,2},{3,19},{19,3},{4,20},{20... | collective-permute-start | bytes 73736 | tf_op jit(solution)/shard_map/ppermute | solution.py:109
  76.0 35.3 %all-to-all-start.1 = ((bf16[16,8,1536]{2,1,0:T(8,128)(2,1)}), bf16[16,8,1536]{2,1,0:T(8,128)(2,1)S(1)}, u32[]{:S(2)}, u32[]{:S(2)}) async-start(bf16[16,8,1536]{2,1,0:T(8,128)(2,1)} %broadcast_in_dim.58), calls=%async_computation.1 | async-start | bytes 786432 | tf_op jit(solution)/shard_map/all_to_all | solution.py:29
  88.5 17.5 %collective-permute-start.3 = (bf16[32,5632]{1,0:T(8,128)(2,1)S(1)}, bf16[32,5632]{1,0:T(8,128)(2,1)}, u32[]{:S(2)}, u32[]{:S(2)}) collective-permute-start(bf16[32,5632]{1,0:T(8,128)(2,1)S(1)} %pad_maximum_fusion.2), channel_id=1, source_target_pairs={{0,128},{128,0},{256,384},{384,256},{1,129},{129,1},{257,385},{385... | collective-permute-start | bytes 1081352 | tf_op jit(solution)/shard_map/ppermute | solution.py:65
  91.7 18.6 %collective-permute-start.4 = (bf16[32,5632]{1,0:T(8,128)(2,1)S(1)}, bf16[32,5632]{1,0:T(8,128)(2,1)}, u32[]{:S(2)}, u32[]{:S(2)}) collective-permute-start(bf16[32,5632]{1,0:T(8,128)(2,1)S(1)} %pad_maximum_fusion.2), channel_id=1, source_target_pairs={{0,256},{128,384},{256,0},{384,128},{1,257},{129,385},{257,1},{385... | collective-permute-start | bytes 1081352 | tf_op jit(solution)/shard_map/ppermute | solution.py:65
  96.1 20.3 %collective-permute-start.5 = (bf16[32,5632]{1,0:T(8,128)(2,1)S(1)}, bf16[32,5632]{1,0:T(8,128)(2,1)S(1)}, u32[]{:S(2)}, u32[]{:S(2)}) collective-permute-start(bf16[32,5632]{1,0:T(8,128)(2,1)S(1)} %pad_maximum_fusion.2), channel_id=1, source_target_pairs={{0,384},{128,256},{256,128},{384,0},{1,385},{129,257},{257,129},{3... | collective-permute-start | bytes 1081352 | tf_op jit(solution)/shard_map/ppermute | solution.py:65
  102.9 13.5 %collective-permute-start.8 = (bf16[128,4096]{0,1:T(8,128)(2,1)}, bf16[128,4096]{0,1:T(8,128)(2,1)}, u32[]{:S(2)}, u32[]{:S(2)}) collective-permute-start(bf16[128,4096]{0,1:T(8,128)(2,1)} %bitcast.11), channel_id=1, source_target_pairs={{0,16},{16,0},{1,17},{17,1},{2,18},{18,2},{3,19},{19,3},{4,20},{20... | collective-permute-start | bytes 3145736 | tf_op jit(solution)/shard_map/ppermute | solution.py:112
  111.3 7.2 %collective-permute-start.6 = (bf16[128,1536]{1,0:T(8,128)(2,1)S(1)}, bf16[128,1536]{1,0:T(8,128)(2,1)S(1)}, u32[]{:S(2)}, u32[]{:S(2)}) collective-permute-start(bf16[128,1536]{1,0:T(8,128)(2,1)S(1)} %bitcast.44), channel_id=1, source_target_pairs={{0,16},{16,0},{1,17},{17,1},{2,18},{18,2},{3,19},{19,3},{4,20},{20... | collective-permute-start | bytes 1179656 | tf_op jit(solution)/shard_map/ppermute | solution.py:111
  120.1 17.5 %copy-start.3 = (f32[8]{0:T(128)S(1)}, f32[8]{0:T(128)}, u32[]{:S(2)}) copy-start(f32[8]{0:T(128)} %copy-done.2) | copy-start | bytes 100
  121.2 16.4 %all-to-all-start.2 = ((bf16[16,8,1536]{2,1,0:T(8,128)(2,1)}), bf16[16,8,1536]{2,1,0:T(8,128)(2,1)S(1)}, u32[]{:S(2)}, u32[]{:S(2)}) async-start(bf16[16,8,1536]{2,1,0:T(8,128)(2,1)} %fusion.2), calls=%async_computation.2 | async-start | bytes 786432 | tf_op jit(solution)/shard_map/all_to_all | solution.py:29
  124.7 4.2 %collective-permute-start.9 = (f32[]{:T(128)}, f32[]{:T(128)}, u32[]{:S(2)}, u32[]{:S(2)}) collective-permute-start(f32[]{:T(128)} %get-tuple-element.11), channel_id=1, source_target_pairs={{0,16},{16,0},{1,17},{17,1},{2,18},{18,2},{3,19},{19,3},{4,20},{20... | collective-permute-start | bytes 20 | tf_op jit(solution)/shard_map/ppermute | solution.py:117
  138.8 26.3 %all-to-all-start.3 = ((bf16[16,8,1664]{2,1,0:T(8,128)(2,1)}), bf16[16,8,1664]{2,1,0:T(8,128)(2,1)S(1)}, u32[]{:S(2)}, u32[]{:S(2)}) async-start(bf16[16,8,1664]{2,1,0:T(8,128)(2,1)} %broadcast_in_dim.63), calls=%async_computation.3 | async-start | bytes 851968 | tf_op jit(solution)/shard_map/all_to_all | solution.py:29
  165.1 11.7 %collective-permute-start.10 = (bf16[128,1536]{1,0:T(8,128)(2,1)S(1)}, bf16[128,1536]{1,0:T(8,128)(2,1)S(1)}, u32[]{:S(2)}, u32[]{:S(2)}) collective-permute-start(bf16[128,1536]{1,0:T(8,128)(2,1)S(1)} %slice.37), channel_id=1, source_target_pairs={{0,16},{16,0},{1,17},{17,1},{2,18},{18,2},{3,19},{19,3},{4,20},{20... | collective-permute-start | bytes 1179656 | tf_op jit(solution)/shard_map/ppermute | solution.py:128
  190.9 11.3 %all-to-all-start.5 = ((bf16[16,3,1536]{2,1,0:T(4,128)(2,1)}), bf16[16,3,1536]{2,1,0:T(4,128)(2,1)S(1)}, u32[]{:S(2)}, u32[]{:S(2)}) async-start(bf16[16,3,1536]{2,1,0:T(4,128)(2,1)} %broadcast_in_dim.69), calls=%async_computation.5 | async-start | bytes 393216 | tf_op jit(solution)/shard_map/all_to_all | solution.py:29

commit v7 on v5

--- a/solution.py
+++ b/solution.py
@@ -96,13 +96,15 @@
     target = normal(got[:, :, full:].astype(jnp.float32), (0, 2))
     target = target.transpose(1, 0, 2).reshape(mine, -1)
 
-    both, hidden_sent = lax.optimization_barrier(
-        (jnp.concatenate([student, target], axis=1), hidden)
-    )
-    here = gather(jnp.concatenate([student, -target], axis=1), FS).reshape(rows, -1)
+    near = around(jnp.concatenate([student, target], axis=1), "zl")
+    mine_cols = jnp.concatenate([student, -target], axis=1)
+    pair = jnp.concatenate([mine_cols, lax.ppermute(mine_cols, "zh", SWAP)], axis=0)
+    here = gather(pair, ("y",)).reshape(rows, -1)
+    _, hidden_sent = lax.optimization_barrier((pair, hidden))
     hidden_there = lax.ppermute(hidden_sent, "c", SWAP)
-    both, hidden_there = lax.optimization_barrier((both, hidden_there))
-    row_block = around(around(both, "zl"), "x")
+    near, hidden_there = lax.optimization_barrier((near, hidden_there))
+    row_block = around(near, "x")
+    here, row_block = lax.optimization_barrier((here, row_block))
     columns = jnp.concatenate([here, lax.ppermute(here, "c", SWAP)], axis=0)
     s_cols = columns[:, :full]
     differ = dot(row_block, columns, ROWS_T)

time: 217 us -> 192 us (0.88)
  waiting for transfers between devices: 70 us -> 54 us
  starting transfers between devices: 64.4 us -> 60 us
  local copies, waits for them, and re-layouts: 8.87 us -> 5.56 us
    ppermute x6, waiting for transfers between devices: 45.4 us -> 17.2 us  [around(): lax.ppermute(block, axis, [(at, at ^ step) for at in range(4)])]
    all_to_all x4, starting transfers between devices: 28.6 us -> 21 us  [exchange(): return lax.all_to_all(blocks, axes, split_axis=0, concat_axis=0, tiled=True)]
    ppermute x0 -> x1, waiting for transfers between devices: none -> 6.81 us  [body(): lax.ppermute(mine_cols, 'zh', SWAP)]
    unnamed x9 -> x5, local copies, waits for them, and re-layouts: 4.41 us -> 1.06 us
    ppermute x1, waiting for transfers between devices: 0.01 us -> 2.84 us  [body(): columns = jnp.concatenate([here, lax.ppermute(here, 'c', SWAP)], axis=0)]
    ppermute x0 -> x1, starting transfers between devices: none -> 2.47 us  [body(): lax.ppermute(mine_cols, 'zh', SWAP)]
  transfers between devices with their start and end apart: 14 -> 15, of which waited for: 8 -> 10; matrix products, arithmetic and copies ran while one was open for 4% -> 1% of each run, Pallas kernels for 0% -> 0%
where the time goes in v7:
time: 192 us; the launch traced here: 191 us
  starting transfers between devices  60 us (31%)
  waiting for transfers between devices  54 us (28%)
  blocking collectives  48.6 us (25%)
  between operations  12.7 us (7%)
  local copies, waits for them, and re-layouts  5.56 us (3%)
  other arithmetic  5.01 us (3%)
  matrix products  4.86 us (3%)
    all_to_all x2, blocking collectives, exchange(): return lax.all_to_all(blocks, axes, split_axis=0, concat_axis=0, tiled=True)  44.1 us
    all_to_all x4, waiting for transfers between devices, exchange(): return lax.all_to_all(blocks, axes, split_axis=0, concat_axis=0, tiled=True)  25.5 us
    all_to_all x4, starting transfers between devices, exchange(): return lax.all_to_all(blocks, axes, split_axis=0, concat_axis=0, tiled=True)  21 us
    ppermute x6, starting transfers between devices, around(): lax.ppermute(block, axis, [(at, at ^ step) for at in range(4)])  19.2 us
    ppermute x6, waiting for transfers between devices, around(): lax.ppermute(block, axis, [(at, at ^ step) for at in range(4)])  17.2 us
    ppermute x1, waiting for transfers between devices, body(): lax.ppermute(mine_cols, 'zh', SWAP)  6.81 us
    ppermute x1, starting transfers between devices, body(): hidden_there = lax.ppermute(hidden_sent, 'c', SWAP)  6.42 us
    ppermute x1, starting transfers between devices, body(): piece_there = lax.ppermute(piece, 'c', SWAP)  4.87 us
  transfers between devices with their start and end apart: 15, of which 10 were waited for; matrix products, arithmetic and copies ran while one was open for 1% of the time, Pallas kernels for 0%

profile of v7, /device:TPU:1, one launch (start us, length us, event | category | flops | bytes accessed | tf_op | source)
XLA Modules:
  0.0 190.7 jit_solution(12332020332180974470)
XLA Ops:
  0.6 0.0 copy-start
  0.6 1.0 copy-done
  1.6 1.0 fusion.2
  2.6 0.9 pad_maximum_fusion.1
  3.5 32.0 %all_to_all.30 = bf16[16,8,1792]{2,1,0:T(8,128)(2,1)S(1)} all-to-all(bf16[16,8,1792]{2,1,0:T(8,128)(2,1)S(1)} %pad_maximum_fusion.1), channel_id=1, replica_groups=mesh['x'=4,'zl'=4,'c'=2,'zh'=2,'y'=8] {'zh','y'}, dimensions={0} | all-to-all | bytes 917504 | tf_op jit(solution)/shard_map/all_to_all | solution.py:29
  35.5 0.1 convert_reduce_fusion.1
  35.5 0.0 copy-start.1
  35.6 0.1 multiply_reduce_fusion.2
  35.7 0.1 multiply_convert_fusion.1
  35.8 0.1 fusion.10
  35.9 0.1 fusion.11
  36.1 2.5 %collective-permute-start = (bf16[8,5632]{1,0:T(8,128)(2,1)S(1)}, bf16[8,5632]{1,0:T(8,128)(2,1)S(1)}, u32[]{:S(2)}, u32[]{:S(2)}) collective-permute-start(bf16[8,5632]{1,0:T(8,128)(2,1)S(1)} %get-tuple-element.19), channel_id=1, source_target_pairs={{0,8},{8,0},{1,9},{9,1},{2,10},{10,2},{3,11},{11,3},{4,12},{12,4},... | collective-permute-start | bytes 270344 | tf_op jit(solution)/shard_map/ppermute | solution.py:101
  38.5 6.8 %collective-permute-done = bf16[8,5632]{1,0:T(8,128)(2,1)S(1)} collective-permute-done((bf16[8,5632]{1,0:T(8,128)(2,1)S(1)}, bf16[8,5632]{1,0:T(8,128)(2,1)S(1)}, u32[]{:S(2)}, u32[]{:S(2)}) %collective-permute-start) | collective-permute-done | bytes 90144 | tf_op jit(solution)/shard_map/ppermute | solution.py:101
  45.4 1.2 broadcast_in_dim.50
  46.6 5.8 %all-to-all-start.1 = ((bf16[8,16,5632]{2,1,0:T(8,128)(2,1)}), bf16[8,16,5632]{2,1,0:T(8,128)(2,1)S(1)}, u32[]{:S(2)}, u32[]{:S(2)}) async-start(bf16[8,16,5632]{2,1,0:T(8,128)(2,1)} %broadcast_in_dim.50), calls=%async_computation.1 | async-start | bytes 2883584 | tf_op jit(solution)/shard_map/all_to_all | solution.py:29
  52.4 2.8 %collective-permute-start.1 = (bf16[8,5632]{1,0:T(8,128)(2,1)S(1)}, bf16[8,5632]{1,0:T(8,128)(2,1)S(1)}, u32[]{:S(2)}, u32[]{:S(2)}) collective-permute-start(bf16[8,5632]{1,0:T(8,128)(2,1)S(1)} %get-tuple-element.18), channel_id=1, source_target_pairs={{0,32},{32,0},{64,96},{96,64},{1,33},{33,1},{65,97},{97,65},{2,34}... | collective-permute-start | bytes 270344 | tf_op jit(solution)/shard_map/ppermute | solution.py:61
  55.2 4.3 %collective-permute-start.2 = (bf16[8,5632]{1,0:T(8,128)(2,1)S(1)}, bf16[8,5632]{1,0:T(8,128)(2,1)S(1)}, u32[]{:S(2)}, u32[]{:S(2)}) collective-permute-start(bf16[8,5632]{1,0:T(8,128)(2,1)S(1)} %get-tuple-element.18), channel_id=1, source_target_pairs={{0,64},{32,96},{64,0},{96,32},{1,65},{33,97},{65,1},{97,33},{2,66}... | collective-permute-start | bytes 270344 | tf_op jit(solution)/shard_map/ppermute | solution.py:61
  59.5 2.6 %collective-permute-start.3 = (bf16[8,5632]{1,0:T(8,128)(2,1)S(1)}, bf16[8,5632]{1,0:T(8,128)(2,1)S(1)}, u32[]{:S(2)}, u32[]{:S(2)}) collective-permute-start(bf16[8,5632]{1,0:T(8,128)(2,1)S(1)} %get-tuple-element.18), channel_id=1, source_target_pairs={{0,96},{32,64},{64,32},{96,0},{1,97},{33,65},{65,33},{97,1},{2,98}... | collective-permute-start | bytes 270344 | tf_op jit(solution)/shard_map/ppermute | solution.py:61
  62.1 6.4 %collective-permute-start.4 = (bf16[128,96]{0,1:T(8,128)(2,1)S(1)}, bf16[128,96]{0,1:T(8,128)(2,1)S(1)}, u32[]{:S(2)}, u32[]{:S(2)}) collective-permute-start(bf16[128,96]{0,1:T(8,128)(2,1)S(1)} %copy-done.1), channel_id=1, source_target_pairs={{0,16},{16,0},{1,17},{17,1},{2,18},{18,2},{3,19},{19,3},{4,20},{20... | collective-permute-start | bytes 73736 | tf_op jit(solution)/shard_map/ppermute | solution.py:104
  68.5 0.0 collective-permute-done.2
  68.6 0.8 collective-permute-done.4
  69.3 3.1 %collective-permute-start.5 = (bf16[32,5632]{1,0:T(8,128)(2,1)S(1)}, bf16[32,5632]{1,0:T(8,128)(2,1)S(1)}, u32[]{:S(2)}, u32[]{:S(2)}) collective-permute-start(bf16[32,5632]{1,0:T(8,128)(2,1)S(1)} %pad_maximum_fusion.2), channel_id=1, source_target_pairs={{0,128},{128,0},{256,384},{384,256},{1,129},{129,1},{257,385},{385... | collective-permute-start | bytes 1081352 | tf_op jit(solution)/shard_map/ppermute | solution.py:61
  72.5 4.4 %collective-permute-start.6 = (bf16[32,5632]{1,0:T(8,128)(2,1)S(1)}, bf16[32,5632]{1,0:T(8,128)(2,1)S(1)}, u32[]{:S(2)}, u32[]{:S(2)}) collective-permute-start(bf16[32,5632]{1,0:T(8,128)(2,1)S(1)} %pad_maximum_fusion.2), channel_id=1, source_target_pairs={{0,256},{128,384},{256,0},{384,128},{1,257},{129,385},{257,1},{385... | collective-permute-start | bytes 1081352 | tf_op jit(solution)/shard_map/ppermute | solution.py:61
  76.8 2.1 %collective-permute-start.7 = (bf16[32,5632]{1,0:T(8,128)(2,1)S(1)}, bf16[32,5632]{1,0:T(8,128)(2,1)S(1)}, u32[]{:S(2)}, u32[]{:S(2)}) collective-permute-start(bf16[32,5632]{1,0:T(8,128)(2,1)S(1)} %pad_maximum_fusion.2), channel_id=1, source_target_pairs={{0,384},{128,256},{256,128},{384,0},{1,385},{129,257},{257,129},{3... | collective-permute-start | bytes 1081352 | tf_op jit(solution)/shard_map/ppermute | solution.py:61
  78.9 0.5 collective-permute-done.5
  79.4 10.0 %collective-permute-done.6 = bf16[32,5632]{1,0:T(8,128)(2,1)S(1)} collective-permute-done((bf16[32,5632]{1,0:T(8,128)(2,1)S(1)}, bf16[32,5632]{1,0:T(8,128)(2,1)S(1)}, u32[]{:S(2)}, u32[]{:S(2)}) %collective-permute-start.6) | collective-permute-done | bytes 360480 | tf_op jit(solution)/shard_map/ppermute | solution.py:61
  89.4 6.8 %collective-permute-done.7 = bf16[32,5632]{1,0:T(8,128)(2,1)S(1)} collective-permute-done((bf16[32,5632]{1,0:T(8,128)(2,1)S(1)}, bf16[32,5632]{1,0:T(8,128)(2,1)S(1)}, u32[]{:S(2)}, u32[]{:S(2)}) %collective-permute-start.7) | collective-permute-done | bytes 360480 | tf_op jit(solution)/shard_map/ppermute | solution.py:61
  96.1 0.1 pad_maximum_fusion
  96.2 3.7 %collective-permute-start.8 = (bf16[128,5632]{1,0:T(8,128)(2,1)S(1)}, bf16[128,5632]{1,0:T(8,128)(2,1)}, u32[]{:S(2)}, u32[]{:S(2)}) collective-permute-start(bf16[128,5632]{1,0:T(8,128)(2,1)S(1)} %bitcast.30), channel_id=1, source_target_pairs={{0,16},{16,0},{1,17},{17,1},{2,18},{18,2},{3,19},{19,3},{4,20},{20... | collective-permute-start | bytes 4325384 | tf_op jit(solution)/shard_map/ppermute | solution.py:108
  100.0 0.1 constant_dynamic-update-slice_fusion.1
  100.1 2.8 %collective-permute-done.8 = bf16[128,5632]{1,0:T(8,128)(2,1)} collective-permute-done((bf16[128,5632]{1,0:T(8,128)(2,1)S(1)}, bf16[128,5632]{1,0:T(8,128)(2,1)}, u32[]{:S(2)}, u32[]{:S(2)}) %collective-permute-start.8) | collective-permute-done | bytes 1441824 | tf_op jit(solution)/shard_map/ppermute | solution.py:108
  103.0 1.5 constant_dynamic-update-slice_fusion
  104.4 1.0 fusion.24
  105.5 0.6 multiply_reduce_fusion
  106.2 0.3 fusion.7
  106.5 0.3 fusion.5
  106.7 1.0 fusion.3
  107.8 3.6 %all-to-all-start.2 = ((bf16[16,8,1536]{2,1,0:T(8,128)(2,1)}), bf16[16,8,1536]{2,1,0:T(8,128)(2,1)S(1)}, u32[]{:S(2)}, u32[]{:S(2)}) async-start(bf16[16,8,1536]{2,1,0:T(8,128)(2,1)} %fusion.3), calls=%async_computation.2 | async-start | bytes 786432 | tf_op jit(solution)/shard_map/all_to_all | solution.py:29
  111.3 2.3 %collective-permute-start.9 = (f32[]{:T(128)}, f32[]{:T(128)}, u32[]{:S(2)}, u32[]{:S(2)}) collective-permute-start(f32[]{:T(128)} %get-tuple-element.13), channel_id=1, source_target_pairs={{0,16},{16,0},{1,17},{17,1},{2,18},{18,2},{3,19},{19,3},{4,20},{20... | collective-permute-start | bytes 20 | tf_op jit(solution)/shard_map/ppermute | solution.py:113
  113.6 0.9 collective-permute-done.9
  119.6 4.9 %all-to-all-done.2 = bf16[16,8,1536]{2,1,0:T(8,128)(2,1)S(1)} async-done(((bf16[16,8,1536]{2,1,0:T(8,128)(2,1)}), bf16[16,8,1536]{2,1,0:T(8,128)(2,1)S(1)}, u32[]{:S(2)}, u32[]{:S(2)}) %all-to-all-start.2) | async-done | bytes 393248 | tf_op jit(solution)/shard_map/all_to_all | solution.py:29
  124.4 0.1 convert_reduce_fusion
  124.5 0.2 multiply_reduce_fusion.1
  124.7 0.1 multiply_convert_fusion
  124.8 0.8 broadcast_in_dim.55
  125.6 7.9 %all-to-all-start.3 = ((bf16[16,8,1664]{2,1,0:T(8,128)(2,1)}), bf16[16,8,1664]{2,1,0:T(8,128)(2,1)S(1)}, u32[]{:S(2)}, u32[]{:S(2)}) async-start(bf16[16,8,1664]{2,1,0:T(8,128)(2,1)} %broadcast_in_dim.55), calls=%async_computation.3 | async-start | bytes 851968 | tf_op jit(solution)/shard_map/all_to_all | solution.py:29
  133.5 15.1 %all-to-all-done.3 = bf16[16,8,1664]{2,1,0:T(8,128)(2,1)S(1)} async-done(((bf16[16,8,1664]{2,1,0:T(8,128)(2,1)}), bf16[16,8,1664]{2,1,0:T(8,128)(2,1)S(1)}, u32[]{:S(2)}, u32[]{:S(2)}) %all-to-all-start.3) | async-done | bytes 426016 | tf_op jit(solution)/shard_map/all_to_all | solution.py:29
  148.6 4.9 %collective-permute-start.10 = (bf16[128,1536]{1,0:T(8,128)(2,1)S(1)}, bf16[128,1536]{1,0:T(8,128)(2,1)S(1)}, u32[]{:S(2)}, u32[]{:S(2)}) collective-permute-start(bf16[128,1536]{1,0:T(8,128)(2,1)S(1)} %slice.32), channel_id=1, source_target_pairs={{0,16},{16,0},{1,17},{17,1},{2,18},{18,2},{3,19},{19,3},{4,20},{20... | collective-permute-start | bytes 1179656 | tf_op jit(solution)/shard_map/ppermute | solution.py:124
  153.5 0.6 convert_reduce_fusion.3
  159.1 0.2 fusion.14
  159.3 0.2 fusion.4
  159.5 0.1 reshape.72
  159.6 0.1 broadcast_in_dim.60
  159.6 0.2 pad_maximum_fusion.3
  159.8 12.1 %all_to_all.31 = bf16[16,4,1536]{2,1,0:T(4,128)(2,1)S(1)} all-to-all(bf16[16,4,1536]{2,1,0:T(4,128)(2,1)S(1)} %pad_maximum_fusion.3), channel_id=1, replica_groups=mesh['x'=4,'zl'=4,'c'=2,'zh'=2,'y'=8] {'x','zl'}, dimensions={0} | all-to-all | bytes 393216 | tf_op jit(solution)/shard_map/all_to_all | solution.py:29
  171.9 0.1 convert_reduce_fusion.2
  172.0 0.7 broadcast_in_dim.61
  172.8 3.7 %all-to-all-start.5 = ((bf16[16,3,1536]{2,1,0:T(4,128)(2,1)}), bf16[16,3,1536]{2,1,0:T(4,128)(2,1)S(1)}, u32[]{:S(2)}, u32[]{:S(2)}) async-start(bf16[16,3,1536]{2,1,0:T(4,128)(2,1)} %broadcast_in_dim.61), calls=%async_computation.5 | async-start | bytes 393216 | tf_op jit(solution)/shard_map/all_to_all | solution.py:29
  176.5 0.9 fusion.22
  177.4 0.6 slice_reduce_fusion
  178.6 5.5 %all-to-all-done.5 = bf16[16,3,1536]{2,1,0:T(4,128)(2,1)S(1)} async-done(((bf16[16,3,1536]{2,1,0:T(4,128)(2,1)}), bf16[16,3,1536]{2,1,0:T(4,128)(2,1)S(1)}, u32[]{:S(2)}, u32[]{:S(2)}) %all-to-all-start.5) | async-done | bytes 147488 | tf_op jit(solution)/shard_map/all_to_all | solution.py:29
  184.1 0.1 reshape.73
  184.2 4.5 %all_gather.3 = bf16[96,1536]{1,0:T(8,128)(2,1)S(1)} all-gather(bf16[48,1536]{1,0:T(8,128)(2,1)S(1)} %reshape.73), channel_id=1, replica_groups=mesh['x'=4,'zl'=4,'c'=2,'zh'=2,'y'=8] {'c'}, dimensions={0}, use_global_device_ids=true | all-gather | bytes 442368 | tf_op jit(solution)/shard_map/all_gather | solution.py:144
  188.7 0.9 convert_element_type.85
  (23 shorter events, 0.2 us)
Async XLA Ops:
  0.6 1.0 copy-start
  35.5 26.5 %copy-start.1 = (bf16[128,96]{0,1:T(8,128)(2,1)S(1)}, bf16[128,96]{0,1:T(8,128)(2,1)}, u32[]{:S(2)}) copy-start(bf16[128,96]{0,1:T(8,128)(2,1)} %param.3) | copy-start | bytes 73732
  36.1 9.3 %collective-permute-start = (bf16[8,5632]{1,0:T(8,128)(2,1)S(1)}, bf16[8,5632]{1,0:T(8,128)(2,1)S(1)}, u32[]{:S(2)}, u32[]{:S(2)}) collective-permute-start(bf16[8,5632]{1,0:T(8,128)(2,1)S(1)} %get-tuple-element.19), channel_id=1, source_target_pairs={{0,8},{8,0},{1,9},{9,1},{2,10},{10,2},{3,11},{11,3},{4,12},{12,4},... | collective-permute-start | bytes 270344 | tf_op jit(solution)/shard_map/ppermute | solution.py:101
  46.6 49.7 %all-to-all-start.1 = ((bf16[8,16,5632]{2,1,0:T(8,128)(2,1)}), bf16[8,16,5632]{2,1,0:T(8,128)(2,1)S(1)}, u32[]{:S(2)}, u32[]{:S(2)}) async-start(bf16[8,16,5632]{2,1,0:T(8,128)(2,1)} %broadcast_in_dim.50), calls=%async_computation.1 | async-start | bytes 2883584 | tf_op jit(solution)/shard_map/all_to_all | solution.py:29
  52.4 16.1 %collective-permute-start.1 = (bf16[8,5632]{1,0:T(8,128)(2,1)S(1)}, bf16[8,5632]{1,0:T(8,128)(2,1)S(1)}, u32[]{:S(2)}, u32[]{:S(2)}) collective-permute-start(bf16[8,5632]{1,0:T(8,128)(2,1)S(1)} %get-tuple-element.18), channel_id=1, source_target_pairs={{0,32},{32,0},{64,96},{96,64},{1,33},{33,1},{65,97},{97,65},{2,34}... | collective-permute-start | bytes 270344 | tf_op jit(solution)/shard_map/ppermute | solution.py:61
  55.2 13.3 %collective-permute-start.2 = (bf16[8,5632]{1,0:T(8,128)(2,1)S(1)}, bf16[8,5632]{1,0:T(8,128)(2,1)S(1)}, u32[]{:S(2)}, u32[]{:S(2)}) collective-permute-start(bf16[8,5632]{1,0:T(8,128)(2,1)S(1)} %get-tuple-element.18), channel_id=1, source_target_pairs={{0,64},{32,96},{64,0},{96,32},{1,65},{33,97},{65,1},{97,33},{2,66}... | collective-permute-start | bytes 270344 | tf_op jit(solution)/shard_map/ppermute | solution.py:61
  59.5 9.1 %collective-permute-start.3 = (bf16[8,5632]{1,0:T(8,128)(2,1)S(1)}, bf16[8,5632]{1,0:T(8,128)(2,1)S(1)}, u32[]{:S(2)}, u32[]{:S(2)}) collective-permute-start(bf16[8,5632]{1,0:T(8,128)(2,1)S(1)} %get-tuple-element.18), channel_id=1, source_target_pairs={{0,96},{32,64},{64,32},{96,0},{1,97},{33,65},{65,33},{97,1},{2,98}... | collective-permute-start | bytes 270344 | tf_op jit(solution)/shard_map/ppermute | solution.py:61
  62.1 7.3 %collective-permute-start.4 = (bf16[128,96]{0,1:T(8,128)(2,1)S(1)}, bf16[128,96]{0,1:T(8,128)(2,1)S(1)}, u32[]{:S(2)}, u32[]{:S(2)}) collective-permute-start(bf16[128,96]{0,1:T(8,128)(2,1)S(1)} %copy-done.1), channel_id=1, source_target_pairs={{0,16},{16,0},{1,17},{17,1},{2,18},{18,2},{3,19},{19,3},{4,20},{20... | collective-permute-start | bytes 73736 | tf_op jit(solution)/shard_map/ppermute | solution.py:104
  69.3 10.1 %collective-permute-start.5 = (bf16[32,5632]{1,0:T(8,128)(2,1)S(1)}, bf16[32,5632]{1,0:T(8,128)(2,1)S(1)}, u32[]{:S(2)}, u32[]{:S(2)}) collective-permute-start(bf16[32,5632]{1,0:T(8,128)(2,1)S(1)} %pad_maximum_fusion.2), channel_id=1, source_target_pairs={{0,128},{128,0},{256,384},{384,256},{1,129},{129,1},{257,385},{385... | collective-permute-start | bytes 1081352 | tf_op jit(solution)/shard_map/ppermute | solution.py:61
  72.5 16.9 %collective-permute-start.6 = (bf16[32,5632]{1,0:T(8,128)(2,1)S(1)}, bf16[32,5632]{1,0:T(8,128)(2,1)S(1)}, u32[]{:S(2)}, u32[]{:S(2)}) collective-permute-start(bf16[32,5632]{1,0:T(8,128)(2,1)S(1)} %pad_maximum_fusion.2), channel_id=1, source_target_pairs={{0,256},{128,384},{256,0},{384,128},{1,257},{129,385},{257,1},{385... | collective-permute-start | bytes 1081352 | tf_op jit(solution)/shard_map/ppermute | solution.py:61
  76.8 19.3 %collective-permute-start.7 = (bf16[32,5632]{1,0:T(8,128)(2,1)S(1)}, bf16[32,5632]{1,0:T(8,128)(2,1)S(1)}, u32[]{:S(2)}, u32[]{:S(2)}) collective-permute-start(bf16[32,5632]{1,0:T(8,128)(2,1)S(1)} %pad_maximum_fusion.2), channel_id=1, source_target_pairs={{0,384},{128,256},{256,128},{384,0},{1,385},{129,257},{257,129},{3... | collective-permute-start | bytes 1081352 | tf_op jit(solution)/shard_map/ppermute | solution.py:61
  96.2 6.7 %collective-permute-start.8 = (bf16[128,5632]{1,0:T(8,128)(2,1)S(1)}, bf16[128,5632]{1,0:T(8,128)(2,1)}, u32[]{:S(2)}, u32[]{:S(2)}) collective-permute-start(bf16[128,5632]{1,0:T(8,128)(2,1)S(1)} %bitcast.30), channel_id=1, source_target_pairs={{0,16},{16,0},{1,17},{17,1},{2,18},{18,2},{3,19},{19,3},{4,20},{20... | collective-permute-start | bytes 4325384 | tf_op jit(solution)/shard_map/ppermute | solution.py:108
  107.8 16.7 %all-to-all-start.2 = ((bf16[16,8,1536]{2,1,0:T(8,128)(2,1)}), bf16[16,8,1536]{2,1,0:T(8,128)(2,1)S(1)}, u32[]{:S(2)}, u32[]{:S(2)}) async-start(bf16[16,8,1536]{2,1,0:T(8,128)(2,1)} %fusion.3), calls=%async_computation.2 | async-start | bytes 786432 | tf_op jit(solution)/shard_map/all_to_all | solution.py:29
  111.3 3.2 %collective-permute-start.9 = (f32[]{:T(128)}, f32[]{:T(128)}, u32[]{:S(2)}, u32[]{:S(2)}) collective-permute-start(f32[]{:T(128)} %get-tuple-element.13), channel_id=1, source_target_pairs={{0,16},{16,0},{1,17},{17,1},{2,18},{18,2},{3,19},{19,3},{4,20},{20... | collective-permute-start | bytes 20 | tf_op jit(solution)/shard_map/ppermute | solution.py:113
  125.6 23.0 %all-to-all-start.3 = ((bf16[16,8,1664]{2,1,0:T(8,128)(2,1)}), bf16[16,8,1664]{2,1,0:T(8,128)(2,1)S(1)}, u32[]{:S(2)}, u32[]{:S(2)}) async-start(bf16[16,8,1664]{2,1,0:T(8,128)(2,1)} %broadcast_in_dim.55), calls=%async_computation.3 | async-start | bytes 851968 | tf_op jit(solution)/shard_map/all_to_all | solution.py:29
  148.6 10.6 %collective-permute-start.10 = (bf16[128,1536]{1,0:T(8,128)(2,1)S(1)}, bf16[128,1536]{1,0:T(8,128)(2,1)S(1)}, u32[]{:S(2)}, u32[]{:S(2)}) collective-permute-start(bf16[128,1536]{1,0:T(8,128)(2,1)S(1)} %slice.32), channel_id=1, source_target_pairs={{0,16},{16,0},{1,17},{17,1},{2,18},{18,2},{3,19},{19,3},{4,20},{20... | collective-permute-start | bytes 1179656 | tf_op jit(solution)/shard_map/ppermute | solution.py:124
  172.8 11.3 %all-to-all-start.5 = ((bf16[16,3,1536]{2,1,0:T(4,128)(2,1)}), bf16[16,3,1536]{2,1,0:T(4,128)(2,1)S(1)}, u32[]{:S(2)}, u32[]{:S(2)}) async-start(bf16[16,3,1536]{2,1,0:T(4,128)(2,1)} %broadcast_in_dim.61), calls=%async_computation.5 | async-start | bytes 393216 | tf_op jit(solution)/shard_map/all_to_all | solution.py:29

commit v8 on v7

--- a/solution.py
+++ b/solution.py
@@ -47,8 +47,8 @@
     return (values * lax.rsqrt(total + EPSILON)).astype(jnp.bfloat16)
 
 
-def spread(value, shape):
-    lane = lax.broadcasted_iota(jnp.int32, shape, 1)
+def spread(value, shape, place):
+    lane = lax.broadcasted_iota(jnp.int32, shape, 1) - 3 * place
     lanes = jnp.zeros(shape, jnp.bfloat16)
     for index, part in enumerate(pieces(value)):
         lanes = jnp.where(lane == index, part, lanes)
@@ -99,8 +99,8 @@
     near = around(jnp.concatenate([student, target], axis=1), "zl")
     mine_cols = jnp.concatenate([student, -target], axis=1)
     pair = jnp.concatenate([mine_cols, lax.ppermute(mine_cols, "zh", SWAP)], axis=0)
+    pair, near, hidden_sent = lax.optimization_barrier((pair, near, hidden))
     here = gather(pair, ("y",)).reshape(rows, -1)
-    _, hidden_sent = lax.optimization_barrier((pair, hidden))
     hidden_there = lax.ppermute(hidden_sent, "c", SWAP)
     near, hidden_there = lax.optimization_barrier((near, hidden_there))
     row_block = around(near, "x")
@@ -118,7 +118,7 @@
     grad_embed = (inv_student * (grad_unit - unit * radial)).astype(jnp.bfloat16)
 
     wide = gather(
-        jnp.concatenate([grad_embed, spread(squares, (mine, 128))], axis=1), FS
+        jnp.concatenate([grad_embed, spread(squares, (mine, 128), lax.axis_index(FS))], axis=1), FS
     ).reshape(rows, -1)
     piece = wide[:, :full]
     piece_there = lax.ppermute(piece, "c", SWAP)
@@ -128,13 +128,14 @@
     left_there = lax.dynamic_slice_in_dim(hidden_there, core * half, half, 1)
     proj_piece = dot(left, piece, COLS_T) + dot(left_there, piece_there, COLS_T)
 
-    loss_part = jnp.sum(
-        wide.reshape(group_fs, mine, -1)[:, 0, full:].astype(jnp.float32)
+    loss_row = jnp.sum(
+        wide.reshape(group_fs, mine, -1)[:, 0, full:].astype(jnp.float32), axis=0
     )
+    loss_row = jnp.pad(loss_row.astype(jnp.bfloat16), (0, full - 128))
     blocks = jnp.concatenate(
         [
             proj_piece.astype(jnp.bfloat16).reshape(group_xz, half // group_xz, full),
-            jnp.broadcast_to(spread(loss_part, (1, full)), (group_xz, 1, full)),
+            jnp.broadcast_to(loss_row, (group_xz, 1, full)),
         ],
         axis=1,
     )

time: 192 us -> 188 us (0.979)
  blocking collectives: 48.6 us -> 67.7 us
  waiting for transfers between devices: 54 us -> 40.2 us
  between operations: 12.7 us -> 7.71 us
  starting transfers between devices: 60 us -> 57.1 us
    all_to_all x2 -> x3, blocking collectives: 44.1 us -> 63.1 us  [exchange(): return lax.all_to_all(blocks, axes, split_axis=0, concat_axis=0, tiled=True)]
    all_to_all x4 -> x3, waiting for transfers between devices: 25.5 us -> 11.1 us  [exchange(): return lax.all_to_all(blocks, axes, split_axis=0, concat_axis=0, tiled=True)]
    ppermute x1, waiting for transfers between devices: 6.81 us -> 0.01 us  [body(): lax.ppermute(mine_cols, 'zh', SWAP)]
    ppermute x6, waiting for transfers between devices: 17.2 us -> 23.2 us  [around(): lax.ppermute(block, axis, [(at, at ^ step) for at in range(4)])]
    all_to_all x4 -> x3, starting transfers between devices: 21 us -> 18.8 us  [exchange(): return lax.all_to_all(blocks, axes, split_axis=0, concat_axis=0, tiled=True)]
  transfers between devices with their start and end apart: 15 -> 14, of which waited for: 10 -> 12; matrix products, arithmetic and copies ran while one was open for 1% -> 1% of each run, Pallas kernels for 0% -> 0%
where the time goes in v8:
time: 188 us; the launch traced here: 187 us
  blocking collectives  67.7 us (36%)
  starting transfers between devices  57.1 us (30%)
  waiting for transfers between devices  40.2 us (21%)
  between operations  7.71 us (4%)
  matrix products  4.87 us (3%)
  local copies, waits for them, and re-layouts  4.84 us (3%)
  other arithmetic  4.45 us (2%)
    all_to_all x3, blocking collectives, exchange(): return lax.all_to_all(blocks, axes, split_axis=0, concat_axis=0, tiled=True)  63.1 us
    ppermute x6, waiting for transfers between devices, around(): lax.ppermute(block, axis, [(at, at ^ step) for at in range(4)])  23.2 us
    ppermute x6, starting transfers between devices, around(): lax.ppermute(block, axis, [(at, at ^ step) for at in range(4)])  18.8 us
    all_to_all x3, starting transfers between devices, exchange(): return lax.all_to_all(blocks, axes, split_axis=0, concat_axis=0, tiled=True)  18.8 us
    all_to_all x3, waiting for transfers between devices, exchange(): return lax.all_to_all(blocks, axes, split_axis=0, concat_axis=0, tiled=True)  11.1 us
    ppermute x1, starting transfers between devices, body(): hidden_there = lax.ppermute(hidden_sent, 'c', SWAP)  5.2 us
    dot_general x8, matrix products, dot(): return lax.dot_general(a, b, dims, preferred_element_type=jnp.float32)  4.87 us
    ppermute x1, starting transfers between devices, body(): columns = jnp.concatenate([here, lax.ppermute(here, 'c', SWAP)], axis=0)  4.66 us
  transfers between devices with their start and end apart: 14, of which 12 were waited for; matrix products, arithmetic and copies ran while one was open for 1% of the time, Pallas kernels for 0%

profile of v8, /device:TPU:1, one launch (start us, length us, event | category | flops | bytes accessed | tf_op | source)
XLA Modules:
  0.0 186.9 jit_solution(7822482328644901641)
XLA Ops:
  0.6 0.0 copy-start
  0.6 1.0 copy-done
  1.6 1.0 fusion.2
  2.6 0.9 pad_maximum_fusion.1
  3.5 32.0 %all_to_all.30 = bf16[16,8,1792]{2,1,0:T(8,128)(2,1)S(1)} all-to-all(bf16[16,8,1792]{2,1,0:T(8,128)(2,1)S(1)} %pad_maximum_fusion.1), channel_id=1, replica_groups=mesh['x'=4,'zl'=4,'c'=2,'zh'=2,'y'=8] {'zh','y'}, dimensions={0} | all-to-all | bytes 917504 | tf_op jit(solution)/shard_map/all_to_all | solution.py:29
  35.5 0.1 convert_reduce_fusion.1
  35.6 0.1 multiply_reduce_fusion.2
  35.7 0.1 multiply_convert_fusion.1
  35.8 0.1 fusion.10
  35.9 0.1 fusion.11
  36.1 2.5 %collective-permute-start = (bf16[8,5632]{1,0:T(8,128)(2,1)S(1)}, bf16[8,5632]{1,0:T(8,128)(2,1)S(1)}, u32[]{:S(2)}, u32[]{:S(2)}) collective-permute-start(bf16[8,5632]{1,0:T(8,128)(2,1)S(1)} %get-tuple-element.23), channel_id=1, source_target_pairs={{0,8},{8,0},{1,9},{9,1},{2,10},{10,2},{3,11},{11,3},{4,12},{12,4},... | collective-permute-start | bytes 270344 | tf_op jit(solution)/shard_map/ppermute | solution.py:101
  38.5 3.1 %collective-permute-start.1 = (bf16[8,5632]{1,0:T(8,128)(2,1)S(1)}, bf16[8,5632]{1,0:T(8,128)(2,1)S(1)}, u32[]{:S(2)}, u32[]{:S(2)}) collective-permute-start(bf16[8,5632]{1,0:T(8,128)(2,1)S(1)} %get-tuple-element.22), channel_id=1, source_target_pairs={{0,32},{32,0},{64,96},{96,64},{1,33},{33,1},{65,97},{97,65},{2,34}... | collective-permute-start | bytes 270344 | tf_op jit(solution)/shard_map/ppermute | solution.py:61
  41.7 4.0 %collective-permute-start.2 = (bf16[8,5632]{1,0:T(8,128)(2,1)S(1)}, bf16[8,5632]{1,0:T(8,128)(2,1)S(1)}, u32[]{:S(2)}, u32[]{:S(2)}) collective-permute-start(bf16[8,5632]{1,0:T(8,128)(2,1)S(1)} %get-tuple-element.22), channel_id=1, source_target_pairs={{0,64},{32,96},{64,0},{96,32},{1,65},{33,97},{65,1},{97,33},{2,66}... | collective-permute-start | bytes 270344 | tf_op jit(solution)/shard_map/ppermute | solution.py:61
  45.7 2.2 %collective-permute-start.3 = (bf16[8,5632]{1,0:T(8,128)(2,1)S(1)}, bf16[8,5632]{1,0:T(8,128)(2,1)S(1)}, u32[]{:S(2)}, u32[]{:S(2)}) collective-permute-start(bf16[8,5632]{1,0:T(8,128)(2,1)S(1)} %get-tuple-element.22), channel_id=1, source_target_pairs={{0,96},{32,64},{64,32},{96,0},{1,97},{33,65},{65,33},{97,1},{2,98}... | collective-permute-start | bytes 270344 | tf_op jit(solution)/shard_map/ppermute | solution.py:61
  47.9 2.5 %collective-permute-done.2 = bf16[8,5632]{1,0:T(8,128)(2,1)S(1)} collective-permute-done((bf16[8,5632]{1,0:T(8,128)(2,1)S(1)}, bf16[8,5632]{1,0:T(8,128)(2,1)S(1)}, u32[]{:S(2)}, u32[]{:S(2)}) %collective-permute-start.2) | collective-permute-done | bytes 90144 | tf_op jit(solution)/shard_map/ppermute | solution.py:61
  50.4 2.5 %collective-permute-done.3 = bf16[8,5632]{1,0:T(8,128)(2,1)S(1)} collective-permute-done((bf16[8,5632]{1,0:T(8,128)(2,1)S(1)}, bf16[8,5632]{1,0:T(8,128)(2,1)S(1)}, u32[]{:S(2)}, u32[]{:S(2)}) %collective-permute-start.3) | collective-permute-done | bytes 90144 | tf_op jit(solution)/shard_map/ppermute | solution.py:61
  53.0 1.2 broadcast_in_dim.37
  54.2 6.0 %all-to-all-start.1 = ((bf16[8,16,5632]{2,1,0:T(8,128)(2,1)}), bf16[8,16,5632]{2,1,0:T(8,128)(2,1)S(1)}, u32[]{:S(2)}, u32[]{:S(2)}) async-start(bf16[8,16,5632]{2,1,0:T(8,128)(2,1)} %broadcast_in_dim.37), calls=%async_computation.1 | async-start | bytes 2883584 | tf_op jit(solution)/shard_map/all_to_all | solution.py:29
  60.1 5.2 %collective-permute-start.4 = (bf16[128,96]{0,1:T(8,128)(2,1)S(1)}, bf16[128,96]{0,1:T(8,128)(2,1)S(1)}, u32[]{:S(2)}, u32[]{:S(2)}) collective-permute-start(bf16[128,96]{0,1:T(8,128)(2,1)S(1)} %copy-done.3), channel_id=1, source_target_pairs={{0,16},{16,0},{1,17},{17,1},{2,18},{18,2},{3,19},{19,3},{4,20},{20... | collective-permute-start | bytes 73736 | tf_op jit(solution)/shard_map/ppermute | solution.py:104
  65.3 0.8 collective-permute-done.4
  66.2 3.1 %collective-permute-start.5 = (bf16[32,5632]{1,0:T(8,128)(2,1)S(1)}, bf16[32,5632]{1,0:T(8,128)(2,1)S(1)}, u32[]{:S(2)}, u32[]{:S(2)}) collective-permute-start(bf16[32,5632]{1,0:T(8,128)(2,1)S(1)} %pad_maximum_fusion.2), channel_id=1, source_target_pairs={{0,128},{128,0},{256,384},{384,256},{1,129},{129,1},{257,385},{385... | collective-permute-start | bytes 1081352 | tf_op jit(solution)/shard_map/ppermute | solution.py:61
  69.3 4.4 %collective-permute-start.6 = (bf16[32,5632]{1,0:T(8,128)(2,1)S(1)}, bf16[32,5632]{1,0:T(8,128)(2,1)S(1)}, u32[]{:S(2)}, u32[]{:S(2)}) collective-permute-start(bf16[32,5632]{1,0:T(8,128)(2,1)S(1)} %pad_maximum_fusion.2), channel_id=1, source_target_pairs={{0,256},{128,384},{256,0},{384,128},{1,257},{129,385},{257,1},{385... | collective-permute-start | bytes 1081352 | tf_op jit(solution)/shard_map/ppermute | solution.py:61
  73.7 2.1 %collective-permute-start.7 = (bf16[32,5632]{1,0:T(8,128)(2,1)S(1)}, bf16[32,5632]{1,0:T(8,128)(2,1)S(1)}, u32[]{:S(2)}, u32[]{:S(2)}) collective-permute-start(bf16[32,5632]{1,0:T(8,128)(2,1)S(1)} %pad_maximum_fusion.2), channel_id=1, source_target_pairs={{0,384},{128,256},{256,128},{384,0},{1,385},{129,257},{257,129},{3... | collective-permute-start | bytes 1081352 | tf_op jit(solution)/shard_map/ppermute | solution.py:61
  75.8 1.9 %collective-permute-done.5 = bf16[32,5632]{1,0:T(8,128)(2,1)S(1)} collective-permute-done((bf16[32,5632]{1,0:T(8,128)(2,1)S(1)}, bf16[32,5632]{1,0:T(8,128)(2,1)S(1)}, u32[]{:S(2)}, u32[]{:S(2)}) %collective-permute-start.5) | collective-permute-done | bytes 360480 | tf_op jit(solution)/shard_map/ppermute | solution.py:61
  77.7 10.0 %collective-permute-done.6 = bf16[32,5632]{1,0:T(8,128)(2,1)S(1)} collective-permute-done((bf16[32,5632]{1,0:T(8,128)(2,1)S(1)}, bf16[32,5632]{1,0:T(8,128)(2,1)S(1)}, u32[]{:S(2)}, u32[]{:S(2)}) %collective-permute-start.6) | collective-permute-done | bytes 360480 | tf_op jit(solution)/shard_map/ppermute | solution.py:61
  87.7 6.3 %collective-permute-done.7 = bf16[32,5632]{1,0:T(8,128)(2,1)S(1)} collective-permute-done((bf16[32,5632]{1,0:T(8,128)(2,1)S(1)}, bf16[32,5632]{1,0:T(8,128)(2,1)S(1)}, u32[]{:S(2)}, u32[]{:S(2)}) %collective-permute-start.7) | collective-permute-done | bytes 360480 | tf_op jit(solution)/shard_map/ppermute | solution.py:61
  94.0 0.1 pad_maximum_fusion
  94.1 1.4 all-to-all-done.1
  95.5 4.7 %collective-permute-start.8 = (bf16[128,5632]{1,0:T(8,128)(2,1)S(1)}, bf16[128,5632]{1,0:T(8,128)(2,1)}, u32[]{:S(2)}, u32[]{:S(2)}) collective-permute-start(bf16[128,5632]{1,0:T(8,128)(2,1)S(1)} %bitcast.30), channel_id=1, source_target_pairs={{0,16},{16,0},{1,17},{17,1},{2,18},{18,2},{3,19},{19,3},{4,20},{20... | collective-permute-start | bytes 4325384 | tf_op jit(solution)/shard_map/ppermute | solution.py:108
  100.2 0.1 constant_dynamic-update-slice_fusion.1
  100.3 2.8 %collective-permute-done.8 = bf16[128,5632]{1,0:T(8,128)(2,1)} collective-permute-done((bf16[128,5632]{1,0:T(8,128)(2,1)S(1)}, bf16[128,5632]{1,0:T(8,128)(2,1)}, u32[]{:S(2)}, u32[]{:S(2)}) %collective-permute-start.8) | collective-permute-done | bytes 1441824 | tf_op jit(solution)/shard_map/ppermute | solution.py:108
  103.1 1.5 constant_dynamic-update-slice_fusion
  104.6 1.0 fusion.23
  105.7 0.6 multiply_reduce_fusion
  106.4 0.3 fusion.7
  106.6 0.0 copy-start.2
  106.6 0.3 fusion.5
  106.9 0.0 copy-start.4
  106.9 1.0 fusion.3
  108.0 7.9 %all-to-all-start.2 = ((bf16[16,8,1536]{2,1,0:T(8,128)(2,1)}), bf16[16,8,1536]{2,1,0:T(8,128)(2,1)S(1)}, u32[]{:S(2)}, u32[]{:S(2)}) async-start(bf16[16,8,1536]{2,1,0:T(8,128)(2,1)} %fusion.3), calls=%async_computation.2 | async-start | bytes 786432 | tf_op jit(solution)/shard_map/all_to_all | solution.py:29
  115.9 2.6 %collective-permute-start.9 = (f32[]{:T(128)}, f32[]{:T(128)}, u32[]{:S(2)}, u32[]{:S(2)}) collective-permute-start(f32[]{:T(128)} %get-tuple-element.17), channel_id=1, source_target_pairs={{0,16},{16,0},{1,17},{17,1},{2,18},{18,2},{3,19},{19,3},{4,20},{20... | collective-permute-start | bytes 20 | tf_op jit(solution)/shard_map/ppermute | solution.py:113
  118.4 1.1 collective-permute-done.9
  124.4 4.4 %all-to-all-done.2 = bf16[16,8,1536]{2,1,0:T(8,128)(2,1)S(1)} async-done(((bf16[16,8,1536]{2,1,0:T(8,128)(2,1)}), bf16[16,8,1536]{2,1,0:T(8,128)(2,1)S(1)}, u32[]{:S(2)}, u32[]{:S(2)}) %all-to-all-start.2) | async-done | bytes 393248 | tf_op jit(solution)/shard_map/all_to_all | solution.py:29
  128.8 0.1 convert_reduce_fusion
  128.9 0.2 multiply_reduce_fusion.1
  129.1 0.1 multiply_convert_fusion
  129.2 19.8 %all_to_all.31 = bf16[16,8,1664]{2,1,0:T(8,128)(2,1)S(1)} all-to-all(bf16[16,8,1664]{2,1,0:T(8,128)(2,1)S(1)} %broadcast_in_dim.42), channel_id=1, replica_groups=mesh['x'=4,'zl'=4,'c'=2,'zh'=2,'y'=8] {'zh','y'}, dimensions={0} | all-to-all | bytes 851968 | tf_op jit(solution)/shard_map/all_to_all | solution.py:29
  149.0 4.6 %collective-permute-start.10 = (bf16[128,1536]{1,0:T(8,128)(2,1)S(1)}, bf16[128,1536]{1,0:T(8,128)(2,1)S(1)}, u32[]{:S(2)}, u32[]{:S(2)}) collective-permute-start(bf16[128,1536]{1,0:T(8,128)(2,1)S(1)} %slice.32), channel_id=1, source_target_pairs={{0,16},{16,0},{1,17},{17,1},{2,18},{18,2},{3,19},{19,3},{4,20},{20... | collective-permute-start | bytes 1179656 | tf_op jit(solution)/shard_map/ppermute | solution.py:124
  153.7 0.2 fusion.14
  153.9 1.1 collective-permute-done.10
  154.9 0.2 fusion.4
  155.1 0.1 reshape.60
  155.2 0.1 broadcast_in_dim.43
  155.3 0.2 pad_maximum_fusion.3
  155.5 11.4 %all_to_all.32 = bf16[16,4,1536]{2,1,0:T(4,128)(2,1)S(1)} all-to-all(bf16[16,4,1536]{2,1,0:T(4,128)(2,1)S(1)} %pad_maximum_fusion.3), channel_id=1, replica_groups=mesh['x'=4,'zl'=4,'c'=2,'zh'=2,'y'=8] {'x','zl'}, dimensions={0} | all-to-all | bytes 393216 | tf_op jit(solution)/shard_map/all_to_all | solution.py:29
  166.9 0.1 convert_reduce_fusion.2
  167.0 0.7 broadcast_in_dim.44
  167.7 5.0 %all-to-all-start.5 = ((bf16[16,3,1536]{2,1,0:T(4,128)(2,1)}), bf16[16,3,1536]{2,1,0:T(4,128)(2,1)S(1)}, u32[]{:S(2)}, u32[]{:S(2)}) async-start(bf16[16,3,1536]{2,1,0:T(4,128)(2,1)} %broadcast_in_dim.44), calls=%async_computation.5 | async-start | bytes 393216 | tf_op jit(solution)/shard_map/all_to_all | solution.py:29
  172.7 0.9 fusion.21
  173.6 0.6 slice_reduce_fusion.1
  174.8 5.4 %all-to-all-done.5 = bf16[16,3,1536]{2,1,0:T(4,128)(2,1)S(1)} async-done(((bf16[16,3,1536]{2,1,0:T(4,128)(2,1)}), bf16[16,3,1536]{2,1,0:T(4,128)(2,1)S(1)}, u32[]{:S(2)}, u32[]{:S(2)}) %all-to-all-start.5) | async-done | bytes 147488 | tf_op jit(solution)/shard_map/all_to_all | solution.py:29
  180.2 0.1 reshape.61
  180.3 4.6 %all_gather.3 = bf16[96,1536]{1,0:T(8,128)(2,1)S(1)} all-gather(bf16[48,1536]{1,0:T(8,128)(2,1)S(1)} %reshape.61), channel_id=1, replica_groups=mesh['x'=4,'zl'=4,'c'=2,'zh'=2,'y'=8] {'c'}, dimensions={0}, use_global_device_ids=true | all-gather | bytes 442368 | tf_op jit(solution)/shard_map/all_gather | solution.py:145
  184.9 0.9 convert_element_type.72
  (31 shorter events, 0.3 us)
Async XLA Ops:
  0.6 1.0 copy-start
  35.5 14.8 %copy-start.1 = (f32[8,1536]{1,0:T(8,128)}, f32[8,1536]{1,0:T(8,128)S(1)}, u32[]{:S(2)}) copy-start(f32[8,1536]{1,0:T(8,128)S(1)} %convert_reduce_fusion.1) | copy-start | bytes 147460
  36.0 24.1 %copy-start.3 = (bf16[128,96]{0,1:T(8,128)(2,1)S(1)}, bf16[128,96]{0,1:T(8,128)(2,1)}, u32[]{:S(2)}) copy-start(bf16[128,96]{0,1:T(8,128)(2,1)} %param.3) | copy-start | bytes 73732
  36.1 11.8 %collective-permute-start = (bf16[8,5632]{1,0:T(8,128)(2,1)S(1)}, bf16[8,5632]{1,0:T(8,128)(2,1)S(1)}, u32[]{:S(2)}, u32[]{:S(2)}) collective-permute-start(bf16[8,5632]{1,0:T(8,128)(2,1)S(1)} %get-tuple-element.23), channel_id=1, source_target_pairs={{0,8},{8,0},{1,9},{9,1},{2,10},{10,2},{3,11},{11,3},{4,12},{12,4},... | collective-permute-start | bytes 270344 | tf_op jit(solution)/shard_map/ppermute | solution.py:101
  38.5 9.3 %collective-permute-start.1 = (bf16[8,5632]{1,0:T(8,128)(2,1)S(1)}, bf16[8,5632]{1,0:T(8,128)(2,1)S(1)}, u32[]{:S(2)}, u32[]{:S(2)}) collective-permute-start(bf16[8,5632]{1,0:T(8,128)(2,1)S(1)} %get-tuple-element.22), channel_id=1, source_target_pairs={{0,32},{32,0},{64,96},{96,64},{1,33},{33,1},{65,97},{97,65},{2,34}... | collective-permute-start | bytes 270344 | tf_op jit(solution)/shard_map/ppermute | solution.py:61
  41.7 8.7 %collective-permute-start.2 = (bf16[8,5632]{1,0:T(8,128)(2,1)S(1)}, bf16[8,5632]{1,0:T(8,128)(2,1)S(1)}, u32[]{:S(2)}, u32[]{:S(2)}) collective-permute-start(bf16[8,5632]{1,0:T(8,128)(2,1)S(1)} %get-tuple-element.22), channel_id=1, source_target_pairs={{0,64},{32,96},{64,0},{96,32},{1,65},{33,97},{65,1},{97,33},{2,66}... | collective-permute-start | bytes 270344 | tf_op jit(solution)/shard_map/ppermute | solution.py:61
  45.7 7.3 %collective-permute-start.3 = (bf16[8,5632]{1,0:T(8,128)(2,1)S(1)}, bf16[8,5632]{1,0:T(8,128)(2,1)S(1)}, u32[]{:S(2)}, u32[]{:S(2)}) collective-permute-start(bf16[8,5632]{1,0:T(8,128)(2,1)S(1)} %get-tuple-element.22), channel_id=1, source_target_pairs={{0,96},{32,64},{64,32},{96,0},{1,97},{33,65},{65,33},{97,1},{2,98}... | collective-permute-start | bytes 270344 | tf_op jit(solution)/shard_map/ppermute | solution.py:61
  54.2 41.3 %all-to-all-start.1 = ((bf16[8,16,5632]{2,1,0:T(8,128)(2,1)}), bf16[8,16,5632]{2,1,0:T(8,128)(2,1)S(1)}, u32[]{:S(2)}, u32[]{:S(2)}) async-start(bf16[8,16,5632]{2,1,0:T(8,128)(2,1)} %broadcast_in_dim.37), calls=%async_computation.1 | async-start | bytes 2883584 | tf_op jit(solution)/shard_map/all_to_all | solution.py:29
  60.1 6.0 %collective-permute-start.4 = (bf16[128,96]{0,1:T(8,128)(2,1)S(1)}, bf16[128,96]{0,1:T(8,128)(2,1)S(1)}, u32[]{:S(2)}, u32[]{:S(2)}) collective-permute-start(bf16[128,96]{0,1:T(8,128)(2,1)S(1)} %copy-done.3), channel_id=1, source_target_pairs={{0,16},{16,0},{1,17},{17,1},{2,18},{18,2},{3,19},{19,3},{4,20},{20... | collective-permute-start | bytes 73736 | tf_op jit(solution)/shard_map/ppermute | solution.py:104
  66.2 21.5 %copy-start.5 = (bf16[128,96]{0,1:T(8,128)(2,1)}, bf16[128,96]{0,1:T(8,128)(2,1)S(1)}, u32[]{:S(2)}) copy-start(bf16[128,96]{0,1:T(8,128)(2,1)S(1)} %collective-permute-done.4) | copy-start | bytes 73732
  66.2 11.5 %collective-permute-start.5 = (bf16[32,5632]{1,0:T(8,128)(2,1)S(1)}, bf16[32,5632]{1,0:T(8,128)(2,1)S(1)}, u32[]{:S(2)}, u32[]{:S(2)}) collective-permute-start(bf16[32,5632]{1,0:T(8,128)(2,1)S(1)} %pad_maximum_fusion.2), channel_id=1, source_target_pairs={{0,128},{128,0},{256,384},{384,256},{1,129},{129,1},{257,385},{385... | collective-permute-start | bytes 1081352 | tf_op jit(solution)/shard_map/ppermute | solution.py:61
  69.3 18.4 %collective-permute-start.6 = (bf16[32,5632]{1,0:T(8,128)(2,1)S(1)}, bf16[32,5632]{1,0:T(8,128)(2,1)S(1)}, u32[]{:S(2)}, u32[]{:S(2)}) collective-permute-start(bf16[32,5632]{1,0:T(8,128)(2,1)S(1)} %pad_maximum_fusion.2), channel_id=1, source_target_pairs={{0,256},{128,384},{256,0},{384,128},{1,257},{129,385},{257,1},{385... | collective-permute-start | bytes 1081352 | tf_op jit(solution)/shard_map/ppermute | solution.py:61
  73.7 20.3 %collective-permute-start.7 = (bf16[32,5632]{1,0:T(8,128)(2,1)S(1)}, bf16[32,5632]{1,0:T(8,128)(2,1)S(1)}, u32[]{:S(2)}, u32[]{:S(2)}) collective-permute-start(bf16[32,5632]{1,0:T(8,128)(2,1)S(1)} %pad_maximum_fusion.2), channel_id=1, source_target_pairs={{0,384},{128,256},{256,128},{384,0},{1,385},{129,257},{257,129},{3... | collective-permute-start | bytes 1081352 | tf_op jit(solution)/shard_map/ppermute | solution.py:61
  95.5 7.6 %collective-permute-start.8 = (bf16[128,5632]{1,0:T(8,128)(2,1)S(1)}, bf16[128,5632]{1,0:T(8,128)(2,1)}, u32[]{:S(2)}, u32[]{:S(2)}) collective-permute-start(bf16[128,5632]{1,0:T(8,128)(2,1)S(1)} %bitcast.30), channel_id=1, source_target_pairs={{0,16},{16,0},{1,17},{17,1},{2,18},{18,2},{3,19},{19,3},{4,20},{20... | collective-permute-start | bytes 4325384 | tf_op jit(solution)/shard_map/ppermute | solution.py:108
  106.6 22.2 %copy-start.2 = (f32[8,1536]{1,0:T(8,128)S(1)}, f32[8,1536]{1,0:T(8,128)}, u32[]{:S(2)}) copy-start(f32[8,1536]{1,0:T(8,128)} %copy-done.1) | copy-start | bytes 147460
  106.9 46.8 %copy-start.4 = (bf16[128,96]{0,1:T(8,128)(2,1)S(1)}, bf16[128,96]{0,1:T(8,128)(2,1)}, u32[]{:S(2)}) copy-start(bf16[128,96]{0,1:T(8,128)(2,1)} %param.3) | copy-start | bytes 73732
  108.0 47.0 %copy-start.6 = (bf16[128,96]{0,1:T(8,128)(2,1)S(1)}, bf16[128,96]{0,1:T(8,128)(2,1)}, u32[]{:S(2)}) copy-start(bf16[128,96]{0,1:T(8,128)(2,1)} %copy-done.5) | copy-start | bytes 73732
  108.0 20.8 %all-to-all-start.2 = ((bf16[16,8,1536]{2,1,0:T(8,128)(2,1)}), bf16[16,8,1536]{2,1,0:T(8,128)(2,1)S(1)}, u32[]{:S(2)}, u32[]{:S(2)}) async-start(bf16[16,8,1536]{2,1,0:T(8,128)(2,1)} %fusion.3), calls=%async_computation.2 | async-start | bytes 786432 | tf_op jit(solution)/shard_map/all_to_all | solution.py:29
  115.9 3.6 %collective-permute-start.9 = (f32[]{:T(128)}, f32[]{:T(128)}, u32[]{:S(2)}, u32[]{:S(2)}) collective-permute-start(f32[]{:T(128)} %get-tuple-element.17), channel_id=1, source_target_pairs={{0,16},{16,0},{1,17},{17,1},{2,18},{18,2},{3,19},{19,3},{4,20},{20... | collective-permute-start | bytes 20 | tf_op jit(solution)/shard_map/ppermute | solution.py:113
  149.0 5.9 %collective-permute-start.10 = (bf16[128,1536]{1,0:T(8,128)(2,1)S(1)}, bf16[128,1536]{1,0:T(8,128)(2,1)S(1)}, u32[]{:S(2)}, u32[]{:S(2)}) collective-permute-start(bf16[128,1536]{1,0:T(8,128)(2,1)S(1)} %slice.32), channel_id=1, source_target_pairs={{0,16},{16,0},{1,17},{17,1},{2,18},{18,2},{3,19},{19,3},{4,20},{20... | collective-permute-start | bytes 1179656 | tf_op jit(solution)/shard_map/ppermute | solution.py:124
  167.7 12.5 %all-to-all-start.5 = ((bf16[16,3,1536]{2,1,0:T(4,128)(2,1)}), bf16[16,3,1536]{2,1,0:T(4,128)(2,1)S(1)}, u32[]{:S(2)}, u32[]{:S(2)}) async-start(bf16[16,3,1536]{2,1,0:T(4,128)(2,1)} %broadcast_in_dim.44), calls=%async_computation.5 | async-start | bytes 393216 | tf_op jit(solution)/shard_map/all_to_all | solution.py:29

commit v9 on v8

--- a/solution.py
+++ b/solution.py
@@ -59,7 +59,7 @@
     blocks = [block]
     for step in (1, 2, 3):
         blocks.append(lax.ppermute(block, axis, [(at, at ^ step) for at in range(4)]))
-    return jnp.concatenate(blocks, axis=0)
+    return blocks
 
 
 def in_order(values):
@@ -80,6 +80,13 @@
     width_t = teacher.shape[1]
     core = lax.axis_index("c")
 
+    over = lax.ppermute(teacher, "zh", SWAP)
+    first = lax.axis_index("zh") == 0
+    both = jnp.concatenate(
+        [jnp.where(first, teacher, over), jnp.where(first, over, teacher)], axis=1
+    )
+    teach = lax.all_gather(both, "y", axis=0)
+
     partial_embed = dot(hidden, projector).astype(jnp.bfloat16)
     sent = jnp.concatenate(
         [
@@ -93,21 +100,30 @@
     inv_student = lax.rsqrt(jnp.sum(embed * embed, axis=1, keepdims=True) + EPSILON)
     unit = embed * inv_student
     student = unit.astype(jnp.bfloat16)
-    target = normal(got[:, :, full:].astype(jnp.float32), (0, 2))
-    target = target.transpose(1, 0, 2).reshape(mine, -1)
+    target_mine = (
+        normal(got[:, :, full:].astype(jnp.float32), (0, 2))
+        .reshape(SIZES["zh"], SIZES["y"], mine, width_t)
+        .transpose(2, 1, 0, 3)
+        .reshape(mine, -1)
+    )
 
-    near = around(jnp.concatenate([student, target], axis=1), "zl")
-    mine_cols = jnp.concatenate([student, -target], axis=1)
-    pair = jnp.concatenate([mine_cols, lax.ppermute(mine_cols, "zh", SWAP)], axis=0)
-    pair, near, hidden_sent = lax.optimization_barrier((pair, near, hidden))
-    here = gather(pair, ("y",)).reshape(rows, -1)
+    near = jnp.concatenate(
+        around(jnp.concatenate([student, target_mine], axis=1), "zl"), axis=0
+    )
+    student_sent, near, hidden_sent = lax.optimization_barrier((student, near, hidden))
+    s_here = gather(student_sent, FS).reshape(rows, full)
     hidden_there = lax.ppermute(hidden_sent, "c", SWAP)
     near, hidden_there = lax.optimization_barrier((near, hidden_there))
-    row_block = around(near, "x")
-    here, row_block = lax.optimization_barrier((here, row_block))
-    columns = jnp.concatenate([here, lax.ppermute(here, "c", SWAP)], axis=0)
-    s_cols = columns[:, :full]
-    differ = dot(row_block, columns, ROWS_T)
+    far = around(near, "x")
+    far[1], teach = lax.optimization_barrier((far[1], teach))
+    target = normal(teach.astype(jnp.float32), (0, 2)).transpose(1, 0, 2)
+    target = target.reshape(rows, -1)
+    t_cols = jnp.concatenate([target, lax.ppermute(target, "c", SWAP)], axis=0)
+    row_block = jnp.concatenate(far, axis=0)
+    s_here, row_block = lax.optimization_barrier((s_here, row_block))
+    s_cols = jnp.concatenate([s_here, lax.ppermute(s_here, "c", SWAP)], axis=0)
+    s_rows, t_rows = row_block[:, :full], row_block[:, full:]
+    differ = dot(s_rows, s_cols, ROWS_T) - dot(t_rows, t_cols, ROWS_T)
     differ = in_order(differ)
     squares = jnp.sum(differ * differ)
     squares = squares + lax.ppermute(squares, "c", SWAP)

time: 188 us -> 199 us (1.059)
  blocking collectives: 67.7 us -> 41.9 us
  starting transfers between devices: 57.1 us -> 82.2 us
  between operations: 7.71 us -> 21.2 us
  waiting for transfers between devices: 40.2 us -> 33 us
  other arithmetic: 4.45 us -> 8.89 us
    all_to_all x3 -> x2, blocking collectives: 63.1 us -> 37.3 us  [exchange(): return lax.all_to_all(blocks, axes, split_axis=0, concat_axis=0, tiled=True)]
    ppermute x6, waiting for transfers between devices: 23.2 us -> 8.7 us  [around(): lax.ppermute(block, axis, [(at, at ^ step) for at in range(4)])]
    all_to_all x3 -> x4, starting transfers between devices: 18.8 us -> 32.6 us  [exchange(): return lax.all_to_all(blocks, axes, split_axis=0, concat_axis=0, tiled=True)]
    ppermute x2 -> x3, starting transfers between devices: 7.12 us -> 17 us  [the longest x1 7.38 us: body(): t_cols = jnp.concatenate([target, lax.ppermute(target, 'c', SWAP)], axis=0)]
    ppermute x2 -> x3, waiting for transfers between devices: 2.85 us -> 11.5 us  [the longest x1 10.3 us: body(): over = lax.ppermute(teacher, 'zh', SWAP)]
    ppermute x6, starting transfers between devices: 18.8 us -> 21.1 us  [around(): lax.ppermute(block, axis, [(at, at ^ step) for at in range(4)])]
    all_to_all x3 -> x4, waiting for transfers between devices: 11.1 us -> 9.73 us  [exchange(): return lax.all_to_all(blocks, axes, split_axis=0, concat_axis=0, tiled=True)]
    dot_general x8 -> x9, matrix products: 4.87 us -> 6.22 us  [dot(): return lax.dot_general(a, b, dims, preferred_element_type=jnp.float32)]
  transfers between devices with their start and end apart: 14 -> 17, of which waited for: 12 -> 10; matrix products, arithmetic and copies ran while one was open for 1% -> 4% of each run, Pallas kernels for 0% -> 0%
where the time goes in v9:
time: 199 us; the launch traced here: 198 us
  starting transfers between devices  82.2 us (41%)
  blocking collectives  41.9 us (21%)
  waiting for transfers between devices  33 us (17%)
  between operations  21.2 us (11%)
  other arithmetic  8.89 us (4%)
  matrix products  6.22 us (3%)
  local copies, waits for them, and re-layouts  4.29 us (2%)
    all_to_all x2, blocking collectives, exchange(): return lax.all_to_all(blocks, axes, split_axis=0, concat_axis=0, tiled=True)  37.3 us
    all_to_all x4, starting transfers between devices, exchange(): return lax.all_to_all(blocks, axes, split_axis=0, concat_axis=0, tiled=True)  32.6 us
    ppermute x6, starting transfers between devices, around(): lax.ppermute(block, axis, [(at, at ^ step) for at in range(4)])  21.1 us
    ppermute x1, waiting for transfers between devices, body(): over = lax.ppermute(teacher, 'zh', SWAP)  10.3 us
    all_to_all x4, waiting for transfers between devices, exchange(): return lax.all_to_all(blocks, axes, split_axis=0, concat_axis=0, tiled=True)  9.73 us
    ppermute x6, waiting for transfers between devices, around(): lax.ppermute(block, axis, [(at, at ^ step) for at in range(4)])  8.7 us
    ppermute x1, starting transfers between devices, body(): t_cols = jnp.concatenate([target, lax.ppermute(target, 'c', SWAP)], axis=0)  7.38 us
    ppermute x1, starting transfers between devices, body(): over = lax.ppermute(teacher, 'zh', SWAP)  7.18 us
  transfers between devices with their start and end apart: 17, of which 10 were waited for; matrix products, arithmetic and copies ran while one was open for 4% of the time, Pallas kernels for 0%

profile of v9, /device:TPU:1, one launch (start us, length us, event | category | flops | bytes accessed | tf_op | source)
XLA Modules:
  0.0 197.7 jit_solution(8480405416157341213)
XLA Ops:
  7.2 1.0 copy-done
  8.1 1.0 fusion.2
  9.2 1.6 pad_maximum_fusion.1
  10.8 16.2 %all-to-all-start = ((bf16[16,8,1792]{2,1,0:T(8,128)(2,1)}), bf16[16,8,1792]{2,1,0:T(8,128)(2,1)S(1)}, u32[]{:S(2)}, u32[]{:S(2)}) async-start(bf16[16,8,1792]{2,1,0:T(8,128)(2,1)} %pad_maximum_fusion.1), calls=%async_computation | async-start | bytes 917504 | tf_op jit(solution)/shard_map/all_to_all | solution.py:29
  27.1 7.2 %collective-permute-start.5 = (bf16[128,256]{1,0:T(8,128)(2,1)S(1)}, bf16[128,256]{1,0:T(8,128)(2,1)S(1)}, u32[]{:S(2)}, u32[]{:S(2)}) collective-permute-start(bf16[128,256]{1,0:T(8,128)(2,1)S(1)} %copy-done.2), channel_id=1, source_target_pairs={{0,8},{8,0},{1,9},{9,1},{2,10},{10,2},{3,11},{11,3},{4,12},{12,4},... | collective-permute-start | bytes 196616 | tf_op jit(solution)/shard_map/ppermute | solution.py:83
  34.3 10.3 %collective-permute-done.5 = bf16[128,256]{1,0:T(8,128)(2,1)S(1)} collective-permute-done((bf16[128,256]{1,0:T(8,128)(2,1)S(1)}, bf16[128,256]{1,0:T(8,128)(2,1)S(1)}, u32[]{:S(2)}, u32[]{:S(2)}) %collective-permute-start.5) | collective-permute-done | bytes 65568 | tf_op jit(solution)/shard_map/ppermute | solution.py:83
  44.6 0.7 pad_maximum_fusion.4
  45.3 0.1 convert_reduce_fusion.1
  45.3 0.1 multiply_reduce_fusion.2
  45.5 0.1 multiply_convert_fusion.1
  45.5 0.1 fusion.14
  45.7 0.1 fusion.15
  45.8 0.1 copy.10
  45.9 2.9 %collective-permute-start = (bf16[8,5632]{1,0:T(8,128)(2,1)S(1)}, bf16[8,5632]{1,0:T(8,128)(2,1)S(1)}, u32[]{:S(2)}, u32[]{:S(2)}) collective-permute-start(bf16[8,5632]{1,0:T(8,128)(2,1)S(1)} %pad_maximum_fusion.5), channel_id=1, source_target_pairs={{0,32},{32,0},{64,96},{96,64},{1,33},{33,1},{65,97},{97,65},{2,34}... | collective-permute-start | bytes 270344 | tf_op jit(solution)/shard_map/ppermute | solution.py:61
  48.9 5.9 %collective-permute-start.1 = (bf16[8,5632]{1,0:T(8,128)(2,1)S(1)}, bf16[8,5632]{1,0:T(8,128)(2,1)S(1)}, u32[]{:S(2)}, u32[]{:S(2)}) collective-permute-start(bf16[8,5632]{1,0:T(8,128)(2,1)S(1)} %pad_maximum_fusion.5), channel_id=1, source_target_pairs={{0,64},{32,96},{64,0},{96,32},{1,65},{33,97},{65,1},{97,33},{2,66}... | collective-permute-start | bytes 270344 | tf_op jit(solution)/shard_map/ppermute | solution.py:61
  54.8 2.7 %collective-permute-start.2 = (bf16[8,5632]{1,0:T(8,128)(2,1)S(1)}, bf16[8,5632]{1,0:T(8,128)(2,1)S(1)}, u32[]{:S(2)}, u32[]{:S(2)}) collective-permute-start(bf16[8,5632]{1,0:T(8,128)(2,1)S(1)} %pad_maximum_fusion.5), channel_id=1, source_target_pairs={{0,96},{32,64},{64,32},{96,0},{1,97},{33,65},{65,33},{97,1},{2,98}... | collective-permute-start | bytes 270344 | tf_op jit(solution)/shard_map/ppermute | solution.py:61
  57.4 1.6 collective-permute-done.1
  59.0 2.9 %collective-permute-done.2 = bf16[8,5632]{1,0:T(8,128)(2,1)S(1)} collective-permute-done((bf16[8,5632]{1,0:T(8,128)(2,1)S(1)}, bf16[8,5632]{1,0:T(8,128)(2,1)S(1)}, u32[]{:S(2)}, u32[]{:S(2)}) %collective-permute-start.2) | collective-permute-done | bytes 90144 | tf_op jit(solution)/shard_map/ppermute | solution.py:61
  61.9 4.2 %collective-permute-start.3 = (bf16[128,96]{0,1:T(8,128)(2,1)S(1)}, bf16[128,96]{0,1:T(8,128)(2,1)S(1)}, u32[]{:S(2)}, u32[]{:S(2)}) collective-permute-start(bf16[128,96]{0,1:T(8,128)(2,1)S(1)} %copy-done.3), channel_id=1, source_target_pairs={{0,16},{16,0},{1,17},{17,1},{2,18},{18,2},{3,19},{19,3},{4,20},{20... | collective-permute-start | bytes 73736 | tf_op jit(solution)/shard_map/ppermute | solution.py:115
  66.1 0.8 collective-permute-done.3
  67.0 3.1 %collective-permute-start.4 = (bf16[32,5632]{1,0:T(8,128)(2,1)S(1)}, bf16[32,5632]{1,0:T(8,128)(2,1)S(1)}, u32[]{:S(2)}, u32[]{:S(2)}) collective-permute-start(bf16[32,5632]{1,0:T(8,128)(2,1)S(1)} %pad_maximum_fusion.2), channel_id=1, source_target_pairs={{0,128},{128,0},{256,384},{384,256},{1,129},{129,1},{257,385},{385... | collective-permute-start | bytes 1081352 | tf_op jit(solution)/shard_map/ppermute | solution.py:61
  70.1 0.8 broadcast_in_dim.38
  70.8 6.2 %all-to-all-start.1 = ((bf16[16,8,1536]{2,1,0:T(8,128)(2,1)}), bf16[16,8,1536]{2,1,0:T(8,128)(2,1)S(1)}, u32[]{:S(2)}, u32[]{:S(2)}) async-start(bf16[16,8,1536]{2,1,0:T(8,128)(2,1)} %broadcast_in_dim.38), calls=%async_computation.1 | async-start | bytes 786432 | tf_op jit(solution)/shard_map/all_to_all | solution.py:29
  77.1 4.4 %collective-permute-start.6 = (bf16[32,5632]{1,0:T(8,128)(2,1)S(1)}, bf16[32,5632]{1,0:T(8,128)(2,1)S(1)}, u32[]{:S(2)}, u32[]{:S(2)}) collective-permute-start(bf16[32,5632]{1,0:T(8,128)(2,1)S(1)} %pad_maximum_fusion.2), channel_id=1, source_target_pairs={{0,256},{128,384},{256,0},{384,128},{1,257},{129,385},{257,1},{385... | collective-permute-start | bytes 1081352 | tf_op jit(solution)/shard_map/ppermute | solution.py:61
  81.4 2.1 %collective-permute-start.7 = (bf16[32,5632]{1,0:T(8,128)(2,1)S(1)}, bf16[32,5632]{1,0:T(8,128)(2,1)}, u32[]{:S(2)}, u32[]{:S(2)}) collective-permute-start(bf16[32,5632]{1,0:T(8,128)(2,1)S(1)} %pad_maximum_fusion.2), channel_id=1, source_target_pairs={{0,384},{128,256},{256,128},{384,0},{1,385},{129,257},{257,129},{3... | collective-permute-start | bytes 1081352 | tf_op jit(solution)/shard_map/ppermute | solution.py:61
  83.6 1.6 fusion.5
  85.2 0.4 fusion.11
  85.7 1.3 copy.11
  87.0 7.4 %collective-permute-start.9 = (bf16[128,4096]{0,1:T(8,128)(2,1)}, bf16[128,4096]{0,1:T(8,128)(2,1)}, u32[]{:S(2)}, u32[]{:S(2)}) collective-permute-start(bf16[128,4096]{0,1:T(8,128)(2,1)} %bitcast.40), channel_id=1, source_target_pairs={{0,16},{16,0},{1,17},{17,1},{2,18},{18,2},{3,19},{19,3},{4,20},{20... | collective-permute-start | bytes 3145736 | tf_op jit(solution)/shard_map/ppermute | solution.py:121
  94.4 4.3 %collective-permute-done.7 = bf16[32,5632]{1,0:T(8,128)(2,1)} collective-permute-done((bf16[32,5632]{1,0:T(8,128)(2,1)S(1)}, bf16[32,5632]{1,0:T(8,128)(2,1)}, u32[]{:S(2)}, u32[]{:S(2)}) %collective-permute-start.7) | collective-permute-done | bytes 360480 | tf_op jit(solution)/shard_map/ppermute | solution.py:61
  98.6 1.1 pad_maximum_fusion
  99.7 2.4 %collective-permute-start.8 = (bf16[128,1536]{1,0:T(8,128)(2,1)S(1)}, bf16[128,1536]{1,0:T(8,128)(2,1)S(1)}, u32[]{:S(2)}, u32[]{:S(2)}) collective-permute-start(bf16[128,1536]{1,0:T(8,128)(2,1)S(1)} %bitcast.38), channel_id=1, source_target_pairs={{0,16},{16,0},{1,17},{17,1},{2,18},{18,2},{3,19},{19,3},{4,20},{20... | collective-permute-start | bytes 1179656 | tf_op jit(solution)/shard_map/ppermute | solution.py:124
  102.2 1.3 collective-permute-done.8
  103.5 2.0 %fusion.7 = f32[128,256]{1,0:T(8,128)S(1)} fusion(bf16[128,4096]{0,1:T(8,128)(2,1)} %collective-permute-done.9, bf16[128,4096]{0,1:T(8,128)(2,1)} %bitcast.41, bf16[128,5632]{1,0:T(8,128)(2,1)S(1)} %pad_maximum_fusion), kind=kOutput, calls=%fused_computation.12 | convolution fusion | flops 272629760 | bytes 3276800 | tf_op jit(solution)/shard_map/dot_general | solution.py:18
  105.5 0.4 convolution_subtract_fusion
  106.0 0.6 multiply_reduce_fusion
  106.6 0.3 fusion.28
  106.9 0.3 fusion.29
  107.2 1.0 fusion.3
  108.2 5.2 %all-to-all-start.2 = ((bf16[16,8,1536]{2,1,0:T(8,128)(2,1)}), bf16[16,8,1536]{2,1,0:T(8,128)(2,1)S(1)}, u32[]{:S(2)}, u32[]{:S(2)}) async-start(bf16[16,8,1536]{2,1,0:T(8,128)(2,1)} %fusion.3), calls=%async_computation.2 | async-start | bytes 786432 | tf_op jit(solution)/shard_map/all_to_all | solution.py:29
  113.4 2.6 %collective-permute-start.10 = (f32[]{:T(128)}, f32[]{:T(128)}, u32[]{:S(2)}, u32[]{:S(2)}) collective-permute-start(f32[]{:T(128)} %get-tuple-element.21), channel_id=1, source_target_pairs={{0,16},{16,0},{1,17},{17,1},{2,18},{18,2},{3,19},{19,3},{4,20},{20... | collective-permute-start | bytes 20 | tf_op jit(solution)/shard_map/ppermute | solution.py:129
  116.0 1.1 collective-permute-done.10
  122.0 4.4 %all-to-all-done.2 = bf16[16,8,1536]{2,1,0:T(8,128)(2,1)S(1)} async-done(((bf16[16,8,1536]{2,1,0:T(8,128)(2,1)}), bf16[16,8,1536]{2,1,0:T(8,128)(2,1)S(1)}, u32[]{:S(2)}, u32[]{:S(2)}) %all-to-all-start.2) | async-done | bytes 393248 | tf_op jit(solution)/shard_map/all_to_all | solution.py:29
  126.3 0.1 convert_reduce_fusion
  126.4 0.2 multiply_reduce_fusion.1
  126.6 0.1 multiply_convert_fusion
  126.7 26.4 %all_to_all.30 = bf16[16,8,1664]{2,1,0:T(8,128)(2,1)S(1)} all-to-all(bf16[16,8,1664]{2,1,0:T(8,128)(2,1)S(1)} %broadcast_in_dim.43), channel_id=1, replica_groups=mesh['x'=4,'zl'=4,'c'=2,'zh'=2,'y'=8] {'zh','y'}, dimensions={0} | all-to-all | bytes 851968 | tf_op jit(solution)/shard_map/all_to_all | solution.py:29
  153.2 4.9 %collective-permute-start.11 = (bf16[128,1536]{1,0:T(8,128)(2,1)S(1)}, bf16[128,1536]{1,0:T(8,128)(2,1)S(1)}, u32[]{:S(2)}, u32[]{:S(2)}) collective-permute-start(bf16[128,1536]{1,0:T(8,128)(2,1)S(1)} %slice.35), channel_id=1, source_target_pairs={{0,16},{16,0},{1,17},{17,1},{2,18},{18,2},{3,19},{19,3},{4,20},{20... | collective-permute-start | bytes 1179656 | tf_op jit(solution)/shard_map/ppermute | solution.py:140
  158.1 0.2 fusion.18
  158.3 1.1 collective-permute-done.11
  159.4 0.2 fusion.4
  159.6 0.1 reshape.74
  159.7 0.1 broadcast_in_dim.44
  159.7 0.2 pad_maximum_fusion.3
  159.9 10.9 %all_to_all.31 = bf16[16,4,1536]{2,1,0:T(4,128)(2,1)S(1)} all-to-all(bf16[16,4,1536]{2,1,0:T(4,128)(2,1)S(1)} %pad_maximum_fusion.3), channel_id=1, replica_groups=mesh['x'=4,'zl'=4,'c'=2,'zh'=2,'y'=8] {'x','zl'}, dimensions={0} | all-to-all | bytes 393216 | tf_op jit(solution)/shard_map/all_to_all | solution.py:29
  170.9 0.1 convert_reduce_fusion.2
  171.0 0.7 broadcast_in_dim.45
  171.7 5.0 %all-to-all-start.5 = ((bf16[16,3,1536]{2,1,0:T(4,128)(2,1)}), bf16[16,3,1536]{2,1,0:T(4,128)(2,1)S(1)}, u32[]{:S(2)}, u32[]{:S(2)}) async-start(bf16[16,3,1536]{2,1,0:T(4,128)(2,1)} %broadcast_in_dim.45), calls=%async_computation.5 | async-start | bytes 393216 | tf_op jit(solution)/shard_map/all_to_all | solution.py:29
  176.7 0.9 fusion.26
  177.6 0.6 slice_reduce_fusion.1
  178.8 5.4 %all-to-all-done.5 = bf16[16,3,1536]{2,1,0:T(4,128)(2,1)S(1)} async-done(((bf16[16,3,1536]{2,1,0:T(4,128)(2,1)}), bf16[16,3,1536]{2,1,0:T(4,128)(2,1)S(1)}, u32[]{:S(2)}, u32[]{:S(2)}) %all-to-all-start.5) | async-done | bytes 147488 | tf_op jit(solution)/shard_map/all_to_all | solution.py:29
  184.2 0.1 reshape.75
  184.3 4.6 %all_gather.11 = bf16[96,1536]{1,0:T(8,128)(2,1)S(1)} all-gather(bf16[48,1536]{1,0:T(8,128)(2,1)S(1)} %reshape.75), channel_id=1, replica_groups=mesh['x'=4,'zl'=4,'c'=2,'zh'=2,'y'=8] {'c'}, dimensions={0}, use_global_device_ids=true | all-gather | bytes 442368 | tf_op jit(solution)/shard_map/all_gather | solution.py:161
  188.9 0.9 convert_element_type.80
  (38 shorter events, 0.5 us)
Async XLA Ops:
  7.2 1.0 copy-start
  8.1 19.0 %copy-start.2 = (bf16[128,256]{1,0:T(8,128)(2,1)S(1)}, bf16[128,256]{1,0:T(8,128)(2,1)}, u32[]{:S(2)}) copy-start(bf16[128,256]{1,0:T(8,128)(2,1)} %param.4) | copy-start | bytes 196612
  10.8 34.4 %all-to-all-start = ((bf16[16,8,1792]{2,1,0:T(8,128)(2,1)}), bf16[16,8,1792]{2,1,0:T(8,128)(2,1)S(1)}, u32[]{:S(2)}, u32[]{:S(2)}) async-start(bf16[16,8,1792]{2,1,0:T(8,128)(2,1)} %pad_maximum_fusion.1), calls=%async_computation | async-start | bytes 917504 | tf_op jit(solution)/shard_map/all_to_all | solution.py:29
  27.0 34.9 %copy-start.3 = (bf16[128,96]{0,1:T(8,128)(2,1)S(1)}, bf16[128,96]{0,1:T(8,128)(2,1)}, u32[]{:S(2)}) copy-start(bf16[128,96]{0,1:T(8,128)(2,1)} %param.3) | copy-start | bytes 73732
  27.0 56.5 %all-gather.3.cloned.1.call-start = ((), (), s32[]{:S(2)}) async-start(), calls=%async_computation.6 | async-start | bytes 1179648 | tf_op jit(solution)/shard_map/all_gather | solution.py:88
  27.1 17.5 %collective-permute-start.5 = (bf16[128,256]{1,0:T(8,128)(2,1)S(1)}, bf16[128,256]{1,0:T(8,128)(2,1)S(1)}, u32[]{:S(2)}, u32[]{:S(2)}) collective-permute-start(bf16[128,256]{1,0:T(8,128)(2,1)S(1)} %copy-done.2), channel_id=1, source_target_pairs={{0,8},{8,0},{1,9},{9,1},{2,10},{10,2},{3,11},{11,3},{4,12},{12,4},... | collective-permute-start | bytes 196616 | tf_op jit(solution)/shard_map/ppermute | solution.py:83
  45.9 11.5 %collective-permute-start = (bf16[8,5632]{1,0:T(8,128)(2,1)S(1)}, bf16[8,5632]{1,0:T(8,128)(2,1)S(1)}, u32[]{:S(2)}, u32[]{:S(2)}) collective-permute-start(bf16[8,5632]{1,0:T(8,128)(2,1)S(1)} %pad_maximum_fusion.5), channel_id=1, source_target_pairs={{0,32},{32,0},{64,96},{96,64},{1,33},{33,1},{65,97},{97,65},{2,34}... | collective-permute-start | bytes 270344 | tf_op jit(solution)/shard_map/ppermute | solution.py:61
  48.9 10.2 %collective-permute-start.1 = (bf16[8,5632]{1,0:T(8,128)(2,1)S(1)}, bf16[8,5632]{1,0:T(8,128)(2,1)S(1)}, u32[]{:S(2)}, u32[]{:S(2)}) collective-permute-start(bf16[8,5632]{1,0:T(8,128)(2,1)S(1)} %pad_maximum_fusion.5), channel_id=1, source_target_pairs={{0,64},{32,96},{64,0},{96,32},{1,65},{33,97},{65,1},{97,33},{2,66}... | collective-permute-start | bytes 270344 | tf_op jit(solution)/shard_map/ppermute | solution.py:61
  54.8 7.1 %collective-permute-start.2 = (bf16[8,5632]{1,0:T(8,128)(2,1)S(1)}, bf16[8,5632]{1,0:T(8,128)(2,1)S(1)}, u32[]{:S(2)}, u32[]{:S(2)}) collective-permute-start(bf16[8,5632]{1,0:T(8,128)(2,1)S(1)} %pad_maximum_fusion.5), channel_id=1, source_target_pairs={{0,96},{32,64},{64,32},{96,0},{1,97},{33,65},{65,33},{97,1},{2,98}... | collective-permute-start | bytes 270344 | tf_op jit(solution)/shard_map/ppermute | solution.py:61
  61.9 5.0 %collective-permute-start.3 = (bf16[128,96]{0,1:T(8,128)(2,1)S(1)}, bf16[128,96]{0,1:T(8,128)(2,1)S(1)}, u32[]{:S(2)}, u32[]{:S(2)}) collective-permute-start(bf16[128,96]{0,1:T(8,128)(2,1)S(1)} %copy-done.3), channel_id=1, source_target_pairs={{0,16},{16,0},{1,17},{17,1},{2,18},{18,2},{3,19},{19,3},{4,20},{20... | collective-permute-start | bytes 73736 | tf_op jit(solution)/shard_map/ppermute | solution.py:115
  67.0 16.6 %collective-permute-start.4 = (bf16[32,5632]{1,0:T(8,128)(2,1)S(1)}, bf16[32,5632]{1,0:T(8,128)(2,1)S(1)}, u32[]{:S(2)}, u32[]{:S(2)}) collective-permute-start(bf16[32,5632]{1,0:T(8,128)(2,1)S(1)} %pad_maximum_fusion.2), channel_id=1, source_target_pairs={{0,128},{128,0},{256,384},{384,256},{1,129},{129,1},{257,385},{385... | collective-permute-start | bytes 1081352 | tf_op jit(solution)/shard_map/ppermute | solution.py:61
  70.8 28.9 %all-to-all-start.1 = ((bf16[16,8,1536]{2,1,0:T(8,128)(2,1)}), bf16[16,8,1536]{2,1,0:T(8,128)(2,1)S(1)}, u32[]{:S(2)}, u32[]{:S(2)}) async-start(bf16[16,8,1536]{2,1,0:T(8,128)(2,1)} %broadcast_in_dim.38), calls=%async_computation.1 | async-start | bytes 786432 | tf_op jit(solution)/shard_map/all_to_all | solution.py:29
  77.1 17.3 %collective-permute-start.6 = (bf16[32,5632]{1,0:T(8,128)(2,1)S(1)}, bf16[32,5632]{1,0:T(8,128)(2,1)S(1)}, u32[]{:S(2)}, u32[]{:S(2)}) collective-permute-start(bf16[32,5632]{1,0:T(8,128)(2,1)S(1)} %pad_maximum_fusion.2), channel_id=1, source_target_pairs={{0,256},{128,384},{256,0},{384,128},{1,257},{129,385},{257,1},{385... | collective-permute-start | bytes 1081352 | tf_op jit(solution)/shard_map/ppermute | solution.py:61
  81.4 17.2 %collective-permute-start.7 = (bf16[32,5632]{1,0:T(8,128)(2,1)S(1)}, bf16[32,5632]{1,0:T(8,128)(2,1)}, u32[]{:S(2)}, u32[]{:S(2)}) collective-permute-start(bf16[32,5632]{1,0:T(8,128)(2,1)S(1)} %pad_maximum_fusion.2), channel_id=1, source_target_pairs={{0,384},{128,256},{256,128},{384,0},{1,385},{129,257},{257,129},{3... | collective-permute-start | bytes 1081352 | tf_op jit(solution)/shard_map/ppermute | solution.py:61
  83.6 1.6 copy-start.1
  87.0 16.5 %collective-permute-start.9 = (bf16[128,4096]{0,1:T(8,128)(2,1)}, bf16[128,4096]{0,1:T(8,128)(2,1)}, u32[]{:S(2)}, u32[]{:S(2)}) collective-permute-start(bf16[128,4096]{0,1:T(8,128)(2,1)} %bitcast.40), channel_id=1, source_target_pairs={{0,16},{16,0},{1,17},{17,1},{2,18},{18,2},{3,19},{19,3},{4,20},{20... | collective-permute-start | bytes 3145736 | tf_op jit(solution)/shard_map/ppermute | solution.py:121
  99.7 3.7 %collective-permute-start.8 = (bf16[128,1536]{1,0:T(8,128)(2,1)S(1)}, bf16[128,1536]{1,0:T(8,128)(2,1)S(1)}, u32[]{:S(2)}, u32[]{:S(2)}) collective-permute-start(bf16[128,1536]{1,0:T(8,128)(2,1)S(1)} %bitcast.38), channel_id=1, source_target_pairs={{0,16},{16,0},{1,17},{17,1},{2,18},{18,2},{3,19},{19,3},{4,20},{20... | collective-permute-start | bytes 1179656 | tf_op jit(solution)/shard_map/ppermute | solution.py:124
  108.2 18.1 %all-to-all-start.2 = ((bf16[16,8,1536]{2,1,0:T(8,128)(2,1)}), bf16[16,8,1536]{2,1,0:T(8,128)(2,1)S(1)}, u32[]{:S(2)}, u32[]{:S(2)}) async-start(bf16[16,8,1536]{2,1,0:T(8,128)(2,1)} %fusion.3), calls=%async_computation.2 | async-start | bytes 786432 | tf_op jit(solution)/shard_map/all_to_all | solution.py:29
  113.4 3.6 %collective-permute-start.10 = (f32[]{:T(128)}, f32[]{:T(128)}, u32[]{:S(2)}, u32[]{:S(2)}) collective-permute-start(f32[]{:T(128)} %get-tuple-element.21), channel_id=1, source_target_pairs={{0,16},{16,0},{1,17},{17,1},{2,18},{18,2},{3,19},{19,3},{4,20},{20... | collective-permute-start | bytes 20 | tf_op jit(solution)/shard_map/ppermute | solution.py:129
  153.2 6.2 %collective-permute-start.11 = (bf16[128,1536]{1,0:T(8,128)(2,1)S(1)}, bf16[128,1536]{1,0:T(8,128)(2,1)S(1)}, u32[]{:S(2)}, u32[]{:S(2)}) collective-permute-start(bf16[128,1536]{1,0:T(8,128)(2,1)S(1)} %slice.35), channel_id=1, source_target_pairs={{0,16},{16,0},{1,17},{17,1},{2,18},{18,2},{3,19},{19,3},{4,20},{20... | collective-permute-start | bytes 1179656 | tf_op jit(solution)/shard_map/ppermute | solution.py:140
  171.7 12.5 %all-to-all-start.5 = ((bf16[16,3,1536]{2,1,0:T(4,128)(2,1)}), bf16[16,3,1536]{2,1,0:T(4,128)(2,1)S(1)}, u32[]{:S(2)}, u32[]{:S(2)}) async-start(bf16[16,3,1536]{2,1,0:T(4,128)(2,1)} %broadcast_in_dim.45), calls=%async_computation.5 | async-start | bytes 393216 | tf_op jit(solution)/shard_map/all_to_all | solution.py:29
Sparse Core Ops, SparseCore 0:
  45.4 35.9 all-gather.2

commit v10 on v8

--- a/solution.py
+++ b/solution.py
@@ -5,10 +5,12 @@
 from jax.sharding import PartitionSpec as P
 
 EPSILON = 1e-06
-DP = ("x", "zl", "c")
+DP = ("x", "zb", "za", "c")
 FS = ("zh", "y")
-XZ = ("x", "zl")
-SIZES = {"x": 4, "zl": 4, "c": 2, "zh": 2, "y": 8}
+XZ = ("x", "zb", "za")
+STRIDE = ("zb", "zh")
+ROW = ("x",) + STRIDE
+SIZES = {"x": 4, "zb": 2, "za": 2, "c": 2, "zh": 2, "y": 8}
 SWAP = [(0, 1), (1, 0)]
 ROWS_T = (((1,), (1,)), ((), ()))
 COLS_T = (((0,), (0,)), ((), ()))
@@ -65,7 +67,7 @@
 def in_order(values):
     shape = values.shape
     values = values.reshape(2, 2, 2, 2, -1, shape[1])
-    for dim, (axis, bit) in enumerate((("x", 2), ("x", 1), ("zl", 2), ("zl", 1))):
+    for dim, (axis, bit) in enumerate((("x", 2), ("x", 1), ("zb", 1), ("zh", 1))):
         swap = (lax.axis_index(axis) & bit) != 0
         values = jnp.where(swap, jnp.flip(values, dim), values)
     return values.reshape(shape)
@@ -96,24 +98,27 @@
     target = normal(got[:, :, full:].astype(jnp.float32), (0, 2))
     target = target.transpose(1, 0, 2).reshape(mine, -1)
 
-    near = around(jnp.concatenate([student, target], axis=1), "zl")
-    mine_cols = jnp.concatenate([student, -target], axis=1)
-    pair = jnp.concatenate([mine_cols, lax.ppermute(mine_cols, "zh", SWAP)], axis=0)
-    pair, near, hidden_sent = lax.optimization_barrier((pair, near, hidden))
-    here = gather(pair, ("y",)).reshape(rows, -1)
+    mine_rows, hidden_sent = lax.optimization_barrier(
+        (jnp.concatenate([student, target], axis=1), hidden)
+    )
+    here = gather(jnp.concatenate([student, -target], axis=1), ("y",))
+    here = here.reshape(-1, here.shape[2])
     hidden_there = lax.ppermute(hidden_sent, "c", SWAP)
-    near, hidden_there = lax.optimization_barrier((near, hidden_there))
-    row_block = around(near, "x")
-    here, row_block = lax.optimization_barrier((here, row_block))
-    columns = jnp.concatenate([here, lax.ppermute(here, "c", SWAP)], axis=0)
+    mine_rows, hidden_there = lax.optimization_barrier((mine_rows, hidden_there))
+    row_block = around(around(mine_rows, STRIDE), "x")
+    there = lax.ppermute(here, "za", SWAP)
+    columns = jnp.concatenate(
+        [here, lax.ppermute(here, "c", SWAP), there, lax.ppermute(there, "c", SWAP)],
+        axis=0,
+    )
     s_cols = columns[:, :full]
     differ = dot(row_block, columns, ROWS_T)
     differ = in_order(differ)
     squares = jnp.sum(differ * differ)
     squares = squares + lax.ppermute(squares, "c", SWAP)
     partial_grad = sum(dot(part, s_cols) for part in pieces(differ)[::-1])
-    partial_grad = partial_grad.astype(jnp.bfloat16).reshape(group_xz, mine, full)
-    grad_unit = 4.0 * jnp.sum(exchange(partial_grad, XZ).astype(jnp.float32), axis=0)
+    partial_grad = partial_grad.astype(jnp.bfloat16).reshape(-1, mine, full)
+    grad_unit = 4.0 * jnp.sum(exchange(partial_grad, ROW).astype(jnp.float32), axis=0)
     radial = jnp.sum(unit * grad_unit, axis=1, keepdims=True)
     grad_embed = (inv_student * (grad_unit - unit * radial)).astype(jnp.bfloat16)
 

time: 188 us -> 182 us (0.968)
  waiting for transfers between devices: 40.2 us -> 22.4 us
  blocking collectives: 67.7 us -> 73.9 us
  local copies, waits for them, and re-layouts: 4.84 us -> 7.83 us
    ppermute x6, waiting for transfers between devices: 23.2 us -> 3.34 us  [around(): lax.ppermute(block, axis, [(at, at ^ step) for at in range(4)])]
    all_to_all x3, blocking collectives: 63.1 us -> 69.4 us  [exchange(): return lax.all_to_all(blocks, axes, split_axis=0, concat_axis=0, tiled=True)]
    all_to_all x3, starting transfers between devices: 18.8 us -> 15.5 us  [exchange(): return lax.all_to_all(blocks, axes, split_axis=0, concat_axis=0, tiled=True)]
    unnamed x15 -> x9, local copies, waits for them, and re-layouts: 1.09 us -> 4.41 us
    ppermute x6, starting transfers between devices: 18.8 us -> 21.9 us  [around(): lax.ppermute(block, axis, [(at, at ^ step) for at in range(4)])]
    ppermute x2 -> x3, waiting for transfers between devices: 2.85 us -> 5.14 us  [the longest x1 5.14 us: body(): there = lax.ppermute(here, 'za', SWAP)]
    ppermute x2 -> x3, starting transfers between devices: 7.12 us -> 8.96 us  [the longest x1 3.21 us: body(): lax.ppermute(there, 'c', SWAP)]
  transfers between devices with their start and end apart: 14 -> 15, of which waited for: 12 -> 9; matrix products, arithmetic and copies ran while one was open for 1% -> 4% of each run, Pallas kernels for 0% -> 0%
where the time goes in v10:
time: 182 us; the launch traced here: 181 us
  blocking collectives  73.9 us (41%)
  starting transfers between devices  58.6 us (32%)
  waiting for transfers between devices  22.4 us (12%)
  local copies, waits for them, and re-layouts  7.83 us (4%)
  between operations  7.7 us (4%)
  matrix products  6.21 us (3%)
  other arithmetic  4.36 us (2%)
    all_to_all x3, blocking collectives, exchange(): return lax.all_to_all(blocks, axes, split_axis=0, concat_axis=0, tiled=True)  69.4 us
    ppermute x6, starting transfers between devices, around(): lax.ppermute(block, axis, [(at, at ^ step) for at in range(4)])  21.9 us
    all_to_all x3, starting transfers between devices, exchange(): return lax.all_to_all(blocks, axes, split_axis=0, concat_axis=0, tiled=True)  15.5 us
    all_to_all x3, waiting for transfers between devices, exchange(): return lax.all_to_all(blocks, axes, split_axis=0, concat_axis=0, tiled=True)  11.8 us
    dot_general x8, matrix products, dot(): return lax.dot_general(a, b, dims, preferred_element_type=jnp.float32)  6.21 us
    ppermute x1, waiting for transfers between devices, body(): there = lax.ppermute(here, 'za', SWAP)  5.14 us
    ppermute x1, starting transfers between devices, body(): hidden_there = lax.ppermute(hidden_sent, 'c', SWAP)  4.89 us
    ppermute x1, starting transfers between devices, body(): piece_there = lax.ppermute(piece, 'c', SWAP)  4.72 us
  transfers between devices with their start and end apart: 15, of which 9 were waited for; matrix products, arithmetic and copies ran while one was open for 4% of the time, Pallas kernels for 0%

profile of v10, /device:TPU:1, one launch (start us, length us, event | category | flops | bytes accessed | tf_op | source)
XLA Modules:
  0.0 181.1 jit_solution(1261184733269847368)
XLA Ops:
  0.6 1.0 copy-done
  1.6 1.0 fusion.10
  2.6 0.9 pad_maximum_fusion.1
  3.5 32.0 %all_to_all.30 = bf16[16,8,1792]{2,1,0:T(8,128)(2,1)S(1)} all-to-all(bf16[16,8,1792]{2,1,0:T(8,128)(2,1)S(1)} %pad_maximum_fusion.1), channel_id=1, replica_groups=mesh['x'=4,'zb'=2,'za'=2,'c'=2,'zh'=2,'y'=8] {'zh','y'}, dimensions={0} | all-to-all | bytes 917504 | tf_op jit(solution)/shard_map/all_to_all | solution.py:31
  35.5 0.1 convert_reduce_fusion.1
  35.6 0.1 multiply_reduce_fusion.2
  35.7 0.1 multiply_convert_fusion.1
  35.8 0.1 fusion.13
  35.9 0.1 fusion.14
  36.1 4.9 %collective-permute-start = (bf16[128,96]{0,1:T(8,128)(2,1)S(1)}, bf16[128,96]{0,1:T(8,128)(2,1)S(1)}, u32[]{:S(2)}, u32[]{:S(2)}) collective-permute-start(bf16[128,96]{0,1:T(8,128)(2,1)S(1)} %copy-done.1), channel_id=1, source_target_pairs={{0,16},{16,0},{1,17},{17,1},{2,18},{18,2},{3,19},{19,3},{4,20},{20... | collective-permute-start | bytes 73736 | tf_op jit(solution)/shard_map/ppermute | solution.py:106
  41.0 0.9 broadcast_in_dim.37
  41.9 4.6 %all-to-all-start.1 = ((bf16[8,8,5632]{2,1,0:T(8,128)(2,1)}), bf16[8,8,5632]{2,1,0:T(8,128)(2,1)S(1)}, u32[]{:S(2)}, u32[]{:S(2)}) async-start(bf16[8,8,5632]{2,1,0:T(8,128)(2,1)} %broadcast_in_dim.37), calls=%async_computation.1 | async-start | bytes 1441792 | tf_op jit(solution)/shard_map/all_to_all | solution.py:31
  46.5 1.9 %collective-permute-start.1 = (bf16[8,5632]{1,0:T(8,128)(2,1)S(1)}, bf16[8,5632]{1,0:T(8,128)(2,1)S(1)}, u32[]{:S(2)}, u32[]{:S(2)}) collective-permute-start(bf16[8,5632]{1,0:T(8,128)(2,1)S(1)} %get-tuple-element.9), channel_id=1, source_target_pairs={{0,8},{8,0},{64,72},{72,64},{1,9},{9,1},{65,73},{73,65},{2,10},{10... | collective-permute-start | bytes 270344 | tf_op jit(solution)/shard_map/ppermute | solution.py:63
  48.5 0.6 constant_dynamic-update-slice_fusion.3
  49.1 4.2 %collective-permute-start.2 = (bf16[8,5632]{1,0:T(8,128)(2,1)S(1)}, bf16[8,5632]{1,0:T(8,128)(2,1)S(1)}, u32[]{:S(2)}, u32[]{:S(2)}) collective-permute-start(bf16[8,5632]{1,0:T(8,128)(2,1)S(1)} %get-tuple-element.9), channel_id=1, source_target_pairs={{0,64},{8,72},{64,0},{72,8},{1,65},{9,73},{65,1},{73,9},{2,66},{10... | collective-permute-start | bytes 270344 | tf_op jit(solution)/shard_map/ppermute | solution.py:63
  53.3 5.2 %collective-permute-start.3 = (bf16[8,5632]{1,0:T(8,128)(2,1)S(1)}, bf16[8,5632]{1,0:T(8,128)(2,1)S(1)}, u32[]{:S(2)}, u32[]{:S(2)}) collective-permute-start(bf16[8,5632]{1,0:T(8,128)(2,1)S(1)} %get-tuple-element.9), channel_id=1, source_target_pairs={{0,72},{8,64},{64,8},{72,0},{1,73},{9,65},{65,9},{73,1},{2,74},{10... | collective-permute-start | bytes 270344 | tf_op jit(solution)/shard_map/ppermute | solution.py:63
  58.6 0.7 constant_dynamic-update-slice_fusion.2
  59.2 0.4 collective-permute-done.2
  59.6 0.6 constant_dynamic-update-slice_fusion.1
  60.2 2.0 %collective-permute-done.3 = bf16[8,5632]{1,0:T(8,128)(2,1)S(1)} collective-permute-done((bf16[8,5632]{1,0:T(8,128)(2,1)S(1)}, bf16[8,5632]{1,0:T(8,128)(2,1)S(1)}, u32[]{:S(2)}, u32[]{:S(2)}) %collective-permute-start.3) | collective-permute-done | bytes 90144 | tf_op jit(solution)/shard_map/ppermute | solution.py:63
  62.3 0.7 constant_dynamic-update-slice_fusion
  62.9 3.1 %collective-permute-start.4 = (bf16[32,5632]{1,0:T(8,128)(2,1)S(1)}, bf16[32,5632]{1,0:T(8,128)(2,1)S(1)}, u32[]{:S(2)}, u32[]{:S(2)}) collective-permute-start(bf16[32,5632]{1,0:T(8,128)(2,1)S(1)} %get-tuple-element.16), channel_id=1, source_target_pairs={{0,128},{128,0},{256,384},{384,256},{1,129},{129,1},{257,385},{385... | collective-permute-start | bytes 1081352 | tf_op jit(solution)/shard_map/ppermute | solution.py:63
  66.0 2.7 %all-to-all-done.1 = bf16[8,8,5632]{2,1,0:T(8,128)(2,1)S(1)} async-done(((bf16[8,8,5632]{2,1,0:T(8,128)(2,1)}), bf16[8,8,5632]{2,1,0:T(8,128)(2,1)S(1)}, u32[]{:S(2)}, u32[]{:S(2)}) %all-to-all-start.1) | async-done | bytes 720928 | tf_op jit(solution)/shard_map/all_to_all | solution.py:31
  68.7 2.5 %collective-permute-start.8 = (bf16[64,5632]{1,0:T(8,128)(2,1)S(1)}, bf16[64,5632]{1,0:T(8,128)(2,1)S(1)}, u32[]{:S(2)}, u32[]{:S(2)}) collective-permute-start(bf16[64,5632]{1,0:T(8,128)(2,1)S(1)} %bitcast.32), channel_id=1, source_target_pairs={{0,32},{32,0},{1,33},{33,1},{2,34},{34,2},{3,35},{35,3},{4,36},{36... | collective-permute-start | bytes 2162696 | tf_op jit(solution)/shard_map/ppermute | solution.py:109
  71.3 4.7 %collective-permute-start.5 = (bf16[32,5632]{1,0:T(8,128)(2,1)S(1)}, bf16[32,5632]{1,0:T(8,128)(2,1)S(1)}, u32[]{:S(2)}, u32[]{:S(2)}) collective-permute-start(bf16[32,5632]{1,0:T(8,128)(2,1)S(1)} %get-tuple-element.16), channel_id=1, source_target_pairs={{0,256},{128,384},{256,0},{384,128},{1,257},{129,385},{257,1},{385... | collective-permute-start | bytes 1081352 | tf_op jit(solution)/shard_map/ppermute | solution.py:63
  76.0 2.8 %collective-permute-start.6 = (bf16[32,5632]{1,0:T(8,128)(2,1)S(1)}, bf16[32,5632]{1,0:T(8,128)(2,1)S(1)}, u32[]{:S(2)}, u32[]{:S(2)}) collective-permute-start(bf16[32,5632]{1,0:T(8,128)(2,1)S(1)} %get-tuple-element.16), channel_id=1, source_target_pairs={{0,384},{128,256},{256,128},{384,0},{1,385},{129,257},{257,129},{3... | collective-permute-start | bytes 1081352 | tf_op jit(solution)/shard_map/ppermute | solution.py:63
  78.7 0.8 constant_dynamic-update-slice_fusion.6
  79.5 3.2 %collective-permute-start.7 = (bf16[64,5632]{1,0:T(8,128)(2,1)S(1)}, bf16[64,5632]{1,0:T(8,128)(2,1)S(1)}, u32[]{:S(2)}, u32[]{:S(2)}) collective-permute-start(bf16[64,5632]{1,0:T(8,128)(2,1)S(1)} %bitcast.33), channel_id=1, source_target_pairs={{0,16},{16,0},{1,17},{17,1},{2,18},{18,2},{3,19},{19,3},{4,20},{20... | collective-permute-start | bytes 2162696 | tf_op jit(solution)/shard_map/ppermute | solution.py:111
  82.7 5.1 %collective-permute-done.8 = bf16[64,5632]{1,0:T(8,128)(2,1)S(1)} collective-permute-done((bf16[64,5632]{1,0:T(8,128)(2,1)S(1)}, bf16[64,5632]{1,0:T(8,128)(2,1)S(1)}, u32[]{:S(2)}, u32[]{:S(2)}) %collective-permute-start.8) | collective-permute-done | bytes 720928 | tf_op jit(solution)/shard_map/ppermute | solution.py:109
  87.9 3.2 %collective-permute-start.9 = (bf16[64,5632]{1,0:T(8,128)(2,1)S(1)}, bf16[64,5632]{1,0:T(8,128)(2,1)S(1)}, u32[]{:S(2)}, u32[]{:S(2)}) collective-permute-start(bf16[64,5632]{1,0:T(8,128)(2,1)S(1)} %collective-permute-done.8), channel_id=1, source_target_pairs={{0,16},{16,0},{1,17},{17,1},{2,18},{18,2},{3,19},{19,3},{4,20},{20... | collective-permute-start | bytes 2162696 | tf_op jit(solution)/shard_map/ppermute | solution.py:111
  91.1 0.7 constant_dynamic-update-slice_fusion.5
  91.8 1.0 collective-permute-done.6
  92.8 0.8 constant_dynamic-update-slice_fusion.4
  93.6 2.4 %fusion = f32[128,256]{1,0:T(8,128)S(1)} fusion(bf16[128,5632]{1,0:T(8,128)(2,1)} %constant_dynamic-update-slice_fusion.4, bf16[64,5632]{1,0:T(8,128)(2,1)S(1)} %collective-permute-done.9, bf16[64,5632]{1,0:T(8,128)(2,1)S(1)} %collective-permute-done.8, bf16[64,5632]{1,0:T(8,128)(2,1)S(1)} %collective-permute-done.7, bf16[64,5632]{1,0:T(8,128)(2,1)S(1)} %bitcast.34), kind=kOutput, calls=%fused_computation | convolution fusion | flops 380633088 | bytes 4456448 | tf_op jit(solution)/shard_map/dot_general | solution.py:20
  96.0 0.6 multiply_reduce_fusion
  96.7 0.1 pad_maximum_fusion
  96.8 0.3 fusion.27
  97.0 0.3 fusion.28
  97.3 1.0 fusion.11
  98.3 5.9 %all-to-all-start.2 = ((bf16[16,8,1536]{2,1,0:T(8,128)(2,1)}), bf16[16,8,1536]{2,1,0:T(8,128)(2,1)S(1)}, u32[]{:S(2)}, u32[]{:S(2)}) async-start(bf16[16,8,1536]{2,1,0:T(8,128)(2,1)} %fusion.11), calls=%async_computation.2 | async-start | bytes 786432 | tf_op jit(solution)/shard_map/all_to_all | solution.py:31
  104.2 2.7 %collective-permute-start.10 = (f32[]{:T(128)}, f32[]{:T(128)}, u32[]{:S(2)}, u32[]{:S(2)}) collective-permute-start(f32[]{:T(128)} %get-tuple-element.11), channel_id=1, source_target_pairs={{0,16},{16,0},{1,17},{17,1},{2,18},{18,2},{3,19},{19,3},{4,20},{20... | collective-permute-start | bytes 20 | tf_op jit(solution)/shard_map/ppermute | solution.py:118
  106.9 1.1 collective-permute-done.10
  112.9 3.7 %all-to-all-done.2 = bf16[16,8,1536]{2,1,0:T(8,128)(2,1)S(1)} async-done(((bf16[16,8,1536]{2,1,0:T(8,128)(2,1)}), bf16[16,8,1536]{2,1,0:T(8,128)(2,1)S(1)}, u32[]{:S(2)}, u32[]{:S(2)}) %all-to-all-start.2) | async-done | bytes 393248 | tf_op jit(solution)/shard_map/all_to_all | solution.py:31
  116.6 0.1 convert_reduce_fusion
  116.7 0.2 multiply_reduce_fusion.1
  116.9 0.1 multiply_convert_fusion
  117.0 22.8 %all_to_all.31 = bf16[16,8,1664]{2,1,0:T(8,128)(2,1)S(1)} all-to-all(bf16[16,8,1664]{2,1,0:T(8,128)(2,1)S(1)} %broadcast_in_dim.42), channel_id=1, replica_groups=mesh['x'=4,'zb'=2,'za'=2,'c'=2,'zh'=2,'y'=8] {'zh','y'}, dimensions={0} | all-to-all | bytes 851968 | tf_op jit(solution)/shard_map/all_to_all | solution.py:31
  139.8 4.7 %collective-permute-start.11 = (bf16[128,1536]{1,0:T(8,128)(2,1)S(1)}, bf16[128,1536]{1,0:T(8,128)(2,1)S(1)}, u32[]{:S(2)}, u32[]{:S(2)}) collective-permute-start(bf16[128,1536]{1,0:T(8,128)(2,1)S(1)} %slice.31), channel_id=1, source_target_pairs={{0,16},{16,0},{1,17},{17,1},{2,18},{18,2},{3,19},{19,3},{4,20},{20... | collective-permute-start | bytes 1179656 | tf_op jit(solution)/shard_map/ppermute | solution.py:129
  144.6 0.2 fusion.17
  144.8 1.1 collective-permute-done.11
  145.9 0.2 fusion.12
  146.0 0.1 reshape.60
  146.1 0.1 broadcast_in_dim.43
  146.2 0.2 pad_maximum_fusion.2
  146.4 14.6 %all_to_all.32 = bf16[16,4,1536]{2,1,0:T(4,128)(2,1)S(1)} all-to-all(bf16[16,4,1536]{2,1,0:T(4,128)(2,1)S(1)} %pad_maximum_fusion.2), channel_id=1, replica_groups=mesh['x'=4,'zb'=2,'za'=2,'c'=2,'zh'=2,'y'=8] {'x','zb','za'}, dimensions={0} | all-to-all | bytes 393216 | tf_op jit(solution)/shard_map/all_to_all | solution.py:31
  161.1 0.1 convert_reduce_fusion.2
  161.2 0.7 broadcast_in_dim.44
  161.9 5.0 %all-to-all-start.5 = ((bf16[16,3,1536]{2,1,0:T(4,128)(2,1)}), bf16[16,3,1536]{2,1,0:T(4,128)(2,1)S(1)}, u32[]{:S(2)}, u32[]{:S(2)}) async-start(bf16[16,3,1536]{2,1,0:T(4,128)(2,1)} %broadcast_in_dim.44), calls=%async_computation.5 | async-start | bytes 393216 | tf_op jit(solution)/shard_map/all_to_all | solution.py:31
  166.9 0.9 fusion.25
  167.8 0.6 slice_reduce_fusion.1
  169.0 5.4 %all-to-all-done.5 = bf16[16,3,1536]{2,1,0:T(4,128)(2,1)S(1)} async-done(((bf16[16,3,1536]{2,1,0:T(4,128)(2,1)}), bf16[16,3,1536]{2,1,0:T(4,128)(2,1)S(1)}, u32[]{:S(2)}, u32[]{:S(2)}) %all-to-all-start.5) | async-done | bytes 147488 | tf_op jit(solution)/shard_map/all_to_all | solution.py:31
  174.4 0.1 reshape.61
  174.5 4.6 %all_gather.3 = bf16[96,1536]{1,0:T(8,128)(2,1)S(1)} all-gather(bf16[48,1536]{1,0:T(8,128)(2,1)S(1)} %reshape.61), channel_id=1, replica_groups=mesh['x'=4,'zb'=2,'za'=2,'c'=2,'zh'=2,'y'=8] {'c'}, dimensions={0}, use_global_device_ids=true | all-gather | bytes 442368 | tf_op jit(solution)/shard_map/all_gather | solution.py:150
  179.1 0.9 convert_element_type.72
  (26 shorter events, 0.3 us)
Async XLA Ops:
  0.6 1.0 copy-start
  2.6 33.4 %copy-start.1 = (bf16[128,96]{0,1:T(8,128)(2,1)S(1)}, bf16[128,96]{0,1:T(8,128)(2,1)}, u32[]{:S(2)}) copy-start(bf16[128,96]{0,1:T(8,128)(2,1)} %param.3) | copy-start | bytes 73732
  36.1 10.5 %collective-permute-start = (bf16[128,96]{0,1:T(8,128)(2,1)S(1)}, bf16[128,96]{0,1:T(8,128)(2,1)S(1)}, u32[]{:S(2)}, u32[]{:S(2)}) collective-permute-start(bf16[128,96]{0,1:T(8,128)(2,1)S(1)} %copy-done.1), channel_id=1, source_target_pairs={{0,16},{16,0},{1,17},{17,1},{2,18},{18,2},{3,19},{19,3},{4,20},{20... | collective-permute-start | bytes 73736 | tf_op jit(solution)/shard_map/ppermute | solution.py:106
  41.9 26.8 %all-to-all-start.1 = ((bf16[8,8,5632]{2,1,0:T(8,128)(2,1)}), bf16[8,8,5632]{2,1,0:T(8,128)(2,1)S(1)}, u32[]{:S(2)}, u32[]{:S(2)}) async-start(bf16[8,8,5632]{2,1,0:T(8,128)(2,1)} %broadcast_in_dim.37), calls=%async_computation.1 | async-start | bytes 1441792 | tf_op jit(solution)/shard_map/all_to_all | solution.py:31
  46.5 12.0 %collective-permute-start.1 = (bf16[8,5632]{1,0:T(8,128)(2,1)S(1)}, bf16[8,5632]{1,0:T(8,128)(2,1)S(1)}, u32[]{:S(2)}, u32[]{:S(2)}) collective-permute-start(bf16[8,5632]{1,0:T(8,128)(2,1)S(1)} %get-tuple-element.9), channel_id=1, source_target_pairs={{0,8},{8,0},{64,72},{72,64},{1,9},{9,1},{65,73},{73,65},{2,10},{10... | collective-permute-start | bytes 270344 | tf_op jit(solution)/shard_map/ppermute | solution.py:63
  49.1 10.5 %collective-permute-start.2 = (bf16[8,5632]{1,0:T(8,128)(2,1)S(1)}, bf16[8,5632]{1,0:T(8,128)(2,1)S(1)}, u32[]{:S(2)}, u32[]{:S(2)}) collective-permute-start(bf16[8,5632]{1,0:T(8,128)(2,1)S(1)} %get-tuple-element.9), channel_id=1, source_target_pairs={{0,64},{8,72},{64,0},{72,8},{1,65},{9,73},{65,1},{73,9},{2,66},{10... | collective-permute-start | bytes 270344 | tf_op jit(solution)/shard_map/ppermute | solution.py:63
  53.3 8.9 %collective-permute-start.3 = (bf16[8,5632]{1,0:T(8,128)(2,1)S(1)}, bf16[8,5632]{1,0:T(8,128)(2,1)S(1)}, u32[]{:S(2)}, u32[]{:S(2)}) collective-permute-start(bf16[8,5632]{1,0:T(8,128)(2,1)S(1)} %get-tuple-element.9), channel_id=1, source_target_pairs={{0,72},{8,64},{64,8},{72,0},{1,73},{9,65},{65,9},{73,1},{2,74},{10... | collective-permute-start | bytes 270344 | tf_op jit(solution)/shard_map/ppermute | solution.py:63
  62.9 15.8 %collective-permute-start.4 = (bf16[32,5632]{1,0:T(8,128)(2,1)S(1)}, bf16[32,5632]{1,0:T(8,128)(2,1)S(1)}, u32[]{:S(2)}, u32[]{:S(2)}) collective-permute-start(bf16[32,5632]{1,0:T(8,128)(2,1)S(1)} %get-tuple-element.16), channel_id=1, source_target_pairs={{0,128},{128,0},{256,384},{384,256},{1,129},{129,1},{257,385},{385... | collective-permute-start | bytes 1081352 | tf_op jit(solution)/shard_map/ppermute | solution.py:63
  68.7 19.1 %collective-permute-start.8 = (bf16[64,5632]{1,0:T(8,128)(2,1)S(1)}, bf16[64,5632]{1,0:T(8,128)(2,1)S(1)}, u32[]{:S(2)}, u32[]{:S(2)}) collective-permute-start(bf16[64,5632]{1,0:T(8,128)(2,1)S(1)} %bitcast.32), channel_id=1, source_target_pairs={{0,32},{32,0},{1,33},{33,1},{2,34},{34,2},{3,35},{35,3},{4,36},{36... | collective-permute-start | bytes 2162696 | tf_op jit(solution)/shard_map/ppermute | solution.py:109
  71.3 19.8 %collective-permute-start.5 = (bf16[32,5632]{1,0:T(8,128)(2,1)S(1)}, bf16[32,5632]{1,0:T(8,128)(2,1)S(1)}, u32[]{:S(2)}, u32[]{:S(2)}) collective-permute-start(bf16[32,5632]{1,0:T(8,128)(2,1)S(1)} %get-tuple-element.16), channel_id=1, source_target_pairs={{0,256},{128,384},{256,0},{384,128},{1,257},{129,385},{257,1},{385... | collective-permute-start | bytes 1081352 | tf_op jit(solution)/shard_map/ppermute | solution.py:63
  76.0 16.8 %collective-permute-start.6 = (bf16[32,5632]{1,0:T(8,128)(2,1)S(1)}, bf16[32,5632]{1,0:T(8,128)(2,1)S(1)}, u32[]{:S(2)}, u32[]{:S(2)}) collective-permute-start(bf16[32,5632]{1,0:T(8,128)(2,1)S(1)} %get-tuple-element.16), channel_id=1, source_target_pairs={{0,384},{128,256},{256,128},{384,0},{1,385},{129,257},{257,129},{3... | collective-permute-start | bytes 1081352 | tf_op jit(solution)/shard_map/ppermute | solution.py:63
  79.5 14.0 %collective-permute-start.7 = (bf16[64,5632]{1,0:T(8,128)(2,1)S(1)}, bf16[64,5632]{1,0:T(8,128)(2,1)S(1)}, u32[]{:S(2)}, u32[]{:S(2)}) collective-permute-start(bf16[64,5632]{1,0:T(8,128)(2,1)S(1)} %bitcast.33), channel_id=1, source_target_pairs={{0,16},{16,0},{1,17},{17,1},{2,18},{18,2},{3,19},{19,3},{4,20},{20... | collective-permute-start | bytes 2162696 | tf_op jit(solution)/shard_map/ppermute | solution.py:111
  87.9 5.7 %collective-permute-start.9 = (bf16[64,5632]{1,0:T(8,128)(2,1)S(1)}, bf16[64,5632]{1,0:T(8,128)(2,1)S(1)}, u32[]{:S(2)}, u32[]{:S(2)}) collective-permute-start(bf16[64,5632]{1,0:T(8,128)(2,1)S(1)} %collective-permute-done.8), channel_id=1, source_target_pairs={{0,16},{16,0},{1,17},{17,1},{2,18},{18,2},{3,19},{19,3},{4,20},{20... | collective-permute-start | bytes 2162696 | tf_op jit(solution)/shard_map/ppermute | solution.py:111
  98.3 18.3 %all-to-all-start.2 = ((bf16[16,8,1536]{2,1,0:T(8,128)(2,1)}), bf16[16,8,1536]{2,1,0:T(8,128)(2,1)S(1)}, u32[]{:S(2)}, u32[]{:S(2)}) async-start(bf16[16,8,1536]{2,1,0:T(8,128)(2,1)} %fusion.11), calls=%async_computation.2 | async-start | bytes 786432 | tf_op jit(solution)/shard_map/all_to_all | solution.py:31
  104.2 3.7 %collective-permute-start.10 = (f32[]{:T(128)}, f32[]{:T(128)}, u32[]{:S(2)}, u32[]{:S(2)}) collective-permute-start(f32[]{:T(128)} %get-tuple-element.11), channel_id=1, source_target_pairs={{0,16},{16,0},{1,17},{17,1},{2,18},{18,2},{3,19},{19,3},{4,20},{20... | collective-permute-start | bytes 20 | tf_op jit(solution)/shard_map/ppermute | solution.py:118
  139.8 6.1 %collective-permute-start.11 = (bf16[128,1536]{1,0:T(8,128)(2,1)S(1)}, bf16[128,1536]{1,0:T(8,128)(2,1)S(1)}, u32[]{:S(2)}, u32[]{:S(2)}) collective-permute-start(bf16[128,1536]{1,0:T(8,128)(2,1)S(1)} %slice.31), channel_id=1, source_target_pairs={{0,16},{16,0},{1,17},{17,1},{2,18},{18,2},{3,19},{19,3},{4,20},{20... | collective-permute-start | bytes 1179656 | tf_op jit(solution)/shard_map/ppermute | solution.py:129
  161.9 12.5 %all-to-all-start.5 = ((bf16[16,3,1536]{2,1,0:T(4,128)(2,1)}), bf16[16,3,1536]{2,1,0:T(4,128)(2,1)S(1)}, u32[]{:S(2)}, u32[]{:S(2)}) async-start(bf16[16,3,1536]{2,1,0:T(4,128)(2,1)} %broadcast_in_dim.44), calls=%async_computation.5 | async-start | bytes 393216 | tf_op jit(solution)/shard_map/all_to_all | solution.py:31

commit v11 on v10

--- a/solution.py
+++ b/solution.py
@@ -66,10 +66,9 @@
 
 def in_order(values):
     shape = values.shape
-    values = values.reshape(2, 2, 2, 2, -1, shape[1])
-    for dim, (axis, bit) in enumerate((("x", 2), ("x", 1), ("zb", 1), ("zh", 1))):
-        swap = (lax.axis_index(axis) & bit) != 0
-        values = jnp.where(swap, jnp.flip(values, dim), values)
+    values = values.reshape(SIZES["x"], 2, 2, -1, shape[1])
+    for dim, axis in ((1, "zb"), (2, "zh")):
+        values = jnp.where(lax.axis_index(axis) != 0, jnp.flip(values, dim), values)
     return values.reshape(shape)
 
 
@@ -105,7 +104,8 @@
     here = here.reshape(-1, here.shape[2])
     hidden_there = lax.ppermute(hidden_sent, "c", SWAP)
     mine_rows, hidden_there = lax.optimization_barrier((mine_rows, hidden_there))
-    row_block = around(around(mine_rows, STRIDE), "x")
+    near, here = lax.optimization_barrier((around(mine_rows, STRIDE), here))
+    row_block = gather(near, ("x",)).reshape(rows, -1)
     there = lax.ppermute(here, "za", SWAP)
     columns = jnp.concatenate(
         [here, lax.ppermute(here, "c", SWAP), there, lax.ppermute(there, "c", SWAP)],

time: 182 us -> 183 us (level)
  waiting for transfers between devices: 22.4 us -> 27.4 us
  starting transfers between devices: 58.6 us -> 56.2 us
    ppermute x6 -> x3, starting transfers between devices: 21.9 us -> 11.4 us  [around(): lax.ppermute(block, axis, [(at, at ^ step) for at in range(4)])]
    all_to_all x3 -> x4, waiting for transfers between devices: 11.8 us -> 18.7 us  [exchange(): return lax.all_to_all(blocks, axes, split_axis=0, concat_axis=0, tiled=True)]
    all_to_all x3 -> x4, starting transfers between devices: 15.5 us -> 21 us  [exchange(): return lax.all_to_all(blocks, axes, split_axis=0, concat_axis=0, tiled=True)]
    ppermute x1, starting transfers between devices: 3.21 us -> 5.09 us  [body(): lax.ppermute(there, 'c', SWAP)]
    unnamed x9 -> x7, local copies, waits for them, and re-layouts: 4.41 us -> 4.43 us
  transfers between devices with their start and end apart: 15 -> 13, of which waited for: 9 -> 9; matrix products, arithmetic and copies ran while one was open for 4% -> 4% of each run, Pallas kernels for 0% -> 0%
where the time goes in v11:
time: 183 us; the launch traced here: 182 us
  blocking collectives  72.8 us (40%)
  starting transfers between devices  56.2 us (31%)
  waiting for transfers between devices  27.4 us (15%)
  between operations  7.72 us (4%)
  local copies, waits for them, and re-layouts  7.66 us (4%)
  matrix products  6.24 us (3%)
  other arithmetic  4.29 us (2%)
    all_to_all x3, blocking collectives, exchange(): return lax.all_to_all(blocks, axes, split_axis=0, concat_axis=0, tiled=True)  68.2 us
    all_to_all x4, starting transfers between devices, exchange(): return lax.all_to_all(blocks, axes, split_axis=0, concat_axis=0, tiled=True)  21 us
    all_to_all x4, waiting for transfers between devices, exchange(): return lax.all_to_all(blocks, axes, split_axis=0, concat_axis=0, tiled=True)  18.7 us
    ppermute x3, starting transfers between devices, around(): lax.ppermute(block, axis, [(at, at ^ step) for at in range(4)])  11.4 us
    dot_general x8, matrix products, dot(): return lax.dot_general(a, b, dims, preferred_element_type=jnp.float32)  6.24 us
    ppermute x1, starting transfers between devices, body(): lax.ppermute(there, 'c', SWAP)  5.09 us
    all_gather x1, blocking collectives, body(): lax.all_gather(gather(summed, XZ).reshape(half, full), 'c', axis=0, tiled...  4.55 us
    ppermute x1, starting transfers between devices, body(): piece_there = lax.ppermute(piece, 'c', SWAP)  4.53 us
  transfers between devices with their start and end apart: 13, of which 9 were waited for; matrix products, arithmetic and copies ran while one was open for 4% of the time, Pallas kernels for 0%

profile of v11, /device:TPU:1, one launch (start us, length us, event | category | flops | bytes accessed | tf_op | source)
XLA Modules:
  0.0 182.3 jit_solution(14573605982442012842)
XLA Ops:
  0.6 0.0 copy-start
  0.6 0.0 copy-start.1
  0.7 0.9 copy-done
  1.6 1.0 fusion.4
  2.6 0.9 pad_maximum_fusion
  3.5 32.0 %all_to_all.35 = bf16[16,8,1792]{2,1,0:T(8,128)(2,1)S(1)} all-to-all(bf16[16,8,1792]{2,1,0:T(8,128)(2,1)S(1)} %pad_maximum_fusion), channel_id=1, replica_groups=mesh['x'=4,'zb'=2,'za'=2,'c'=2,'zh'=2,'y'=8] {'zh','y'}, dimensions={0} | all-to-all | bytes 917504 | tf_op jit(solution)/shard_map/all_to_all | solution.py:31
  35.5 0.1 convert_reduce_fusion.1
  35.5 0.1 multiply_reduce_fusion.2
  35.7 0.1 multiply_convert_fusion.1
  35.8 0.1 fusion.12
  35.9 0.1 fusion.13
  36.0 0.9 broadcast_in_dim.22
  37.0 5.8 %all-to-all-start.1 = ((bf16[8,8,5632]{2,1,0:T(8,128)(2,1)}), bf16[8,8,5632]{2,1,0:T(8,128)(2,1)}, u32[]{:S(2)}, u32[]{:S(2)}) async-start(bf16[8,8,5632]{2,1,0:T(8,128)(2,1)} %broadcast_in_dim.22), calls=%async_computation.1 | async-start | bytes 1441792 | tf_op jit(solution)/shard_map/all_to_all | solution.py:31
  42.8 4.0 %collective-permute-start = (bf16[128,96]{0,1:T(8,128)(2,1)S(1)}, bf16[128,96]{0,1:T(8,128)(2,1)S(1)}, u32[]{:S(2)}, u32[]{:S(2)}) collective-permute-start(bf16[128,96]{0,1:T(8,128)(2,1)S(1)} %copy-done.1), channel_id=1, source_target_pairs={{0,16},{16,0},{1,17},{17,1},{2,18},{18,2},{3,19},{19,3},{4,20},{20... | collective-permute-start | bytes 73736 | tf_op jit(solution)/shard_map/ppermute | solution.py:105
  46.8 0.8 collective-permute-done
  47.6 1.9 %collective-permute-start.1 = (bf16[8,5632]{1,0:T(8,128)(2,1)S(1)}, bf16[8,5632]{1,0:T(8,128)(2,1)S(1)}, u32[]{:S(2)}, u32[]{:S(2)}) collective-permute-start(bf16[8,5632]{1,0:T(8,128)(2,1)S(1)} %get-tuple-element.11), channel_id=1, source_target_pairs={{0,8},{8,0},{64,72},{72,64},{1,9},{9,1},{65,73},{73,65},{2,10},{10... | collective-permute-start | bytes 270344 | tf_op jit(solution)/shard_map/ppermute | solution.py:63
  49.5 4.2 %collective-permute-start.2 = (bf16[8,5632]{1,0:T(8,128)(2,1)S(1)}, bf16[8,5632]{1,0:T(8,128)(2,1)S(1)}, u32[]{:S(2)}, u32[]{:S(2)}) collective-permute-start(bf16[8,5632]{1,0:T(8,128)(2,1)S(1)} %get-tuple-element.11), channel_id=1, source_target_pairs={{0,64},{8,72},{64,0},{72,8},{1,65},{9,73},{65,1},{73,9},{2,66},{10... | collective-permute-start | bytes 270344 | tf_op jit(solution)/shard_map/ppermute | solution.py:63
  53.8 5.2 %collective-permute-start.3 = (bf16[8,5632]{1,0:T(8,128)(2,1)S(1)}, bf16[8,5632]{1,0:T(8,128)(2,1)S(1)}, u32[]{:S(2)}, u32[]{:S(2)}) collective-permute-start(bf16[8,5632]{1,0:T(8,128)(2,1)S(1)} %get-tuple-element.11), channel_id=1, source_target_pairs={{0,72},{8,64},{64,8},{72,0},{1,73},{9,65},{65,9},{73,1},{2,74},{10... | collective-permute-start | bytes 270344 | tf_op jit(solution)/shard_map/ppermute | solution.py:63
  59.0 0.0 collective-permute-done.1
  59.0 2.3 %collective-permute-done.2 = bf16[8,5632]{1,0:T(8,128)(2,1)S(1)} collective-permute-done((bf16[8,5632]{1,0:T(8,128)(2,1)S(1)}, bf16[8,5632]{1,0:T(8,128)(2,1)S(1)}, u32[]{:S(2)}, u32[]{:S(2)}) %collective-permute-start.2) | collective-permute-done | bytes 90144 | tf_op jit(solution)/shard_map/ppermute | solution.py:63
  61.3 0.0 collective-permute-done.3
  61.3 2.0 %all-to-all-done.1 = bf16[8,8,5632]{2,1,0:T(8,128)(2,1)} async-done(((bf16[8,8,5632]{2,1,0:T(8,128)(2,1)}), bf16[8,8,5632]{2,1,0:T(8,128)(2,1)}, u32[]{:S(2)}, u32[]{:S(2)}) %all-to-all-start.1) | async-done | bytes 720928 | tf_op jit(solution)/shard_map/all_to_all | solution.py:31
  63.3 3.1 %collective-permute-start.5 = (bf16[64,5632]{1,0:T(8,128)(2,1)}, bf16[64,5632]{1,0:T(8,128)(2,1)}, u32[]{:S(2)}, u32[]{:S(2)}) collective-permute-start(bf16[64,5632]{1,0:T(8,128)(2,1)} %bitcast.5), channel_id=1, source_target_pairs={{0,32},{32,0},{1,33},{33,1},{2,34},{34,2},{3,35},{35,3},{4,36},{36... | collective-permute-start | bytes 2162696 | tf_op jit(solution)/shard_map/ppermute | solution.py:109
  66.4 4.1 %collective-permute-start.4 = (bf16[64,5632]{1,0:T(8,128)(2,1)}, bf16[64,5632]{1,0:T(8,128)(2,1)}, u32[]{:S(2)}, u32[]{:S(2)}) collective-permute-start(bf16[64,5632]{1,0:T(8,128)(2,1)} %bitcast.5), channel_id=1, source_target_pairs={{0,16},{16,0},{1,17},{17,1},{2,18},{18,2},{3,19},{19,3},{4,20},{20... | collective-permute-start | bytes 2162696 | tf_op jit(solution)/shard_map/ppermute | solution.py:111
  70.5 1.2 broadcast_in_dim.44
  71.8 4.3 %all-to-all-start.2 = ((bf16[4,32,5632]{2,1,0:T(8,128)(2,1)}), bf16[4,32,5632]{2,1,0:T(8,128)(2,1)}, u32[]{:S(2)}, u32[]{:S(2)}) async-start(bf16[4,32,5632]{2,1,0:T(8,128)(2,1)} %broadcast_in_dim.44), calls=%async_computation.2 | async-start | bytes 2883584 | tf_op jit(solution)/shard_map/all_to_all | solution.py:31
  76.1 1.2 constant_dynamic-update-slice_fusion.3
  77.2 3.6 %collective-permute-done.5 = bf16[64,5632]{1,0:T(8,128)(2,1)} collective-permute-done((bf16[64,5632]{1,0:T(8,128)(2,1)}, bf16[64,5632]{1,0:T(8,128)(2,1)}, u32[]{:S(2)}, u32[]{:S(2)}) %collective-permute-start.5) | collective-permute-done | bytes 720928 | tf_op jit(solution)/shard_map/ppermute | solution.py:109
  80.8 5.1 %collective-permute-start.6 = (bf16[64,5632]{1,0:T(8,128)(2,1)}, bf16[64,5632]{1,0:T(8,128)(2,1)S(1)}, u32[]{:S(2)}, u32[]{:S(2)}) collective-permute-start(bf16[64,5632]{1,0:T(8,128)(2,1)} %collective-permute-done.5), channel_id=1, source_target_pairs={{0,16},{16,0},{1,17},{17,1},{2,18},{18,2},{3,19},{19,3},{4,20},{20... | collective-permute-start | bytes 2162696 | tf_op jit(solution)/shard_map/ppermute | solution.py:111
  85.9 0.0 collective-permute-done.4
  86.0 1.2 constant_dynamic-update-slice_fusion.2
  87.1 1.2 constant_dynamic-update-slice_fusion.1
  88.3 0.0 collective-permute-done.6
  88.3 7.3 %all-to-all-done.2 = bf16[4,32,5632]{2,1,0:T(8,128)(2,1)} async-done(((bf16[4,32,5632]{2,1,0:T(8,128)(2,1)}), bf16[4,32,5632]{2,1,0:T(8,128)(2,1)}, u32[]{:S(2)}, u32[]{:S(2)}) %all-to-all-start.2) | async-done | bytes 1441824 | tf_op jit(solution)/shard_map/all_to_all | solution.py:31
  95.6 2.4 %fusion = f32[4,2,2,8,256]{4,3,2,1,0:T(8,128)S(1)} fusion(bf16[4,2,2,8,5632]{4,3,2,1,0:T(8,128)(2,1)} %bitcast.6, bf16[256,5632]{1,0:T(8,128)(2,1)S(1)} %constant_dynamic-update-slice_fusion), kind=kOutput, calls=%fused_computation | convolution fusion | flops 369098752 | bytes 4456448 | tf_op jit(solution)/shard_map/dot_general | solution.py:20
  98.0 0.6 multiply_reduce_fusion
  98.7 0.3 fusion.9
  99.0 0.3 fusion.7
  99.3 1.0 fusion.5
  100.3 6.0 %all-to-all-start.3 = ((bf16[16,8,1536]{2,1,0:T(8,128)(2,1)}), bf16[16,8,1536]{2,1,0:T(8,128)(2,1)S(1)}, u32[]{:S(2)}, u32[]{:S(2)}) async-start(bf16[16,8,1536]{2,1,0:T(8,128)(2,1)} %fusion.5), calls=%async_computation.3 | async-start | bytes 786432 | tf_op jit(solution)/shard_map/all_to_all | solution.py:31
  106.3 3.0 %collective-permute-start.7 = (f32[]{:T(128)}, f32[]{:T(128)}, u32[]{:S(2)}, u32[]{:S(2)}) collective-permute-start(f32[]{:T(128)} %get-tuple-element.15), channel_id=1, source_target_pairs={{0,16},{16,0},{1,17},{17,1},{2,18},{18,2},{3,19},{19,3},{4,20},{20... | collective-permute-start | bytes 20 | tf_op jit(solution)/shard_map/ppermute | solution.py:118
  109.4 0.9 collective-permute-done.7
  115.3 4.1 %all-to-all-done.3 = bf16[16,8,1536]{2,1,0:T(8,128)(2,1)S(1)} async-done(((bf16[16,8,1536]{2,1,0:T(8,128)(2,1)}), bf16[16,8,1536]{2,1,0:T(8,128)(2,1)S(1)}, u32[]{:S(2)}, u32[]{:S(2)}) %all-to-all-start.3) | async-done | bytes 393248 | tf_op jit(solution)/shard_map/all_to_all | solution.py:31
  119.4 0.1 convert_reduce_fusion
  119.5 0.2 multiply_reduce_fusion.1
  119.6 0.1 multiply_convert_fusion
  119.8 26.0 %all_to_all.36 = bf16[16,8,1664]{2,1,0:T(8,128)(2,1)S(1)} all-to-all(bf16[16,8,1664]{2,1,0:T(8,128)(2,1)S(1)} %broadcast_in_dim.49), channel_id=1, replica_groups=mesh['x'=4,'zb'=2,'za'=2,'c'=2,'zh'=2,'y'=8] {'zh','y'}, dimensions={0} | all-to-all | bytes 851968 | tf_op jit(solution)/shard_map/all_to_all | solution.py:31
  145.8 4.5 %collective-permute-start.8 = (bf16[128,1536]{1,0:T(8,128)(2,1)S(1)}, bf16[128,1536]{1,0:T(8,128)(2,1)S(1)}, u32[]{:S(2)}, u32[]{:S(2)}) collective-permute-start(bf16[128,1536]{1,0:T(8,128)(2,1)S(1)} %slice.32), channel_id=1, source_target_pairs={{0,16},{16,0},{1,17},{17,1},{2,18},{18,2},{3,19},{19,3},{4,20},{20... | collective-permute-start | bytes 1179656 | tf_op jit(solution)/shard_map/ppermute | solution.py:129
  150.4 0.2 fusion.16
  150.6 1.1 collective-permute-done.8
  151.7 0.2 fusion.6
  151.8 0.1 reshape.61
  151.9 0.1 broadcast_in_dim.50
  152.0 0.2 pad_maximum_fusion.2
  152.2 10.3 %all_to_all.37 = bf16[16,4,1536]{2,1,0:T(4,128)(2,1)S(1)} all-to-all(bf16[16,4,1536]{2,1,0:T(4,128)(2,1)S(1)} %pad_maximum_fusion.2), channel_id=1, replica_groups=mesh['x'=4,'zb'=2,'za'=2,'c'=2,'zh'=2,'y'=8] {'x','zb','za'}, dimensions={0} | all-to-all | bytes 393216 | tf_op jit(solution)/shard_map/all_to_all | solution.py:31
  162.5 0.1 convert_reduce_fusion.2
  162.6 0.7 broadcast_in_dim.51
  163.3 4.8 %all-to-all-start.6 = ((bf16[16,3,1536]{2,1,0:T(4,128)(2,1)}), bf16[16,3,1536]{2,1,0:T(4,128)(2,1)S(1)}, u32[]{:S(2)}, u32[]{:S(2)}) async-start(bf16[16,3,1536]{2,1,0:T(4,128)(2,1)} %broadcast_in_dim.51), calls=%async_computation.6 | async-start | bytes 393216 | tf_op jit(solution)/shard_map/all_to_all | solution.py:31
  168.1 0.9 fusion.23
  169.0 0.6 slice_reduce_fusion.1
  170.3 5.4 %all-to-all-done.6 = bf16[16,3,1536]{2,1,0:T(4,128)(2,1)S(1)} async-done(((bf16[16,3,1536]{2,1,0:T(4,128)(2,1)}), bf16[16,3,1536]{2,1,0:T(4,128)(2,1)S(1)}, u32[]{:S(2)}, u32[]{:S(2)}) %all-to-all-start.6) | async-done | bytes 147488 | tf_op jit(solution)/shard_map/all_to_all | solution.py:31
  175.7 0.1 reshape.62
  175.8 4.6 %all_gather.3 = bf16[96,1536]{1,0:T(8,128)(2,1)S(1)} all-gather(bf16[48,1536]{1,0:T(8,128)(2,1)S(1)} %reshape.62), channel_id=1, replica_groups=mesh['x'=4,'zb'=2,'za'=2,'c'=2,'zh'=2,'y'=8] {'c'}, dimensions={0}, use_global_device_ids=true | all-gather | bytes 442368 | tf_op jit(solution)/shard_map/all_gather | solution.py:150
  180.3 0.9 convert_element_type.72
  (18 shorter events, 0.3 us)
Async XLA Ops:
  0.6 1.0 copy-start
  0.6 42.1 %copy-start.1 = (bf16[128,96]{0,1:T(8,128)(2,1)S(1)}, bf16[128,96]{0,1:T(8,128)(2,1)}, u32[]{:S(2)}) copy-start(bf16[128,96]{0,1:T(8,128)(2,1)} %param.3) | copy-start | bytes 73732
  37.0 26.3 %all-to-all-start.1 = ((bf16[8,8,5632]{2,1,0:T(8,128)(2,1)}), bf16[8,8,5632]{2,1,0:T(8,128)(2,1)}, u32[]{:S(2)}, u32[]{:S(2)}) async-start(bf16[8,8,5632]{2,1,0:T(8,128)(2,1)} %broadcast_in_dim.22), calls=%async_computation.1 | async-start | bytes 1441792 | tf_op jit(solution)/shard_map/all_to_all | solution.py:31
  42.8 4.8 %collective-permute-start = (bf16[128,96]{0,1:T(8,128)(2,1)S(1)}, bf16[128,96]{0,1:T(8,128)(2,1)S(1)}, u32[]{:S(2)}, u32[]{:S(2)}) collective-permute-start(bf16[128,96]{0,1:T(8,128)(2,1)S(1)} %copy-done.1), channel_id=1, source_target_pairs={{0,16},{16,0},{1,17},{17,1},{2,18},{18,2},{3,19},{19,3},{4,20},{20... | collective-permute-start | bytes 73736 | tf_op jit(solution)/shard_map/ppermute | solution.py:105
  47.6 11.4 %collective-permute-start.1 = (bf16[8,5632]{1,0:T(8,128)(2,1)S(1)}, bf16[8,5632]{1,0:T(8,128)(2,1)S(1)}, u32[]{:S(2)}, u32[]{:S(2)}) collective-permute-start(bf16[8,5632]{1,0:T(8,128)(2,1)S(1)} %get-tuple-element.11), channel_id=1, source_target_pairs={{0,8},{8,0},{64,72},{72,64},{1,9},{9,1},{65,73},{73,65},{2,10},{10... | collective-permute-start | bytes 270344 | tf_op jit(solution)/shard_map/ppermute | solution.py:63
  49.5 11.8 %collective-permute-start.2 = (bf16[8,5632]{1,0:T(8,128)(2,1)S(1)}, bf16[8,5632]{1,0:T(8,128)(2,1)S(1)}, u32[]{:S(2)}, u32[]{:S(2)}) collective-permute-start(bf16[8,5632]{1,0:T(8,128)(2,1)S(1)} %get-tuple-element.11), channel_id=1, source_target_pairs={{0,64},{8,72},{64,0},{72,8},{1,65},{9,73},{65,1},{73,9},{2,66},{10... | collective-permute-start | bytes 270344 | tf_op jit(solution)/shard_map/ppermute | solution.py:63
  53.8 7.5 %collective-permute-start.3 = (bf16[8,5632]{1,0:T(8,128)(2,1)S(1)}, bf16[8,5632]{1,0:T(8,128)(2,1)S(1)}, u32[]{:S(2)}, u32[]{:S(2)}) collective-permute-start(bf16[8,5632]{1,0:T(8,128)(2,1)S(1)} %get-tuple-element.11), channel_id=1, source_target_pairs={{0,72},{8,64},{64,8},{72,0},{1,73},{9,65},{65,9},{73,1},{2,74},{10... | collective-permute-start | bytes 270344 | tf_op jit(solution)/shard_map/ppermute | solution.py:63
  63.3 17.6 %collective-permute-start.5 = (bf16[64,5632]{1,0:T(8,128)(2,1)}, bf16[64,5632]{1,0:T(8,128)(2,1)}, u32[]{:S(2)}, u32[]{:S(2)}) collective-permute-start(bf16[64,5632]{1,0:T(8,128)(2,1)} %bitcast.5), channel_id=1, source_target_pairs={{0,32},{32,0},{1,33},{33,1},{2,34},{34,2},{3,35},{35,3},{4,36},{36... | collective-permute-start | bytes 2162696 | tf_op jit(solution)/shard_map/ppermute | solution.py:109
  66.4 19.5 %collective-permute-start.4 = (bf16[64,5632]{1,0:T(8,128)(2,1)}, bf16[64,5632]{1,0:T(8,128)(2,1)}, u32[]{:S(2)}, u32[]{:S(2)}) collective-permute-start(bf16[64,5632]{1,0:T(8,128)(2,1)} %bitcast.5), channel_id=1, source_target_pairs={{0,16},{16,0},{1,17},{17,1},{2,18},{18,2},{3,19},{19,3},{4,20},{20... | collective-permute-start | bytes 2162696 | tf_op jit(solution)/shard_map/ppermute | solution.py:111
  71.8 23.8 %all-to-all-start.2 = ((bf16[4,32,5632]{2,1,0:T(8,128)(2,1)}), bf16[4,32,5632]{2,1,0:T(8,128)(2,1)}, u32[]{:S(2)}, u32[]{:S(2)}) async-start(bf16[4,32,5632]{2,1,0:T(8,128)(2,1)} %broadcast_in_dim.44), calls=%async_computation.2 | async-start | bytes 2883584 | tf_op jit(solution)/shard_map/all_to_all | solution.py:31
  80.8 7.4 %collective-permute-start.6 = (bf16[64,5632]{1,0:T(8,128)(2,1)}, bf16[64,5632]{1,0:T(8,128)(2,1)S(1)}, u32[]{:S(2)}, u32[]{:S(2)}) collective-permute-start(bf16[64,5632]{1,0:T(8,128)(2,1)} %collective-permute-done.5), channel_id=1, source_target_pairs={{0,16},{16,0},{1,17},{17,1},{2,18},{18,2},{3,19},{19,3},{4,20},{20... | collective-permute-start | bytes 2162696 | tf_op jit(solution)/shard_map/ppermute | solution.py:111
  100.3 19.1 %all-to-all-start.3 = ((bf16[16,8,1536]{2,1,0:T(8,128)(2,1)}), bf16[16,8,1536]{2,1,0:T(8,128)(2,1)S(1)}, u32[]{:S(2)}, u32[]{:S(2)}) async-start(bf16[16,8,1536]{2,1,0:T(8,128)(2,1)} %fusion.5), calls=%async_computation.3 | async-start | bytes 786432 | tf_op jit(solution)/shard_map/all_to_all | solution.py:31
  106.3 4.0 %collective-permute-start.7 = (f32[]{:T(128)}, f32[]{:T(128)}, u32[]{:S(2)}, u32[]{:S(2)}) collective-permute-start(f32[]{:T(128)} %get-tuple-element.15), channel_id=1, source_target_pairs={{0,16},{16,0},{1,17},{17,1},{2,18},{18,2},{3,19},{19,3},{4,20},{20... | collective-permute-start | bytes 20 | tf_op jit(solution)/shard_map/ppermute | solution.py:118
  145.8 5.9 %collective-permute-start.8 = (bf16[128,1536]{1,0:T(8,128)(2,1)S(1)}, bf16[128,1536]{1,0:T(8,128)(2,1)S(1)}, u32[]{:S(2)}, u32[]{:S(2)}) collective-permute-start(bf16[128,1536]{1,0:T(8,128)(2,1)S(1)} %slice.32), channel_id=1, source_target_pairs={{0,16},{16,0},{1,17},{17,1},{2,18},{18,2},{3,19},{19,3},{4,20},{20... | collective-permute-start | bytes 1179656 | tf_op jit(solution)/shard_map/ppermute | solution.py:129
  163.3 12.3 %all-to-all-start.6 = ((bf16[16,3,1536]{2,1,0:T(4,128)(2,1)}), bf16[16,3,1536]{2,1,0:T(4,128)(2,1)S(1)}, u32[]{:S(2)}, u32[]{:S(2)}) async-start(bf16[16,3,1536]{2,1,0:T(4,128)(2,1)} %broadcast_in_dim.51), calls=%async_computation.6 | async-start | bytes 393216 | tf_op jit(solution)/shard_map/all_to_all | solution.py:31

commit v12 on v10

--- a/solution.py
+++ b/solution.py
@@ -57,11 +57,8 @@
     return lanes
 
 
-def around(block, axis):
-    blocks = [block]
-    for step in (1, 2, 3):
-        blocks.append(lax.ppermute(block, axis, [(at, at ^ step) for at in range(4)]))
-    return jnp.concatenate(blocks, axis=0)
+def from_peer(block, axis, step):
+    return lax.ppermute(block, axis, [(at, at ^ step) for at in range(4)])
 
 
 def in_order(values):
@@ -98,24 +95,31 @@
     target = normal(got[:, :, full:].astype(jnp.float32), (0, 2))
     target = target.transpose(1, 0, 2).reshape(mine, -1)
 
-    mine_rows, hidden_sent = lax.optimization_barrier(
-        (jnp.concatenate([student, target], axis=1), hidden)
-    )
+    mine_rows = jnp.concatenate([student, target], axis=1)
     here = gather(jnp.concatenate([student, -target], axis=1), ("y",))
     here = here.reshape(-1, here.shape[2])
-    hidden_there = lax.ppermute(hidden_sent, "c", SWAP)
-    mine_rows, hidden_there = lax.optimization_barrier((mine_rows, hidden_there))
-    row_block = around(around(mine_rows, STRIDE), "x")
+    rows_1 = from_peer(mine_rows, STRIDE, 1)
+    later, rows_1 = lax.optimization_barrier((mine_rows, rows_1))
+    near = [mine_rows, rows_1] + [from_peer(later, STRIDE, step) for step in (2, 3)]
+    near, here = lax.optimization_barrier((jnp.concatenate(near, axis=0), here))
+    far_1 = from_peer(near, "x", 1)
     there = lax.ppermute(here, "za", SWAP)
+    here_core = lax.ppermute(here, "c", SWAP)
+    later, here_core = lax.optimization_barrier((near, here_core))
+    far = [near, far_1] + [from_peer(later, "x", step) for step in (2, 3)]
+    far = lax.optimization_barrier((there, *far))[1:]
+    row_block = jnp.concatenate(far, axis=0)
     columns = jnp.concatenate(
-        [here, lax.ppermute(here, "c", SWAP), there, lax.ppermute(there, "c", SWAP)],
-        axis=0,
+        [here, here_core, there, lax.ppermute(there, "c", SWAP)], axis=0
     )
     s_cols = columns[:, :full]
     differ = dot(row_block, columns, ROWS_T)
     differ = in_order(differ)
     squares = jnp.sum(differ * differ)
+    squares, hidden_sent = lax.optimization_barrier((squares, hidden))
     squares = squares + lax.ppermute(squares, "c", SWAP)
+    hidden_there = lax.ppermute(hidden_sent, "c", SWAP)
+    squares, hidden_there = lax.optimization_barrier((squares, hidden_there))
     partial_grad = sum(dot(part, s_cols) for part in pieces(differ)[::-1])
     partial_grad = partial_grad.astype(jnp.bfloat16).reshape(-1, mine, full)
     grad_unit = 4.0 * jnp.sum(exchange(partial_grad, ROW).astype(jnp.float32), axis=0)

time: 182 us -> 188 us (1.033)
  waiting for transfers between devices: 22.4 us -> 34.3 us
  local copies, waits for them, and re-layouts: 7.83 us -> 3.14 us
  blocking collectives: 73.9 us -> 76.5 us
  starting transfers between devices: 58.6 us -> 56.3 us
    ppermute x7, waiting for transfers between devices: 3.34 us -> 20 us  [the longest x6 20 us: from_peer(): return lax.ppermute(block, axis, [(at, at ^ step) for at in range(4)])]
    all_to_all x3, waiting for transfers between devices: 11.8 us -> 5.37 us  [exchange(): return lax.all_to_all(blocks, axes, split_axis=0, concat_axis=0, tiled=True)]
    unnamed x9 -> x7, local copies, waits for them, and re-layouts: 4.41 us -> 1.11 us
    all_to_all x3, blocking collectives: 69.4 us -> 72 us  [exchange(): return lax.all_to_all(blocks, axes, split_axis=0, concat_axis=0, tiled=True)]
  transfers between devices with their start and end apart: 15 -> 15, of which waited for: 9 -> 9; matrix products, arithmetic and copies ran while one was open for 4% -> 1% of each run, Pallas kernels for 0% -> 0%
where the time goes in v12:
time: 188 us; the launch traced here: 187 us
  blocking collectives  76.5 us (41%)
  starting transfers between devices  56.3 us (30%)
  waiting for transfers between devices  34.3 us (18%)
  between operations  7.79 us (4%)
  matrix products  4.85 us (3%)
  other arithmetic  4.33 us (2%)
  local copies, waits for them, and re-layouts  3.14 us (2%)
    all_to_all x3, blocking collectives, exchange(): return lax.all_to_all(blocks, axes, split_axis=0, concat_axis=0, tiled=True)  72 us
    ppermute x6, waiting for transfers between devices, from_peer(): return lax.ppermute(block, axis, [(at, at ^ step) for at in range(4)])  20 us
    ppermute x6, starting transfers between devices, from_peer(): return lax.ppermute(block, axis, [(at, at ^ step) for at in range(4)])  18.9 us
    all_to_all x3, starting transfers between devices, exchange(): return lax.all_to_all(blocks, axes, split_axis=0, concat_axis=0, tiled=True)  16.2 us
    ppermute x1, waiting for transfers between devices, body(): there = lax.ppermute(here, 'za', SWAP)  6.72 us
    all_to_all x3, waiting for transfers between devices, exchange(): return lax.all_to_all(blocks, axes, split_axis=0, concat_axis=0, tiled=True)  5.37 us
    ppermute x1, starting transfers between devices, body(): piece_there = lax.ppermute(piece, 'c', SWAP)  4.91 us
    dot_general x8, matrix products, dot(): return lax.dot_general(a, b, dims, preferred_element_type=jnp.float32)  4.85 us
  transfers between devices with their start and end apart: 15, of which 9 were waited for; matrix products, arithmetic and copies ran while one was open for 1% of the time, Pallas kernels for 0%

profile of v12, /device:TPU:1, one launch (start us, length us, event | category | flops | bytes accessed | tf_op | source)
XLA Modules:
  0.0 187.3 jit_solution(4966920726703781896)
XLA Ops:
  0.6 0.0 copy-start
  0.6 1.0 copy-done
  1.6 1.0 fusion.2
  2.6 0.9 pad_maximum_fusion
  3.5 32.0 %all_to_all.30 = bf16[16,8,1792]{2,1,0:T(8,128)(2,1)S(1)} all-to-all(bf16[16,8,1792]{2,1,0:T(8,128)(2,1)S(1)} %pad_maximum_fusion), channel_id=1, replica_groups=mesh['x'=4,'zb'=2,'za'=2,'c'=2,'zh'=2,'y'=8] {'zh','y'}, dimensions={0} | all-to-all | bytes 917504 | tf_op jit(solution)/shard_map/all_to_all | solution.py:31
  35.5 0.1 convert_reduce_fusion.1
  35.5 0.1 multiply_reduce_fusion.2
  35.7 0.1 multiply_convert_fusion.1
  35.8 0.1 fusion.18
  35.9 0.1 fusion.19
  36.0 0.9 broadcast_in_dim.37
  37.0 5.8 %all-to-all-start.1 = ((bf16[8,8,5632]{2,1,0:T(8,128)(2,1)}), bf16[8,8,5632]{2,1,0:T(8,128)(2,1)S(1)}, u32[]{:S(2)}, u32[]{:S(2)}) async-start(bf16[8,8,5632]{2,1,0:T(8,128)(2,1)} %broadcast_in_dim.37), calls=%async_computation.1 | async-start | bytes 1441792 | tf_op jit(solution)/shard_map/all_to_all | solution.py:31
  42.8 2.7 %collective-permute-start = (bf16[8,5632]{1,0:T(8,128)(2,1)S(1)}, bf16[8,5632]{1,0:T(8,128)(2,1)S(1)}, u32[]{:S(2)}, u32[]{:S(2)}) collective-permute-start(bf16[8,5632]{1,0:T(8,128)(2,1)S(1)} %get-tuple-element.18), channel_id=1, source_target_pairs={{0,8},{8,0},{64,72},{72,64},{1,9},{9,1},{65,73},{73,65},{2,10},{10... | collective-permute-start | bytes 270344 | tf_op jit(solution)/shard_map/ppermute | solution.py:61
  45.5 6.6 %collective-permute-done = bf16[8,5632]{1,0:T(8,128)(2,1)S(1)} collective-permute-done((bf16[8,5632]{1,0:T(8,128)(2,1)S(1)}, bf16[8,5632]{1,0:T(8,128)(2,1)S(1)}, u32[]{:S(2)}, u32[]{:S(2)}) %collective-permute-start) | collective-permute-done | bytes 90144 | tf_op jit(solution)/shard_map/ppermute | solution.py:61
  52.1 4.8 %collective-permute-start.2 = (bf16[8,5632]{1,0:T(8,128)(2,1)S(1)}, bf16[8,5632]{1,0:T(8,128)(2,1)S(1)}, u32[]{:S(2)}, u32[]{:S(2)}) collective-permute-start(bf16[8,5632]{1,0:T(8,128)(2,1)S(1)} %get-tuple-element.18), channel_id=1, source_target_pairs={{0,72},{8,64},{64,8},{72,0},{1,73},{9,65},{65,9},{73,1},{2,74},{10... | collective-permute-start | bytes 270344 | tf_op jit(solution)/shard_map/ppermute | solution.py:61
  56.9 1.9 %collective-permute-start.1 = (bf16[8,5632]{1,0:T(8,128)(2,1)S(1)}, bf16[8,5632]{1,0:T(8,128)(2,1)S(1)}, u32[]{:S(2)}, u32[]{:S(2)}) collective-permute-start(bf16[8,5632]{1,0:T(8,128)(2,1)S(1)} %get-tuple-element.18), channel_id=1, source_target_pairs={{0,64},{8,72},{64,0},{72,8},{1,65},{9,73},{65,1},{73,9},{2,66},{10... | collective-permute-start | bytes 270344 | tf_op jit(solution)/shard_map/ppermute | solution.py:61
  58.8 0.8 collective-permute-done.2
  59.5 3.8 %collective-permute-done.1 = bf16[8,5632]{1,0:T(8,128)(2,1)S(1)} collective-permute-done((bf16[8,5632]{1,0:T(8,128)(2,1)S(1)}, bf16[8,5632]{1,0:T(8,128)(2,1)S(1)}, u32[]{:S(2)}, u32[]{:S(2)}) %collective-permute-start.1) | collective-permute-done | bytes 90144 | tf_op jit(solution)/shard_map/ppermute | solution.py:61
  63.3 0.0 all-to-all-done.1
  63.4 4.7 %collective-permute-start.5 = (bf16[64,5632]{1,0:T(8,128)(2,1)S(1)}, bf16[64,5632]{1,0:T(8,128)(2,1)S(1)}, u32[]{:S(2)}, u32[]{:S(2)}) collective-permute-start(bf16[64,5632]{1,0:T(8,128)(2,1)S(1)} %bitcast.29), channel_id=1, source_target_pairs={{0,16},{16,0},{1,17},{17,1},{2,18},{18,2},{3,19},{19,3},{4,20},{20... | collective-permute-start | bytes 2162696 | tf_op jit(solution)/shard_map/ppermute | solution.py:107
  68.1 3.6 %collective-permute-start.3 = (bf16[64,5632]{1,0:T(8,128)(2,1)S(1)}, bf16[64,5632]{1,0:T(8,128)(2,1)S(1)}, u32[]{:S(2)}, u32[]{:S(2)}) collective-permute-start(bf16[64,5632]{1,0:T(8,128)(2,1)S(1)} %bitcast.30), channel_id=1, source_target_pairs={{0,32},{32,0},{1,33},{33,1},{2,34},{34,2},{3,35},{35,3},{4,36},{36... | collective-permute-start | bytes 2162696 | tf_op jit(solution)/shard_map/ppermute | solution.py:106
  71.7 3.1 %collective-permute-start.4 = (bf16[32,5632]{1,0:T(8,128)(2,1)S(1)}, bf16[32,5632]{1,0:T(8,128)(2,1)S(1)}, u32[]{:S(2)}, u32[]{:S(2)}) collective-permute-start(bf16[32,5632]{1,0:T(8,128)(2,1)S(1)} %pad_maximum_fusion.1), channel_id=1, source_target_pairs={{0,128},{128,0},{256,384},{384,256},{1,129},{129,1},{257,385},{385... | collective-permute-start | bytes 1081352 | tf_op jit(solution)/shard_map/ppermute | solution.py:61
  74.9 0.0 collective-permute-done.5
  74.9 4.4 %collective-permute-start.6 = (bf16[32,5632]{1,0:T(8,128)(2,1)S(1)}, bf16[32,5632]{1,0:T(8,128)(2,1)S(1)}, u32[]{:S(2)}, u32[]{:S(2)}) collective-permute-start(bf16[32,5632]{1,0:T(8,128)(2,1)S(1)} %pad_maximum_fusion.1), channel_id=1, source_target_pairs={{0,256},{128,384},{256,0},{384,128},{1,257},{129,385},{257,1},{385... | collective-permute-start | bytes 1081352 | tf_op jit(solution)/shard_map/ppermute | solution.py:61
  79.2 2.1 %collective-permute-start.7 = (bf16[32,5632]{1,0:T(8,128)(2,1)S(1)}, bf16[32,5632]{1,0:T(8,128)(2,1)S(1)}, u32[]{:S(2)}, u32[]{:S(2)}) collective-permute-start(bf16[32,5632]{1,0:T(8,128)(2,1)S(1)} %pad_maximum_fusion.1), channel_id=1, source_target_pairs={{0,384},{128,256},{256,128},{384,0},{1,385},{129,257},{257,129},{3... | collective-permute-start | bytes 1081352 | tf_op jit(solution)/shard_map/ppermute | solution.py:61
  81.4 6.7 %collective-permute-done.3 = bf16[64,5632]{1,0:T(8,128)(2,1)S(1)} collective-permute-done((bf16[64,5632]{1,0:T(8,128)(2,1)S(1)}, bf16[64,5632]{1,0:T(8,128)(2,1)S(1)}, u32[]{:S(2)}, u32[]{:S(2)}) %collective-permute-start.3) | collective-permute-done | bytes 720928 | tf_op jit(solution)/shard_map/ppermute | solution.py:106
  88.1 2.6 %collective-permute-start.8 = (bf16[64,5632]{1,0:T(8,128)(2,1)S(1)}, bf16[64,5632]{1,0:T(8,128)(2,1)S(1)}, u32[]{:S(2)}, u32[]{:S(2)}) collective-permute-start(bf16[64,5632]{1,0:T(8,128)(2,1)S(1)} %collective-permute-done.3), channel_id=1, source_target_pairs={{0,16},{16,0},{1,17},{17,1},{2,18},{18,2},{3,19},{19,3},{4,20},{20... | collective-permute-start | bytes 2162696 | tf_op jit(solution)/shard_map/ppermute | solution.py:113
  90.8 0.0 collective-permute-done.4
  90.8 2.5 %collective-permute-done.6 = bf16[32,5632]{1,0:T(8,128)(2,1)S(1)} collective-permute-done((bf16[32,5632]{1,0:T(8,128)(2,1)S(1)}, bf16[32,5632]{1,0:T(8,128)(2,1)S(1)}, u32[]{:S(2)}, u32[]{:S(2)}) %collective-permute-start.6) | collective-permute-done | bytes 360480 | tf_op jit(solution)/shard_map/ppermute | solution.py:61
  93.3 6.3 %collective-permute-done.7 = bf16[32,5632]{1,0:T(8,128)(2,1)S(1)} collective-permute-done((bf16[32,5632]{1,0:T(8,128)(2,1)S(1)}, bf16[32,5632]{1,0:T(8,128)(2,1)S(1)}, u32[]{:S(2)}, u32[]{:S(2)}) %collective-permute-start.7) | collective-permute-done | bytes 360480 | tf_op jit(solution)/shard_map/ppermute | solution.py:61
  99.6 0.0 collective-permute-done.8
  99.6 1.0 fusion.5
  100.7 0.6 multiply_reduce_fusion
  101.4 0.3 fusion.13
  101.7 0.0 copy-start.1
  101.7 0.3 fusion.15
  102.0 1.0 fusion.3
  103.0 5.4 %all-to-all-start.2 = ((bf16[16,8,1536]{2,1,0:T(8,128)(2,1)}), bf16[16,8,1536]{2,1,0:T(8,128)(2,1)S(1)}, u32[]{:S(2)}, u32[]{:S(2)}) async-start(bf16[16,8,1536]{2,1,0:T(8,128)(2,1)} %fusion.3), calls=%async_computation.2 | async-start | bytes 786432 | tf_op jit(solution)/shard_map/all_to_all | solution.py:31
  108.4 3.5 %collective-permute-start.10 = (bf16[128,96]{0,1:T(8,128)(2,1)S(1)}, bf16[128,96]{0,1:T(8,128)(2,1)S(1)}, u32[]{:S(2)}, u32[]{:S(2)}) collective-permute-start(bf16[128,96]{0,1:T(8,128)(2,1)S(1)} %copy-done.1), channel_id=1, source_target_pairs={{0,16},{16,0},{1,17},{17,1},{2,18},{18,2},{3,19},{19,3},{4,20},{20... | collective-permute-start | bytes 73736 | tf_op jit(solution)/shard_map/ppermute | solution.py:121
  111.9 1.9 %collective-permute-start.9 = (f32[]{:T(128)}, f32[]{:T(128)}, u32[]{:S(2)}, u32[]{:S(2)}) collective-permute-start(f32[]{:T(128)} %get-tuple-element.27), channel_id=1, source_target_pairs={{0,16},{16,0},{1,17},{17,1},{2,18},{18,2},{3,19},{19,3},{4,20},{20... | collective-permute-start | bytes 20 | tf_op jit(solution)/shard_map/ppermute | solution.py:120
  113.8 1.2 collective-permute-done.9
  116.4 0.0 collective-permute-done.10
  120.0 0.0 all-to-all-done.2
  120.1 0.1 convert_reduce_fusion
  120.1 0.2 multiply_reduce_fusion.1
  120.3 0.1 multiply_convert_fusion
  120.5 27.0 %all_to_all.31 = bf16[16,8,1664]{2,1,0:T(8,128)(2,1)S(1)} all-to-all(bf16[16,8,1664]{2,1,0:T(8,128)(2,1)S(1)} %broadcast_in_dim.42), channel_id=1, replica_groups=mesh['x'=4,'zb'=2,'za'=2,'c'=2,'zh'=2,'y'=8] {'zh','y'}, dimensions={0} | all-to-all | bytes 851968 | tf_op jit(solution)/shard_map/all_to_all | solution.py:31
  147.5 4.9 %collective-permute-start.11 = (bf16[128,1536]{1,0:T(8,128)(2,1)S(1)}, bf16[128,1536]{1,0:T(8,128)(2,1)S(1)}, u32[]{:S(2)}, u32[]{:S(2)}) collective-permute-start(bf16[128,1536]{1,0:T(8,128)(2,1)S(1)} %slice.32), channel_id=1, source_target_pairs={{0,16},{16,0},{1,17},{17,1},{2,18},{18,2},{3,19},{19,3},{4,20},{20... | collective-permute-start | bytes 1179656 | tf_op jit(solution)/shard_map/ppermute | solution.py:133
  152.4 0.2 fusion.22
  152.6 1.1 collective-permute-done.11
  153.7 0.2 fusion.4
  153.9 0.1 reshape.60
  154.0 0.1 broadcast_in_dim.43
  154.1 0.2 pad_maximum_fusion.2
  154.3 13.0 %all_to_all.32 = bf16[16,4,1536]{2,1,0:T(4,128)(2,1)S(1)} all-to-all(bf16[16,4,1536]{2,1,0:T(4,128)(2,1)S(1)} %pad_maximum_fusion.2), channel_id=1, replica_groups=mesh['x'=4,'zb'=2,'za'=2,'c'=2,'zh'=2,'y'=8] {'x','zb','za'}, dimensions={0} | all-to-all | bytes 393216 | tf_op jit(solution)/shard_map/all_to_all | solution.py:31
  167.3 0.1 convert_reduce_fusion.2
  167.4 0.7 broadcast_in_dim.44
  168.1 5.0 %all-to-all-start.5 = ((bf16[16,3,1536]{2,1,0:T(4,128)(2,1)}), bf16[16,3,1536]{2,1,0:T(4,128)(2,1)S(1)}, u32[]{:S(2)}, u32[]{:S(2)}) async-start(bf16[16,3,1536]{2,1,0:T(4,128)(2,1)} %broadcast_in_dim.44), calls=%async_computation.5 | async-start | bytes 393216 | tf_op jit(solution)/shard_map/all_to_all | solution.py:31
  173.1 0.9 fusion.30
  174.0 0.6 slice_reduce_fusion.1
  175.3 5.4 %all-to-all-done.5 = bf16[16,3,1536]{2,1,0:T(4,128)(2,1)S(1)} async-done(((bf16[16,3,1536]{2,1,0:T(4,128)(2,1)}), bf16[16,3,1536]{2,1,0:T(4,128)(2,1)S(1)}, u32[]{:S(2)}, u32[]{:S(2)}) %all-to-all-start.5) | async-done | bytes 147488 | tf_op jit(solution)/shard_map/all_to_all | solution.py:31
  180.6 0.1 reshape.61
  180.8 4.6 %all_gather.3 = bf16[96,1536]{1,0:T(8,128)(2,1)S(1)} all-gather(bf16[48,1536]{1,0:T(8,128)(2,1)S(1)} %reshape.61), channel_id=1, replica_groups=mesh['x'=4,'zb'=2,'za'=2,'c'=2,'zh'=2,'y'=8] {'c'}, dimensions={0}, use_global_device_ids=true | all-gather | bytes 442368 | tf_op jit(solution)/shard_map/all_gather | solution.py:154
  185.3 0.9 convert_element_type.72
  (23 shorter events, 0.5 us)
Async XLA Ops:
  0.6 1.0 copy-start
  37.0 26.4 %all-to-all-start.1 = ((bf16[8,8,5632]{2,1,0:T(8,128)(2,1)}), bf16[8,8,5632]{2,1,0:T(8,128)(2,1)S(1)}, u32[]{:S(2)}, u32[]{:S(2)}) async-start(bf16[8,8,5632]{2,1,0:T(8,128)(2,1)} %broadcast_in_dim.37), calls=%async_computation.1 | async-start | bytes 1441792 | tf_op jit(solution)/shard_map/all_to_all | solution.py:31
  42.8 9.3 %collective-permute-start = (bf16[8,5632]{1,0:T(8,128)(2,1)S(1)}, bf16[8,5632]{1,0:T(8,128)(2,1)S(1)}, u32[]{:S(2)}, u32[]{:S(2)}) collective-permute-start(bf16[8,5632]{1,0:T(8,128)(2,1)S(1)} %get-tuple-element.18), channel_id=1, source_target_pairs={{0,8},{8,0},{64,72},{72,64},{1,9},{9,1},{65,73},{73,65},{2,10},{10... | collective-permute-start | bytes 270344 | tf_op jit(solution)/shard_map/ppermute | solution.py:61
  52.1 7.5 %collective-permute-start.2 = (bf16[8,5632]{1,0:T(8,128)(2,1)S(1)}, bf16[8,5632]{1,0:T(8,128)(2,1)S(1)}, u32[]{:S(2)}, u32[]{:S(2)}) collective-permute-start(bf16[8,5632]{1,0:T(8,128)(2,1)S(1)} %get-tuple-element.18), channel_id=1, source_target_pairs={{0,72},{8,64},{64,8},{72,0},{1,73},{9,65},{65,9},{73,1},{2,74},{10... | collective-permute-start | bytes 270344 | tf_op jit(solution)/shard_map/ppermute | solution.py:61
  56.9 6.5 %collective-permute-start.1 = (bf16[8,5632]{1,0:T(8,128)(2,1)S(1)}, bf16[8,5632]{1,0:T(8,128)(2,1)S(1)}, u32[]{:S(2)}, u32[]{:S(2)}) collective-permute-start(bf16[8,5632]{1,0:T(8,128)(2,1)S(1)} %get-tuple-element.18), channel_id=1, source_target_pairs={{0,64},{8,72},{64,0},{72,8},{1,65},{9,73},{65,1},{73,9},{2,66},{10... | collective-permute-start | bytes 270344 | tf_op jit(solution)/shard_map/ppermute | solution.py:61
  63.4 11.5 %collective-permute-start.5 = (bf16[64,5632]{1,0:T(8,128)(2,1)S(1)}, bf16[64,5632]{1,0:T(8,128)(2,1)S(1)}, u32[]{:S(2)}, u32[]{:S(2)}) collective-permute-start(bf16[64,5632]{1,0:T(8,128)(2,1)S(1)} %bitcast.29), channel_id=1, source_target_pairs={{0,16},{16,0},{1,17},{17,1},{2,18},{18,2},{3,19},{19,3},{4,20},{20... | collective-permute-start | bytes 2162696 | tf_op jit(solution)/shard_map/ppermute | solution.py:107
  68.1 20.0 %collective-permute-start.3 = (bf16[64,5632]{1,0:T(8,128)(2,1)S(1)}, bf16[64,5632]{1,0:T(8,128)(2,1)S(1)}, u32[]{:S(2)}, u32[]{:S(2)}) collective-permute-start(bf16[64,5632]{1,0:T(8,128)(2,1)S(1)} %bitcast.30), channel_id=1, source_target_pairs={{0,32},{32,0},{1,33},{33,1},{2,34},{34,2},{3,35},{35,3},{4,36},{36... | collective-permute-start | bytes 2162696 | tf_op jit(solution)/shard_map/ppermute | solution.py:106
  71.7 19.1 %collective-permute-start.4 = (bf16[32,5632]{1,0:T(8,128)(2,1)S(1)}, bf16[32,5632]{1,0:T(8,128)(2,1)S(1)}, u32[]{:S(2)}, u32[]{:S(2)}) collective-permute-start(bf16[32,5632]{1,0:T(8,128)(2,1)S(1)} %pad_maximum_fusion.1), channel_id=1, source_target_pairs={{0,128},{128,0},{256,384},{384,256},{1,129},{129,1},{257,385},{385... | collective-permute-start | bytes 1081352 | tf_op jit(solution)/shard_map/ppermute | solution.py:61
  74.9 18.4 %collective-permute-start.6 = (bf16[32,5632]{1,0:T(8,128)(2,1)S(1)}, bf16[32,5632]{1,0:T(8,128)(2,1)S(1)}, u32[]{:S(2)}, u32[]{:S(2)}) collective-permute-start(bf16[32,5632]{1,0:T(8,128)(2,1)S(1)} %pad_maximum_fusion.1), channel_id=1, source_target_pairs={{0,256},{128,384},{256,0},{384,128},{1,257},{129,385},{257,1},{385... | collective-permute-start | bytes 1081352 | tf_op jit(solution)/shard_map/ppermute | solution.py:61
  79.2 20.3 %collective-permute-start.7 = (bf16[32,5632]{1,0:T(8,128)(2,1)S(1)}, bf16[32,5632]{1,0:T(8,128)(2,1)S(1)}, u32[]{:S(2)}, u32[]{:S(2)}) collective-permute-start(bf16[32,5632]{1,0:T(8,128)(2,1)S(1)} %pad_maximum_fusion.1), channel_id=1, source_target_pairs={{0,384},{128,256},{256,128},{384,0},{1,385},{129,257},{257,129},{3... | collective-permute-start | bytes 1081352 | tf_op jit(solution)/shard_map/ppermute | solution.py:61
  88.1 11.5 %collective-permute-start.8 = (bf16[64,5632]{1,0:T(8,128)(2,1)S(1)}, bf16[64,5632]{1,0:T(8,128)(2,1)S(1)}, u32[]{:S(2)}, u32[]{:S(2)}) collective-permute-start(bf16[64,5632]{1,0:T(8,128)(2,1)S(1)} %collective-permute-done.3), channel_id=1, source_target_pairs={{0,16},{16,0},{1,17},{17,1},{2,18},{18,2},{3,19},{19,3},{4,20},{20... | collective-permute-start | bytes 2162696 | tf_op jit(solution)/shard_map/ppermute | solution.py:113
  101.7 6.7 %copy-start.1 = (bf16[128,96]{0,1:T(8,128)(2,1)S(1)}, bf16[128,96]{0,1:T(8,128)(2,1)}, u32[]{:S(2)}) copy-start(bf16[128,96]{0,1:T(8,128)(2,1)} %param.3) | copy-start | bytes 73732
  103.0 17.1 %all-to-all-start.2 = ((bf16[16,8,1536]{2,1,0:T(8,128)(2,1)}), bf16[16,8,1536]{2,1,0:T(8,128)(2,1)S(1)}, u32[]{:S(2)}, u32[]{:S(2)}) async-start(bf16[16,8,1536]{2,1,0:T(8,128)(2,1)} %fusion.3), calls=%async_computation.2 | async-start | bytes 786432 | tf_op jit(solution)/shard_map/all_to_all | solution.py:31
  108.4 8.0 %collective-permute-start.10 = (bf16[128,96]{0,1:T(8,128)(2,1)S(1)}, bf16[128,96]{0,1:T(8,128)(2,1)S(1)}, u32[]{:S(2)}, u32[]{:S(2)}) collective-permute-start(bf16[128,96]{0,1:T(8,128)(2,1)S(1)} %copy-done.1), channel_id=1, source_target_pairs={{0,16},{16,0},{1,17},{17,1},{2,18},{18,2},{3,19},{19,3},{4,20},{20... | collective-permute-start | bytes 73736 | tf_op jit(solution)/shard_map/ppermute | solution.py:121
  111.9 3.1 %collective-permute-start.9 = (f32[]{:T(128)}, f32[]{:T(128)}, u32[]{:S(2)}, u32[]{:S(2)}) collective-permute-start(f32[]{:T(128)} %get-tuple-element.27), channel_id=1, source_target_pairs={{0,16},{16,0},{1,17},{17,1},{2,18},{18,2},{3,19},{19,3},{4,20},{20... | collective-permute-start | bytes 20 | tf_op jit(solution)/shard_map/ppermute | solution.py:120
  147.5 6.2 %collective-permute-start.11 = (bf16[128,1536]{1,0:T(8,128)(2,1)S(1)}, bf16[128,1536]{1,0:T(8,128)(2,1)S(1)}, u32[]{:S(2)}, u32[]{:S(2)}) collective-permute-start(bf16[128,1536]{1,0:T(8,128)(2,1)S(1)} %slice.32), channel_id=1, source_target_pairs={{0,16},{16,0},{1,17},{17,1},{2,18},{18,2},{3,19},{19,3},{4,20},{20... | collective-permute-start | bytes 1179656 | tf_op jit(solution)/shard_map/ppermute | solution.py:133
  168.1 12.5 %all-to-all-start.5 = ((bf16[16,3,1536]{2,1,0:T(4,128)(2,1)}), bf16[16,3,1536]{2,1,0:T(4,128)(2,1)S(1)}, u32[]{:S(2)}, u32[]{:S(2)}) async-start(bf16[16,3,1536]{2,1,0:T(4,128)(2,1)} %broadcast_in_dim.44), calls=%async_computation.5 | async-start | bytes 393216 | tf_op jit(solution)/shard_map/all_to_all | solution.py:31

commit v13 on v10

--- a/solution.py
+++ b/solution.py
@@ -8,7 +8,7 @@
 DP = ("x", "zb", "za", "c")
 FS = ("zh", "y")
 XZ = ("x", "zb", "za")
-STRIDE = ("zb", "zh")
+STRIDE = ("zb", "za")
 ROW = ("x",) + STRIDE
 SIZES = {"x": 4, "zb": 2, "za": 2, "c": 2, "zh": 2, "y": 8}
 SWAP = [(0, 1), (1, 0)]
@@ -67,7 +67,7 @@
 def in_order(values):
     shape = values.shape
     values = values.reshape(2, 2, 2, 2, -1, shape[1])
-    for dim, (axis, bit) in enumerate((("x", 2), ("x", 1), ("zb", 1), ("zh", 1))):
+    for dim, (axis, bit) in enumerate((("x", 2), ("x", 1), ("zb", 1), ("za", 1))):
         swap = (lax.axis_index(axis) & bit) != 0
         values = jnp.where(swap, jnp.flip(values, dim), values)
     return values.reshape(shape)
@@ -106,7 +106,7 @@
     hidden_there = lax.ppermute(hidden_sent, "c", SWAP)
     mine_rows, hidden_there = lax.optimization_barrier((mine_rows, hidden_there))
     row_block = around(around(mine_rows, STRIDE), "x")
-    there = lax.ppermute(here, "za", SWAP)
+    there = lax.ppermute(here, "zh", SWAP)
     columns = jnp.concatenate(
         [here, lax.ppermute(here, "c", SWAP), there, lax.ppermute(there, "c", SWAP)],
         axis=0,

time: 182 us -> 193 us (1.060)
  starting transfers between devices: 58.6 us -> 70.8 us
  blocking collectives: 73.9 us -> 65.4 us
  waiting for transfers between devices: 22.4 us -> 29.4 us
    ppermute x1, starting transfers between devices: 3.21 us -> 18.3 us  [body(): lax.ppermute(there, 'c', SWAP)]
    all_to_all x3, blocking collectives: 69.4 us -> 60.8 us  [exchange(): return lax.all_to_all(blocks, axes, split_axis=0, concat_axis=0, tiled=True)]
    ppermute x1, waiting for transfers between devices: 5.14 us -> 10.1 us  [body(): there = lax.ppermute(here, 'zh', SWAP)]
    ppermute x6, starting transfers between devices: 21.9 us -> 19.8 us  [around(): lax.ppermute(block, axis, [(at, at ^ step) for at in range(4)])]
where the time goes in v13:
time: 193 us; the launch traced here: 192 us
  starting transfers between devices  70.8 us (37%)
  blocking collectives  65.4 us (34%)
  waiting for transfers between devices  29.4 us (15%)
  local copies, waits for them, and re-layouts  7.83 us (4%)
  between operations  7.69 us (4%)
  matrix products  6.21 us (3%)
  other arithmetic  4.36 us (2%)
    all_to_all x3, blocking collectives, exchange(): return lax.all_to_all(blocks, axes, split_axis=0, concat_axis=0, tiled=True)  60.8 us
    ppermute x6, starting transfers between devices, around(): lax.ppermute(block, axis, [(at, at ^ step) for at in range(4)])  19.8 us
    ppermute x1, starting transfers between devices, body(): lax.ppermute(there, 'c', SWAP)  18.3 us
    all_to_all x3, starting transfers between devices, exchange(): return lax.all_to_all(blocks, axes, split_axis=0, concat_axis=0, tiled=True)  15.3 us
    all_to_all x3, waiting for transfers between devices, exchange(): return lax.all_to_all(blocks, axes, split_axis=0, concat_axis=0, tiled=True)  13.6 us
    ppermute x1, waiting for transfers between devices, body(): there = lax.ppermute(here, 'zh', SWAP)  10.1 us
    dot_general x8, matrix products, dot(): return lax.dot_general(a, b, dims, preferred_element_type=jnp.float32)  6.21 us
    ppermute x1, starting transfers between devices, body(): hidden_there = lax.ppermute(hidden_sent, 'c', SWAP)  4.89 us
  transfers between devices with their start and end apart: 15, of which 9 were waited for; matrix products, arithmetic and copies ran while one was open for 4% of the time, Pallas kernels for 0%

profile of v13, /device:TPU:1, one launch (start us, length us, event | category | flops | bytes accessed | tf_op | source)
XLA Modules:
  0.0 191.7 jit_solution(2079010979739271100)
XLA Ops:
  0.6 1.0 copy-done
  1.6 1.0 fusion.10
  2.6 0.9 pad_maximum_fusion.1
  3.5 32.0 %all_to_all.30 = bf16[16,8,1792]{2,1,0:T(8,128)(2,1)S(1)} all-to-all(bf16[16,8,1792]{2,1,0:T(8,128)(2,1)S(1)} %pad_maximum_fusion.1), channel_id=1, replica_groups=mesh['x'=4,'zb'=2,'za'=2,'c'=2,'zh'=2,'y'=8] {'zh','y'}, dimensions={0} | all-to-all | bytes 917504 | tf_op jit(solution)/shard_map/all_to_all | solution.py:31
  35.5 0.1 convert_reduce_fusion.1
  35.6 0.1 multiply_reduce_fusion.2
  35.7 0.1 multiply_convert_fusion.1
  35.8 0.1 fusion.13
  35.9 0.1 fusion.14
  36.1 4.9 %collective-permute-start = (bf16[128,96]{0,1:T(8,128)(2,1)S(1)}, bf16[128,96]{0,1:T(8,128)(2,1)S(1)}, u32[]{:S(2)}, u32[]{:S(2)}) collective-permute-start(bf16[128,96]{0,1:T(8,128)(2,1)S(1)} %copy-done.1), channel_id=1, source_target_pairs={{0,16},{16,0},{1,17},{17,1},{2,18},{18,2},{3,19},{19,3},{4,20},{20... | collective-permute-start | bytes 73736 | tf_op jit(solution)/shard_map/ppermute | solution.py:106
  41.0 0.9 broadcast_in_dim.37
  41.9 4.6 %all-to-all-start.1 = ((bf16[8,8,5632]{2,1,0:T(8,128)(2,1)}), bf16[8,8,5632]{2,1,0:T(8,128)(2,1)S(1)}, u32[]{:S(2)}, u32[]{:S(2)}) async-start(bf16[8,8,5632]{2,1,0:T(8,128)(2,1)} %broadcast_in_dim.37), calls=%async_computation.1 | async-start | bytes 1441792 | tf_op jit(solution)/shard_map/all_to_all | solution.py:31
  46.5 2.6 %collective-permute-start.1 = (bf16[8,5632]{1,0:T(8,128)(2,1)S(1)}, bf16[8,5632]{1,0:T(8,128)(2,1)S(1)}, u32[]{:S(2)}, u32[]{:S(2)}) collective-permute-start(bf16[8,5632]{1,0:T(8,128)(2,1)S(1)} %get-tuple-element.9), channel_id=1, source_target_pairs={{0,32},{32,0},{64,96},{96,64},{1,33},{33,1},{65,97},{97,65},{2,34}... | collective-permute-start | bytes 270344 | tf_op jit(solution)/shard_map/ppermute | solution.py:63
  49.1 0.6 constant_dynamic-update-slice_fusion.3
  49.7 3.9 %collective-permute-start.2 = (bf16[8,5632]{1,0:T(8,128)(2,1)S(1)}, bf16[8,5632]{1,0:T(8,128)(2,1)S(1)}, u32[]{:S(2)}, u32[]{:S(2)}) collective-permute-start(bf16[8,5632]{1,0:T(8,128)(2,1)S(1)} %get-tuple-element.9), channel_id=1, source_target_pairs={{0,64},{32,96},{64,0},{96,32},{1,65},{33,97},{65,1},{97,33},{2,66}... | collective-permute-start | bytes 270344 | tf_op jit(solution)/shard_map/ppermute | solution.py:63
  53.7 2.8 %collective-permute-start.3 = (bf16[8,5632]{1,0:T(8,128)(2,1)S(1)}, bf16[8,5632]{1,0:T(8,128)(2,1)S(1)}, u32[]{:S(2)}, u32[]{:S(2)}) collective-permute-start(bf16[8,5632]{1,0:T(8,128)(2,1)S(1)} %get-tuple-element.9), channel_id=1, source_target_pairs={{0,96},{32,64},{64,32},{96,0},{1,97},{33,65},{65,33},{97,1},{2,98}... | collective-permute-start | bytes 270344 | tf_op jit(solution)/shard_map/ppermute | solution.py:63
  56.5 0.7 constant_dynamic-update-slice_fusion.2
  57.1 1.3 collective-permute-done.2
  58.5 0.6 constant_dynamic-update-slice_fusion.1
  59.1 2.0 %collective-permute-done.3 = bf16[8,5632]{1,0:T(8,128)(2,1)S(1)} collective-permute-done((bf16[8,5632]{1,0:T(8,128)(2,1)S(1)}, bf16[8,5632]{1,0:T(8,128)(2,1)S(1)}, u32[]{:S(2)}, u32[]{:S(2)}) %collective-permute-start.3) | collective-permute-done | bytes 90144 | tf_op jit(solution)/shard_map/ppermute | solution.py:63
  61.1 0.7 constant_dynamic-update-slice_fusion
  61.7 3.1 %collective-permute-start.4 = (bf16[32,5632]{1,0:T(8,128)(2,1)S(1)}, bf16[32,5632]{1,0:T(8,128)(2,1)S(1)}, u32[]{:S(2)}, u32[]{:S(2)}) collective-permute-start(bf16[32,5632]{1,0:T(8,128)(2,1)S(1)} %get-tuple-element.16), channel_id=1, source_target_pairs={{0,128},{128,0},{256,384},{384,256},{1,129},{129,1},{257,385},{385... | collective-permute-start | bytes 1081352 | tf_op jit(solution)/shard_map/ppermute | solution.py:63
  64.8 3.9 %all-to-all-done.1 = bf16[8,8,5632]{2,1,0:T(8,128)(2,1)S(1)} async-done(((bf16[8,8,5632]{2,1,0:T(8,128)(2,1)}), bf16[8,8,5632]{2,1,0:T(8,128)(2,1)S(1)}, u32[]{:S(2)}, u32[]{:S(2)}) %all-to-all-start.1) | async-done | bytes 720928 | tf_op jit(solution)/shard_map/all_to_all | solution.py:31
  68.7 1.9 collective-permute-start.8
  70.7 4.7 %collective-permute-start.5 = (bf16[32,5632]{1,0:T(8,128)(2,1)S(1)}, bf16[32,5632]{1,0:T(8,128)(2,1)S(1)}, u32[]{:S(2)}, u32[]{:S(2)}) collective-permute-start(bf16[32,5632]{1,0:T(8,128)(2,1)S(1)} %get-tuple-element.16), channel_id=1, source_target_pairs={{0,256},{128,384},{256,0},{384,128},{1,257},{129,385},{257,1},{385... | collective-permute-start | bytes 1081352 | tf_op jit(solution)/shard_map/ppermute | solution.py:63
  75.3 2.8 %collective-permute-start.6 = (bf16[32,5632]{1,0:T(8,128)(2,1)S(1)}, bf16[32,5632]{1,0:T(8,128)(2,1)S(1)}, u32[]{:S(2)}, u32[]{:S(2)}) collective-permute-start(bf16[32,5632]{1,0:T(8,128)(2,1)S(1)} %get-tuple-element.16), channel_id=1, source_target_pairs={{0,384},{128,256},{256,128},{384,0},{1,385},{129,257},{257,129},{3... | collective-permute-start | bytes 1081352 | tf_op jit(solution)/shard_map/ppermute | solution.py:63
  78.1 0.8 constant_dynamic-update-slice_fusion.6
  78.9 3.2 %collective-permute-start.7 = (bf16[64,5632]{1,0:T(8,128)(2,1)S(1)}, bf16[64,5632]{1,0:T(8,128)(2,1)S(1)}, u32[]{:S(2)}, u32[]{:S(2)}) collective-permute-start(bf16[64,5632]{1,0:T(8,128)(2,1)S(1)} %bitcast.33), channel_id=1, source_target_pairs={{0,16},{16,0},{1,17},{17,1},{2,18},{18,2},{3,19},{19,3},{4,20},{20... | collective-permute-start | bytes 2162696 | tf_op jit(solution)/shard_map/ppermute | solution.py:111
  82.1 10.1 %collective-permute-done.8 = bf16[64,5632]{1,0:T(8,128)(2,1)S(1)} collective-permute-done((bf16[64,5632]{1,0:T(8,128)(2,1)S(1)}, bf16[64,5632]{1,0:T(8,128)(2,1)S(1)}, u32[]{:S(2)}, u32[]{:S(2)}) %collective-permute-start.8) | collective-permute-done | bytes 720928 | tf_op jit(solution)/shard_map/ppermute | solution.py:109
  92.1 18.3 %collective-permute-start.9 = (bf16[64,5632]{1,0:T(8,128)(2,1)S(1)}, bf16[64,5632]{1,0:T(8,128)(2,1)S(1)}, u32[]{:S(2)}, u32[]{:S(2)}) collective-permute-start(bf16[64,5632]{1,0:T(8,128)(2,1)S(1)} %collective-permute-done.8), channel_id=1, source_target_pairs={{0,16},{16,0},{1,17},{17,1},{2,18},{18,2},{3,19},{19,3},{4,20},{20... | collective-permute-start | bytes 2162696 | tf_op jit(solution)/shard_map/ppermute | solution.py:111
  110.4 0.7 constant_dynamic-update-slice_fusion.5
  111.2 0.8 constant_dynamic-update-slice_fusion.4
  112.0 0.3 collective-permute-done.9
  112.2 2.4 %fusion = f32[128,256]{1,0:T(8,128)S(1)} fusion(bf16[128,5632]{1,0:T(8,128)(2,1)} %constant_dynamic-update-slice_fusion.4, bf16[64,5632]{1,0:T(8,128)(2,1)S(1)} %collective-permute-done.9, bf16[64,5632]{1,0:T(8,128)(2,1)S(1)} %collective-permute-done.8, bf16[64,5632]{1,0:T(8,128)(2,1)S(1)} %collective-permute-done.7, bf16[64,5632]{1,0:T(8,128)(2,1)S(1)} %bitcast.34), kind=kOutput, calls=%fused_computation | convolution fusion | flops 380633088 | bytes 4456448 | tf_op jit(solution)/shard_map/dot_general | solution.py:20
  114.7 0.6 multiply_reduce_fusion
  115.4 0.1 pad_maximum_fusion
  115.4 0.3 fusion.27
  115.7 0.3 fusion.28
  116.0 1.0 fusion.11
  117.0 5.7 %all-to-all-start.2 = ((bf16[16,8,1536]{2,1,0:T(8,128)(2,1)}), bf16[16,8,1536]{2,1,0:T(8,128)(2,1)S(1)}, u32[]{:S(2)}, u32[]{:S(2)}) async-start(bf16[16,8,1536]{2,1,0:T(8,128)(2,1)} %fusion.11), calls=%async_computation.2 | async-start | bytes 786432 | tf_op jit(solution)/shard_map/all_to_all | solution.py:31
  122.8 2.6 %collective-permute-start.10 = (f32[]{:T(128)}, f32[]{:T(128)}, u32[]{:S(2)}, u32[]{:S(2)}) collective-permute-start(f32[]{:T(128)} %get-tuple-element.11), channel_id=1, source_target_pairs={{0,16},{16,0},{1,17},{17,1},{2,18},{18,2},{3,19},{19,3},{4,20},{20... | collective-permute-start | bytes 20 | tf_op jit(solution)/shard_map/ppermute | solution.py:118
  125.3 1.1 collective-permute-done.10
  131.3 4.4 %all-to-all-done.2 = bf16[16,8,1536]{2,1,0:T(8,128)(2,1)S(1)} async-done(((bf16[16,8,1536]{2,1,0:T(8,128)(2,1)}), bf16[16,8,1536]{2,1,0:T(8,128)(2,1)S(1)}, u32[]{:S(2)}, u32[]{:S(2)}) %all-to-all-start.2) | async-done | bytes 393248 | tf_op jit(solution)/shard_map/all_to_all | solution.py:31
  135.7 0.1 convert_reduce_fusion
  135.7 0.2 multiply_reduce_fusion.1
  135.9 0.1 multiply_convert_fusion
  136.1 17.9 %all_to_all.31 = bf16[16,8,1664]{2,1,0:T(8,128)(2,1)S(1)} all-to-all(bf16[16,8,1664]{2,1,0:T(8,128)(2,1)S(1)} %broadcast_in_dim.42), channel_id=1, replica_groups=mesh['x'=4,'zb'=2,'za'=2,'c'=2,'zh'=2,'y'=8] {'zh','y'}, dimensions={0} | all-to-all | bytes 851968 | tf_op jit(solution)/shard_map/all_to_all | solution.py:31
  154.0 4.9 %collective-permute-start.11 = (bf16[128,1536]{1,0:T(8,128)(2,1)S(1)}, bf16[128,1536]{1,0:T(8,128)(2,1)S(1)}, u32[]{:S(2)}, u32[]{:S(2)}) collective-permute-start(bf16[128,1536]{1,0:T(8,128)(2,1)S(1)} %slice.31), channel_id=1, source_target_pairs={{0,16},{16,0},{1,17},{17,1},{2,18},{18,2},{3,19},{19,3},{4,20},{20... | collective-permute-start | bytes 1179656 | tf_op jit(solution)/shard_map/ppermute | solution.py:129
  158.9 0.2 fusion.17
  159.1 1.1 collective-permute-done.11
  160.2 0.2 fusion.12
  160.4 0.1 reshape.60
  160.5 0.1 broadcast_in_dim.43
  160.6 0.2 pad_maximum_fusion.2
  160.8 10.9 %all_to_all.32 = bf16[16,4,1536]{2,1,0:T(4,128)(2,1)S(1)} all-to-all(bf16[16,4,1536]{2,1,0:T(4,128)(2,1)S(1)} %pad_maximum_fusion.2), channel_id=1, replica_groups=mesh['x'=4,'zb'=2,'za'=2,'c'=2,'zh'=2,'y'=8] {'x','zb','za'}, dimensions={0} | all-to-all | bytes 393216 | tf_op jit(solution)/shard_map/all_to_all | solution.py:31
  171.7 0.1 convert_reduce_fusion.2
  171.8 0.7 broadcast_in_dim.44
  172.6 5.0 %all-to-all-start.5 = ((bf16[16,3,1536]{2,1,0:T(4,128)(2,1)}), bf16[16,3,1536]{2,1,0:T(4,128)(2,1)S(1)}, u32[]{:S(2)}, u32[]{:S(2)}) async-start(bf16[16,3,1536]{2,1,0:T(4,128)(2,1)} %broadcast_in_dim.44), calls=%async_computation.5 | async-start | bytes 393216 | tf_op jit(solution)/shard_map/all_to_all | solution.py:31
  177.5 0.9 fusion.25
  178.4 0.6 slice_reduce_fusion.1
  179.7 5.4 %all-to-all-done.5 = bf16[16,3,1536]{2,1,0:T(4,128)(2,1)S(1)} async-done(((bf16[16,3,1536]{2,1,0:T(4,128)(2,1)}), bf16[16,3,1536]{2,1,0:T(4,128)(2,1)S(1)}, u32[]{:S(2)}, u32[]{:S(2)}) %all-to-all-start.5) | async-done | bytes 147488 | tf_op jit(solution)/shard_map/all_to_all | solution.py:31
  185.0 0.1 reshape.61
  185.2 4.6 %all_gather.3 = bf16[96,1536]{1,0:T(8,128)(2,1)S(1)} all-gather(bf16[48,1536]{1,0:T(8,128)(2,1)S(1)} %reshape.61), channel_id=1, replica_groups=mesh['x'=4,'zb'=2,'za'=2,'c'=2,'zh'=2,'y'=8] {'c'}, dimensions={0}, use_global_device_ids=true | all-gather | bytes 442368 | tf_op jit(solution)/shard_map/all_gather | solution.py:150
  189.7 0.9 convert_element_type.72
  (26 shorter events, 0.3 us)
Async XLA Ops:
  0.6 1.0 copy-start
  2.6 33.4 %copy-start.1 = (bf16[128,96]{0,1:T(8,128)(2,1)S(1)}, bf16[128,96]{0,1:T(8,128)(2,1)}, u32[]{:S(2)}) copy-start(bf16[128,96]{0,1:T(8,128)(2,1)} %param.3) | copy-start | bytes 73732
  36.1 10.5 %collective-permute-start = (bf16[128,96]{0,1:T(8,128)(2,1)S(1)}, bf16[128,96]{0,1:T(8,128)(2,1)S(1)}, u32[]{:S(2)}, u32[]{:S(2)}) collective-permute-start(bf16[128,96]{0,1:T(8,128)(2,1)S(1)} %copy-done.1), channel_id=1, source_target_pairs={{0,16},{16,0},{1,17},{17,1},{2,18},{18,2},{3,19},{19,3},{4,20},{20... | collective-permute-start | bytes 73736 | tf_op jit(solution)/shard_map/ppermute | solution.py:106
  41.9 26.8 %all-to-all-start.1 = ((bf16[8,8,5632]{2,1,0:T(8,128)(2,1)}), bf16[8,8,5632]{2,1,0:T(8,128)(2,1)S(1)}, u32[]{:S(2)}, u32[]{:S(2)}) async-start(bf16[8,8,5632]{2,1,0:T(8,128)(2,1)} %broadcast_in_dim.37), calls=%async_computation.1 | async-start | bytes 1441792 | tf_op jit(solution)/shard_map/all_to_all | solution.py:31
  46.5 9.9 %collective-permute-start.1 = (bf16[8,5632]{1,0:T(8,128)(2,1)S(1)}, bf16[8,5632]{1,0:T(8,128)(2,1)S(1)}, u32[]{:S(2)}, u32[]{:S(2)}) collective-permute-start(bf16[8,5632]{1,0:T(8,128)(2,1)S(1)} %get-tuple-element.9), channel_id=1, source_target_pairs={{0,32},{32,0},{64,96},{96,64},{1,33},{33,1},{65,97},{97,65},{2,34}... | collective-permute-start | bytes 270344 | tf_op jit(solution)/shard_map/ppermute | solution.py:63
  49.7 8.7 %collective-permute-start.2 = (bf16[8,5632]{1,0:T(8,128)(2,1)S(1)}, bf16[8,5632]{1,0:T(8,128)(2,1)S(1)}, u32[]{:S(2)}, u32[]{:S(2)}) collective-permute-start(bf16[8,5632]{1,0:T(8,128)(2,1)S(1)} %get-tuple-element.9), channel_id=1, source_target_pairs={{0,64},{32,96},{64,0},{96,32},{1,65},{33,97},{65,1},{97,33},{2,66}... | collective-permute-start | bytes 270344 | tf_op jit(solution)/shard_map/ppermute | solution.py:63
  53.7 7.4 %collective-permute-start.3 = (bf16[8,5632]{1,0:T(8,128)(2,1)S(1)}, bf16[8,5632]{1,0:T(8,128)(2,1)S(1)}, u32[]{:S(2)}, u32[]{:S(2)}) collective-permute-start(bf16[8,5632]{1,0:T(8,128)(2,1)S(1)} %get-tuple-element.9), channel_id=1, source_target_pairs={{0,96},{32,64},{64,32},{96,0},{1,97},{33,65},{65,33},{97,1},{2,98}... | collective-permute-start | bytes 270344 | tf_op jit(solution)/shard_map/ppermute | solution.py:63
  61.7 16.4 %collective-permute-start.4 = (bf16[32,5632]{1,0:T(8,128)(2,1)S(1)}, bf16[32,5632]{1,0:T(8,128)(2,1)S(1)}, u32[]{:S(2)}, u32[]{:S(2)}) collective-permute-start(bf16[32,5632]{1,0:T(8,128)(2,1)S(1)} %get-tuple-element.16), channel_id=1, source_target_pairs={{0,128},{128,0},{256,384},{384,256},{1,129},{129,1},{257,385},{385... | collective-permute-start | bytes 1081352 | tf_op jit(solution)/shard_map/ppermute | solution.py:63
  68.7 23.4 %collective-permute-start.8 = (bf16[64,5632]{1,0:T(8,128)(2,1)S(1)}, bf16[64,5632]{1,0:T(8,128)(2,1)S(1)}, u32[]{:S(2)}, u32[]{:S(2)}) collective-permute-start(bf16[64,5632]{1,0:T(8,128)(2,1)S(1)} %bitcast.32), channel_id=1, source_target_pairs={{0,8},{8,0},{1,9},{9,1},{2,10},{10,2},{3,11},{11,3},{4,12},{12,4},... | collective-permute-start | bytes 2162696 | tf_op jit(solution)/shard_map/ppermute | solution.py:109
  70.7 39.8 %collective-permute-start.5 = (bf16[32,5632]{1,0:T(8,128)(2,1)S(1)}, bf16[32,5632]{1,0:T(8,128)(2,1)S(1)}, u32[]{:S(2)}, u32[]{:S(2)}) collective-permute-start(bf16[32,5632]{1,0:T(8,128)(2,1)S(1)} %get-tuple-element.16), channel_id=1, source_target_pairs={{0,256},{128,384},{256,0},{384,128},{1,257},{129,385},{257,1},{385... | collective-permute-start | bytes 1081352 | tf_op jit(solution)/shard_map/ppermute | solution.py:63
  75.3 35.9 %collective-permute-start.6 = (bf16[32,5632]{1,0:T(8,128)(2,1)S(1)}, bf16[32,5632]{1,0:T(8,128)(2,1)S(1)}, u32[]{:S(2)}, u32[]{:S(2)}) collective-permute-start(bf16[32,5632]{1,0:T(8,128)(2,1)S(1)} %get-tuple-element.16), channel_id=1, source_target_pairs={{0,384},{128,256},{256,128},{384,0},{1,385},{129,257},{257,129},{3... | collective-permute-start | bytes 1081352 | tf_op jit(solution)/shard_map/ppermute | solution.py:63
  78.9 33.1 %collective-permute-start.7 = (bf16[64,5632]{1,0:T(8,128)(2,1)S(1)}, bf16[64,5632]{1,0:T(8,128)(2,1)S(1)}, u32[]{:S(2)}, u32[]{:S(2)}) collective-permute-start(bf16[64,5632]{1,0:T(8,128)(2,1)S(1)} %bitcast.33), channel_id=1, source_target_pairs={{0,16},{16,0},{1,17},{17,1},{2,18},{18,2},{3,19},{19,3},{4,20},{20... | collective-permute-start | bytes 2162696 | tf_op jit(solution)/shard_map/ppermute | solution.py:111
  92.1 20.1 %collective-permute-start.9 = (bf16[64,5632]{1,0:T(8,128)(2,1)S(1)}, bf16[64,5632]{1,0:T(8,128)(2,1)S(1)}, u32[]{:S(2)}, u32[]{:S(2)}) collective-permute-start(bf16[64,5632]{1,0:T(8,128)(2,1)S(1)} %collective-permute-done.8), channel_id=1, source_target_pairs={{0,16},{16,0},{1,17},{17,1},{2,18},{18,2},{3,19},{19,3},{4,20},{20... | collective-permute-start | bytes 2162696 | tf_op jit(solution)/shard_map/ppermute | solution.py:111
  117.0 18.7 %all-to-all-start.2 = ((bf16[16,8,1536]{2,1,0:T(8,128)(2,1)}), bf16[16,8,1536]{2,1,0:T(8,128)(2,1)S(1)}, u32[]{:S(2)}, u32[]{:S(2)}) async-start(bf16[16,8,1536]{2,1,0:T(8,128)(2,1)} %fusion.11), calls=%async_computation.2 | async-start | bytes 786432 | tf_op jit(solution)/shard_map/all_to_all | solution.py:31
  122.8 3.6 %collective-permute-start.10 = (f32[]{:T(128)}, f32[]{:T(128)}, u32[]{:S(2)}, u32[]{:S(2)}) collective-permute-start(f32[]{:T(128)} %get-tuple-element.11), channel_id=1, source_target_pairs={{0,16},{16,0},{1,17},{17,1},{2,18},{18,2},{3,19},{19,3},{4,20},{20... | collective-permute-start | bytes 20 | tf_op jit(solution)/shard_map/ppermute | solution.py:118
  154.0 6.2 %collective-permute-start.11 = (bf16[128,1536]{1,0:T(8,128)(2,1)S(1)}, bf16[128,1536]{1,0:T(8,128)(2,1)S(1)}, u32[]{:S(2)}, u32[]{:S(2)}) collective-permute-start(bf16[128,1536]{1,0:T(8,128)(2,1)S(1)} %slice.31), channel_id=1, source_target_pairs={{0,16},{16,0},{1,17},{17,1},{2,18},{18,2},{3,19},{19,3},{4,20},{20... | collective-permute-start | bytes 1179656 | tf_op jit(solution)/shard_map/ppermute | solution.py:129
  172.6 12.5 %all-to-all-start.5 = ((bf16[16,3,1536]{2,1,0:T(4,128)(2,1)}), bf16[16,3,1536]{2,1,0:T(4,128)(2,1)S(1)}, u32[]{:S(2)}, u32[]{:S(2)}) async-start(bf16[16,3,1536]{2,1,0:T(4,128)(2,1)} %broadcast_in_dim.44), calls=%async_computation.5 | async-start | bytes 393216 | tf_op jit(solution)/shard_map/all_to_all | solution.py:31

commit v14 on v11

--- a/solution.py
+++ b/solution.py
@@ -64,11 +64,27 @@
     return jnp.concatenate(blocks, axis=0)
 
 
+def along_ring(block, other):
+    size = SIZES["x"]
+    left = [(at, (at + 1) % size) for at in range(size)]
+    right = [(at, (at - 1) % size) for at in range(size)]
+    after = lax.ppermute(block, "x", right)
+    before = lax.ppermute(block, "x", left)
+    cut = block.shape[0] // 2
+    after, before, other = lax.optimization_barrier((after, before, other))
+    upper = lax.ppermute(after[:cut], "x", right)
+    lower = lax.ppermute(before[cut:], "x", left)
+    return jnp.concatenate([block, after, upper, lower, before], axis=0), other
+
+
 def in_order(values):
     shape = values.shape
     values = values.reshape(SIZES["x"], 2, 2, -1, shape[1])
     for dim, axis in ((1, "zb"), (2, "zh")):
         values = jnp.where(lax.axis_index(axis) != 0, jnp.flip(values, dim), values)
+    for bit in (1, 2):
+        swap = (lax.axis_index("x") & bit) != 0
+        values = jnp.where(swap, jnp.roll(values, bit, axis=0), values)
     return values.reshape(shape)
 
 
@@ -104,9 +120,8 @@
     here = here.reshape(-1, here.shape[2])
     hidden_there = lax.ppermute(hidden_sent, "c", SWAP)
     mine_rows, hidden_there = lax.optimization_barrier((mine_rows, hidden_there))
-    near, here = lax.optimization_barrier((around(mine_rows, STRIDE), here))
-    row_block = gather(near, ("x",)).reshape(rows, -1)
     there = lax.ppermute(here, "za", SWAP)
+    row_block, _ = along_ring(around(mine_rows, STRIDE), here)
     columns = jnp.concatenate(
         [here, lax.ppermute(here, "c", SWAP), there, lax.ppermute(there, "c", SWAP)],
         axis=0,

time: 183 us -> 183 us (level)
  waiting for transfers between devices: 27.4 us -> 19.7 us
  starting transfers between devices: 56.2 us -> 63.4 us
    ppermute x0 -> x4, starting transfers between devices: none -> 11.6 us  [the longest x1 4.38 us: along_ring(): after = lax.ppermute(block, 'x', right)]
    all_to_all x4 -> x3, waiting for transfers between devices: 18.7 us -> 10.6 us  [exchange(): return lax.all_to_all(blocks, axes, split_axis=0, concat_axis=0, tiled=True)]
    all_to_all x4 -> x3, starting transfers between devices: 21 us -> 17 us  [exchange(): return lax.all_to_all(blocks, axes, split_axis=0, concat_axis=0, tiled=True)]
    ppermute x0 -> x4, waiting for transfers between devices: none -> 2.57 us  [the longest x1 2.11 us: along_ring(): before = lax.ppermute(block, 'x', left)]
    ppermute x1, waiting for transfers between devices: 3.61 us -> 1.7 us  [body(): there = lax.ppermute(here, 'za', SWAP)]
    unnamed x7 -> x10, local copies, waits for them, and re-layouts: 4.43 us -> 5.02 us
  transfers between devices with their start and end apart: 13 -> 16, of which waited for: 9 -> 10; matrix products, arithmetic and copies ran while one was open for 4% -> 4% of each run, Pallas kernels for 0% -> 0%
where the time goes in v14:
time: 183 us; the launch traced here: 182 us
  blocking collectives  72.4 us (40%)
  starting transfers between devices  63.4 us (35%)
  waiting for transfers between devices  19.7 us (11%)
  local copies, waits for them, and re-layouts  8.49 us (5%)
  between operations  7.72 us (4%)
  matrix products  6.2 us (3%)
  other arithmetic  4.36 us (2%)
    all_to_all x3, blocking collectives, exchange(): return lax.all_to_all(blocks, axes, split_axis=0, concat_axis=0, tiled=True)  67.8 us
    all_to_all x3, starting transfers between devices, exchange(): return lax.all_to_all(blocks, axes, split_axis=0, concat_axis=0, tiled=True)  17 us
    ppermute x3, starting transfers between devices, around(): lax.ppermute(block, axis, [(at, at ^ step) for at in range(4)])  11.4 us
    all_to_all x3, waiting for transfers between devices, exchange(): return lax.all_to_all(blocks, axes, split_axis=0, concat_axis=0, tiled=True)  10.6 us
    dot_general x8, matrix products, dot(): return lax.dot_general(a, b, dims, preferred_element_type=jnp.float32)  6.2 us
    unnamed x10, local copies, waits for them, and re-layouts  5.02 us
    ppermute x1, starting transfers between devices, body(): hidden_there = lax.ppermute(hidden_sent, 'c', SWAP)  4.89 us
    ppermute x1, starting transfers between devices, body(): lax.ppermute(there, 'c', SWAP)  4.65 us
  transfers between devices with their start and end apart: 16, of which 10 were waited for; matrix products, arithmetic and copies ran while one was open for 4% of the time, Pallas kernels for 0%

profile of v14, /device:TPU:1, one launch (start us, length us, event | category | flops | bytes accessed | tf_op | source)
XLA Modules:
  0.0 182.2 jit_solution(1101346289600190921)
XLA Ops:
  0.6 1.0 copy-done
  1.6 1.0 fusion.10
  2.6 0.9 pad_maximum_fusion.1
  3.5 32.0 %all_to_all.30 = bf16[16,8,1792]{2,1,0:T(8,128)(2,1)S(1)} all-to-all(bf16[16,8,1792]{2,1,0:T(8,128)(2,1)S(1)} %pad_maximum_fusion.1), channel_id=1, replica_groups=mesh['x'=4,'zb'=2,'za'=2,'c'=2,'zh'=2,'y'=8] {'zh','y'}, dimensions={0} | all-to-all | bytes 917504 | tf_op jit(solution)/shard_map/all_to_all | solution.py:31
  35.6 0.1 multiply_reduce_fusion.2
  35.7 0.1 multiply_convert_fusion.1
  35.8 0.1 fusion.13
  35.9 0.1 fusion.14
  36.1 4.9 %collective-permute-start = (bf16[128,96]{0,1:T(8,128)(2,1)S(1)}, bf16[128,96]{0,1:T(8,128)(2,1)S(1)}, u32[]{:S(2)}, u32[]{:S(2)}) collective-permute-start(bf16[128,96]{0,1:T(8,128)(2,1)S(1)} %copy-done.1), channel_id=1, source_target_pairs={{0,16},{16,0},{1,17},{17,1},{2,18},{18,2},{3,19},{19,3},{4,20},{20... | collective-permute-start | bytes 73736 | tf_op jit(solution)/shard_map/ppermute | solution.py:121
  41.0 0.9 broadcast_in_dim.37
  41.9 4.6 %all-to-all-start.1 = ((bf16[8,8,5632]{2,1,0:T(8,128)(2,1)}), bf16[8,8,5632]{2,1,0:T(8,128)(2,1)S(1)}, u32[]{:S(2)}, u32[]{:S(2)}) async-start(bf16[8,8,5632]{2,1,0:T(8,128)(2,1)} %broadcast_in_dim.37), calls=%async_computation.1 | async-start | bytes 1441792 | tf_op jit(solution)/shard_map/all_to_all | solution.py:31
  46.5 1.9 %collective-permute-start.1 = (bf16[8,5632]{1,0:T(8,128)(2,1)S(1)}, bf16[8,5632]{1,0:T(8,128)(2,1)S(1)}, u32[]{:S(2)}, u32[]{:S(2)}) collective-permute-start(bf16[8,5632]{1,0:T(8,128)(2,1)S(1)} %get-tuple-element.11), channel_id=1, source_target_pairs={{0,8},{8,0},{64,72},{72,64},{1,9},{9,1},{65,73},{73,65},{2,10},{10... | collective-permute-start | bytes 270344 | tf_op jit(solution)/shard_map/ppermute | solution.py:63
  48.5 0.6 constant_dynamic-update-slice_fusion.3
  49.1 4.2 %collective-permute-start.2 = (bf16[8,5632]{1,0:T(8,128)(2,1)S(1)}, bf16[8,5632]{1,0:T(8,128)(2,1)S(1)}, u32[]{:S(2)}, u32[]{:S(2)}) collective-permute-start(bf16[8,5632]{1,0:T(8,128)(2,1)S(1)} %get-tuple-element.11), channel_id=1, source_target_pairs={{0,64},{8,72},{64,0},{72,8},{1,65},{9,73},{65,1},{73,9},{2,66},{10... | collective-permute-start | bytes 270344 | tf_op jit(solution)/shard_map/ppermute | solution.py:63
  53.3 5.2 %collective-permute-start.3 = (bf16[8,5632]{1,0:T(8,128)(2,1)S(1)}, bf16[8,5632]{1,0:T(8,128)(2,1)S(1)}, u32[]{:S(2)}, u32[]{:S(2)}) collective-permute-start(bf16[8,5632]{1,0:T(8,128)(2,1)S(1)} %get-tuple-element.11), channel_id=1, source_target_pairs={{0,72},{8,64},{64,8},{72,0},{1,73},{9,65},{65,9},{73,1},{2,74},{10... | collective-permute-start | bytes 270344 | tf_op jit(solution)/shard_map/ppermute | solution.py:63
  58.6 0.6 constant_dynamic-update-slice_fusion.2
  59.2 0.4 collective-permute-done.2
  59.6 0.6 constant_dynamic-update-slice_fusion.1
  60.2 2.0 %collective-permute-done.3 = bf16[8,5632]{1,0:T(8,128)(2,1)S(1)} collective-permute-done((bf16[8,5632]{1,0:T(8,128)(2,1)S(1)}, bf16[8,5632]{1,0:T(8,128)(2,1)S(1)}, u32[]{:S(2)}, u32[]{:S(2)}) %collective-permute-start.3) | collective-permute-done | bytes 90144 | tf_op jit(solution)/shard_map/ppermute | solution.py:63
  62.3 0.6 constant_dynamic-update-slice_fusion
  62.9 4.4 %collective-permute-start.4 = (bf16[32,5632]{1,0:T(8,128)(2,1)S(1)}, bf16[32,5632]{1,0:T(8,128)(2,1)S(1)}, u32[]{:S(2)}, u32[]{:S(2)}) collective-permute-start(bf16[32,5632]{1,0:T(8,128)(2,1)S(1)} %get-tuple-element.22), channel_id=1, source_target_pairs={{0,384},{128,0},{256,128},{384,256},{1,385},{129,1},{257,129},{385... | collective-permute-start | bytes 1081352 | tf_op jit(solution)/shard_map/ppermute | solution.py:71
  67.3 1.9 %collective-permute-start.5 = (bf16[32,5632]{1,0:T(8,128)(2,1)S(1)}, bf16[32,5632]{1,0:T(8,128)(2,1)S(1)}, u32[]{:S(2)}, u32[]{:S(2)}) collective-permute-start(bf16[32,5632]{1,0:T(8,128)(2,1)S(1)} %get-tuple-element.22), channel_id=1, source_target_pairs={{0,128},{128,256},{256,384},{384,0},{1,129},{129,257},{257,385},{3... | collective-permute-start | bytes 1081352 | tf_op jit(solution)/shard_map/ppermute | solution.py:72
  69.2 3.6 %collective-permute-start.9 = (bf16[64,5632]{1,0:T(8,128)(2,1)S(1)}, bf16[64,5632]{1,0:T(8,128)(2,1)S(1)}, u32[]{:S(2)}, u32[]{:S(2)}) collective-permute-start(bf16[64,5632]{1,0:T(8,128)(2,1)S(1)} %bitcast.32), channel_id=1, source_target_pairs={{0,32},{32,0},{1,33},{33,1},{2,34},{34,2},{3,35},{35,3},{4,36},{36... | collective-permute-start | bytes 2162696 | tf_op jit(solution)/shard_map/ppermute | solution.py:123
  72.8 3.3 %collective-permute-start.8 = (bf16[64,5632]{1,0:T(8,128)(2,1)S(1)}, bf16[64,5632]{1,0:T(8,128)(2,1)S(1)}, u32[]{:S(2)}, u32[]{:S(2)}) collective-permute-start(bf16[64,5632]{1,0:T(8,128)(2,1)S(1)} %bitcast.33), channel_id=1, source_target_pairs={{0,16},{16,0},{1,17},{17,1},{2,18},{18,2},{3,19},{19,3},{4,20},{20... | collective-permute-start | bytes 2162696 | tf_op jit(solution)/shard_map/ppermute | solution.py:126
  76.1 2.1 %collective-permute-done.5 = bf16[32,5632]{1,0:T(8,128)(2,1)S(1)} collective-permute-done((bf16[32,5632]{1,0:T(8,128)(2,1)S(1)}, bf16[32,5632]{1,0:T(8,128)(2,1)S(1)}, u32[]{:S(2)}, u32[]{:S(2)}) %collective-permute-start.5) | collective-permute-done | bytes 360480 | tf_op jit(solution)/shard_map/ppermute | solution.py:72
  78.2 2.8 %collective-permute-start.6 = (bf16[16,5632]{1,0:T(8,128)(2,1)S(1)}, bf16[16,5632]{1,0:T(8,128)(2,1)S(1)}, u32[]{:S(2)}, u32[]{:S(2)}) collective-permute-start(bf16[16,5632]{1,0:T(8,128)(2,1)S(1)} %slice.46), channel_id=1, source_target_pairs={{0,384},{128,0},{256,128},{384,256},{1,385},{129,1},{257,129},{385... | collective-permute-start | bytes 540680 | tf_op jit(solution)/shard_map/ppermute | solution.py:75
  81.0 0.8 constant_dynamic-update-slice_fusion.7
  81.8 2.5 %collective-permute-start.7 = (bf16[16,5632]{1,0:T(8,128)(2,1)S(1)}, bf16[16,5632]{1,0:T(8,128)(2,1)S(1)}, u32[]{:S(2)}, u32[]{:S(2)}) collective-permute-start(bf16[16,5632]{1,0:T(8,128)(2,1)S(1)} %slice.47), channel_id=1, source_target_pairs={{0,128},{128,256},{256,384},{384,0},{1,129},{129,257},{257,385},{3... | collective-permute-start | bytes 540680 | tf_op jit(solution)/shard_map/ppermute | solution.py:76
  84.3 0.5 collective-permute-done.6
  84.8 0.7 constant_dynamic-update-slice_fusion.6
  85.4 1.7 collective-permute-done.9
  87.1 4.6 %collective-permute-start.10 = (bf16[64,5632]{1,0:T(8,128)(2,1)S(1)}, bf16[64,5632]{1,0:T(8,128)(2,1)S(1)}, u32[]{:S(2)}, u32[]{:S(2)}) collective-permute-start(bf16[64,5632]{1,0:T(8,128)(2,1)S(1)} %collective-permute-done.9), channel_id=1, source_target_pairs={{0,16},{16,0},{1,17},{17,1},{2,18},{18,2},{3,19},{19,3},{4,20},{20... | collective-permute-start | bytes 2162696 | tf_op jit(solution)/shard_map/ppermute | solution.py:126
  91.8 0.7 constant_dynamic-update-slice_fusion.5
  92.5 0.8 constant_dynamic-update-slice_fusion.4
  93.3 0.3 collective-permute-done.10
  93.6 2.4 %fusion = f32[128,256]{1,0:T(8,128)S(1)} fusion(bf16[128,5632]{1,0:T(8,128)(2,1)} %constant_dynamic-update-slice_fusion.4, bf16[64,5632]{1,0:T(8,128)(2,1)S(1)} %collective-permute-done.10, bf16[64,5632]{1,0:T(8,128)(2,1)S(1)} %collective-permute-done.9, bf16[64,5632]{1,0:T(8,128)(2,1)S(1)} %collective-permute-done.8, bf16[64,5632]{1,0:T(8,128)(2,1)S(1)} %bitcast.34), kind=kOutput, calls=%fused_computation | convolution fusion | flops 380633088 | bytes 4456448 | tf_op jit(solution)/shard_map/dot_general | solution.py:20
  96.1 0.6 multiply_reduce_fusion
  96.8 0.3 fusion.28
  97.1 0.3 fusion.29
  97.4 1.0 fusion.11
  98.4 8.0 %all-to-all-start.2 = ((bf16[16,8,1536]{2,1,0:T(8,128)(2,1)}), bf16[16,8,1536]{2,1,0:T(8,128)(2,1)S(1)}, u32[]{:S(2)}, u32[]{:S(2)}) async-start(bf16[16,8,1536]{2,1,0:T(8,128)(2,1)} %fusion.11), calls=%async_computation.2 | async-start | bytes 786432 | tf_op jit(solution)/shard_map/all_to_all | solution.py:31
  106.5 2.6 %collective-permute-start.11 = (f32[]{:T(128)}, f32[]{:T(128)}, u32[]{:S(2)}, u32[]{:S(2)}) collective-permute-start(f32[]{:T(128)} %get-tuple-element.15), channel_id=1, source_target_pairs={{0,16},{16,0},{1,17},{17,1},{2,18},{18,2},{3,19},{19,3},{4,20},{20... | collective-permute-start | bytes 20 | tf_op jit(solution)/shard_map/ppermute | solution.py:133
  109.0 0.9 collective-permute-done.11
  114.9 5.2 %all-to-all-done.2 = bf16[16,8,1536]{2,1,0:T(8,128)(2,1)S(1)} async-done(((bf16[16,8,1536]{2,1,0:T(8,128)(2,1)}), bf16[16,8,1536]{2,1,0:T(8,128)(2,1)S(1)}, u32[]{:S(2)}, u32[]{:S(2)}) %all-to-all-start.2) | async-done | bytes 393248 | tf_op jit(solution)/shard_map/all_to_all | solution.py:31
  120.0 0.1 convert_reduce_fusion
  120.1 0.2 multiply_reduce_fusion.1
  120.3 0.1 multiply_convert_fusion
  120.4 25.3 %all_to_all.31 = bf16[16,8,1664]{2,1,0:T(8,128)(2,1)S(1)} all-to-all(bf16[16,8,1664]{2,1,0:T(8,128)(2,1)S(1)} %broadcast_in_dim.42), channel_id=1, replica_groups=mesh['x'=4,'zb'=2,'za'=2,'c'=2,'zh'=2,'y'=8] {'zh','y'}, dimensions={0} | all-to-all | bytes 851968 | tf_op jit(solution)/shard_map/all_to_all | solution.py:31
  145.7 4.5 %collective-permute-start.12 = (bf16[128,1536]{1,0:T(8,128)(2,1)S(1)}, bf16[128,1536]{1,0:T(8,128)(2,1)S(1)}, u32[]{:S(2)}, u32[]{:S(2)}) collective-permute-start(bf16[128,1536]{1,0:T(8,128)(2,1)S(1)} %slice.63), channel_id=1, source_target_pairs={{0,16},{16,0},{1,17},{17,1},{2,18},{18,2},{3,19},{19,3},{4,20},{20... | collective-permute-start | bytes 1179656 | tf_op jit(solution)/shard_map/ppermute | solution.py:144
  150.3 0.2 fusion.17
  150.5 1.1 collective-permute-done.12
  151.6 0.2 fusion.12
  151.8 0.1 reshape.60
  151.9 0.2 pad_maximum_fusion.2
  152.2 10.5 %all_to_all.32 = bf16[16,4,1536]{2,1,0:T(4,128)(2,1)S(1)} all-to-all(bf16[16,4,1536]{2,1,0:T(4,128)(2,1)S(1)} %pad_maximum_fusion.2), channel_id=1, replica_groups=mesh['x'=4,'zb'=2,'za'=2,'c'=2,'zh'=2,'y'=8] {'x','zb','za'}, dimensions={0} | all-to-all | bytes 393216 | tf_op jit(solution)/shard_map/all_to_all | solution.py:31
  162.7 0.1 convert_reduce_fusion.2
  162.8 0.7 broadcast_in_dim.44
  163.5 4.4 %all-to-all-start.5 = ((bf16[16,3,1536]{2,1,0:T(4,128)(2,1)}), bf16[16,3,1536]{2,1,0:T(4,128)(2,1)S(1)}, u32[]{:S(2)}, u32[]{:S(2)}) async-start(bf16[16,3,1536]{2,1,0:T(4,128)(2,1)} %broadcast_in_dim.44), calls=%async_computation.5 | async-start | bytes 393216 | tf_op jit(solution)/shard_map/all_to_all | solution.py:31
  167.9 0.9 fusion.25
  168.8 0.6 slice_reduce_fusion.1
  170.0 5.5 %all-to-all-done.5 = bf16[16,3,1536]{2,1,0:T(4,128)(2,1)S(1)} async-done(((bf16[16,3,1536]{2,1,0:T(4,128)(2,1)}), bf16[16,3,1536]{2,1,0:T(4,128)(2,1)S(1)}, u32[]{:S(2)}, u32[]{:S(2)}) %all-to-all-start.5) | async-done | bytes 147488 | tf_op jit(solution)/shard_map/all_to_all | solution.py:31
  175.5 0.1 reshape.61
  175.6 4.6 %all_gather.3 = bf16[96,1536]{1,0:T(8,128)(2,1)S(1)} all-gather(bf16[48,1536]{1,0:T(8,128)(2,1)S(1)} %reshape.61), channel_id=1, replica_groups=mesh['x'=4,'zb'=2,'za'=2,'c'=2,'zh'=2,'y'=8] {'c'}, dimensions={0}, use_global_device_ids=true | all-gather | bytes 442368 | tf_op jit(solution)/shard_map/all_gather | solution.py:165
  180.2 0.9 convert_element_type.72
  (34 shorter events, 0.5 us)
Async XLA Ops:
  0.6 1.0 copy-start
  2.6 33.4 %copy-start.1 = (bf16[128,96]{0,1:T(8,128)(2,1)S(1)}, bf16[128,96]{0,1:T(8,128)(2,1)}, u32[]{:S(2)}) copy-start(bf16[128,96]{0,1:T(8,128)(2,1)} %param.3) | copy-start | bytes 73732
  36.1 10.5 %collective-permute-start = (bf16[128,96]{0,1:T(8,128)(2,1)S(1)}, bf16[128,96]{0,1:T(8,128)(2,1)S(1)}, u32[]{:S(2)}, u32[]{:S(2)}) collective-permute-start(bf16[128,96]{0,1:T(8,128)(2,1)S(1)} %copy-done.1), channel_id=1, source_target_pairs={{0,16},{16,0},{1,17},{17,1},{2,18},{18,2},{3,19},{19,3},{4,20},{20... | collective-permute-start | bytes 73736 | tf_op jit(solution)/shard_map/ppermute | solution.py:121
  41.9 27.3 %all-to-all-start.1 = ((bf16[8,8,5632]{2,1,0:T(8,128)(2,1)}), bf16[8,8,5632]{2,1,0:T(8,128)(2,1)S(1)}, u32[]{:S(2)}, u32[]{:S(2)}) async-start(bf16[8,8,5632]{2,1,0:T(8,128)(2,1)} %broadcast_in_dim.37), calls=%async_computation.1 | async-start | bytes 1441792 | tf_op jit(solution)/shard_map/all_to_all | solution.py:31
  46.5 12.0 %collective-permute-start.1 = (bf16[8,5632]{1,0:T(8,128)(2,1)S(1)}, bf16[8,5632]{1,0:T(8,128)(2,1)S(1)}, u32[]{:S(2)}, u32[]{:S(2)}) collective-permute-start(bf16[8,5632]{1,0:T(8,128)(2,1)S(1)} %get-tuple-element.11), channel_id=1, source_target_pairs={{0,8},{8,0},{64,72},{72,64},{1,9},{9,1},{65,73},{73,65},{2,10},{10... | collective-permute-start | bytes 270344 | tf_op jit(solution)/shard_map/ppermute | solution.py:63
  49.1 10.5 %collective-permute-start.2 = (bf16[8,5632]{1,0:T(8,128)(2,1)S(1)}, bf16[8,5632]{1,0:T(8,128)(2,1)S(1)}, u32[]{:S(2)}, u32[]{:S(2)}) collective-permute-start(bf16[8,5632]{1,0:T(8,128)(2,1)S(1)} %get-tuple-element.11), channel_id=1, source_target_pairs={{0,64},{8,72},{64,0},{72,8},{1,65},{9,73},{65,1},{73,9},{2,66},{10... | collective-permute-start | bytes 270344 | tf_op jit(solution)/shard_map/ppermute | solution.py:63
  53.3 8.9 %collective-permute-start.3 = (bf16[8,5632]{1,0:T(8,128)(2,1)S(1)}, bf16[8,5632]{1,0:T(8,128)(2,1)S(1)}, u32[]{:S(2)}, u32[]{:S(2)}) collective-permute-start(bf16[8,5632]{1,0:T(8,128)(2,1)S(1)} %get-tuple-element.11), channel_id=1, source_target_pairs={{0,72},{8,64},{64,8},{72,0},{1,73},{9,65},{65,9},{73,1},{2,74},{10... | collective-permute-start | bytes 270344 | tf_op jit(solution)/shard_map/ppermute | solution.py:63
  62.9 13.2 %collective-permute-start.4 = (bf16[32,5632]{1,0:T(8,128)(2,1)S(1)}, bf16[32,5632]{1,0:T(8,128)(2,1)S(1)}, u32[]{:S(2)}, u32[]{:S(2)}) collective-permute-start(bf16[32,5632]{1,0:T(8,128)(2,1)S(1)} %get-tuple-element.22), channel_id=1, source_target_pairs={{0,384},{128,0},{256,128},{384,256},{1,385},{129,1},{257,129},{385... | collective-permute-start | bytes 1081352 | tf_op jit(solution)/shard_map/ppermute | solution.py:71
  67.3 10.9 %collective-permute-start.5 = (bf16[32,5632]{1,0:T(8,128)(2,1)S(1)}, bf16[32,5632]{1,0:T(8,128)(2,1)S(1)}, u32[]{:S(2)}, u32[]{:S(2)}) collective-permute-start(bf16[32,5632]{1,0:T(8,128)(2,1)S(1)} %get-tuple-element.22), channel_id=1, source_target_pairs={{0,128},{128,256},{256,384},{384,0},{1,129},{129,257},{257,385},{3... | collective-permute-start | bytes 1081352 | tf_op jit(solution)/shard_map/ppermute | solution.py:72
  69.2 17.9 %collective-permute-start.9 = (bf16[64,5632]{1,0:T(8,128)(2,1)S(1)}, bf16[64,5632]{1,0:T(8,128)(2,1)S(1)}, u32[]{:S(2)}, u32[]{:S(2)}) collective-permute-start(bf16[64,5632]{1,0:T(8,128)(2,1)S(1)} %bitcast.32), channel_id=1, source_target_pairs={{0,32},{32,0},{1,33},{33,1},{2,34},{34,2},{3,35},{35,3},{4,36},{36... | collective-permute-start | bytes 2162696 | tf_op jit(solution)/shard_map/ppermute | solution.py:123
  72.8 20.5 %collective-permute-start.8 = (bf16[64,5632]{1,0:T(8,128)(2,1)S(1)}, bf16[64,5632]{1,0:T(8,128)(2,1)S(1)}, u32[]{:S(2)}, u32[]{:S(2)}) collective-permute-start(bf16[64,5632]{1,0:T(8,128)(2,1)S(1)} %bitcast.33), channel_id=1, source_target_pairs={{0,16},{16,0},{1,17},{17,1},{2,18},{18,2},{3,19},{19,3},{4,20},{20... | collective-permute-start | bytes 2162696 | tf_op jit(solution)/shard_map/ppermute | solution.py:126
  78.2 6.5 %collective-permute-start.6 = (bf16[16,5632]{1,0:T(8,128)(2,1)S(1)}, bf16[16,5632]{1,0:T(8,128)(2,1)S(1)}, u32[]{:S(2)}, u32[]{:S(2)}) collective-permute-start(bf16[16,5632]{1,0:T(8,128)(2,1)S(1)} %slice.46), channel_id=1, source_target_pairs={{0,384},{128,0},{256,128},{384,256},{1,385},{129,1},{257,129},{385... | collective-permute-start | bytes 540680 | tf_op jit(solution)/shard_map/ppermute | solution.py:75
  81.8 10.0 %collective-permute-start.7 = (bf16[16,5632]{1,0:T(8,128)(2,1)S(1)}, bf16[16,5632]{1,0:T(8,128)(2,1)S(1)}, u32[]{:S(2)}, u32[]{:S(2)}) collective-permute-start(bf16[16,5632]{1,0:T(8,128)(2,1)S(1)} %slice.47), channel_id=1, source_target_pairs={{0,128},{128,256},{256,384},{384,0},{1,129},{129,257},{257,385},{3... | collective-permute-start | bytes 540680 | tf_op jit(solution)/shard_map/ppermute | solution.py:76
  87.1 6.4 %collective-permute-start.10 = (bf16[64,5632]{1,0:T(8,128)(2,1)S(1)}, bf16[64,5632]{1,0:T(8,128)(2,1)S(1)}, u32[]{:S(2)}, u32[]{:S(2)}) collective-permute-start(bf16[64,5632]{1,0:T(8,128)(2,1)S(1)} %collective-permute-done.9), channel_id=1, source_target_pairs={{0,16},{16,0},{1,17},{17,1},{2,18},{18,2},{3,19},{19,3},{4,20},{20... | collective-permute-start | bytes 2162696 | tf_op jit(solution)/shard_map/ppermute | solution.py:126
  98.4 21.6 %all-to-all-start.2 = ((bf16[16,8,1536]{2,1,0:T(8,128)(2,1)}), bf16[16,8,1536]{2,1,0:T(8,128)(2,1)S(1)}, u32[]{:S(2)}, u32[]{:S(2)}) async-start(bf16[16,8,1536]{2,1,0:T(8,128)(2,1)} %fusion.11), calls=%async_computation.2 | async-start | bytes 786432 | tf_op jit(solution)/shard_map/all_to_all | solution.py:31
  106.5 3.5 %collective-permute-start.11 = (f32[]{:T(128)}, f32[]{:T(128)}, u32[]{:S(2)}, u32[]{:S(2)}) collective-permute-start(f32[]{:T(128)} %get-tuple-element.15), channel_id=1, source_target_pairs={{0,16},{16,0},{1,17},{17,1},{2,18},{18,2},{3,19},{19,3},{4,20},{20... | collective-permute-start | bytes 20 | tf_op jit(solution)/shard_map/ppermute | solution.py:133
  145.7 5.9 %collective-permute-start.12 = (bf16[128,1536]{1,0:T(8,128)(2,1)S(1)}, bf16[128,1536]{1,0:T(8,128)(2,1)S(1)}, u32[]{:S(2)}, u32[]{:S(2)}) collective-permute-start(bf16[128,1536]{1,0:T(8,128)(2,1)S(1)} %slice.63), channel_id=1, source_target_pairs={{0,16},{16,0},{1,17},{17,1},{2,18},{18,2},{3,19},{19,3},{4,20},{20... | collective-permute-start | bytes 1179656 | tf_op jit(solution)/shard_map/ppermute | solution.py:144
  163.5 12.0 %all-to-all-start.5 = ((bf16[16,3,1536]{2,1,0:T(4,128)(2,1)}), bf16[16,3,1536]{2,1,0:T(4,128)(2,1)S(1)}, u32[]{:S(2)}, u32[]{:S(2)}) async-start(bf16[16,3,1536]{2,1,0:T(4,128)(2,1)} %broadcast_in_dim.44), calls=%async_computation.5 | async-start | bytes 393216 | tf_op jit(solution)/shard_map/all_to_all | solution.py:31

commit v15 on v12

--- a/solution.py
+++ b/solution.py
@@ -95,18 +95,20 @@
     target = normal(got[:, :, full:].astype(jnp.float32), (0, 2))
     target = target.transpose(1, 0, 2).reshape(mine, -1)
 
-    mine_rows = jnp.concatenate([student, target], axis=1)
+    mine_rows, hidden_sent = lax.optimization_barrier(
+        (jnp.concatenate([student, target], axis=1), hidden)
+    )
     here = gather(jnp.concatenate([student, -target], axis=1), ("y",))
     here = here.reshape(-1, here.shape[2])
-    rows_1 = from_peer(mine_rows, STRIDE, 1)
-    later, rows_1 = lax.optimization_barrier((mine_rows, rows_1))
-    near = [mine_rows, rows_1] + [from_peer(later, STRIDE, step) for step in (2, 3)]
-    near, here = lax.optimization_barrier((jnp.concatenate(near, axis=0), here))
+    hidden_there = lax.ppermute(hidden_sent, "c", SWAP)
+    mine_rows, hidden_there = lax.optimization_barrier((mine_rows, hidden_there))
+    near = [mine_rows] + [from_peer(mine_rows, STRIDE, step) for step in (1, 2, 3)]
+    near = jnp.concatenate(near, axis=0)
+    _, here = lax.optimization_barrier((near, here))
     far_1 = from_peer(near, "x", 1)
     there = lax.ppermute(here, "za", SWAP)
     here_core = lax.ppermute(here, "c", SWAP)
-    later, here_core = lax.optimization_barrier((near, here_core))
-    far = [near, far_1] + [from_peer(later, "x", step) for step in (2, 3)]
+    far = [near, far_1] + [from_peer(near, "x", step) for step in (2, 3)]
     far = lax.optimization_barrier((there, *far))[1:]
     row_block = jnp.concatenate(far, axis=0)
     columns = jnp.concatenate(
@@ -116,10 +118,7 @@
     differ = dot(row_block, columns, ROWS_T)
     differ = in_order(differ)
     squares = jnp.sum(differ * differ)
-    squares, hidden_sent = lax.optimization_barrier((squares, hidden))
     squares = squares + lax.ppermute(squares, "c", SWAP)
-    hidden_there = lax.ppermute(hidden_sent, "c", SWAP)
-    squares, hidden_there = lax.optimization_barrier((squares, hidden_there))
     partial_grad = sum(dot(part, s_cols) for part in pieces(differ)[::-1])
     partial_grad = partial_grad.astype(jnp.bfloat16).reshape(-1, mine, full)
     grad_unit = 4.0 * jnp.sum(exchange(partial_grad, ROW).astype(jnp.float32), axis=0)

time: 188 us -> 183 us (0.973)
  blocking collectives: 76.5 us -> 72 us
    all_to_all x3, waiting for transfers between devices: 5.37 us -> 15.3 us  [exchange(): return lax.all_to_all(blocks, axes, split_axis=0, concat_axis=0, tiled=True)]
    ppermute x6, waiting for transfers between devices: 20 us -> 13.1 us  [from_peer(): return lax.ppermute(block, axis, [(at, at ^ step) for at in range(4)])]
    all_to_all x3, blocking collectives: 72 us -> 67.4 us  [exchange(): return lax.all_to_all(blocks, axes, split_axis=0, concat_axis=0, tiled=True)]
    all_to_all x3, starting transfers between devices: 16.2 us -> 13 us  [exchange(): return lax.all_to_all(blocks, axes, split_axis=0, concat_axis=0, tiled=True)]
    ppermute x1, waiting for transfers between devices: 6.72 us -> 4.23 us  [body(): there = lax.ppermute(here, 'za', SWAP)]
    ppermute x1, starting transfers between devices: 4.73 us -> 2.65 us  [body(): here_core = lax.ppermute(here, 'c', SWAP)]
    ppermute x6, starting transfers between devices: 18.9 us -> 21 us  [from_peer(): return lax.ppermute(block, axis, [(at, at ^ step) for at in range(4)])]
  transfers between devices with their start and end apart: 15 -> 15, of which waited for: 9 -> 10; matrix products, arithmetic and copies ran while one was open for 1% -> 2% of each run, Pallas kernels for 0% -> 0%
where the time goes in v15:
time: 183 us; the launch traced here: 182 us
  blocking collectives  72 us (39%)
  starting transfers between devices  55.2 us (30%)
  waiting for transfers between devices  34.7 us (19%)
  between operations  7.79 us (4%)
  matrix products  4.84 us (3%)
  other arithmetic  4.3 us (2%)
  local copies, waits for them, and re-layouts  3.16 us (2%)
    all_to_all x3, blocking collectives, exchange(): return lax.all_to_all(blocks, axes, split_axis=0, concat_axis=0, tiled=True)  67.4 us
    ppermute x6, starting transfers between devices, from_peer(): return lax.ppermute(block, axis, [(at, at ^ step) for at in range(4)])  21 us
    all_to_all x3, waiting for transfers between devices, exchange(): return lax.all_to_all(blocks, axes, split_axis=0, concat_axis=0, tiled=True)  15.3 us
    ppermute x6, waiting for transfers between devices, from_peer(): return lax.ppermute(block, axis, [(at, at ^ step) for at in range(4)])  13.1 us
    all_to_all x3, starting transfers between devices, exchange(): return lax.all_to_all(blocks, axes, split_axis=0, concat_axis=0, tiled=True)  13 us
    ppermute x1, starting transfers between devices, body(): hidden_there = lax.ppermute(hidden_sent, 'c', SWAP)  4.89 us
    dot_general x8, matrix products, dot(): return lax.dot_general(a, b, dims, preferred_element_type=jnp.float32)  4.84 us
    all_gather x1, blocking collectives, body(): lax.all_gather(gather(summed, XZ).reshape(half, full), 'c', axis=0, tiled...  4.55 us
  transfers between devices with their start and end apart: 15, of which 10 were waited for; matrix products, arithmetic and copies ran while one was open for 2% of the time, Pallas kernels for 0%

profile of v15, /device:TPU:1, one launch (start us, length us, event | category | flops | bytes accessed | tf_op | source)
XLA Modules:
  0.0 182.0 jit_solution(7402060164928851877)
XLA Ops:
  0.6 0.0 copy-start
  0.6 0.0 copy-start.1
  0.7 0.9 copy-done
  1.6 1.0 fusion.2
  2.6 0.9 pad_maximum_fusion
  3.5 32.0 %all_to_all.30 = bf16[16,8,1792]{2,1,0:T(8,128)(2,1)S(1)} all-to-all(bf16[16,8,1792]{2,1,0:T(8,128)(2,1)S(1)} %pad_maximum_fusion), channel_id=1, replica_groups=mesh['x'=4,'zb'=2,'za'=2,'c'=2,'zh'=2,'y'=8] {'zh','y'}, dimensions={0} | all-to-all | bytes 917504 | tf_op jit(solution)/shard_map/all_to_all | solution.py:31
  35.5 0.1 convert_reduce_fusion.1
  35.5 0.1 multiply_reduce_fusion.2
  35.7 0.1 multiply_convert_fusion.1
  35.8 0.1 fusion.18
  35.9 0.1 fusion.19
  36.1 4.9 %collective-permute-start = (bf16[128,96]{0,1:T(8,128)(2,1)S(1)}, bf16[128,96]{0,1:T(8,128)(2,1)S(1)}, u32[]{:S(2)}, u32[]{:S(2)}) collective-permute-start(bf16[128,96]{0,1:T(8,128)(2,1)S(1)} %copy-done.1), channel_id=1, source_target_pairs={{0,16},{16,0},{1,17},{17,1},{2,18},{18,2},{3,19},{19,3},{4,20},{20... | collective-permute-start | bytes 73736 | tf_op jit(solution)/shard_map/ppermute | solution.py:103
  41.0 0.9 broadcast_in_dim.37
  41.9 4.6 %all-to-all-start.1 = ((bf16[8,8,5632]{2,1,0:T(8,128)(2,1)}), bf16[8,8,5632]{2,1,0:T(8,128)(2,1)S(1)}, u32[]{:S(2)}, u32[]{:S(2)}) async-start(bf16[8,8,5632]{2,1,0:T(8,128)(2,1)} %broadcast_in_dim.37), calls=%async_computation.1 | async-start | bytes 1441792 | tf_op jit(solution)/shard_map/all_to_all | solution.py:31
  46.5 0.0 collective-permute-done
  46.5 1.9 %collective-permute-start.1 = (bf16[8,5632]{1,0:T(8,128)(2,1)S(1)}, bf16[8,5632]{1,0:T(8,128)(2,1)S(1)}, u32[]{:S(2)}, u32[]{:S(2)}) collective-permute-start(bf16[8,5632]{1,0:T(8,128)(2,1)S(1)} %get-tuple-element.14), channel_id=1, source_target_pairs={{0,8},{8,0},{64,72},{72,64},{1,9},{9,1},{65,73},{73,65},{2,10},{10... | collective-permute-start | bytes 270344 | tf_op jit(solution)/shard_map/ppermute | solution.py:61
  48.4 4.2 %collective-permute-start.2 = (bf16[8,5632]{1,0:T(8,128)(2,1)S(1)}, bf16[8,5632]{1,0:T(8,128)(2,1)S(1)}, u32[]{:S(2)}, u32[]{:S(2)}) collective-permute-start(bf16[8,5632]{1,0:T(8,128)(2,1)S(1)} %get-tuple-element.14), channel_id=1, source_target_pairs={{0,64},{8,72},{64,0},{72,8},{1,65},{9,73},{65,1},{73,9},{2,66},{10... | collective-permute-start | bytes 270344 | tf_op jit(solution)/shard_map/ppermute | solution.py:61
  52.7 5.2 %collective-permute-start.3 = (bf16[8,5632]{1,0:T(8,128)(2,1)S(1)}, bf16[8,5632]{1,0:T(8,128)(2,1)S(1)}, u32[]{:S(2)}, u32[]{:S(2)}) collective-permute-start(bf16[8,5632]{1,0:T(8,128)(2,1)S(1)} %get-tuple-element.14), channel_id=1, source_target_pairs={{0,72},{8,64},{64,8},{72,0},{1,73},{9,65},{65,9},{73,1},{2,74},{10... | collective-permute-start | bytes 270344 | tf_op jit(solution)/shard_map/ppermute | solution.py:61
  57.9 0.0 collective-permute-done.1
  57.9 2.2 %collective-permute-done.2 = bf16[8,5632]{1,0:T(8,128)(2,1)S(1)} collective-permute-done((bf16[8,5632]{1,0:T(8,128)(2,1)S(1)}, bf16[8,5632]{1,0:T(8,128)(2,1)S(1)}, u32[]{:S(2)}, u32[]{:S(2)}) %collective-permute-start.2) | collective-permute-done | bytes 90144 | tf_op jit(solution)/shard_map/ppermute | solution.py:61
  60.2 0.2 collective-permute-done.3
  60.4 8.3 %all-to-all-done.1 = bf16[8,8,5632]{2,1,0:T(8,128)(2,1)S(1)} async-done(((bf16[8,8,5632]{2,1,0:T(8,128)(2,1)}), bf16[8,8,5632]{2,1,0:T(8,128)(2,1)S(1)}, u32[]{:S(2)}, u32[]{:S(2)}) %all-to-all-start.1) | async-done | bytes 720928 | tf_op jit(solution)/shard_map/all_to_all | solution.py:31
  68.7 2.5 %collective-permute-start.4 = (bf16[64,5632]{1,0:T(8,128)(2,1)S(1)}, bf16[64,5632]{1,0:T(8,128)(2,1)S(1)}, u32[]{:S(2)}, u32[]{:S(2)}) collective-permute-start(bf16[64,5632]{1,0:T(8,128)(2,1)S(1)} %bitcast.29), channel_id=1, source_target_pairs={{0,32},{32,0},{1,33},{33,1},{2,34},{34,2},{3,35},{35,3},{4,36},{36... | collective-permute-start | bytes 2162696 | tf_op jit(solution)/shard_map/ppermute | solution.py:109
  71.2 2.7 %collective-permute-start.8 = (bf16[64,5632]{1,0:T(8,128)(2,1)S(1)}, bf16[64,5632]{1,0:T(8,128)(2,1)S(1)}, u32[]{:S(2)}, u32[]{:S(2)}) collective-permute-start(bf16[64,5632]{1,0:T(8,128)(2,1)S(1)} %bitcast.30), channel_id=1, source_target_pairs={{0,16},{16,0},{1,17},{17,1},{2,18},{18,2},{3,19},{19,3},{4,20},{20... | collective-permute-start | bytes 2162696 | tf_op jit(solution)/shard_map/ppermute | solution.py:110
  73.9 3.1 %collective-permute-start.5 = (bf16[32,5632]{1,0:T(8,128)(2,1)S(1)}, bf16[32,5632]{1,0:T(8,128)(2,1)S(1)}, u32[]{:S(2)}, u32[]{:S(2)}) collective-permute-start(bf16[32,5632]{1,0:T(8,128)(2,1)S(1)} %constant_dynamic-update-slice_fusion), channel_id=1, source_target_pairs={{0,128},{128,0},{256,384},{384,256},{1,129},{129,1},{257,385},{385... | collective-permute-start | bytes 1081352 | tf_op jit(solution)/shard_map/ppermute | solution.py:61
  77.1 4.4 %collective-permute-start.6 = (bf16[32,5632]{1,0:T(8,128)(2,1)S(1)}, bf16[32,5632]{1,0:T(8,128)(2,1)S(1)}, u32[]{:S(2)}, u32[]{:S(2)}) collective-permute-start(bf16[32,5632]{1,0:T(8,128)(2,1)S(1)} %constant_dynamic-update-slice_fusion), channel_id=1, source_target_pairs={{0,256},{128,384},{256,0},{384,128},{1,257},{129,385},{257,1},{385... | collective-permute-start | bytes 1081352 | tf_op jit(solution)/shard_map/ppermute | solution.py:61
  81.4 2.1 %collective-permute-start.7 = (bf16[32,5632]{1,0:T(8,128)(2,1)S(1)}, bf16[32,5632]{1,0:T(8,128)(2,1)S(1)}, u32[]{:S(2)}, u32[]{:S(2)}) collective-permute-start(bf16[32,5632]{1,0:T(8,128)(2,1)S(1)} %constant_dynamic-update-slice_fusion), channel_id=1, source_target_pairs={{0,384},{128,256},{256,128},{384,0},{1,385},{129,257},{257,129},{3... | collective-permute-start | bytes 1081352 | tf_op jit(solution)/shard_map/ppermute | solution.py:61
  83.6 4.2 %collective-permute-done.4 = bf16[64,5632]{1,0:T(8,128)(2,1)S(1)} collective-permute-done((bf16[64,5632]{1,0:T(8,128)(2,1)S(1)}, bf16[64,5632]{1,0:T(8,128)(2,1)S(1)}, u32[]{:S(2)}, u32[]{:S(2)}) %collective-permute-start.4) | collective-permute-done | bytes 720928 | tf_op jit(solution)/shard_map/ppermute | solution.py:109
  87.8 3.2 %collective-permute-start.9 = (bf16[64,5632]{1,0:T(8,128)(2,1)S(1)}, bf16[64,5632]{1,0:T(8,128)(2,1)S(1)}, u32[]{:S(2)}, u32[]{:S(2)}) collective-permute-start(bf16[64,5632]{1,0:T(8,128)(2,1)S(1)} %collective-permute-done.4), channel_id=1, source_target_pairs={{0,16},{16,0},{1,17},{17,1},{2,18},{18,2},{3,19},{19,3},{4,20},{20... | collective-permute-start | bytes 2162696 | tf_op jit(solution)/shard_map/ppermute | solution.py:115
  91.0 0.0 collective-permute-done.8
  91.1 0.0 collective-permute-done.5
  91.1 4.7 %collective-permute-done.6 = bf16[32,5632]{1,0:T(8,128)(2,1)S(1)} collective-permute-done((bf16[32,5632]{1,0:T(8,128)(2,1)S(1)}, bf16[32,5632]{1,0:T(8,128)(2,1)S(1)}, u32[]{:S(2)}, u32[]{:S(2)}) %collective-permute-start.6) | collective-permute-done | bytes 360480 | tf_op jit(solution)/shard_map/ppermute | solution.py:61
  95.8 5.9 %collective-permute-done.7 = bf16[32,5632]{1,0:T(8,128)(2,1)S(1)} collective-permute-done((bf16[32,5632]{1,0:T(8,128)(2,1)S(1)}, bf16[32,5632]{1,0:T(8,128)(2,1)S(1)}, u32[]{:S(2)}, u32[]{:S(2)}) %collective-permute-start.7) | collective-permute-done | bytes 360480 | tf_op jit(solution)/shard_map/ppermute | solution.py:61
  101.8 0.0 collective-permute-done.9
  101.9 1.0 fusion.5
  103.0 0.6 multiply_reduce_fusion
  103.6 0.3 fusion.13
  103.9 0.3 fusion.15
  104.2 1.0 fusion.3
  105.2 3.6 %all-to-all-start.2 = ((bf16[16,8,1536]{2,1,0:T(8,128)(2,1)}), bf16[16,8,1536]{2,1,0:T(8,128)(2,1)S(1)}, u32[]{:S(2)}, u32[]{:S(2)}) async-start(bf16[16,8,1536]{2,1,0:T(8,128)(2,1)} %fusion.3), calls=%async_computation.2 | async-start | bytes 786432 | tf_op jit(solution)/shard_map/all_to_all | solution.py:31
  108.8 3.4 %collective-permute-start.10 = (f32[]{:T(128)}, f32[]{:T(128)}, u32[]{:S(2)}, u32[]{:S(2)}) collective-permute-start(f32[]{:T(128)} %get-tuple-element.21), channel_id=1, source_target_pairs={{0,16},{16,0},{1,17},{17,1},{2,18},{18,2},{3,19},{19,3},{4,20},{20... | collective-permute-start | bytes 20 | tf_op jit(solution)/shard_map/ppermute | solution.py:121
  112.2 0.9 collective-permute-done.10
  118.1 1.7 all-to-all-done.2
  119.8 0.1 convert_reduce_fusion
  119.9 0.2 multiply_reduce_fusion.1
  120.1 0.1 multiply_convert_fusion
  120.2 25.2 %all_to_all.31 = bf16[16,8,1664]{2,1,0:T(8,128)(2,1)S(1)} all-to-all(bf16[16,8,1664]{2,1,0:T(8,128)(2,1)S(1)} %broadcast_in_dim.42), channel_id=1, replica_groups=mesh['x'=4,'zb'=2,'za'=2,'c'=2,'zh'=2,'y'=8] {'zh','y'}, dimensions={0} | all-to-all | bytes 851968 | tf_op jit(solution)/shard_map/all_to_all | solution.py:31
  145.5 4.5 %collective-permute-start.11 = (bf16[128,1536]{1,0:T(8,128)(2,1)S(1)}, bf16[128,1536]{1,0:T(8,128)(2,1)S(1)}, u32[]{:S(2)}, u32[]{:S(2)}) collective-permute-start(bf16[128,1536]{1,0:T(8,128)(2,1)S(1)} %slice.32), channel_id=1, source_target_pairs={{0,16},{16,0},{1,17},{17,1},{2,18},{18,2},{3,19},{19,3},{4,20},{20... | collective-permute-start | bytes 1179656 | tf_op jit(solution)/shard_map/ppermute | solution.py:132
  150.0 0.2 fusion.22
  150.2 1.1 collective-permute-done.11
  151.3 0.2 fusion.4
  151.5 0.1 reshape.60
  151.6 0.1 broadcast_in_dim.43
  151.6 0.2 pad_maximum_fusion.1
  151.8 10.2 %all_to_all.32 = bf16[16,4,1536]{2,1,0:T(4,128)(2,1)S(1)} all-to-all(bf16[16,4,1536]{2,1,0:T(4,128)(2,1)S(1)} %pad_maximum_fusion.1), channel_id=1, replica_groups=mesh['x'=4,'zb'=2,'za'=2,'c'=2,'zh'=2,'y'=8] {'x','zb','za'}, dimensions={0} | all-to-all | bytes 393216 | tf_op jit(solution)/shard_map/all_to_all | solution.py:31
  162.1 0.1 convert_reduce_fusion.2
  162.2 0.7 broadcast_in_dim.44
  162.9 4.8 %all-to-all-start.5 = ((bf16[16,3,1536]{2,1,0:T(4,128)(2,1)}), bf16[16,3,1536]{2,1,0:T(4,128)(2,1)S(1)}, u32[]{:S(2)}, u32[]{:S(2)}) async-start(bf16[16,3,1536]{2,1,0:T(4,128)(2,1)} %broadcast_in_dim.44), calls=%async_computation.5 | async-start | bytes 393216 | tf_op jit(solution)/shard_map/all_to_all | solution.py:31
  167.8 0.9 fusion.30
  168.7 0.6 slice_reduce_fusion.1
  169.9 5.4 %all-to-all-done.5 = bf16[16,3,1536]{2,1,0:T(4,128)(2,1)S(1)} async-done(((bf16[16,3,1536]{2,1,0:T(4,128)(2,1)}), bf16[16,3,1536]{2,1,0:T(4,128)(2,1)S(1)}, u32[]{:S(2)}, u32[]{:S(2)}) %all-to-all-start.5) | async-done | bytes 147488 | tf_op jit(solution)/shard_map/all_to_all | solution.py:31
  175.3 0.1 reshape.61
  175.4 4.6 %all_gather.3 = bf16[96,1536]{1,0:T(8,128)(2,1)S(1)} all-gather(bf16[48,1536]{1,0:T(8,128)(2,1)S(1)} %reshape.61), channel_id=1, replica_groups=mesh['x'=4,'zb'=2,'za'=2,'c'=2,'zh'=2,'y'=8] {'c'}, dimensions={0}, use_global_device_ids=true | all-gather | bytes 442368 | tf_op jit(solution)/shard_map/all_gather | solution.py:153
  180.0 0.9 convert_element_type.72
  (26 shorter events, 0.5 us)
Async XLA Ops:
  0.6 1.0 copy-start
  0.6 35.4 %copy-start.1 = (bf16[128,96]{0,1:T(8,128)(2,1)S(1)}, bf16[128,96]{0,1:T(8,128)(2,1)}, u32[]{:S(2)}) copy-start(bf16[128,96]{0,1:T(8,128)(2,1)} %param.3) | copy-start | bytes 73732
  36.1 10.4 %collective-permute-start = (bf16[128,96]{0,1:T(8,128)(2,1)S(1)}, bf16[128,96]{0,1:T(8,128)(2,1)S(1)}, u32[]{:S(2)}, u32[]{:S(2)}) collective-permute-start(bf16[128,96]{0,1:T(8,128)(2,1)S(1)} %copy-done.1), channel_id=1, source_target_pairs={{0,16},{16,0},{1,17},{17,1},{2,18},{18,2},{3,19},{19,3},{4,20},{20... | collective-permute-start | bytes 73736 | tf_op jit(solution)/shard_map/ppermute | solution.py:103
  41.9 26.8 %all-to-all-start.1 = ((bf16[8,8,5632]{2,1,0:T(8,128)(2,1)}), bf16[8,8,5632]{2,1,0:T(8,128)(2,1)S(1)}, u32[]{:S(2)}, u32[]{:S(2)}) async-start(bf16[8,8,5632]{2,1,0:T(8,128)(2,1)} %broadcast_in_dim.37), calls=%async_computation.1 | async-start | bytes 1441792 | tf_op jit(solution)/shard_map/all_to_all | solution.py:31
  46.5 11.4 %collective-permute-start.1 = (bf16[8,5632]{1,0:T(8,128)(2,1)S(1)}, bf16[8,5632]{1,0:T(8,128)(2,1)S(1)}, u32[]{:S(2)}, u32[]{:S(2)}) collective-permute-start(bf16[8,5632]{1,0:T(8,128)(2,1)S(1)} %get-tuple-element.14), channel_id=1, source_target_pairs={{0,8},{8,0},{64,72},{72,64},{1,9},{9,1},{65,73},{73,65},{2,10},{10... | collective-permute-start | bytes 270344 | tf_op jit(solution)/shard_map/ppermute | solution.py:61
  48.4 11.7 %collective-permute-start.2 = (bf16[8,5632]{1,0:T(8,128)(2,1)S(1)}, bf16[8,5632]{1,0:T(8,128)(2,1)S(1)}, u32[]{:S(2)}, u32[]{:S(2)}) collective-permute-start(bf16[8,5632]{1,0:T(8,128)(2,1)S(1)} %get-tuple-element.14), channel_id=1, source_target_pairs={{0,64},{8,72},{64,0},{72,8},{1,65},{9,73},{65,1},{73,9},{2,66},{10... | collective-permute-start | bytes 270344 | tf_op jit(solution)/shard_map/ppermute | solution.py:61
  52.7 7.7 %collective-permute-start.3 = (bf16[8,5632]{1,0:T(8,128)(2,1)S(1)}, bf16[8,5632]{1,0:T(8,128)(2,1)S(1)}, u32[]{:S(2)}, u32[]{:S(2)}) collective-permute-start(bf16[8,5632]{1,0:T(8,128)(2,1)S(1)} %get-tuple-element.14), channel_id=1, source_target_pairs={{0,72},{8,64},{64,8},{72,0},{1,73},{9,65},{65,9},{73,1},{2,74},{10... | collective-permute-start | bytes 270344 | tf_op jit(solution)/shard_map/ppermute | solution.py:61
  68.7 19.1 %collective-permute-start.4 = (bf16[64,5632]{1,0:T(8,128)(2,1)S(1)}, bf16[64,5632]{1,0:T(8,128)(2,1)S(1)}, u32[]{:S(2)}, u32[]{:S(2)}) collective-permute-start(bf16[64,5632]{1,0:T(8,128)(2,1)S(1)} %bitcast.29), channel_id=1, source_target_pairs={{0,32},{32,0},{1,33},{33,1},{2,34},{34,2},{3,35},{35,3},{4,36},{36... | collective-permute-start | bytes 2162696 | tf_op jit(solution)/shard_map/ppermute | solution.py:109
  71.2 19.8 %collective-permute-start.8 = (bf16[64,5632]{1,0:T(8,128)(2,1)S(1)}, bf16[64,5632]{1,0:T(8,128)(2,1)S(1)}, u32[]{:S(2)}, u32[]{:S(2)}) collective-permute-start(bf16[64,5632]{1,0:T(8,128)(2,1)S(1)} %bitcast.30), channel_id=1, source_target_pairs={{0,16},{16,0},{1,17},{17,1},{2,18},{18,2},{3,19},{19,3},{4,20},{20... | collective-permute-start | bytes 2162696 | tf_op jit(solution)/shard_map/ppermute | solution.py:110
  73.9 17.2 %collective-permute-start.5 = (bf16[32,5632]{1,0:T(8,128)(2,1)S(1)}, bf16[32,5632]{1,0:T(8,128)(2,1)S(1)}, u32[]{:S(2)}, u32[]{:S(2)}) collective-permute-start(bf16[32,5632]{1,0:T(8,128)(2,1)S(1)} %constant_dynamic-update-slice_fusion), channel_id=1, source_target_pairs={{0,128},{128,0},{256,384},{384,256},{1,129},{129,1},{257,385},{385... | collective-permute-start | bytes 1081352 | tf_op jit(solution)/shard_map/ppermute | solution.py:61
  77.1 18.8 %collective-permute-start.6 = (bf16[32,5632]{1,0:T(8,128)(2,1)S(1)}, bf16[32,5632]{1,0:T(8,128)(2,1)S(1)}, u32[]{:S(2)}, u32[]{:S(2)}) collective-permute-start(bf16[32,5632]{1,0:T(8,128)(2,1)S(1)} %constant_dynamic-update-slice_fusion), channel_id=1, source_target_pairs={{0,256},{128,384},{256,0},{384,128},{1,257},{129,385},{257,1},{385... | collective-permute-start | bytes 1081352 | tf_op jit(solution)/shard_map/ppermute | solution.py:61
  81.4 20.3 %collective-permute-start.7 = (bf16[32,5632]{1,0:T(8,128)(2,1)S(1)}, bf16[32,5632]{1,0:T(8,128)(2,1)S(1)}, u32[]{:S(2)}, u32[]{:S(2)}) collective-permute-start(bf16[32,5632]{1,0:T(8,128)(2,1)S(1)} %constant_dynamic-update-slice_fusion), channel_id=1, source_target_pairs={{0,384},{128,256},{256,128},{384,0},{1,385},{129,257},{257,129},{3... | collective-permute-start | bytes 1081352 | tf_op jit(solution)/shard_map/ppermute | solution.py:61
  87.8 14.0 %collective-permute-start.9 = (bf16[64,5632]{1,0:T(8,128)(2,1)S(1)}, bf16[64,5632]{1,0:T(8,128)(2,1)S(1)}, u32[]{:S(2)}, u32[]{:S(2)}) collective-permute-start(bf16[64,5632]{1,0:T(8,128)(2,1)S(1)} %collective-permute-done.4), channel_id=1, source_target_pairs={{0,16},{16,0},{1,17},{17,1},{2,18},{18,2},{3,19},{19,3},{4,20},{20... | collective-permute-start | bytes 2162696 | tf_op jit(solution)/shard_map/ppermute | solution.py:115
  105.2 14.6 %all-to-all-start.2 = ((bf16[16,8,1536]{2,1,0:T(8,128)(2,1)}), bf16[16,8,1536]{2,1,0:T(8,128)(2,1)S(1)}, u32[]{:S(2)}, u32[]{:S(2)}) async-start(bf16[16,8,1536]{2,1,0:T(8,128)(2,1)} %fusion.3), calls=%async_computation.2 | async-start | bytes 786432 | tf_op jit(solution)/shard_map/all_to_all | solution.py:31
  108.8 4.3 %collective-permute-start.10 = (f32[]{:T(128)}, f32[]{:T(128)}, u32[]{:S(2)}, u32[]{:S(2)}) collective-permute-start(f32[]{:T(128)} %get-tuple-element.21), channel_id=1, source_target_pairs={{0,16},{16,0},{1,17},{17,1},{2,18},{18,2},{3,19},{19,3},{4,20},{20... | collective-permute-start | bytes 20 | tf_op jit(solution)/shard_map/ppermute | solution.py:121
  145.5 5.8 %collective-permute-start.11 = (bf16[128,1536]{1,0:T(8,128)(2,1)S(1)}, bf16[128,1536]{1,0:T(8,128)(2,1)S(1)}, u32[]{:S(2)}, u32[]{:S(2)}) collective-permute-start(bf16[128,1536]{1,0:T(8,128)(2,1)S(1)} %slice.32), channel_id=1, source_target_pairs={{0,16},{16,0},{1,17},{17,1},{2,18},{18,2},{3,19},{19,3},{4,20},{20... | collective-permute-start | bytes 1179656 | tf_op jit(solution)/shard_map/ppermute | solution.py:132
  162.9 12.4 %all-to-all-start.5 = ((bf16[16,3,1536]{2,1,0:T(4,128)(2,1)}), bf16[16,3,1536]{2,1,0:T(4,128)(2,1)S(1)}, u32[]{:S(2)}, u32[]{:S(2)}) async-start(bf16[16,3,1536]{2,1,0:T(4,128)(2,1)} %broadcast_in_dim.44), calls=%async_computation.5 | async-start | bytes 393216 | tf_op jit(solution)/shard_map/all_to_all | solution.py:31

commit v16 on v10

--- a/solution.py
+++ b/solution.py
@@ -131,7 +131,11 @@
 
     left = lax.dynamic_slice_in_dim(hidden, core * half, half, 1)
     left_there = lax.dynamic_slice_in_dim(hidden_there, core * half, half, 1)
-    proj_piece = dot(left, piece, COLS_T) + dot(left_there, piece_there, COLS_T)
+    proj_piece = dot(
+        jnp.concatenate([left, left_there], axis=0),
+        jnp.concatenate([piece, piece_there], axis=0),
+        COLS_T,
+    )
 
     loss_row = jnp.sum(
         wide.reshape(group_fs, mine, -1)[:, 0, full:].astype(jnp.float32), axis=0

time: 182 us -> 182 us (level)
    dot_general x8 -> x7, matrix products: 6.21 us -> 6.07 us  [dot(): return lax.dot_general(a, b, dims, preferred_element_type=jnp.float32)]
where the time goes in v16:
time: 182 us; the launch traced here: 181 us
  blocking collectives  73.9 us (41%)
  starting transfers between devices  58.6 us (32%)
  waiting for transfers between devices  22.6 us (12%)
  local copies, waits for them, and re-layouts  7.86 us (4%)
  between operations  7.72 us (4%)
  matrix products  6.07 us (3%)
  other arithmetic  4.36 us (2%)
    all_to_all x3, blocking collectives, exchange(): return lax.all_to_all(blocks, axes, split_axis=0, concat_axis=0, tiled=True)  69.4 us
    ppermute x6, starting transfers between devices, around(): lax.ppermute(block, axis, [(at, at ^ step) for at in range(4)])  21.9 us
    all_to_all x3, starting transfers between devices, exchange(): return lax.all_to_all(blocks, axes, split_axis=0, concat_axis=0, tiled=True)  15.5 us
    all_to_all x3, waiting for transfers between devices, exchange(): return lax.all_to_all(blocks, axes, split_axis=0, concat_axis=0, tiled=True)  11.8 us
    dot_general x7, matrix products, dot(): return lax.dot_general(a, b, dims, preferred_element_type=jnp.float32)  6.07 us
    ppermute x1, waiting for transfers between devices, body(): there = lax.ppermute(here, 'za', SWAP)  5.14 us
    ppermute x1, starting transfers between devices, body(): hidden_there = lax.ppermute(hidden_sent, 'c', SWAP)  4.89 us
    ppermute x1, starting transfers between devices, body(): piece_there = lax.ppermute(piece, 'c', SWAP)  4.72 us
  transfers between devices with their start and end apart: 15, of which 9 were waited for; matrix products, arithmetic and copies ran while one was open for 4% of the time, Pallas kernels for 0%

profile of v16, /device:TPU:1, one launch (start us, length us, event | category | flops | bytes accessed | tf_op | source)
XLA Modules:
  0.0 181.1 jit_solution(15860320370111301574)
XLA Ops:
  0.6 0.0 copy-start
  0.6 1.0 copy-done
  1.6 1.0 fusion.10
  2.6 0.9 pad_maximum_fusion.1
  3.5 32.0 %all_to_all.30 = bf16[16,8,1792]{2,1,0:T(8,128)(2,1)S(1)} all-to-all(bf16[16,8,1792]{2,1,0:T(8,128)(2,1)S(1)} %pad_maximum_fusion.1), channel_id=1, replica_groups=mesh['x'=4,'zb'=2,'za'=2,'c'=2,'zh'=2,'y'=8] {'zh','y'}, dimensions={0} | all-to-all | bytes 917504 | tf_op jit(solution)/shard_map/all_to_all | solution.py:31
  35.5 0.1 convert_reduce_fusion.1
  35.6 0.1 multiply_reduce_fusion.2
  35.7 0.1 multiply_convert_fusion.1
  35.8 0.1 fusion.15
  35.9 0.1 fusion.16
  36.1 4.9 %collective-permute-start = (bf16[128,96]{0,1:T(8,128)(2,1)S(1)}, bf16[128,96]{0,1:T(8,128)(2,1)S(1)}, u32[]{:S(2)}, u32[]{:S(2)}) collective-permute-start(bf16[128,96]{0,1:T(8,128)(2,1)S(1)} %copy-done.1), channel_id=1, source_target_pairs={{0,16},{16,0},{1,17},{17,1},{2,18},{18,2},{3,19},{19,3},{4,20},{20... | collective-permute-start | bytes 73736 | tf_op jit(solution)/shard_map/ppermute | solution.py:106
  41.0 0.9 broadcast_in_dim.37
  41.9 4.6 %all-to-all-start.1 = ((bf16[8,8,5632]{2,1,0:T(8,128)(2,1)}), bf16[8,8,5632]{2,1,0:T(8,128)(2,1)S(1)}, u32[]{:S(2)}, u32[]{:S(2)}) async-start(bf16[8,8,5632]{2,1,0:T(8,128)(2,1)} %broadcast_in_dim.37), calls=%async_computation.1 | async-start | bytes 1441792 | tf_op jit(solution)/shard_map/all_to_all | solution.py:31
  46.5 1.9 %collective-permute-start.1 = (bf16[8,5632]{1,0:T(8,128)(2,1)S(1)}, bf16[8,5632]{1,0:T(8,128)(2,1)S(1)}, u32[]{:S(2)}, u32[]{:S(2)}) collective-permute-start(bf16[8,5632]{1,0:T(8,128)(2,1)S(1)} %get-tuple-element.9), channel_id=1, source_target_pairs={{0,8},{8,0},{64,72},{72,64},{1,9},{9,1},{65,73},{73,65},{2,10},{10... | collective-permute-start | bytes 270344 | tf_op jit(solution)/shard_map/ppermute | solution.py:63
  48.5 0.6 constant_dynamic-update-slice_fusion.3
  49.1 4.2 %collective-permute-start.2 = (bf16[8,5632]{1,0:T(8,128)(2,1)S(1)}, bf16[8,5632]{1,0:T(8,128)(2,1)S(1)}, u32[]{:S(2)}, u32[]{:S(2)}) collective-permute-start(bf16[8,5632]{1,0:T(8,128)(2,1)S(1)} %get-tuple-element.9), channel_id=1, source_target_pairs={{0,64},{8,72},{64,0},{72,8},{1,65},{9,73},{65,1},{73,9},{2,66},{10... | collective-permute-start | bytes 270344 | tf_op jit(solution)/shard_map/ppermute | solution.py:63
  53.3 5.2 %collective-permute-start.3 = (bf16[8,5632]{1,0:T(8,128)(2,1)S(1)}, bf16[8,5632]{1,0:T(8,128)(2,1)S(1)}, u32[]{:S(2)}, u32[]{:S(2)}) collective-permute-start(bf16[8,5632]{1,0:T(8,128)(2,1)S(1)} %get-tuple-element.9), channel_id=1, source_target_pairs={{0,72},{8,64},{64,8},{72,0},{1,73},{9,65},{65,9},{73,1},{2,74},{10... | collective-permute-start | bytes 270344 | tf_op jit(solution)/shard_map/ppermute | solution.py:63
  58.6 0.7 constant_dynamic-update-slice_fusion.2
  59.2 0.4 collective-permute-done.2
  59.6 0.6 constant_dynamic-update-slice_fusion.1
  60.2 2.0 %collective-permute-done.3 = bf16[8,5632]{1,0:T(8,128)(2,1)S(1)} collective-permute-done((bf16[8,5632]{1,0:T(8,128)(2,1)S(1)}, bf16[8,5632]{1,0:T(8,128)(2,1)S(1)}, u32[]{:S(2)}, u32[]{:S(2)}) %collective-permute-start.3) | collective-permute-done | bytes 90144 | tf_op jit(solution)/shard_map/ppermute | solution.py:63
  62.3 0.7 constant_dynamic-update-slice_fusion
  62.9 3.1 %collective-permute-start.4 = (bf16[32,5632]{1,0:T(8,128)(2,1)S(1)}, bf16[32,5632]{1,0:T(8,128)(2,1)S(1)}, u32[]{:S(2)}, u32[]{:S(2)}) collective-permute-start(bf16[32,5632]{1,0:T(8,128)(2,1)S(1)} %get-tuple-element.16), channel_id=1, source_target_pairs={{0,128},{128,0},{256,384},{384,256},{1,129},{129,1},{257,385},{385... | collective-permute-start | bytes 1081352 | tf_op jit(solution)/shard_map/ppermute | solution.py:63
  66.0 2.7 %all-to-all-done.1 = bf16[8,8,5632]{2,1,0:T(8,128)(2,1)S(1)} async-done(((bf16[8,8,5632]{2,1,0:T(8,128)(2,1)}), bf16[8,8,5632]{2,1,0:T(8,128)(2,1)S(1)}, u32[]{:S(2)}, u32[]{:S(2)}) %all-to-all-start.1) | async-done | bytes 720928 | tf_op jit(solution)/shard_map/all_to_all | solution.py:31
  68.7 2.5 %collective-permute-start.8 = (bf16[64,5632]{1,0:T(8,128)(2,1)S(1)}, bf16[64,5632]{1,0:T(8,128)(2,1)S(1)}, u32[]{:S(2)}, u32[]{:S(2)}) collective-permute-start(bf16[64,5632]{1,0:T(8,128)(2,1)S(1)} %bitcast.30), channel_id=1, source_target_pairs={{0,32},{32,0},{1,33},{33,1},{2,34},{34,2},{3,35},{35,3},{4,36},{36... | collective-permute-start | bytes 2162696 | tf_op jit(solution)/shard_map/ppermute | solution.py:109
  71.3 4.7 %collective-permute-start.5 = (bf16[32,5632]{1,0:T(8,128)(2,1)S(1)}, bf16[32,5632]{1,0:T(8,128)(2,1)S(1)}, u32[]{:S(2)}, u32[]{:S(2)}) collective-permute-start(bf16[32,5632]{1,0:T(8,128)(2,1)S(1)} %get-tuple-element.16), channel_id=1, source_target_pairs={{0,256},{128,384},{256,0},{384,128},{1,257},{129,385},{257,1},{385... | collective-permute-start | bytes 1081352 | tf_op jit(solution)/shard_map/ppermute | solution.py:63
  76.0 2.8 %collective-permute-start.6 = (bf16[32,5632]{1,0:T(8,128)(2,1)S(1)}, bf16[32,5632]{1,0:T(8,128)(2,1)S(1)}, u32[]{:S(2)}, u32[]{:S(2)}) collective-permute-start(bf16[32,5632]{1,0:T(8,128)(2,1)S(1)} %get-tuple-element.16), channel_id=1, source_target_pairs={{0,384},{128,256},{256,128},{384,0},{1,385},{129,257},{257,129},{3... | collective-permute-start | bytes 1081352 | tf_op jit(solution)/shard_map/ppermute | solution.py:63
  78.7 0.8 constant_dynamic-update-slice_fusion.6
  79.5 3.2 %collective-permute-start.7 = (bf16[64,5632]{1,0:T(8,128)(2,1)S(1)}, bf16[64,5632]{1,0:T(8,128)(2,1)S(1)}, u32[]{:S(2)}, u32[]{:S(2)}) collective-permute-start(bf16[64,5632]{1,0:T(8,128)(2,1)S(1)} %bitcast.31), channel_id=1, source_target_pairs={{0,16},{16,0},{1,17},{17,1},{2,18},{18,2},{3,19},{19,3},{4,20},{20... | collective-permute-start | bytes 2162696 | tf_op jit(solution)/shard_map/ppermute | solution.py:111
  82.7 5.1 %collective-permute-done.8 = bf16[64,5632]{1,0:T(8,128)(2,1)S(1)} collective-permute-done((bf16[64,5632]{1,0:T(8,128)(2,1)S(1)}, bf16[64,5632]{1,0:T(8,128)(2,1)S(1)}, u32[]{:S(2)}, u32[]{:S(2)}) %collective-permute-start.8) | collective-permute-done | bytes 720928 | tf_op jit(solution)/shard_map/ppermute | solution.py:109
  87.9 3.2 %collective-permute-start.9 = (bf16[64,5632]{1,0:T(8,128)(2,1)S(1)}, bf16[64,5632]{1,0:T(8,128)(2,1)S(1)}, u32[]{:S(2)}, u32[]{:S(2)}) collective-permute-start(bf16[64,5632]{1,0:T(8,128)(2,1)S(1)} %collective-permute-done.8), channel_id=1, source_target_pairs={{0,16},{16,0},{1,17},{17,1},{2,18},{18,2},{3,19},{19,3},{4,20},{20... | collective-permute-start | bytes 2162696 | tf_op jit(solution)/shard_map/ppermute | solution.py:111
  91.1 0.7 constant_dynamic-update-slice_fusion.5
  91.8 1.0 collective-permute-done.6
  92.8 0.8 constant_dynamic-update-slice_fusion.4
  93.6 2.4 %fusion = f32[128,256]{1,0:T(8,128)S(1)} fusion(bf16[128,5632]{1,0:T(8,128)(2,1)} %constant_dynamic-update-slice_fusion.4, bf16[64,5632]{1,0:T(8,128)(2,1)S(1)} %collective-permute-done.9, bf16[64,5632]{1,0:T(8,128)(2,1)S(1)} %collective-permute-done.8, bf16[64,5632]{1,0:T(8,128)(2,1)S(1)} %collective-permute-done.7, bf16[64,5632]{1,0:T(8,128)(2,1)S(1)} %bitcast.32), kind=kOutput, calls=%fused_computation | convolution fusion | flops 380633088 | bytes 4456448 | tf_op jit(solution)/shard_map/dot_general | solution.py:20
  96.0 0.6 multiply_reduce_fusion
  96.7 0.1 pad_maximum_fusion
  96.8 0.3 fusion.27
  97.0 0.3 fusion.28
  97.3 1.0 fusion.11
  98.3 5.9 %all-to-all-start.2 = ((bf16[16,8,1536]{2,1,0:T(8,128)(2,1)}), bf16[16,8,1536]{2,1,0:T(8,128)(2,1)S(1)}, u32[]{:S(2)}, u32[]{:S(2)}) async-start(bf16[16,8,1536]{2,1,0:T(8,128)(2,1)} %fusion.11), calls=%async_computation.2 | async-start | bytes 786432 | tf_op jit(solution)/shard_map/all_to_all | solution.py:31
  104.2 2.7 %collective-permute-start.10 = (f32[]{:T(128)}, f32[]{:T(128)}, u32[]{:S(2)}, u32[]{:S(2)}) collective-permute-start(f32[]{:T(128)} %get-tuple-element.11), channel_id=1, source_target_pairs={{0,16},{16,0},{1,17},{17,1},{2,18},{18,2},{3,19},{19,3},{4,20},{20... | collective-permute-start | bytes 20 | tf_op jit(solution)/shard_map/ppermute | solution.py:118
  106.9 1.1 collective-permute-done.10
  112.9 3.7 %all-to-all-done.2 = bf16[16,8,1536]{2,1,0:T(8,128)(2,1)S(1)} async-done(((bf16[16,8,1536]{2,1,0:T(8,128)(2,1)}), bf16[16,8,1536]{2,1,0:T(8,128)(2,1)S(1)}, u32[]{:S(2)}, u32[]{:S(2)}) %all-to-all-start.2) | async-done | bytes 393248 | tf_op jit(solution)/shard_map/all_to_all | solution.py:31
  116.6 0.1 convert_reduce_fusion
  116.7 0.2 multiply_reduce_fusion.1
  116.9 0.1 multiply_convert_fusion
  117.0 22.8 %all_to_all.31 = bf16[16,8,1664]{2,1,0:T(8,128)(2,1)S(1)} all-to-all(bf16[16,8,1664]{2,1,0:T(8,128)(2,1)S(1)} %broadcast_in_dim.42), channel_id=1, replica_groups=mesh['x'=4,'zb'=2,'za'=2,'c'=2,'zh'=2,'y'=8] {'zh','y'}, dimensions={0} | all-to-all | bytes 851968 | tf_op jit(solution)/shard_map/all_to_all | solution.py:31
  139.8 4.7 %collective-permute-start.11 = (bf16[128,1536]{1,0:T(8,128)(2,1)S(1)}, bf16[128,1536]{1,0:T(8,128)(2,1)S(1)}, u32[]{:S(2)}, u32[]{:S(2)}) collective-permute-start(bf16[128,1536]{1,0:T(8,128)(2,1)S(1)} %slice.31), channel_id=1, source_target_pairs={{0,16},{16,0},{1,17},{17,1},{2,18},{18,2},{3,19},{19,3},{4,20},{20... | collective-permute-start | bytes 1179656 | tf_op jit(solution)/shard_map/ppermute | solution.py:129
  144.6 1.2 collective-permute-done.11
  145.9 0.2 convolution_convert_fusion.1
  146.1 0.1 reshape.60
  146.2 0.1 broadcast_in_dim.43
  146.3 0.2 pad_maximum_fusion.2
  146.5 14.6 %all_to_all.32 = bf16[16,4,1536]{2,1,0:T(4,128)(2,1)S(1)} all-to-all(bf16[16,4,1536]{2,1,0:T(4,128)(2,1)S(1)} %pad_maximum_fusion.2), channel_id=1, replica_groups=mesh['x'=4,'zb'=2,'za'=2,'c'=2,'zh'=2,'y'=8] {'x','zb','za'}, dimensions={0} | all-to-all | bytes 393216 | tf_op jit(solution)/shard_map/all_to_all | solution.py:31
  161.1 0.1 convert_reduce_fusion.2
  161.2 0.7 broadcast_in_dim.44
  162.0 5.0 %all-to-all-start.5 = ((bf16[16,3,1536]{2,1,0:T(4,128)(2,1)}), bf16[16,3,1536]{2,1,0:T(4,128)(2,1)S(1)}, u32[]{:S(2)}, u32[]{:S(2)}) async-start(bf16[16,3,1536]{2,1,0:T(4,128)(2,1)} %broadcast_in_dim.44), calls=%async_computation.5 | async-start | bytes 393216 | tf_op jit(solution)/shard_map/all_to_all | solution.py:31
  166.9 0.9 fusion.25
  167.8 0.6 slice_reduce_fusion.1
  169.1 5.4 %all-to-all-done.5 = bf16[16,3,1536]{2,1,0:T(4,128)(2,1)S(1)} async-done(((bf16[16,3,1536]{2,1,0:T(4,128)(2,1)}), bf16[16,3,1536]{2,1,0:T(4,128)(2,1)S(1)}, u32[]{:S(2)}, u32[]{:S(2)}) %all-to-all-start.5) | async-done | bytes 147488 | tf_op jit(solution)/shard_map/all_to_all | solution.py:31
  174.4 0.1 reshape.61
  174.6 4.6 %all_gather.3 = bf16[96,1536]{1,0:T(8,128)(2,1)S(1)} all-gather(bf16[48,1536]{1,0:T(8,128)(2,1)S(1)} %reshape.61), channel_id=1, replica_groups=mesh['x'=4,'zb'=2,'za'=2,'c'=2,'zh'=2,'y'=8] {'c'}, dimensions={0}, use_global_device_ids=true | all-gather | bytes 442368 | tf_op jit(solution)/shard_map/all_gather | solution.py:154
  179.1 0.9 convert_element_type.72
  (27 shorter events, 0.3 us)
Async XLA Ops:
  0.6 1.0 copy-start
  2.6 33.4 %copy-start.1 = (bf16[128,96]{0,1:T(8,128)(2,1)S(1)}, bf16[128,96]{0,1:T(8,128)(2,1)}, u32[]{:S(2)}) copy-start(bf16[128,96]{0,1:T(8,128)(2,1)} %param.3) | copy-start | bytes 73732
  36.1 10.5 %collective-permute-start = (bf16[128,96]{0,1:T(8,128)(2,1)S(1)}, bf16[128,96]{0,1:T(8,128)(2,1)S(1)}, u32[]{:S(2)}, u32[]{:S(2)}) collective-permute-start(bf16[128,96]{0,1:T(8,128)(2,1)S(1)} %copy-done.1), channel_id=1, source_target_pairs={{0,16},{16,0},{1,17},{17,1},{2,18},{18,2},{3,19},{19,3},{4,20},{20... | collective-permute-start | bytes 73736 | tf_op jit(solution)/shard_map/ppermute | solution.py:106
  41.9 26.8 %all-to-all-start.1 = ((bf16[8,8,5632]{2,1,0:T(8,128)(2,1)}), bf16[8,8,5632]{2,1,0:T(8,128)(2,1)S(1)}, u32[]{:S(2)}, u32[]{:S(2)}) async-start(bf16[8,8,5632]{2,1,0:T(8,128)(2,1)} %broadcast_in_dim.37), calls=%async_computation.1 | async-start | bytes 1441792 | tf_op jit(solution)/shard_map/all_to_all | solution.py:31
  46.5 12.0 %collective-permute-start.1 = (bf16[8,5632]{1,0:T(8,128)(2,1)S(1)}, bf16[8,5632]{1,0:T(8,128)(2,1)S(1)}, u32[]{:S(2)}, u32[]{:S(2)}) collective-permute-start(bf16[8,5632]{1,0:T(8,128)(2,1)S(1)} %get-tuple-element.9), channel_id=1, source_target_pairs={{0,8},{8,0},{64,72},{72,64},{1,9},{9,1},{65,73},{73,65},{2,10},{10... | collective-permute-start | bytes 270344 | tf_op jit(solution)/shard_map/ppermute | solution.py:63
  49.1 10.5 %collective-permute-start.2 = (bf16[8,5632]{1,0:T(8,128)(2,1)S(1)}, bf16[8,5632]{1,0:T(8,128)(2,1)S(1)}, u32[]{:S(2)}, u32[]{:S(2)}) collective-permute-start(bf16[8,5632]{1,0:T(8,128)(2,1)S(1)} %get-tuple-element.9), channel_id=1, source_target_pairs={{0,64},{8,72},{64,0},{72,8},{1,65},{9,73},{65,1},{73,9},{2,66},{10... | collective-permute-start | bytes 270344 | tf_op jit(solution)/shard_map/ppermute | solution.py:63
  53.3 8.9 %collective-permute-start.3 = (bf16[8,5632]{1,0:T(8,128)(2,1)S(1)}, bf16[8,5632]{1,0:T(8,128)(2,1)S(1)}, u32[]{:S(2)}, u32[]{:S(2)}) collective-permute-start(bf16[8,5632]{1,0:T(8,128)(2,1)S(1)} %get-tuple-element.9), channel_id=1, source_target_pairs={{0,72},{8,64},{64,8},{72,0},{1,73},{9,65},{65,9},{73,1},{2,74},{10... | collective-permute-start | bytes 270344 | tf_op jit(solution)/shard_map/ppermute | solution.py:63
  62.9 15.8 %collective-permute-start.4 = (bf16[32,5632]{1,0:T(8,128)(2,1)S(1)}, bf16[32,5632]{1,0:T(8,128)(2,1)S(1)}, u32[]{:S(2)}, u32[]{:S(2)}) collective-permute-start(bf16[32,5632]{1,0:T(8,128)(2,1)S(1)} %get-tuple-element.16), channel_id=1, source_target_pairs={{0,128},{128,0},{256,384},{384,256},{1,129},{129,1},{257,385},{385... | collective-permute-start | bytes 1081352 | tf_op jit(solution)/shard_map/ppermute | solution.py:63
  68.7 19.1 %collective-permute-start.8 = (bf16[64,5632]{1,0:T(8,128)(2,1)S(1)}, bf16[64,5632]{1,0:T(8,128)(2,1)S(1)}, u32[]{:S(2)}, u32[]{:S(2)}) collective-permute-start(bf16[64,5632]{1,0:T(8,128)(2,1)S(1)} %bitcast.30), channel_id=1, source_target_pairs={{0,32},{32,0},{1,33},{33,1},{2,34},{34,2},{3,35},{35,3},{4,36},{36... | collective-permute-start | bytes 2162696 | tf_op jit(solution)/shard_map/ppermute | solution.py:109
  71.3 19.8 %collective-permute-start.5 = (bf16[32,5632]{1,0:T(8,128)(2,1)S(1)}, bf16[32,5632]{1,0:T(8,128)(2,1)S(1)}, u32[]{:S(2)}, u32[]{:S(2)}) collective-permute-start(bf16[32,5632]{1,0:T(8,128)(2,1)S(1)} %get-tuple-element.16), channel_id=1, source_target_pairs={{0,256},{128,384},{256,0},{384,128},{1,257},{129,385},{257,1},{385... | collective-permute-start | bytes 1081352 | tf_op jit(solution)/shard_map/ppermute | solution.py:63
  76.0 16.8 %collective-permute-start.6 = (bf16[32,5632]{1,0:T(8,128)(2,1)S(1)}, bf16[32,5632]{1,0:T(8,128)(2,1)S(1)}, u32[]{:S(2)}, u32[]{:S(2)}) collective-permute-start(bf16[32,5632]{1,0:T(8,128)(2,1)S(1)} %get-tuple-element.16), channel_id=1, source_target_pairs={{0,384},{128,256},{256,128},{384,0},{1,385},{129,257},{257,129},{3... | collective-permute-start | bytes 1081352 | tf_op jit(solution)/shard_map/ppermute | solution.py:63
  79.5 14.0 %collective-permute-start.7 = (bf16[64,5632]{1,0:T(8,128)(2,1)S(1)}, bf16[64,5632]{1,0:T(8,128)(2,1)S(1)}, u32[]{:S(2)}, u32[]{:S(2)}) collective-permute-start(bf16[64,5632]{1,0:T(8,128)(2,1)S(1)} %bitcast.31), channel_id=1, source_target_pairs={{0,16},{16,0},{1,17},{17,1},{2,18},{18,2},{3,19},{19,3},{4,20},{20... | collective-permute-start | bytes 2162696 | tf_op jit(solution)/shard_map/ppermute | solution.py:111
  87.9 5.7 %collective-permute-start.9 = (bf16[64,5632]{1,0:T(8,128)(2,1)S(1)}, bf16[64,5632]{1,0:T(8,128)(2,1)S(1)}, u32[]{:S(2)}, u32[]{:S(2)}) collective-permute-start(bf16[64,5632]{1,0:T(8,128)(2,1)S(1)} %collective-permute-done.8), channel_id=1, source_target_pairs={{0,16},{16,0},{1,17},{17,1},{2,18},{18,2},{3,19},{19,3},{4,20},{20... | collective-permute-start | bytes 2162696 | tf_op jit(solution)/shard_map/ppermute | solution.py:111
  98.3 18.3 %all-to-all-start.2 = ((bf16[16,8,1536]{2,1,0:T(8,128)(2,1)}), bf16[16,8,1536]{2,1,0:T(8,128)(2,1)S(1)}, u32[]{:S(2)}, u32[]{:S(2)}) async-start(bf16[16,8,1536]{2,1,0:T(8,128)(2,1)} %fusion.11), calls=%async_computation.2 | async-start | bytes 786432 | tf_op jit(solution)/shard_map/all_to_all | solution.py:31
  104.2 3.7 %collective-permute-start.10 = (f32[]{:T(128)}, f32[]{:T(128)}, u32[]{:S(2)}, u32[]{:S(2)}) collective-permute-start(f32[]{:T(128)} %get-tuple-element.11), channel_id=1, source_target_pairs={{0,16},{16,0},{1,17},{17,1},{2,18},{18,2},{3,19},{19,3},{4,20},{20... | collective-permute-start | bytes 20 | tf_op jit(solution)/shard_map/ppermute | solution.py:118
  139.8 6.1 %collective-permute-start.11 = (bf16[128,1536]{1,0:T(8,128)(2,1)S(1)}, bf16[128,1536]{1,0:T(8,128)(2,1)S(1)}, u32[]{:S(2)}, u32[]{:S(2)}) collective-permute-start(bf16[128,1536]{1,0:T(8,128)(2,1)S(1)} %slice.31), channel_id=1, source_target_pairs={{0,16},{16,0},{1,17},{17,1},{2,18},{18,2},{3,19},{19,3},{4,20},{20... | collective-permute-start | bytes 1179656 | tf_op jit(solution)/shard_map/ppermute | solution.py:129
  162.0 12.5 %all-to-all-start.5 = ((bf16[16,3,1536]{2,1,0:T(4,128)(2,1)}), bf16[16,3,1536]{2,1,0:T(4,128)(2,1)S(1)}, u32[]{:S(2)}, u32[]{:S(2)}) async-start(bf16[16,3,1536]{2,1,0:T(4,128)(2,1)} %broadcast_in_dim.44), calls=%async_computation.5 | async-start | bytes 393216 | tf_op jit(solution)/shard_map/all_to_all | solution.py:31

commit v17 on v14

--- a/solution.py
+++ b/solution.py
@@ -146,7 +146,11 @@
 
     left = lax.dynamic_slice_in_dim(hidden, core * half, half, 1)
     left_there = lax.dynamic_slice_in_dim(hidden_there, core * half, half, 1)
-    proj_piece = dot(left, piece, COLS_T) + dot(left_there, piece_there, COLS_T)
+    proj_piece = dot(
+        jnp.concatenate([left, left_there], axis=0),
+        jnp.concatenate([piece, piece_there], axis=0),
+        COLS_T,
+    )
 
     loss_row = jnp.sum(
         wide.reshape(group_fs, mine, -1)[:, 0, full:].astype(jnp.float32), axis=0

time: 183 us -> 183 us (level)
    dot_general x8 -> x7, matrix products: 6.2 us -> 6.07 us  [dot(): return lax.dot_general(a, b, dims, preferred_element_type=jnp.float32)]
where the time goes in v17:
time: 183 us; the launch traced here: 182 us
  blocking collectives  72.4 us (40%)
  starting transfers between devices  63.4 us (35%)
  waiting for transfers between devices  19.8 us (11%)
  local copies, waits for them, and re-layouts  8.51 us (5%)
  between operations  7.74 us (4%)
  matrix products  6.07 us (3%)
  other arithmetic  4.36 us (2%)
    all_to_all x3, blocking collectives, exchange(): return lax.all_to_all(blocks, axes, split_axis=0, concat_axis=0, tiled=True)  67.8 us
    all_to_all x3, starting transfers between devices, exchange(): return lax.all_to_all(blocks, axes, split_axis=0, concat_axis=0, tiled=True)  17 us
    ppermute x3, starting transfers between devices, around(): lax.ppermute(block, axis, [(at, at ^ step) for at in range(4)])  11.4 us
    all_to_all x3, waiting for transfers between devices, exchange(): return lax.all_to_all(blocks, axes, split_axis=0, concat_axis=0, tiled=True)  10.6 us
    dot_general x7, matrix products, dot(): return lax.dot_general(a, b, dims, preferred_element_type=jnp.float32)  6.07 us
    unnamed x10, local copies, waits for them, and re-layouts  5.02 us
    ppermute x1, starting transfers between devices, body(): hidden_there = lax.ppermute(hidden_sent, 'c', SWAP)  4.89 us
    ppermute x1, starting transfers between devices, body(): lax.ppermute(there, 'c', SWAP)  4.65 us
  transfers between devices with their start and end apart: 16, of which 10 were waited for; matrix products, arithmetic and copies ran while one was open for 4% of the time, Pallas kernels for 0%

profile of v17, /device:TPU:1, one launch (start us, length us, event | category | flops | bytes accessed | tf_op | source)
XLA Modules:
  0.0 182.3 jit_solution(10234046620411830558)
XLA Ops:
  0.6 1.0 copy-done
  1.6 1.0 fusion.10
  2.6 0.9 pad_maximum_fusion.1
  3.5 32.0 %all_to_all.30 = bf16[16,8,1792]{2,1,0:T(8,128)(2,1)S(1)} all-to-all(bf16[16,8,1792]{2,1,0:T(8,128)(2,1)S(1)} %pad_maximum_fusion.1), channel_id=1, replica_groups=mesh['x'=4,'zb'=2,'za'=2,'c'=2,'zh'=2,'y'=8] {'zh','y'}, dimensions={0} | all-to-all | bytes 917504 | tf_op jit(solution)/shard_map/all_to_all | solution.py:31
  35.5 0.1 convert_reduce_fusion.1
  35.6 0.1 multiply_reduce_fusion.2
  35.7 0.1 multiply_convert_fusion.1
  35.8 0.1 fusion.15
  35.9 0.1 fusion.16
  36.1 4.9 %collective-permute-start = (bf16[128,96]{0,1:T(8,128)(2,1)S(1)}, bf16[128,96]{0,1:T(8,128)(2,1)S(1)}, u32[]{:S(2)}, u32[]{:S(2)}) collective-permute-start(bf16[128,96]{0,1:T(8,128)(2,1)S(1)} %copy-done.1), channel_id=1, source_target_pairs={{0,16},{16,0},{1,17},{17,1},{2,18},{18,2},{3,19},{19,3},{4,20},{20... | collective-permute-start | bytes 73736 | tf_op jit(solution)/shard_map/ppermute | solution.py:121
  41.0 0.9 broadcast_in_dim.37
  41.9 4.6 %all-to-all-start.1 = ((bf16[8,8,5632]{2,1,0:T(8,128)(2,1)}), bf16[8,8,5632]{2,1,0:T(8,128)(2,1)S(1)}, u32[]{:S(2)}, u32[]{:S(2)}) async-start(bf16[8,8,5632]{2,1,0:T(8,128)(2,1)} %broadcast_in_dim.37), calls=%async_computation.1 | async-start | bytes 1441792 | tf_op jit(solution)/shard_map/all_to_all | solution.py:31
  46.5 1.9 %collective-permute-start.1 = (bf16[8,5632]{1,0:T(8,128)(2,1)S(1)}, bf16[8,5632]{1,0:T(8,128)(2,1)S(1)}, u32[]{:S(2)}, u32[]{:S(2)}) collective-permute-start(bf16[8,5632]{1,0:T(8,128)(2,1)S(1)} %get-tuple-element.11), channel_id=1, source_target_pairs={{0,8},{8,0},{64,72},{72,64},{1,9},{9,1},{65,73},{73,65},{2,10},{10... | collective-permute-start | bytes 270344 | tf_op jit(solution)/shard_map/ppermute | solution.py:63
  48.5 0.6 constant_dynamic-update-slice_fusion.3
  49.1 4.2 %collective-permute-start.2 = (bf16[8,5632]{1,0:T(8,128)(2,1)S(1)}, bf16[8,5632]{1,0:T(8,128)(2,1)S(1)}, u32[]{:S(2)}, u32[]{:S(2)}) collective-permute-start(bf16[8,5632]{1,0:T(8,128)(2,1)S(1)} %get-tuple-element.11), channel_id=1, source_target_pairs={{0,64},{8,72},{64,0},{72,8},{1,65},{9,73},{65,1},{73,9},{2,66},{10... | collective-permute-start | bytes 270344 | tf_op jit(solution)/shard_map/ppermute | solution.py:63
  53.3 5.2 %collective-permute-start.3 = (bf16[8,5632]{1,0:T(8,128)(2,1)S(1)}, bf16[8,5632]{1,0:T(8,128)(2,1)S(1)}, u32[]{:S(2)}, u32[]{:S(2)}) collective-permute-start(bf16[8,5632]{1,0:T(8,128)(2,1)S(1)} %get-tuple-element.11), channel_id=1, source_target_pairs={{0,72},{8,64},{64,8},{72,0},{1,73},{9,65},{65,9},{73,1},{2,74},{10... | collective-permute-start | bytes 270344 | tf_op jit(solution)/shard_map/ppermute | solution.py:63
  58.6 0.6 constant_dynamic-update-slice_fusion.2
  59.2 0.4 collective-permute-done.2
  59.6 0.6 constant_dynamic-update-slice_fusion.1
  60.2 2.0 %collective-permute-done.3 = bf16[8,5632]{1,0:T(8,128)(2,1)S(1)} collective-permute-done((bf16[8,5632]{1,0:T(8,128)(2,1)S(1)}, bf16[8,5632]{1,0:T(8,128)(2,1)S(1)}, u32[]{:S(2)}, u32[]{:S(2)}) %collective-permute-start.3) | collective-permute-done | bytes 90144 | tf_op jit(solution)/shard_map/ppermute | solution.py:63
  62.3 0.6 constant_dynamic-update-slice_fusion
  62.9 4.4 %collective-permute-start.4 = (bf16[32,5632]{1,0:T(8,128)(2,1)S(1)}, bf16[32,5632]{1,0:T(8,128)(2,1)S(1)}, u32[]{:S(2)}, u32[]{:S(2)}) collective-permute-start(bf16[32,5632]{1,0:T(8,128)(2,1)S(1)} %get-tuple-element.22), channel_id=1, source_target_pairs={{0,384},{128,0},{256,128},{384,256},{1,385},{129,1},{257,129},{385... | collective-permute-start | bytes 1081352 | tf_op jit(solution)/shard_map/ppermute | solution.py:71
  67.3 1.9 %collective-permute-start.5 = (bf16[32,5632]{1,0:T(8,128)(2,1)S(1)}, bf16[32,5632]{1,0:T(8,128)(2,1)S(1)}, u32[]{:S(2)}, u32[]{:S(2)}) collective-permute-start(bf16[32,5632]{1,0:T(8,128)(2,1)S(1)} %get-tuple-element.22), channel_id=1, source_target_pairs={{0,128},{128,256},{256,384},{384,0},{1,129},{129,257},{257,385},{3... | collective-permute-start | bytes 1081352 | tf_op jit(solution)/shard_map/ppermute | solution.py:72
  69.2 3.6 %collective-permute-start.9 = (bf16[64,5632]{1,0:T(8,128)(2,1)S(1)}, bf16[64,5632]{1,0:T(8,128)(2,1)S(1)}, u32[]{:S(2)}, u32[]{:S(2)}) collective-permute-start(bf16[64,5632]{1,0:T(8,128)(2,1)S(1)} %bitcast.30), channel_id=1, source_target_pairs={{0,32},{32,0},{1,33},{33,1},{2,34},{34,2},{3,35},{35,3},{4,36},{36... | collective-permute-start | bytes 2162696 | tf_op jit(solution)/shard_map/ppermute | solution.py:123
  72.8 3.3 %collective-permute-start.8 = (bf16[64,5632]{1,0:T(8,128)(2,1)S(1)}, bf16[64,5632]{1,0:T(8,128)(2,1)S(1)}, u32[]{:S(2)}, u32[]{:S(2)}) collective-permute-start(bf16[64,5632]{1,0:T(8,128)(2,1)S(1)} %bitcast.31), channel_id=1, source_target_pairs={{0,16},{16,0},{1,17},{17,1},{2,18},{18,2},{3,19},{19,3},{4,20},{20... | collective-permute-start | bytes 2162696 | tf_op jit(solution)/shard_map/ppermute | solution.py:126
  76.1 2.1 %collective-permute-done.5 = bf16[32,5632]{1,0:T(8,128)(2,1)S(1)} collective-permute-done((bf16[32,5632]{1,0:T(8,128)(2,1)S(1)}, bf16[32,5632]{1,0:T(8,128)(2,1)S(1)}, u32[]{:S(2)}, u32[]{:S(2)}) %collective-permute-start.5) | collective-permute-done | bytes 360480 | tf_op jit(solution)/shard_map/ppermute | solution.py:72
  78.2 2.8 %collective-permute-start.6 = (bf16[16,5632]{1,0:T(8,128)(2,1)S(1)}, bf16[16,5632]{1,0:T(8,128)(2,1)S(1)}, u32[]{:S(2)}, u32[]{:S(2)}) collective-permute-start(bf16[16,5632]{1,0:T(8,128)(2,1)S(1)} %slice.46), channel_id=1, source_target_pairs={{0,384},{128,0},{256,128},{384,256},{1,385},{129,1},{257,129},{385... | collective-permute-start | bytes 540680 | tf_op jit(solution)/shard_map/ppermute | solution.py:75
  81.0 0.8 constant_dynamic-update-slice_fusion.7
  81.8 2.5 %collective-permute-start.7 = (bf16[16,5632]{1,0:T(8,128)(2,1)S(1)}, bf16[16,5632]{1,0:T(8,128)(2,1)S(1)}, u32[]{:S(2)}, u32[]{:S(2)}) collective-permute-start(bf16[16,5632]{1,0:T(8,128)(2,1)S(1)} %slice.47), channel_id=1, source_target_pairs={{0,128},{128,256},{256,384},{384,0},{1,129},{129,257},{257,385},{3... | collective-permute-start | bytes 540680 | tf_op jit(solution)/shard_map/ppermute | solution.py:76
  84.3 0.5 collective-permute-done.6
  84.8 0.7 constant_dynamic-update-slice_fusion.6
  85.4 1.7 collective-permute-done.9
  87.1 4.6 %collective-permute-start.10 = (bf16[64,5632]{1,0:T(8,128)(2,1)S(1)}, bf16[64,5632]{1,0:T(8,128)(2,1)S(1)}, u32[]{:S(2)}, u32[]{:S(2)}) collective-permute-start(bf16[64,5632]{1,0:T(8,128)(2,1)S(1)} %collective-permute-done.9), channel_id=1, source_target_pairs={{0,16},{16,0},{1,17},{17,1},{2,18},{18,2},{3,19},{19,3},{4,20},{20... | collective-permute-start | bytes 2162696 | tf_op jit(solution)/shard_map/ppermute | solution.py:126
  91.8 0.7 constant_dynamic-update-slice_fusion.5
  92.5 0.8 constant_dynamic-update-slice_fusion.4
  93.3 0.3 collective-permute-done.10
  93.6 2.4 %fusion = f32[128,256]{1,0:T(8,128)S(1)} fusion(bf16[128,5632]{1,0:T(8,128)(2,1)} %constant_dynamic-update-slice_fusion.4, bf16[64,5632]{1,0:T(8,128)(2,1)S(1)} %collective-permute-done.10, bf16[64,5632]{1,0:T(8,128)(2,1)S(1)} %collective-permute-done.9, bf16[64,5632]{1,0:T(8,128)(2,1)S(1)} %collective-permute-done.8, bf16[64,5632]{1,0:T(8,128)(2,1)S(1)} %bitcast.32), kind=kOutput, calls=%fused_computation | convolution fusion | flops 380633088 | bytes 4456448 | tf_op jit(solution)/shard_map/dot_general | solution.py:20
  96.1 0.6 multiply_reduce_fusion
  96.8 0.3 fusion.28
  97.1 0.3 fusion.29
  97.4 1.0 fusion.11
  98.4 8.0 %all-to-all-start.2 = ((bf16[16,8,1536]{2,1,0:T(8,128)(2,1)}), bf16[16,8,1536]{2,1,0:T(8,128)(2,1)S(1)}, u32[]{:S(2)}, u32[]{:S(2)}) async-start(bf16[16,8,1536]{2,1,0:T(8,128)(2,1)} %fusion.11), calls=%async_computation.2 | async-start | bytes 786432 | tf_op jit(solution)/shard_map/all_to_all | solution.py:31
  106.5 2.6 %collective-permute-start.11 = (f32[]{:T(128)}, f32[]{:T(128)}, u32[]{:S(2)}, u32[]{:S(2)}) collective-permute-start(f32[]{:T(128)} %get-tuple-element.15), channel_id=1, source_target_pairs={{0,16},{16,0},{1,17},{17,1},{2,18},{18,2},{3,19},{19,3},{4,20},{20... | collective-permute-start | bytes 20 | tf_op jit(solution)/shard_map/ppermute | solution.py:133
  109.0 0.9 collective-permute-done.11
  114.9 5.2 %all-to-all-done.2 = bf16[16,8,1536]{2,1,0:T(8,128)(2,1)S(1)} async-done(((bf16[16,8,1536]{2,1,0:T(8,128)(2,1)}), bf16[16,8,1536]{2,1,0:T(8,128)(2,1)S(1)}, u32[]{:S(2)}, u32[]{:S(2)}) %all-to-all-start.2) | async-done | bytes 393248 | tf_op jit(solution)/shard_map/all_to_all | solution.py:31
  120.0 0.1 convert_reduce_fusion
  120.1 0.2 multiply_reduce_fusion.1
  120.3 0.1 multiply_convert_fusion
  120.4 25.3 %all_to_all.31 = bf16[16,8,1664]{2,1,0:T(8,128)(2,1)S(1)} all-to-all(bf16[16,8,1664]{2,1,0:T(8,128)(2,1)S(1)} %broadcast_in_dim.42), channel_id=1, replica_groups=mesh['x'=4,'zb'=2,'za'=2,'c'=2,'zh'=2,'y'=8] {'zh','y'}, dimensions={0} | all-to-all | bytes 851968 | tf_op jit(solution)/shard_map/all_to_all | solution.py:31
  145.7 4.5 %collective-permute-start.12 = (bf16[128,1536]{1,0:T(8,128)(2,1)S(1)}, bf16[128,1536]{1,0:T(8,128)(2,1)S(1)}, u32[]{:S(2)}, u32[]{:S(2)}) collective-permute-start(bf16[128,1536]{1,0:T(8,128)(2,1)S(1)} %slice.63), channel_id=1, source_target_pairs={{0,16},{16,0},{1,17},{17,1},{2,18},{18,2},{3,19},{19,3},{4,20},{20... | collective-permute-start | bytes 1179656 | tf_op jit(solution)/shard_map/ppermute | solution.py:144
  150.3 1.2 collective-permute-done.12
  151.6 0.2 convolution_convert_fusion.1
  151.8 0.1 reshape.60
  152.0 0.2 pad_maximum_fusion.2
  152.2 10.5 %all_to_all.32 = bf16[16,4,1536]{2,1,0:T(4,128)(2,1)S(1)} all-to-all(bf16[16,4,1536]{2,1,0:T(4,128)(2,1)S(1)} %pad_maximum_fusion.2), channel_id=1, replica_groups=mesh['x'=4,'zb'=2,'za'=2,'c'=2,'zh'=2,'y'=8] {'x','zb','za'}, dimensions={0} | all-to-all | bytes 393216 | tf_op jit(solution)/shard_map/all_to_all | solution.py:31
  162.7 0.1 convert_reduce_fusion.2
  162.8 0.7 broadcast_in_dim.44
  163.6 4.4 %all-to-all-start.5 = ((bf16[16,3,1536]{2,1,0:T(4,128)(2,1)}), bf16[16,3,1536]{2,1,0:T(4,128)(2,1)S(1)}, u32[]{:S(2)}, u32[]{:S(2)}) async-start(bf16[16,3,1536]{2,1,0:T(4,128)(2,1)} %broadcast_in_dim.44), calls=%async_computation.5 | async-start | bytes 393216 | tf_op jit(solution)/shard_map/all_to_all | solution.py:31
  168.0 0.9 fusion.25
  168.8 0.6 slice_reduce_fusion.1
  170.1 5.5 %all-to-all-done.5 = bf16[16,3,1536]{2,1,0:T(4,128)(2,1)S(1)} async-done(((bf16[16,3,1536]{2,1,0:T(4,128)(2,1)}), bf16[16,3,1536]{2,1,0:T(4,128)(2,1)S(1)}, u32[]{:S(2)}, u32[]{:S(2)}) %all-to-all-start.5) | async-done | bytes 147488 | tf_op jit(solution)/shard_map/all_to_all | solution.py:31
  175.6 0.1 reshape.61
  175.7 4.6 %all_gather.3 = bf16[96,1536]{1,0:T(8,128)(2,1)S(1)} all-gather(bf16[48,1536]{1,0:T(8,128)(2,1)S(1)} %reshape.61), channel_id=1, replica_groups=mesh['x'=4,'zb'=2,'za'=2,'c'=2,'zh'=2,'y'=8] {'c'}, dimensions={0}, use_global_device_ids=true | all-gather | bytes 442368 | tf_op jit(solution)/shard_map/all_gather | solution.py:169
  180.3 0.9 convert_element_type.72
  (35 shorter events, 0.5 us)
Async XLA Ops:
  0.6 1.0 copy-start
  2.6 33.4 %copy-start.1 = (bf16[128,96]{0,1:T(8,128)(2,1)S(1)}, bf16[128,96]{0,1:T(8,128)(2,1)}, u32[]{:S(2)}) copy-start(bf16[128,96]{0,1:T(8,128)(2,1)} %param.3) | copy-start | bytes 73732
  36.1 10.5 %collective-permute-start = (bf16[128,96]{0,1:T(8,128)(2,1)S(1)}, bf16[128,96]{0,1:T(8,128)(2,1)S(1)}, u32[]{:S(2)}, u32[]{:S(2)}) collective-permute-start(bf16[128,96]{0,1:T(8,128)(2,1)S(1)} %copy-done.1), channel_id=1, source_target_pairs={{0,16},{16,0},{1,17},{17,1},{2,18},{18,2},{3,19},{19,3},{4,20},{20... | collective-permute-start | bytes 73736 | tf_op jit(solution)/shard_map/ppermute | solution.py:121
  41.9 27.3 %all-to-all-start.1 = ((bf16[8,8,5632]{2,1,0:T(8,128)(2,1)}), bf16[8,8,5632]{2,1,0:T(8,128)(2,1)S(1)}, u32[]{:S(2)}, u32[]{:S(2)}) async-start(bf16[8,8,5632]{2,1,0:T(8,128)(2,1)} %broadcast_in_dim.37), calls=%async_computation.1 | async-start | bytes 1441792 | tf_op jit(solution)/shard_map/all_to_all | solution.py:31
  46.5 12.0 %collective-permute-start.1 = (bf16[8,5632]{1,0:T(8,128)(2,1)S(1)}, bf16[8,5632]{1,0:T(8,128)(2,1)S(1)}, u32[]{:S(2)}, u32[]{:S(2)}) collective-permute-start(bf16[8,5632]{1,0:T(8,128)(2,1)S(1)} %get-tuple-element.11), channel_id=1, source_target_pairs={{0,8},{8,0},{64,72},{72,64},{1,9},{9,1},{65,73},{73,65},{2,10},{10... | collective-permute-start | bytes 270344 | tf_op jit(solution)/shard_map/ppermute | solution.py:63
  49.1 10.5 %collective-permute-start.2 = (bf16[8,5632]{1,0:T(8,128)(2,1)S(1)}, bf16[8,5632]{1,0:T(8,128)(2,1)S(1)}, u32[]{:S(2)}, u32[]{:S(2)}) collective-permute-start(bf16[8,5632]{1,0:T(8,128)(2,1)S(1)} %get-tuple-element.11), channel_id=1, source_target_pairs={{0,64},{8,72},{64,0},{72,8},{1,65},{9,73},{65,1},{73,9},{2,66},{10... | collective-permute-start | bytes 270344 | tf_op jit(solution)/shard_map/ppermute | solution.py:63
  53.3 8.9 %collective-permute-start.3 = (bf16[8,5632]{1,0:T(8,128)(2,1)S(1)}, bf16[8,5632]{1,0:T(8,128)(2,1)S(1)}, u32[]{:S(2)}, u32[]{:S(2)}) collective-permute-start(bf16[8,5632]{1,0:T(8,128)(2,1)S(1)} %get-tuple-element.11), channel_id=1, source_target_pairs={{0,72},{8,64},{64,8},{72,0},{1,73},{9,65},{65,9},{73,1},{2,74},{10... | collective-permute-start | bytes 270344 | tf_op jit(solution)/shard_map/ppermute | solution.py:63
  62.9 13.2 %collective-permute-start.4 = (bf16[32,5632]{1,0:T(8,128)(2,1)S(1)}, bf16[32,5632]{1,0:T(8,128)(2,1)S(1)}, u32[]{:S(2)}, u32[]{:S(2)}) collective-permute-start(bf16[32,5632]{1,0:T(8,128)(2,1)S(1)} %get-tuple-element.22), channel_id=1, source_target_pairs={{0,384},{128,0},{256,128},{384,256},{1,385},{129,1},{257,129},{385... | collective-permute-start | bytes 1081352 | tf_op jit(solution)/shard_map/ppermute | solution.py:71
  67.3 10.9 %collective-permute-start.5 = (bf16[32,5632]{1,0:T(8,128)(2,1)S(1)}, bf16[32,5632]{1,0:T(8,128)(2,1)S(1)}, u32[]{:S(2)}, u32[]{:S(2)}) collective-permute-start(bf16[32,5632]{1,0:T(8,128)(2,1)S(1)} %get-tuple-element.22), channel_id=1, source_target_pairs={{0,128},{128,256},{256,384},{384,0},{1,129},{129,257},{257,385},{3... | collective-permute-start | bytes 1081352 | tf_op jit(solution)/shard_map/ppermute | solution.py:72
  69.2 17.9 %collective-permute-start.9 = (bf16[64,5632]{1,0:T(8,128)(2,1)S(1)}, bf16[64,5632]{1,0:T(8,128)(2,1)S(1)}, u32[]{:S(2)}, u32[]{:S(2)}) collective-permute-start(bf16[64,5632]{1,0:T(8,128)(2,1)S(1)} %bitcast.30), channel_id=1, source_target_pairs={{0,32},{32,0},{1,33},{33,1},{2,34},{34,2},{3,35},{35,3},{4,36},{36... | collective-permute-start | bytes 2162696 | tf_op jit(solution)/shard_map/ppermute | solution.py:123
  72.8 20.5 %collective-permute-start.8 = (bf16[64,5632]{1,0:T(8,128)(2,1)S(1)}, bf16[64,5632]{1,0:T(8,128)(2,1)S(1)}, u32[]{:S(2)}, u32[]{:S(2)}) collective-permute-start(bf16[64,5632]{1,0:T(8,128)(2,1)S(1)} %bitcast.31), channel_id=1, source_target_pairs={{0,16},{16,0},{1,17},{17,1},{2,18},{18,2},{3,19},{19,3},{4,20},{20... | collective-permute-start | bytes 2162696 | tf_op jit(solution)/shard_map/ppermute | solution.py:126
  78.2 6.5 %collective-permute-start.6 = (bf16[16,5632]{1,0:T(8,128)(2,1)S(1)}, bf16[16,5632]{1,0:T(8,128)(2,1)S(1)}, u32[]{:S(2)}, u32[]{:S(2)}) collective-permute-start(bf16[16,5632]{1,0:T(8,128)(2,1)S(1)} %slice.46), channel_id=1, source_target_pairs={{0,384},{128,0},{256,128},{384,256},{1,385},{129,1},{257,129},{385... | collective-permute-start | bytes 540680 | tf_op jit(solution)/shard_map/ppermute | solution.py:75
  81.8 10.0 %collective-permute-start.7 = (bf16[16,5632]{1,0:T(8,128)(2,1)S(1)}, bf16[16,5632]{1,0:T(8,128)(2,1)S(1)}, u32[]{:S(2)}, u32[]{:S(2)}) collective-permute-start(bf16[16,5632]{1,0:T(8,128)(2,1)S(1)} %slice.47), channel_id=1, source_target_pairs={{0,128},{128,256},{256,384},{384,0},{1,129},{129,257},{257,385},{3... | collective-permute-start | bytes 540680 | tf_op jit(solution)/shard_map/ppermute | solution.py:76
  87.1 6.4 %collective-permute-start.10 = (bf16[64,5632]{1,0:T(8,128)(2,1)S(1)}, bf16[64,5632]{1,0:T(8,128)(2,1)S(1)}, u32[]{:S(2)}, u32[]{:S(2)}) collective-permute-start(bf16[64,5632]{1,0:T(8,128)(2,1)S(1)} %collective-permute-done.9), channel_id=1, source_target_pairs={{0,16},{16,0},{1,17},{17,1},{2,18},{18,2},{3,19},{19,3},{4,20},{20... | collective-permute-start | bytes 2162696 | tf_op jit(solution)/shard_map/ppermute | solution.py:126
  98.4 21.6 %all-to-all-start.2 = ((bf16[16,8,1536]{2,1,0:T(8,128)(2,1)}), bf16[16,8,1536]{2,1,0:T(8,128)(2,1)S(1)}, u32[]{:S(2)}, u32[]{:S(2)}) async-start(bf16[16,8,1536]{2,1,0:T(8,128)(2,1)} %fusion.11), calls=%async_computation.2 | async-start | bytes 786432 | tf_op jit(solution)/shard_map/all_to_all | solution.py:31
  106.5 3.5 %collective-permute-start.11 = (f32[]{:T(128)}, f32[]{:T(128)}, u32[]{:S(2)}, u32[]{:S(2)}) collective-permute-start(f32[]{:T(128)} %get-tuple-element.15), channel_id=1, source_target_pairs={{0,16},{16,0},{1,17},{17,1},{2,18},{18,2},{3,19},{19,3},{4,20},{20... | collective-permute-start | bytes 20 | tf_op jit(solution)/shard_map/ppermute | solution.py:133
  145.7 5.9 %collective-permute-start.12 = (bf16[128,1536]{1,0:T(8,128)(2,1)S(1)}, bf16[128,1536]{1,0:T(8,128)(2,1)S(1)}, u32[]{:S(2)}, u32[]{:S(2)}) collective-permute-start(bf16[128,1536]{1,0:T(8,128)(2,1)S(1)} %slice.63), channel_id=1, source_target_pairs={{0,16},{16,0},{1,17},{17,1},{2,18},{18,2},{3,19},{19,3},{4,20},{20... | collective-permute-start | bytes 1179656 | tf_op jit(solution)/shard_map/ppermute | solution.py:144
  163.6 12.0 %all-to-all-start.5 = ((bf16[16,3,1536]{2,1,0:T(4,128)(2,1)}), bf16[16,3,1536]{2,1,0:T(4,128)(2,1)S(1)}, u32[]{:S(2)}, u32[]{:S(2)}) async-start(bf16[16,3,1536]{2,1,0:T(4,128)(2,1)} %broadcast_in_dim.44), calls=%async_computation.5 | async-start | bytes 393216 | tf_op jit(solution)/shard_map/all_to_all | solution.py:31
